TPU v7x, 32 devices: a whole 2x2x4 slice. The times are simulated.
32 devices in a mesh: lat: 4 (over z), lon: 8 (over y, x, core).
Axes of the slice: x: 2, y: 2, z: 4, core: 2. Of those that a mesh axis runs over, the one named last changes fastest.
Arguments:
- state: bfloat16 [32, 3072, 128], P('lat', 'lon'), may hold values from -6 to 6
- forcing: bfloat16 [32, 3072, 128], P('lat', 'lon'), may hold values from -4 to 4
- cotangent: bfloat16 [32, 3072, 128], P('lat', 'lon'), may hold values from -6 to 6
- land_mask: int32 [32, 3072], P('lat', 'lon'), may hold values 0 or 1
- dw_weight: bfloat16 [7, 7, 128], replicated, may hold values from -0.875 to 0.875
- dw_bias: float32 [128], replicated, may hold values from -3 to 3
- norm_gain: float32 [128], replicated, may hold values from 0.5 to 1.5
- norm_bias: float32 [128], replicated, may hold values from -3 to 3
- up_weight: bfloat16 [128, 512], replicated, may hold values from -0.5 to 0.5
- up_bias: float32 [512], replicated, may hold values from -3 to 3
- down_weight: bfloat16 [512, 128], replicated, may hold values from -0.25 to 0.25
- down_bias: float32 [128], replicated, may hold values from -3 to 3
- layer_scale: float32 [128], replicated, may hold values from 0.3 to 1
- owner: int32 [196608, 1], P(('lat', 'lon')), may hold values from 0 to 31; in each aligned block of 6144 rows (0 to 6143, 6144 to 12287, ...) at most 384 rows name the same one
- atmos_cell: int32 [196608], P(('lat', 'lon')), may hold values from 0 to 511
- weight_index: int32 [196608], P(('lat', 'lon')), may hold values from 0 to 15
- intersection_weights: float32 [16], replicated, may hold values from 0.1 to 1
Outputs:
- result: bfloat16 [32, 3072, 128], P('lat', 'lon')
- grad_dw: float32 [7, 7, 128], replicated
- grad_up: float32 [128, 512], replicated
- grad_down: float32 [512, 128], replicated
- forcing_grad: float32 [16384, 128], P(('lat', 'lon'))
Inputs may be any that keep to these rules, and one draw needn't show every extreme that they name: At most 384 entries of one device name the same owner, and in every draw some device's entries name some owner exactly 384 times.
All inputs are finite; a program needn't handle non-finite values. No bound on the sum of `land_mask` on one device may be relied on, other than what follows from the above.
Results may differ from a plain program's by a relative error of at most 0.0071.
Values may be sent and summed in bfloat16 or wider, within the bound.
No kernel may reach another device: no remote copies, remote signals or barrier semaphores. Data moves between devices by JAX's collectives and lax.ppermute only.
A program may use at most 128 MiB of HBM per device.

v0:
```python
import jax
import jax.numpy as jnp
from jax import lax
from jax.sharding import PartitionSpec as P

A_DEV = 512


gelu_scale = 0.7978845608028654
cubic_coef = 0.044715


def extended(block, sides, width, periodic):
    for axis, dim in sides:
        count = lax.axis_size(axis)
        forward = [(i, i + 1) for i in range(count - 1)]
        if periodic:
            forward.append((count - 1, 0))
        backward = [(target, source) for source, target in forward]
        low = lax.ppermute(
            lax.slice_in_dim(block, block.shape[dim] - width, None, axis=dim), axis, forward
        )
        high = lax.ppermute(lax.slice_in_dim(block, 0, width, axis=dim), axis, backward)
        block = jnp.concatenate([low, block, high], axis=dim)
    return block


def partner_2(array, axis, distance):
    return lax.ppermute(array, axis, [(i, i ^ 1 << distance) for i in range(lax.axis_size(axis))])


def gelu_pair(pre):
    inner = gelu_scale * (pre + cubic_coef * pre * pre * pre)
    tanh_value = jnp.tanh(inner)
    value = 0.5 * pre * (1.0 + tanh_value)
    slope = 0.5 * (1.0 + tanh_value) + 0.5 * pre * (1.0 - tanh_value * tanh_value) * gelu_scale * (
        1.0 + 3.0 * cubic_coef * pre * pre
    )
    return (value, slope)


def depthwise(padded, kernel):
    channels = padded.shape[-1]
    convolved = lax.conv_general_dilated(
        padded[None],
        kernel[:, :, None, :],
        (1, 1),
        "VALID",
        dimension_numbers=("NHWC", "HWIO", "NHWC"),
        feature_group_count=channels,
        preferred_element_type=jnp.float32,
    )
    return convolved[0]


def block_pass(
    padded,
    state,
    forcing,
    cotangent,
    land,
    dw_weight,
    dw_bias,
    norm_gain,
    norm_bias,
    up_weight,
    up_bias,
    down_weight,
    down_bias,
    layer_scale,
):
    tile_rows, tile_cols, channels = state.shape
    conv = depthwise(padded, dw_weight) + dw_bias
    average = jnp.mean(conv, axis=-1, keepdims=True)
    centred = conv - average
    variance = jnp.mean(centred * centred, axis=-1, keepdims=True)
    inv_std = lax.rsqrt(variance + 1e-06)
    normed = centred * inv_std
    mixed = (normed * norm_gain + norm_bias + forcing.astype(jnp.float32)).astype(jnp.bfloat16)
    flat = mixed.reshape(-1, channels)
    pre = jnp.dot(flat, up_weight, preferred_element_type=jnp.float32) + up_bias
    activated, slope = gelu_pair(pre)
    hidden = activated.astype(jnp.bfloat16)
    projected = jnp.dot(hidden, down_weight, preferred_element_type=jnp.float32) + down_bias
    ocean = land.astype(jnp.float32).reshape(-1, 1)
    result = (
        ocean * (state.reshape(-1, channels).astype(jnp.float32) + layer_scale * projected)
    ).astype(jnp.bfloat16)
    grad_out = (ocean * layer_scale * cotangent.reshape(-1, channels).astype(jnp.float32)).astype(
        jnp.bfloat16
    )
    down_term = jnp.dot(hidden.T, grad_out, preferred_element_type=jnp.float32)
    grad_hidden = jnp.dot(grad_out, down_weight.T, preferred_element_type=jnp.float32)
    grad_pre = (grad_hidden * slope).astype(jnp.bfloat16)
    up_term = jnp.dot(flat.T, grad_pre, preferred_element_type=jnp.float32)
    grad_mixed = jnp.dot(grad_pre, up_weight.T, preferred_element_type=jnp.float32).reshape(
        tile_rows, tile_cols, channels
    )
    gained = grad_mixed * norm_gain
    grad_conv = (
        inv_std
        * (
            gained
            - jnp.mean(gained, axis=-1, keepdims=True)
            - normed * jnp.mean(gained * normed, axis=-1, keepdims=True)
        )
    ).astype(jnp.bfloat16)
    conv_term = depthwise(padded, grad_conv)
    return (
        result.reshape(tile_rows, tile_cols, channels),
        grad_mixed,
        conv_term,
        up_term,
        down_term,
    )


def on_device(
    state,
    forcing,
    cotangent,
    land_mask,
    dw_weight,
    dw_bias,
    norm_gain,
    norm_bias,
    up_weight,
    up_bias,
    down_weight,
    down_bias,
    layer_scale,
    owner,
    atmos_cell,
    weight_index,
    intersection_weights,
):
    margin = dw_weight.shape[0] // 2
    tile_rows, tile_cols, channels = state.shape
    lat_count = lax.axis_size("lat")
    lon_count = lax.axis_size("lon")
    lon_ext = extended(state, (("lon", 1),), margin, True)
    padded = extended(lon_ext, (("lat", 0),), margin, False)
    north_rim = lon_ext[tile_rows - margin :]
    bit_total = lon_count.bit_length() - 1
    partner = north_rim
    for bit_number in range(bit_total):
        partner = partner_2(partner, "lon", bit_number)
    mirrored = partner[::-1, ::-1]
    northmost = lax.axis_index("lat") == lat_count - 1
    north_rows = jnp.where(northmost, mirrored, padded[tile_rows + margin :])
    padded = jnp.concatenate([padded[: tile_rows + margin], north_rows], axis=0)
    result, grad_mixed, conv_term, up_term, down_term = block_pass(
        padded,
        state,
        forcing,
        cotangent,
        land_mask,
        dw_weight,
        dw_bias,
        norm_gain,
        norm_bias,
        up_weight,
        up_bias,
        down_weight,
        down_bias,
        layer_scale,
    )
    conv_sum, up_sum, down_sum = lax.psum((conv_term, up_term, down_term), ("lat", "lon"))
    scale = float(tile_rows * lat_count * tile_cols * lon_count) ** (-0.5)
    grad_dw = conv_sum * scale
    grad_up = up_sum * scale
    grad_down = down_sum * scale
    entries = owner.shape[0]
    devices = lat_count * lon_count
    capacity = max(2, 2 * entries // devices)
    table_hit = (
        weight_index[:, None] == jnp.arange(intersection_weights.shape[0], dtype=jnp.int32)[None, :]
    )
    entry_weights = jnp.sum(jnp.where(table_hit, intersection_weights[None, :], 0.0), axis=1)
    per_entry = jnp.repeat(
        grad_mixed.reshape(tile_rows * tile_cols, channels),
        entries // (tile_rows * tile_cols),
        axis=0,
    )
    values = (entry_weights[:, None] * per_entry).astype(jnp.bfloat16)
    dest_owner = owner[:, 0]
    sorting = jnp.argsort(dest_owner, stable=True)
    sorted_owner = dest_owner[sorting]
    owner_ids = jnp.arange(devices, dtype=jnp.int32)
    owner_load = jnp.sum((dest_owner[:, None] == owner_ids[None, :]).astype(jnp.int32), axis=0)
    owner_start = jnp.cumsum(owner_load) - owner_load
    first_slot = jnp.sum(
        jnp.where(sorted_owner[:, None] == owner_ids[None, :], owner_start[None, :], 0), axis=1
    )
    slot_rank = jnp.arange(entries, dtype=jnp.int32) - first_slot
    slot_index = sorted_owner * capacity + slot_rank
    send_rows = (
        jnp.zeros((devices * capacity, channels), jnp.bfloat16).at[slot_index].set(values[sorting])
    )
    send_cells = jnp.zeros((devices * capacity,), jnp.int32).at[slot_index].set(atmos_cell[sorting])
    recv_rows, recv_cells = (
        lax.all_to_all(
            send_rows.reshape(devices, capacity, channels),
            ("lat", "lon"),
            split_axis=0,
            concat_axis=0,
            tiled=True,
        ),
        lax.all_to_all(
            send_cells.reshape(devices, capacity),
            ("lat", "lon"),
            split_axis=0,
            concat_axis=0,
            tiled=True,
        ),
    )
    forcing_grad = jax.ops.segment_sum(
        recv_rows.reshape(-1, channels).astype(jnp.float32),
        recv_cells.reshape(-1),
        num_segments=A_DEV,
    )
    return (result, grad_dw, grad_up, grad_down, forcing_grad)


def solution(mesh):
    in_specs = (
        P("lat", "lon", None),
        P("lat", "lon", None),
        P("lat", "lon", None),
        P("lat", "lon"),
        P(),
        P(),
        P(),
        P(),
        P(),
        P(),
        P(),
        P(),
        P(),
        P(("lat", "lon"), None),
        P(("lat", "lon")),
        P(("lat", "lon")),
        P(),
    )
    out_specs = (P("lat", "lon", None), P(), P(), P(), P(("lat", "lon"), None))
    return jax.shard_map(
        on_device, mesh=mesh, in_specs=in_specs, out_specs=out_specs, check_vma=False
    )
```

profile of v0, /device:TPU:4, one launch (start us, length us, event | category | flops | bytes accessed | tf_op | source)
XLA Modules:
  0.0 476.1 jit_solution(713081557946477315)
XLA Ops:
  8.0 2.6 collective-permute-start.1
  10.7 7.4 %sort.17 = (s32[6144]{0:T(1024)}, s32[6144]{0:T(1024)S(1)}) sort(s32[6144]{0:T(1024)} %bitcast.83, s32[6144]{0:T(1024)S(1)} %iota.16), dimensions={0}, to_apply=%region_7.8 | sort | flops 79872 | bytes 98304 | tf_op jit(solution)/shard_map/jit(argsort)/sort | solution.py:187
  19.1 34.3 %gather_fusion = s32[6144]{0:T(1024)S(1)} fusion(s32[6144]{0:T(1024)S(1)} %bitcast.85, s32[6144]{0:T(1024)S(1)} %fusion.47), kind=kCustom, calls=%fused_computation | custom fusion | bytes 73728 | tf_op jit(solution)/shard_map/gather | solution.py:188
  54.2 1.4 collective-permute-done.3
  56.2 34.3 %gather_fusion.1 = s32[6144]{0:T(1024)S(1)} fusion(s32[6144]{0:T(1024)S(1)} %copy-done.2, s32[6144]{0:T(1024)S(1)} %fusion.47), kind=kCustom, calls=%fused_computation.1 | custom fusion | bytes 73728 | tf_op jit(solution)/shard_map/gather | solution.py:200
  90.5 23.6 %scatter_custom_fusion = s32[12288]{0:T(1024)} fusion(s32[6144]{0:T(1024)S(1)} %bitcast.100, s32[6144]{0:T(1024)S(1)} %gather_fusion.1, s32[]{:T(128)} %constant.46.clone.1), kind=kCustom, calls=%fused_computation.83 | custom fusion | bytes 49156 | tf_op jit(solution)/shard_map/scatter | solution.py:200
  114.1 6.1 %all-to-all-start = ((s32[32,1,384]{2,1,0:T(1,128)}), s32[32,1,384]{2,1,0:T(1,128)}, u32[]{:S(2)}, u32[]{:S(2)}) async-start(s32[32,1,384]{2,1,0:T(1,128)} %bitcast.18), calls=%async_computation | async-start | bytes 98304 | tf_op jit(solution)/shard_map/all_to_all | solution.py:209
  122.0 1.4 fusion.23
  123.3 4.7 collective-permute-start.2
  128.2 2.8 collective-permute-done.5
  132.1 1.9 collective-permute-done.2
  134.0 1.5 fusion.54
  136.9 5.5 %fusion.41 = f32[8,8,49,128]{3,1,2,0:T(8,128)S(1)} fusion(bf16[14,1,7,6,128]{4,2,3,0,1:T(8,128)(2,1)S(1)} %slice.25, bf16[14,1,8,49,128]{4,2,3,0,1:T(8,128)(2,1)S(1)} %copy.68, pred[8,49]{0,1:T(8,128)(4,1)S(1)} %copy-done.36, bf16[7,7,1,128]{3,1,0,2:T(8,128)(2,1)S(1)} %bitcast.103), kind=kOutput, calls=%fused_computation.61 | convolution fusion | flops 44470272 | bytes 3174024 | tf_op jit(solution)/shard_map/conv_general_dilated | solution.py:44
  143.5 1.6 multiply_reduce_fusion
  147.4 1.6 copy.77
  149.0 3.2 add_convert_fusion
  157.0 3.6 multiply_convert_fusion
  160.7 4.7 fusion.6
  165.5 2.4 multiply_reduce_fusion.1
  169.0 1.9 multiply_convert_fusion.1
  170.9 55.3 %scatter_custom_fusion.1 = bf16[12288,128]{1,0:T(8,128)(2,1)} fusion(s32[6144]{0:T(1024)} %bitcast.101, bf16[6144,128]{1,0:T(8,128)(2,1)} %multiply_convert_fusion.1, s32[6144]{0:T(1024)S(1)} %fusion.47, bf16[]{:T(256)} %constant.50.clone.1), kind=kCustom, calls=%fused_computation.52 | custom fusion | bytes 3146240 | tf_op jit(solution)/shard_map/scatter | solution.py:198
  226.2 7.0 %all-to-all-start.1 = ((bf16[32,384,128]{2,1,0:T(8,128)(2,1)}), bf16[32,384,128]{2,1,0:T(8,128)(2,1)}, u32[]{:S(2)}, u32[]{:S(2)}) async-start(bf16[32,384,128]{2,1,0:T(8,128)(2,1)} %bitcast.92), calls=%async_computation.1 | async-start | bytes 6291456 | tf_op jit(solution)/shard_map/all_to_all | solution.py:202
  235.0 3.6 fusion.56
  238.6 1.7 fusion.57
  240.4 5.9 %fusion.33 = bf16[8,384,1,128]{3,0,1,2:T(8,128)(2,1)S(1)} fusion(f32[8,384,1,128]{3,1,0,2:T(8,128)S(1)} %bitcast.91, f32[8,384]{0,1:T(8,128)} %copy.78, f32[8,384]{0,1:T(8,128)S(1)} %broadcast_multiply_fusion.2, f32[128]{0:T(128)S(1)} %copy-done.24, f32[8,384]{0,1:T(8,128)} %copy.74, f32[128]{0:T(128)S(1)} %copy-done.27, f32[8,384]{0,1:T(8,128)} %add_rsqrt_fusion, ...), kind=kLoop, calls=%fused_computation.47 | loop fusion | flops 3538944 | bytes 3982336 | tf_op jit(solution)/shard_map/convert_element_type | solution.py:107
  246.4 20.4 %fusion.14 = f32[1,7,7,128]{3,0,2,1:T(1,128)S(1)} fusion(bf16[1,14,390,128]{3,2,1,0:T(8,128)(2,1)S(1)} %copy-done.11, bf16[8,384,1,128]{3,0,1,2:T(8,128)(2,1)S(1)} %fusion.33), kind=kOutput, calls=%fused_computation.26 | convolution fusion | flops 38535168 | bytes 2209280 | tf_op jit(solution)/shard_map/conv_general_dilated | solution.py:44
  266.8 1.9 fusion.12
  268.7 60.1 %psum.21 = f32[7,7,128]{2,1,0:T(8,128)S(1)} all-reduce(f32[7,7,128]{2,1,0:T(8,128)S(1)} %bitcast.97), channel_id=1, replica_groups=mesh['lat'=4,'lon'=8] {'lat','lon'}, use_global_device_ids=true, to_apply=%region_4.5 | all-reduce | flops 6272 | bytes 50176 | tf_op jit(solution)/shard_map/psum | solution.py:168
  329.4 54.5 %all-reduce.3.cloned.1.call-done = (f32[128,512]{1,0:T(8,128)}, f32[512,128]{1,0:T(8,128)}) async-done(((f32[128,512]{1,0:T(8,128)}, f32[512,128]{1,0:T(8,128)}), (f32[128,512]{1,0:T(8,128)}, f32[512,128]{1,0:T(8,128)})) %all-reduce.3.cloned.1.call-update) | async-done | bytes 524304 | tf_op jit(solution)/shard_map/psum | solution.py:168
  383.9 1.7 broadcast_multiply_fusion
  385.6 1.7 broadcast_multiply_fusion.1
  387.3 81.5 %scatter_custom_fusion.2 = f32[512,128]{1,0:T(8,128)} fusion(s32[12288]{0:T(1024)} %bitcast.19, bf16[12288,128]{1,0:T(8,128)(2,1)} %bitcast.25, f32[]{:T(128)} %constant.18.clone.1), kind=kCustom, calls=%fused_computation.15 | custom fusion | flops 3145728 | bytes 3408384 | tf_op jit(solution)/shard_map/scatter-add | solution.py:217
  (126 shorter events, 19.1 us)
Async XLA Ops:
  7.2 149.0 %copy-start = (bf16[128,512]{1,0:T(8,128)(2,1)S(1)}, bf16[128,512]{1,0:T(8,128)(2,1)}, u32[]{:S(2)}) copy-start(bf16[128,512]{1,0:T(8,128)(2,1)} %param.25) | copy-start | bytes 393220
  7.2 11.9 %copy-start.1 = (s32[6144,1]{0,1:T(1,128)S(1)}, s32[6144,1]{0,1:T(1,128)}, u32[]{:S(2)}) copy-start(s32[6144,1]{0,1:T(1,128)} %param.30) | copy-start | bytes 73732
  8.0 45.7 %collective-permute-start = (bf16[8,3,128]{2,1,0:T(4,128)(2,1)S(1)}, bf16[8,3,128]{2,1,0:T(4,128)(2,1)S(1)}, u32[]{:S(2)}, u32[]{:S(2)}) collective-permute-start(bf16[8,3,128]{2,1,0:T(4,128)(2,1)S(1)} %get-tuple-element.15), channel_id=1, source_target_pairs={{0,1},{1,2},{2,3},{3,4},{4,5},{5,6},{6,7},{7,0},{8,9},{9,10},{10,1... | collective-permute-start | bytes 18440 | tf_op jit(solution)/shard_map/ppermute | solution.py:20
  8.0 45.6 %collective-permute-start.1 = (bf16[8,3,128]{2,1,0:T(4,128)(2,1)S(1)}, bf16[8,3,128]{2,1,0:T(4,128)(2,1)S(1)}, u32[]{:S(2)}, u32[]{:S(2)}) collective-permute-start(bf16[8,3,128]{2,1,0:T(4,128)(2,1)S(1)} %get-tuple-element.16), channel_id=1, source_target_pairs={{1,0},{2,1},{3,2},{4,3},{5,4},{6,5},{7,6},{0,7},{9,8},{10,9},{11,1... | collective-permute-start | bytes 18440 | tf_op jit(solution)/shard_map/ppermute | solution.py:23
  19.1 34.6 %copy-start.4 = (bf16[8,384,128]{2,1,0:T(8,128)(2,1)S(1)}, bf16[8,384,128]{2,1,0:T(8,128)(2,1)}, u32[]{:S(2)}) copy-start(bf16[8,384,128]{2,1,0:T(8,128)(2,1)} %param.17) | copy-start | bytes 2359300
  53.9 1.7 collective-permute-start.3
  55.5 66.1 %collective-permute-start.4 = (bf16[3,390,128]{2,1,0:T(8,128)(2,1)S(1)}, bf16[3,390,128]{2,1,0:T(8,128)(2,1)S(1)}, u32[]{:S(2)}, u32[]{:S(2)}) collective-permute-start(bf16[3,390,128]{2,1,0:T(8,128)(2,1)S(1)} %collective-permute-done.3), channel_id=1, source_target_pairs={{0,2},{1,3},{2,0},{3,1},{4,6},{5,7},{6,4},{7,5},{8,10},{9,11},{10,... | collective-permute-start | bytes 898568 | tf_op jit(solution)/shard_map/ppermute | solution.py:29
  56.2 34.4 %copy-start.21 = (s32[6144,1]{0,1:T(1,128)}, s32[6144,1]{0,1:T(1,128)S(1)}, u32[]{:S(2)}) copy-start(s32[6144,1]{0,1:T(1,128)S(1)} %compare_select_fusion) | copy-start | bytes 73732
  56.2 64.0 %copy-start.25 = (s32[8,384]{1,0:T(8,128)S(1)}, s32[8,384]{1,0:T(8,128)}, u32[]{:S(2)}) copy-start(s32[8,384]{1,0:T(8,128)} %param.20) | copy-start | bytes 36868
  56.2 65.8 %copy-start.13 = (bf16[8,384,128]{2,1,0:T(8,128)(2,1)S(1)}, bf16[8,384,128]{2,1,0:T(8,128)(2,1)}, u32[]{:S(2)}) copy-start(bf16[8,384,128]{2,1,0:T(8,128)(2,1)} %param.19) | copy-start | bytes 2359300
  56.2 65.8 %copy-start.29 = (f32[128]{0:T(128)S(1)}, f32[128]{0:T(128)}, u32[]{:S(2)}) copy-start(f32[128]{0:T(128)} %param.29) | copy-start | bytes 1540
  90.5 37.6 %copy-start.20 = (s32[6144]{0:T(1024)S(1)}, s32[6144]{0:T(1024)}, u32[]{:S(2)}) copy-start(s32[6144]{0:T(1024)} %param.32) | copy-start | bytes 73732
  90.5 37.6 %copy-start.28 = (f32[16]{0:T(128)S(1)}, f32[16]{0:T(128)}, u32[]{:S(2)}) copy-start(f32[16]{0:T(128)} %param.33) | copy-start | bytes 196
  114.1 112.1 %all-to-all-start = ((s32[32,1,384]{2,1,0:T(1,128)}), s32[32,1,384]{2,1,0:T(1,128)}, u32[]{:S(2)}, u32[]{:S(2)}) async-start(s32[32,1,384]{2,1,0:T(1,128)} %bitcast.18), calls=%async_computation | async-start | bytes 98304 | tf_op jit(solution)/shard_map/all_to_all | solution.py:209
  120.3 8.0 %copy-start.14 = (f32[3072]{0:T(1024)}, f32[3072]{0:T(1024)S(1)}, u32[]{:S(2)}) copy-start(f32[3072]{0:T(1024)S(1)} %mul.209) | copy-start | bytes 36868
  120.3 11.8 %collective-permute-start.6 = (bf16[3,390,128]{2,1,0:T(8,128)(2,1)S(1)}, bf16[3,390,128]{2,1,0:T(8,128)(2,1)S(1)}, u32[]{:S(2)}, u32[]{:S(2)}) collective-permute-start(bf16[3,390,128]{2,1,0:T(8,128)(2,1)S(1)} %get-tuple-element.13), channel_id=1, source_target_pairs={{8,0},{16,8},{24,16},{9,1},{17,9},{25,17},{10,2},{18,10},{26,18},{... | collective-permute-start | bytes 898568 | tf_op jit(solution)/shard_map/ppermute | solution.py:23
  121.6 9.5 %collective-permute-start.5 = (bf16[3,390,128]{2,1,0:T(8,128)(2,1)S(1)}, bf16[3,390,128]{2,1,0:T(8,128)(2,1)S(1)}, u32[]{:S(2)}, u32[]{:S(2)}) collective-permute-start(bf16[3,390,128]{2,1,0:T(8,128)(2,1)S(1)} %collective-permute-done.4), channel_id=1, source_target_pairs={{0,4},{1,5},{2,6},{3,7},{4,0},{5,1},{6,2},{7,3},{8,12},{9,13},{10,... | collective-permute-start | bytes 898568 | tf_op jit(solution)/shard_map/ppermute | solution.py:29
  123.3 10.7 %collective-permute-start.2 = (bf16[3,390,128]{2,1,0:T(8,128)(2,1)S(1)}, bf16[3,390,128]{2,1,0:T(8,128)(2,1)S(1)}, u32[]{:S(2)}, u32[]{:S(2)}) collective-permute-start(bf16[3,390,128]{2,1,0:T(8,128)(2,1)S(1)} %get-tuple-element.14), channel_id=1, source_target_pairs={{0,8},{8,16},{16,24},{1,9},{9,17},{17,25},{2,10},{10,18},{18,26},{... | collective-permute-start | bytes 898568 | tf_op jit(solution)/shard_map/ppermute | solution.py:20
  160.7 4.8 %copy-start.17 = (f32[3072]{0:T(1024)S(1)}, f32[3072]{0:T(1024)}, u32[]{:S(2)}) copy-start(f32[3072]{0:T(1024)} %div.22) | copy-start | bytes 36868
  160.7 4.8 %copy-start.23 = (f32[128]{0:T(128)S(1)}, f32[128]{0:T(128)}, u32[]{:S(2)}) copy-start(f32[128]{0:T(128)} %param.22) | copy-start | bytes 1540
  160.7 4.8 %copy-start.26 = (f32[128]{0:T(128)S(1)}, f32[128]{0:T(128)}, u32[]{:S(2)}) copy-start(f32[128]{0:T(128)} %param.23) | copy-start | bytes 1540
  226.2 7.1 %copy-start.18 = (f32[3072]{0:T(1024)S(1)}, f32[3072]{0:T(1024)}, u32[]{:S(2)}) copy-start(f32[3072]{0:T(1024)} %get-tuple-element.7) | copy-start | bytes 36868
  226.2 7.1 %copy-start.19 = (f32[3072]{0:T(1024)S(1)}, f32[3072]{0:T(1024)}, u32[]{:S(2)}) copy-start(f32[3072]{0:T(1024)} %get-tuple-element.8) | copy-start | bytes 36868
  226.2 161.1 %all-to-all-start.1 = ((bf16[32,384,128]{2,1,0:T(8,128)(2,1)}), bf16[32,384,128]{2,1,0:T(8,128)(2,1)}, u32[]{:S(2)}, u32[]{:S(2)}) async-start(bf16[32,384,128]{2,1,0:T(8,128)(2,1)} %bitcast.92), calls=%async_computation.1 | async-start | bytes 6291456 | tf_op jit(solution)/shard_map/all_to_all | solution.py:202
  233.2 150.7 %all-reduce.3.cloned.1.call-start = ((), (), s32[]{:S(2)}) async-start(), calls=%async_computation.2 | async-start | bytes 1048576 | tf_op jit(solution)/shard_map/psum | solution.py:168
  240.4 5.9 %copy-start.11 = (bf16[1,14,390,128]{3,2,1,0:T(8,128)(2,1)S(1)}, bf16[1,14,390,128]{3,2,1,0:T(8,128)(2,1)}, u32[]{:S(2)}) copy-start(bf16[1,14,390,128]{3,2,1,0:T(8,128)(2,1)} %get-tuple-element.11) | copy-start | bytes 4193284
  246.3 20.4 %copy-start.5 = (bf16[8,384,128]{2,1,0:T(8,128)(2,1)S(1)}, bf16[8,384,128]{2,1,0:T(8,128)(2,1)}, u32[]{:S(2)}) copy-start(bf16[8,384,128]{2,1,0:T(8,128)(2,1)} %param.17) | copy-start | bytes 2359300
  246.3 20.4 %copy-start.10 = (bf16[3072,512]{1,0:T(8,128)(2,1)S(1)}, bf16[3072,512]{1,0:T(8,128)(2,1)}, u32[]{:S(2)}) copy-start(bf16[3072,512]{1,0:T(8,128)(2,1)} %get-tuple-element.17) | copy-start | bytes 9437188
  246.3 20.4 %copy-start.15 = (f32[3072]{0:T(1024)S(1)}, f32[3072]{0:T(1024)}, u32[]{:S(2)}) copy-start(f32[3072]{0:T(1024)} %copy-done.14) | copy-start | bytes 36868
  246.3 20.4 %copy-start.30 = (f32[128]{0:T(128)S(1)}, f32[128]{0:T(128)}, u32[]{:S(2)}) copy-start(f32[128]{0:T(128)} %param.29) | copy-start | bytes 1540
  246.3 20.4 %copy-start.32 = (bf16[512,128]{1,0:T(8,128)(2,1)S(1)}, bf16[512,128]{1,0:T(8,128)(2,1)}, u32[]{:S(2)}) copy-start(bf16[512,128]{1,0:T(8,128)(2,1)} %param.27) | copy-start | bytes 393220
  246.4 20.4 %copy-start.35 = (f32[128]{0:T(128)S(1)}, f32[128]{0:T(128)}, u32[]{:S(2)}) copy-start(f32[128]{0:T(128)} %param.28) | copy-start | bytes 1540
  (15 other events, 33.3 us)
Sparse Core Ops, SparseCore 0:
  240.5 143.4 all-reduce.2
where the time goes:
time: 482 us; the launch traced here: 476 us
  local copies, waits for them, and re-layouts  162 us (34%)
  other arithmetic  111 us (23%)
  waiting for transfers between devices  60.6 us (13%)
  blocking collectives  60.1 us (12%)
  matrix products  43.8 us (9%)
  starting transfers between devices  22.9 us (5%)
  between operations  15.2 us (3%)
    scatter-add x1, other arithmetic, on_device(): jax.ops.segment_sum(recv_rows.reshape(-1, channels).astype(jnp.float32),...  81.5 us
    psum x1, blocking collectives, on_device(): lax.psum((conv_term, up_term, down_term), ('lat', 'lon'))  60.1 us
    scatter x1, local copies, waits for them, and re-layouts, on_device(): jnp.zeros((devices * capacity, channels), jnp.bfloat16).at[slot_index]  55.3 us
    psum x1, waiting for transfers between devices, on_device(): lax.psum((conv_term, up_term, down_term), ('lat', 'lon'))  54.5 us
    gather x1, local copies, waits for them, and re-layouts, on_device(): sorted_owner = dest_owner[sorting]  34.3 us
    gather x1, local copies, waits for them, and re-layouts, on_device(): atmos_cell[sorting]  34.3 us
    conv_general_dilated x2, matrix products, depthwise(): lax.conv_general_dilated(padded[None], kernel[:, :, None, :], (1, 1), 'VA...  25.8 us
    scatter x1, local copies, waits for them, and re-layouts, on_device(): jnp.zeros((devices * capacity,), jnp.int32).at[slot_index]  23.6 us
  transfers between devices with their start and end apart: 10, of which 4 were waited for; matrix products, arithmetic and copies ran while one was open for 49% of the time, Pallas kernels for 0%

commit v1 on v0

v1 whole, which is shorter than its diff:
```python
import functools

import jax
import jax.numpy as jnp
from jax import lax
from jax.experimental import pallas as pl
from jax.experimental.pallas import tpu as pltpu
from jax.sharding import PartitionSpec as P

A_DEV = 512
PAD = 8
BATCH = 16
gelu_scale = 0.7978845608028654
cubic_coef = 0.044715
f32 = jnp.float32
bf16 = jnp.bfloat16


def params(limit=56 << 20):
    return pltpu.CompilerParams(vmem_limit_bytes=limit)


def vmem():
    return pl.BlockSpec(memory_space=pltpu.VMEM)


def smem():
    return pl.BlockSpec(memory_space=pltpu.SMEM)


def gelu_pair(pre):
    square = pre * pre
    tanh_value = jnp.tanh(pre * (gelu_scale + gelu_scale * cubic_coef * square))
    half = 0.5 + 0.5 * tanh_value
    value = pre * half
    slope = half + pre * (1.0 - tanh_value * tanh_value) * (
        0.5 * gelu_scale + 1.5 * gelu_scale * cubic_coef * square
    )
    return (value, slope)


def main_kernel(
    state, left, right, south, north, forcing, cotangent, land, dw, dwb, gain, nbias,
    up, upb, down, downb, scale, up_t, down_t,
    result, grad_mixed, padded, grad_conv, grads, conv, acc_up, acc_down,
):
    rows, cols, channels = state.shape
    taps = 7
    margin = 3
    height = rows + 2 * margin
    padded[0:margin] = south[...].astype(f32)
    padded[height - margin : height] = north[...].astype(f32)
    for r in range(rows):
        padded[r + margin, PAD : PAD + cols, :] = state[r].astype(f32)
        padded[r + margin, PAD - margin : PAD, :] = left[r].astype(f32)
        padded[r + margin, PAD + cols : PAD + cols + margin, :] = right[r].astype(f32)

    def conv_step(step, _):
        base = pl.multiple_of(step * 8, 8)
        sums = [jnp.broadcast_to(dwb[...], (8, channels)) for _ in range(rows)]
        for b in range(taps):
            weights = [
                jnp.broadcast_to(dw[pl.ds(a * taps + b, 1), :], (8, channels)) for a in range(taps)
            ]
            for h in range(height):
                x = padded[h, pl.ds(base + (PAD - margin + b), 8), :]
                for a in range(taps):
                    if 0 <= h - a < rows:
                        sums[h - a] = sums[h - a] + weights[a] * x
        for r in range(rows):
            conv[r, pl.ds(base, 8), :] = sums[r]
        return 0

    lax.fori_loop(0, cols // 8, conv_step, 0)
    acc_up[...] = jnp.zeros_like(acc_up)
    acc_down[...] = jnp.zeros_like(acc_down)
    group = 2
    size = group * cols

    def mlp_step(step, _):
        first = step * group
        field = conv[pl.ds(first, group)].reshape(size, channels)
        average = jnp.mean(field, axis=-1, keepdims=True)
        centred = field - average
        variance = jnp.mean(centred * centred, axis=-1, keepdims=True)
        inv_std = lax.rsqrt(variance + 1e-06)
        normed = centred * inv_std
        force = forcing[pl.ds(first, group)].reshape(size, channels).astype(f32)
        mixed = (normed * gain[...] + nbias[...] + force).astype(bf16)
        pre = jnp.dot(mixed, up[...], preferred_element_type=f32) + upb[...]
        activated, slope = gelu_pair(pre)
        hidden = activated.astype(bf16)
        projected = jnp.dot(hidden, down[...], preferred_element_type=f32) + downb[...]
        ocean = jnp.concatenate(
            [
                jnp.broadcast_to(land[pl.ds(first + k, 1), :].astype(f32), (channels, cols)).T
                for k in range(group)
            ],
            axis=0,
        )
        own = state[pl.ds(first, group)].reshape(size, channels).astype(f32)
        out = ocean * (own + scale[...] * projected)
        result[pl.ds(first, group)] = out.astype(bf16).reshape(group, cols, channels)
        cot = cotangent[pl.ds(first, group)].reshape(size, channels).astype(f32)
        grad_out = (ocean * scale[...] * cot).astype(bf16)
        grad_hidden = jnp.dot(grad_out, down_t[...], preferred_element_type=f32)
        grad_pre = (grad_hidden * slope).astype(bf16)
        gmix = jnp.dot(grad_pre, up_t[...], preferred_element_type=f32)
        grad_mixed[pl.ds(pl.multiple_of(step * size, 8), size), :] = gmix
        gained = gmix * gain[...]
        gconv = inv_std * (
            gained
            - jnp.mean(gained, axis=-1, keepdims=True)
            - normed * jnp.mean(gained * normed, axis=-1, keepdims=True)
        )
        grad_conv[pl.ds(first, group)] = gconv.reshape(group, cols, channels)
        contract = (((0,), (0,)), ((), ()))
        acc_up[...] += lax.dot_general(mixed, grad_pre, contract, preferred_element_type=f32)
        acc_down[...] += lax.dot_general(grad_out, hidden, contract, preferred_element_type=f32)
        return 0

    lax.fori_loop(0, rows // group, mlp_step, 0)
    blocks = up.shape[1] // channels
    for k in range(blocks):
        part = slice(k * channels, (k + 1) * channels)
        grads[k] = acc_up[:, part]
        grads[blocks + k] = acc_down[:, part].T


def conv_grad_kernel(padded, grad_conv, out):
    rows, cols, channels = grad_conv.shape
    taps = 7
    margin = 3
    height = rows + 2 * margin
    out[...] = jnp.zeros_like(out)
    for b in range(taps):

        def step_of(step, sums):
            base = pl.multiple_of(step * 8, 8)
            sums = list(sums)
            gc = [grad_conv[r, pl.ds(base, 8), :] for r in range(rows)]
            for h in range(height):
                x = padded[h, pl.ds(base + (PAD - margin + b), 8), :]
                for a in range(taps):
                    if 0 <= h - a < rows:
                        sums[a] = sums[a] + gc[h - a] * x
            return tuple(sums)

        zero = jnp.zeros((8, channels), f32)
        sums = lax.fori_loop(0, cols // 8, step_of, (zero,) * taps)
        for a in range(taps):
            out[pl.ds(a * taps + b, 1), :] = jnp.sum(sums[a], axis=0, keepdims=True)


def regrid_kernel(target, weight, clash, terms, keep, send, table, sem):
    half = keep.shape[0]
    chunk = 512

    def clear(step, _):
        table[pl.ds(pl.multiple_of(step * chunk, chunk), chunk), :] = jnp.zeros((chunk, 128), f32)
        return 0

    lax.fori_loop(0, table.shape[0] // chunk, clear, 0)

    def add_batch(step, _):
        first = step * BATCH

        def one(k):
            e = first + k
            row = step * (BATCH // 2) + k // 2
            return target[e], weight[e] * terms[pl.ds(row, 1), :]

        @pl.when(clash[step] == 0)
        def _():
            entries = [one(k) for k in range(BATCH)]
            sums = [table[pl.ds(t, 1), :] + v for t, v in entries]
            for (t, _), s in zip(entries, sums):
                table[pl.ds(t, 1), :] = s

        @pl.when(clash[step] != 0)
        def _():
            for k in range(BATCH):
                t, v = one(k)
                table[pl.ds(t, 1), :] = table[pl.ds(t, 1), :] + v

        return 0

    lax.fori_loop(0, target.shape[0] // BATCH, add_batch, 0)

    copy = pltpu.make_async_copy(table.at[pl.ds(0, half)], keep, sem)
    copy.start()

    def give(step, _):
        at = pl.multiple_of(step * chunk, chunk)
        send[pl.ds(at, chunk), :] = table[pl.ds(half + at, chunk), :].astype(bf16)
        return 0

    lax.fori_loop(0, half // chunk, give, 0)
    copy.wait()


def swap_bit(array, bit, lon_bits):
    axis, distance = ("lon", bit) if bit < lon_bits else ("lat", bit - lon_bits)
    pairs = [(i, i ^ (1 << distance)) for i in range(lax.axis_size(axis))]
    return lax.ppermute(array, axis, pairs)


def on_device(
    state, forcing, cotangent, land_mask, dw_weight, dw_bias, norm_gain, norm_bias,
    up_weight, up_bias, down_weight, down_bias, layer_scale, owner, atmos_cell, weight_index,
    intersection_weights,
):
    margin = dw_weight.shape[0] // 2
    rows, cols, channels = state.shape
    hid = up_weight.shape[1]
    lat_count = lax.axis_size("lat")
    lon_count = lax.axis_size("lon")
    lat = lax.axis_index("lat")
    lon = lax.axis_index("lon")
    lon_bits = lon_count.bit_length() - 1
    lat_bits = lat_count.bit_length() - 1
    devices = lat_count * lon_count

    forward = [(i, (i + 1) % lon_count) for i in range(lon_count)]
    backward = [(t, s) for s, t in forward]
    left = lax.ppermute(state[:, cols - margin :], "lon", forward)
    right = lax.ppermute(state[:, :margin], "lon", backward)

    def widened(lo, hi):
        gap = jnp.zeros((margin, PAD - margin, channels), bf16)
        return jnp.concatenate([gap, left[lo:hi], state[lo:hi], right[lo:hi], gap], axis=1)

    low_rows = widened(0, margin)
    high_rows = widened(rows - margin, rows)
    folded = high_rows[::-1, ::-1]
    odd = lat % 2 == 1
    last = lat == lat_count - 1
    even_pairs, odd_pairs = [], []
    for l in range(lat_count):
        for j in range(lon_count):
            here = l * lon_count + j
            even_pairs.append((here, (l ^ 1) * lon_count + j))
            up_l = l + 1 if l % 2 else l - 1
            if l == lat_count - 1:
                odd_pairs.append((here, l * lon_count + lon_count - 1 - j))
            elif up_l >= 0:
                odd_pairs.append((here, up_l * lon_count + j))
    got_even = lax.ppermute(jnp.where(odd, low_rows, high_rows), ("lat", "lon"), even_pairs)
    got_odd = lax.ppermute(
        jnp.where(last, folded, jnp.where(odd, high_rows, low_rows)), ("lat", "lon"), odd_pairs
    )
    south = jnp.where(odd, got_even, got_odd)
    north = jnp.where(odd, got_odd, got_even)

    me = lat * lon_count + lon
    relative = owner[:, 0] ^ me
    lon_rest = list(range(1, lon_bits))
    lat_rest = list(range(lon_bits + lat_bits - 1, lon_bits - 1, -1))
    orders = [lon_rest + lat_rest, lon_rest[::-1] + lat_rest, lat_rest + lon_rest]
    widths = [160, 160, 192]
    blocks = devices // 2
    half_rows = blocks * A_DEV
    target = jnp.zeros_like(relative)
    start = 0
    for order, width in zip(orders, widths):
        number = jnp.zeros_like(relative)
        for bit in order:
            number = number * 2 + ((relative >> bit) & 1)
        place = blocks * start + number * width + (atmos_cell - start)
        target = jnp.where((atmos_cell >= start) & (atmos_cell < start + width), place, target)
        start += width
    target = target + (relative & 1) * half_rows
    table_hit = (
        weight_index[:, None] == jnp.arange(intersection_weights.shape[0], dtype=jnp.int32)[None, :]
    )
    entry_weights = jnp.sum(jnp.where(table_hit, intersection_weights[None, :], 0.0), axis=1)
    batches = target.reshape(-1, BATCH)
    clash = jnp.zeros((batches.shape[0],), jnp.int32)
    for shift in range(1, BATCH // 2 + 1):
        same = batches == jnp.roll(batches, shift, axis=1)
        clash = clash | jnp.max(same.astype(jnp.int32), axis=1)

    row = lambda v: v.reshape(1, -1)
    cells = rows * cols
    shape = jax.ShapeDtypeStruct
    result, grad_mixed, padded, grad_conv, grads = pl.pallas_call(
        main_kernel,
        out_shape=(
            shape((rows, cols, channels), bf16),
            shape((cells, channels), f32),
            shape((rows + 2 * margin, cols + 2 * PAD, channels), f32),
            shape((rows, cols, channels), f32),
            shape((2 * hid // channels, channels, channels), f32),
        ),
        in_specs=[vmem()] * 19,
        out_specs=[vmem()] * 5,
        scratch_shapes=[
            pltpu.VMEM((rows, cols, channels), f32),
            pltpu.VMEM((channels, hid), f32),
            pltpu.VMEM((channels, hid), f32),
        ],
        compiler_params=params(),
        name="block",
    )(
        state, left, right, south, north, forcing, cotangent, land_mask,
        dw_weight.reshape(-1, channels).astype(f32), row(dw_bias), row(norm_gain), row(norm_bias),
        up_weight, row(up_bias), down_weight, row(down_bias), row(layer_scale),
        up_weight.T, down_weight.T,
    )

    keep, send = pl.pallas_call(
        regrid_kernel,
        out_shape=(shape((half_rows, channels), f32), shape((half_rows, channels), bf16)),
        in_specs=[smem(), smem(), smem(), vmem()],
        out_specs=[pl.BlockSpec(memory_space=pl.ANY), vmem()],
        scratch_shapes=[pltpu.VMEM((2 * half_rows, channels), f32), pltpu.SemaphoreType.DMA],
        compiler_params=params(),
        name="regrid",
    )(target, entry_weights, clash, grad_mixed)

    dw_rows = -(-dw_weight.shape[0] * dw_weight.shape[1] // devices) * devices
    grad_dw = pl.pallas_call(
        conv_grad_kernel,
        out_shape=shape((dw_rows, channels), f32),
        in_specs=[vmem()] * 2,
        out_specs=vmem(),
        compiler_params=params(),
        name="conv_grad",
    )(padded, grad_conv)

    got = swap_bit(send, 0, lon_bits)
    parts = []
    start = 0
    for order, width in zip(orders, widths):
        lo, hi = blocks * start, blocks * (start + width)
        parts.append(keep[lo:hi] + got[lo:hi].astype(f32))
        start += width
    for stage in range(len(orders[0])):
        for q, order in enumerate(orders):
            middle = parts[q].shape[0] // 2
            arrived = swap_bit(parts[q][middle:].astype(bf16), order[stage], lon_bits)
            parts[q] = parts[q][:middle] + arrived.astype(f32)
    forcing_grad = jnp.concatenate(parts, axis=0)

    size_all = 2 * hid + dw_rows
    total = jnp.concatenate([grads.reshape(2 * hid, channels), grad_dw], axis=0)
    bits = list(range(lon_bits + lat_bits))
    for bit in bits:
        middle = total.shape[0] // 2
        mine = (me >> bit) & 1
        out = lax.dynamic_slice_in_dim(total, (1 - mine) * middle, middle, 0).astype(bf16)
        arrived = swap_bit(out, bit, lon_bits)
        total = lax.dynamic_slice_in_dim(total, mine * middle, middle, 0) + arrived.astype(f32)
    total = total.astype(bf16)
    for bit in bits[::-1]:
        arrived = swap_bit(total, bit, lon_bits)
        mine = ((me >> bit) & 1) == 1
        total = jnp.where(
            mine,
            jnp.concatenate([arrived, total], axis=0),
            jnp.concatenate([total, arrived], axis=0),
        )
    scale = float(cells * devices) ** (-0.5)
    total = total.astype(f32) * scale
    grad_up = total[:hid].reshape(hid // channels, channels, channels)
    grad_up = grad_up.transpose(1, 0, 2).reshape(channels, hid)
    grad_down = total[hid : 2 * hid]
    grad_dw = total[2 * hid : 2 * hid + dw_weight.shape[0] * dw_weight.shape[1]]
    return (result, grad_dw.reshape(dw_weight.shape), grad_up, grad_down, forcing_grad)


def solution(mesh):
    grid = P("lat", "lon", None)
    in_specs = (grid, grid, grid, P("lat", "lon")) + (P(),) * 9
    in_specs += (P(("lat", "lon"), None), P(("lat", "lon")), P(("lat", "lon")), P())
    out_specs = (grid, P(), P(), P(), P(("lat", "lon"), None))
    return jax.shard_map(
        on_device, mesh=mesh, in_specs=in_specs, out_specs=out_specs, check_vma=False
    )
```

time: 482 us -> 165 us (0.34)
  the two profiles are of different devices: /device:TPU:4 before, /device:TPU:0 now
where the time goes in v1:
time: 165 us
  Pallas kernels  56.5 us (34%)
  waiting for transfers between devices  49.1 us (30%)
  starting transfers between devices  39.5 us (24%)
  other arithmetic  9.88 us (6%)
  local copies, waits for them, and re-layouts  8.59 us (5%)
    ppermute x23, waiting for transfers between devices, swap_bit(): return lax.ppermute(array, axis, pairs)  45.2 us
    ppermute x23, starting transfers between devices, swap_bit(): return lax.ppermute(array, axis, pairs)  30.2 us
    pallas_call x1, Pallas kernels, on_device(): pl.pallas_call(regrid_kernel, out_shape=(shape((half_rows, channels), f32...  25.4 us
    pallas_call x1, Pallas kernels, on_device(): pl.pallas_call(main_kernel, out_shape=(shape((rows, cols, channels), bf16...  20.8 us
    pallas_call x1, Pallas kernels, on_device(): pl.pallas_call(conv_grad_kernel, out_shape=shape((dw_rows, channels), f32...  10.3 us
    ppermute x1, starting transfers between devices, on_device(): lax.ppermute(jnp.where(odd, low_rows, high_rows), ('lat', 'lon'), even_pa...  5.14 us
    ppermute x1, waiting for transfers between devices, on_device(): lax.ppermute(jnp.where(odd, low_rows, high_rows), ('lat', 'lon'), even_pa...  3.85 us
    add x2, other arithmetic, on_device(): parts.append(keep[lo:hi] + got[lo:hi].astype(f32))  3.46 us
  transfers between devices with their start and end apart: 27, of which 17 were waited for; matrix products, arithmetic and copies ran while one was open for 7% of the time, Pallas kernels for 15%

profile of v1, /device:TPU:0, one launch (start us, length us, event | category | flops | bytes accessed | tf_op | source)
XLA Modules:
  0.0 164.7 jit_solution(14345052372603758456)
XLA Ops:
  1.9 2.9 %collective-permute-start.1 = (bf16[8,3,128]{2,1,0:T(4,128)(2,1)S(1)}, bf16[8,3,128]{2,1,0:T(4,128)(2,1)S(1)}, u32[]{:S(2)}, u32[]{:S(2)}) collective-permute-start(bf16[8,3,128]{2,1,0:T(4,128)(2,1)S(1)} %get-tuple-element.31), channel_id=1, source_target_pairs={{1,0},{2,1},{3,2},{4,3},{5,4},{6,5},{7,6},{0,7},{9,8},{10,9},{11,1... | collective-permute-start | bytes 18440 | tf_op jit(solution)/shard_map/ppermute | solution.py:227
  8.8 5.1 %collective-permute-start.2 = (bf16[3,400,128]{2,1,0:T(8,128)(2,1)S(1)}, bf16[3,400,128]{2,1,0:T(8,128)(2,1)S(1)}, u32[]{:S(2)}, u32[]{:S(2)}) collective-permute-start(bf16[3,400,128]{2,1,0:T(8,128)(2,1)S(1)} %get-tuple-element.36), channel_id=1, source_target_pairs={{0,8},{1,9},{2,10},{3,11},{4,12},{5,13},{6,14},{7,15},{8,0},{9,1},... | collective-permute-start | bytes 921608 | tf_op jit(solution)/shard_map/ppermute | solution.py:248
  17.3 3.9 %collective-permute-done.2 = bf16[3,400,128]{2,1,0:T(8,128)(2,1)S(1)} collective-permute-done((bf16[3,400,128]{2,1,0:T(8,128)(2,1)S(1)}, bf16[3,400,128]{2,1,0:T(8,128)(2,1)S(1)}, u32[]{:S(2)}, u32[]{:S(2)}) %collective-permute-start.2) | collective-permute-done | bytes 307232 | tf_op jit(solution)/shard_map/ppermute | solution.py:248
  22.1 20.8 %block.1 = (bf16[8,384,128]{2,1,0:T(8,128)(2,1)}, f32[3072,128]{1,0:T(8,128)}, f32[14,400,128]{2,1,0:T(8,128)}, f32[8,384,128]{2,1,0:T(8,128)}, f32[8,128,128]{2,1,0:T(8,128)}) custom-call(bf16[8,384,128]{2,1,0:T(8,128)(2,1)} %state.1, bf16[8,3,128]{2,1,0:T(4,128)(2,1)} %copy-done.5, bf16[8,3,128]{2,1,0:T(4,128)(2,1)} %copy-done.6, ...), custom_call_target="tpu_custom_call" | custom-call | tf_op jit(solution)/shard_map/block/pallas_call | solution.py:286
  42.9 10.3 %conv_grad.1 = f32[64,128]{1,0:T(8,128)} custom-call(f32[14,400,128]{2,1,0:T(8,128)} %get-tuple-element.14.padded, f32[8,384,128]{2,1,0:T(8,128)} %get-tuple-element.15.grad_conv), custom_call_target="tpu_custom_call" | custom-call | tf_op jit(solution)/shard_map/conv_grad/pallas_call | solution.py:322
  56.9 3.0 %collective-permute-done.5 = bf16[272,128]{1,0:T(8,128)(2,1)S(1)} collective-permute-done((bf16[272,128]{1,0:T(8,128)(2,1)S(1)}, bf16[272,128]{1,0:T(8,128)(2,1)S(1)}, u32[]{:S(2)}, u32[]{:S(2)}) %collective-permute-start.5) | collective-permute-done | bytes 69664 | tf_op jit(solution)/shard_map/ppermute | solution.py:205
  59.9 1.6 collective-permute-start.6
  62.3 25.4 %regrid.1 = (f32[8192,128]{1,0:T(8,128)}, bf16[8192,128]{1,0:T(8,128)(2,1)}) custom-call(s32[6144]{0:T(1024)} %copy-done.4, f32[6144]{0:T(1024)} %select_reduce_fusion.weight, s32[384]{0:T(512)} %or_or_fusion.clash, f32[3072,128]{1,0:T(8,128)} %get-tuple-element.16.terms), custom_call_target="tpu_custom_call" | custom-call | tf_op jit(solution)/shard_map/regrid/pallas_call | solution.py:311
  87.9 1.8 %collective-permute-start.7 = (bf16[68,128]{1,0:T(8,128)(2,1)S(1)}, bf16[68,128]{1,0:T(8,128)(2,1)S(1)}, u32[]{:S(2)}, u32[]{:S(2)}) collective-permute-start(bf16[68,128]{1,0:T(8,128)(2,1)S(1)} %dynamic-slice_convert_fusion.2), channel_id=1, source_target_pairs={{0,8},{8,0},{16,24},{24,16},{1,9},{9,1},{17,25},{25,17},{2,10},{10... | collective-permute-start | bytes 52232 | tf_op jit(solution)/shard_map/ppermute | solution.py:205
  89.7 2.0 %collective-permute-done.7 = bf16[68,128]{1,0:T(8,128)(2,1)S(1)} collective-permute-done((bf16[68,128]{1,0:T(8,128)(2,1)S(1)}, bf16[68,128]{1,0:T(8,128)(2,1)S(1)}, u32[]{:S(2)}, u32[]{:S(2)}) %collective-permute-start.7) | collective-permute-done | bytes 17440 | tf_op jit(solution)/shard_map/ppermute | solution.py:205
  91.7 2.0 %collective-permute-start.8 = (bf16[34,128]{1,0:T(8,128)(2,1)S(1)}, bf16[34,128]{1,0:T(8,128)(2,1)S(1)}, u32[]{:S(2)}, u32[]{:S(2)}) collective-permute-start(bf16[34,128]{1,0:T(8,128)(2,1)S(1)} %dynamic-slice_convert_fusion.3), channel_id=1, source_target_pairs={{0,16},{8,24},{16,0},{24,8},{1,17},{9,25},{17,1},{25,9},{2,18},{10... | collective-permute-start | bytes 26120 | tf_op jit(solution)/shard_map/ppermute | solution.py:205
  93.8 2.6 %collective-permute-done.8 = bf16[34,128]{1,0:T(8,128)(2,1)S(1)} collective-permute-done((bf16[34,128]{1,0:T(8,128)(2,1)S(1)}, bf16[34,128]{1,0:T(8,128)(2,1)S(1)}, u32[]{:S(2)}, u32[]{:S(2)}) %collective-permute-start.8) | collective-permute-done | bytes 8736 | tf_op jit(solution)/shard_map/ppermute | solution.py:205
  96.4 2.0 %collective-permute-start.9 = (bf16[34,128]{1,0:T(8,128)(2,1)S(1)}, bf16[34,128]{1,0:T(8,128)(2,1)S(1)}, u32[]{:S(2)}, u32[]{:S(2)}) collective-permute-start(bf16[34,128]{1,0:T(8,128)(2,1)S(1)} %add_convert_fusion), channel_id=1, source_target_pairs={{0,16},{8,24},{16,0},{24,8},{1,17},{9,25},{17,1},{25,9},{2,18},{10... | collective-permute-start | bytes 26120 | tf_op jit(solution)/shard_map/ppermute | solution.py:205
  98.4 2.6 %collective-permute-done.9 = bf16[34,128]{1,0:T(8,128)(2,1)S(1)} collective-permute-done((bf16[34,128]{1,0:T(8,128)(2,1)S(1)}, bf16[34,128]{1,0:T(8,128)(2,1)S(1)}, u32[]{:S(2)}, u32[]{:S(2)}) %collective-permute-start.9) | collective-permute-done | bytes 8736 | tf_op jit(solution)/shard_map/ppermute | solution.py:205
  101.1 1.8 %collective-permute-start.10 = (bf16[68,128]{1,0:T(8,128)(2,1)S(1)}, bf16[68,128]{1,0:T(8,128)(2,1)S(1)}, u32[]{:S(2)}, u32[]{:S(2)}) collective-permute-start(bf16[68,128]{1,0:T(8,128)(2,1)S(1)} %maximum_select_fusion.4), channel_id=1, source_target_pairs={{0,8},{8,0},{16,24},{24,16},{1,9},{9,1},{17,25},{25,17},{2,10},{10... | collective-permute-start | bytes 52232 | tf_op jit(solution)/shard_map/ppermute | solution.py:205
  102.9 2.0 %collective-permute-done.10 = bf16[68,128]{1,0:T(8,128)(2,1)S(1)} collective-permute-done((bf16[68,128]{1,0:T(8,128)(2,1)S(1)}, bf16[68,128]{1,0:T(8,128)(2,1)S(1)}, u32[]{:S(2)}, u32[]{:S(2)}) %collective-permute-start.10) | collective-permute-done | bytes 17440 | tf_op jit(solution)/shard_map/ppermute | solution.py:205
  105.4 3.5 %collective-permute-done.11 = bf16[136,128]{1,0:T(8,128)(2,1)S(1)} collective-permute-done((bf16[136,128]{1,0:T(8,128)(2,1)S(1)}, bf16[136,128]{1,0:T(8,128)(2,1)S(1)}, u32[]{:S(2)}, u32[]{:S(2)}) %collective-permute-start.11) | collective-permute-done | bytes 34848 | tf_op jit(solution)/shard_map/ppermute | solution.py:205
  108.9 1.4 collective-permute-start.12
  110.4 2.9 %collective-permute-done.12 = bf16[272,128]{1,0:T(8,128)(2,1)S(1)} collective-permute-done((bf16[272,128]{1,0:T(8,128)(2,1)S(1)}, bf16[272,128]{1,0:T(8,128)(2,1)S(1)}, u32[]{:S(2)}, u32[]{:S(2)}) %collective-permute-start.12) | collective-permute-done | bytes 69664 | tf_op jit(solution)/shard_map/ppermute | solution.py:205
  117.0 1.9 %convert_add_fusion.2 = (f32[2560,128]{1,0:T(8,128)S(1)}, f32[2560,128]{1,0:T(8,128)S(1)}) fusion(f32[8192,128]{1,0:T(8,128)} %get-tuple-element.17, bf16[8192,128]{1,0:T(8,128)(2,1)S(1)} %collective-permute-done.14), kind=kLoop, calls=%fused_computation.2 | loop fusion | flops 1310720 | bytes 6553600 | tf_op jit(solution)/shard_map/add | solution.py:336
  119.5 1.5 convert_add_fusion
  121.1 3.0 %collective-permute-start.23 = (bf16[1536,128]{1,0:T(8,128)(2,1)S(1)}, bf16[1536,128]{1,0:T(8,128)(2,1)S(1)}, u32[]{:S(2)}, u32[]{:S(2)}) collective-permute-start(bf16[1536,128]{1,0:T(8,128)(2,1)S(1)} %slice.336), channel_id=1, source_target_pairs={{0,16},{8,24},{16,0},{24,8},{1,17},{9,25},{17,1},{25,9},{2,18},{10... | collective-permute-start | bytes 1179656 | tf_op jit(solution)/shard_map/ppermute | solution.py:205
  124.1 1.5 collective-permute-start.15
  125.6 3.2 %collective-permute-done.19 = bf16[1280,128]{1,0:T(8,128)(2,1)S(1)} collective-permute-done((bf16[1280,128]{1,0:T(8,128)(2,1)S(1)}, bf16[1280,128]{1,0:T(8,128)(2,1)S(1)}, u32[]{:S(2)}, u32[]{:S(2)}) %collective-permute-start.19) | collective-permute-done | bytes 327712 | tf_op jit(solution)/shard_map/ppermute | solution.py:205
  130.3 4.5 %collective-permute-done.15 = bf16[1280,128]{1,0:T(8,128)(2,1)S(1)} collective-permute-done((bf16[1280,128]{1,0:T(8,128)(2,1)S(1)}, bf16[1280,128]{1,0:T(8,128)(2,1)S(1)}, u32[]{:S(2)}, u32[]{:S(2)}) %collective-permute-start.15) | collective-permute-done | bytes 327712 | tf_op jit(solution)/shard_map/ppermute | solution.py:205
  135.6 6.1 %collective-permute-done.23 = bf16[1536,128]{1,0:T(8,128)(2,1)S(1)} collective-permute-done((bf16[1536,128]{1,0:T(8,128)(2,1)S(1)}, bf16[1536,128]{1,0:T(8,128)(2,1)S(1)}, u32[]{:S(2)}, u32[]{:S(2)}) %collective-permute-start.23) | collective-permute-done | bytes 393248 | tf_op jit(solution)/shard_map/ppermute | solution.py:205
  142.6 3.4 %collective-permute-start.21 = (bf16[320,128]{1,0:T(8,128)(2,1)S(1)}, bf16[320,128]{1,0:T(8,128)(2,1)S(1)}, u32[]{:S(2)}, u32[]{:S(2)}) collective-permute-start(bf16[320,128]{1,0:T(8,128)(2,1)S(1)} %slice.343), channel_id=1, source_target_pairs={{0,16},{8,24},{16,0},{24,8},{1,17},{9,25},{17,1},{25,9},{2,18},{10... | collective-permute-start | bytes 245768 | tf_op jit(solution)/shard_map/ppermute | solution.py:205
  146.2 3.4 %collective-permute-done.21 = bf16[320,128]{1,0:T(8,128)(2,1)S(1)} collective-permute-done((bf16[320,128]{1,0:T(8,128)(2,1)S(1)}, bf16[320,128]{1,0:T(8,128)(2,1)S(1)}, u32[]{:S(2)}, u32[]{:S(2)}) %collective-permute-start.21) | collective-permute-done | bytes 81952 | tf_op jit(solution)/shard_map/ppermute | solution.py:205
  149.6 4.0 %collective-permute-start.22 = (bf16[160,128]{1,0:T(8,128)(2,1)S(1)}, bf16[160,128]{1,0:T(8,128)(2,1)S(1)}, u32[]{:S(2)}, u32[]{:S(2)}) collective-permute-start(bf16[160,128]{1,0:T(8,128)(2,1)S(1)} %slice.346), channel_id=1, source_target_pairs={{0,8},{8,0},{16,24},{24,16},{1,9},{9,1},{17,25},{25,17},{2,10},{10... | collective-permute-start | bytes 122888 | tf_op jit(solution)/shard_map/ppermute | solution.py:205
  155.1 1.5 collective-permute-start.25
  156.6 3.2 %collective-permute-done.25 = bf16[384,128]{1,0:T(8,128)(2,1)S(1)} collective-permute-done((bf16[384,128]{1,0:T(8,128)(2,1)S(1)}, bf16[384,128]{1,0:T(8,128)(2,1)S(1)}, u32[]{:S(2)}, u32[]{:S(2)}) %collective-permute-start.25) | collective-permute-done | bytes 98336 | tf_op jit(solution)/shard_map/ppermute | solution.py:205
  160.5 3.5 %collective-permute-done.26 = bf16[192,128]{1,0:T(8,128)(2,1)S(1)} collective-permute-done((bf16[192,128]{1,0:T(8,128)(2,1)S(1)}, bf16[192,128]{1,0:T(8,128)(2,1)S(1)}, u32[]{:S(2)}, u32[]{:S(2)}) %collective-permute-start.26) | collective-permute-done | bytes 49184 | tf_op jit(solution)/shard_map/ppermute | solution.py:205
  (120 shorter events, 25.1 us)
Async XLA Ops:
  1.4 5.4 %collective-permute-start = (bf16[8,3,128]{2,1,0:T(4,128)(2,1)S(1)}, bf16[8,3,128]{2,1,0:T(4,128)(2,1)S(1)}, u32[]{:S(2)}, u32[]{:S(2)}) collective-permute-start(bf16[8,3,128]{2,1,0:T(4,128)(2,1)S(1)} %get-tuple-element.32), channel_id=1, source_target_pairs={{0,1},{1,2},{2,3},{3,4},{4,5},{5,6},{6,7},{7,0},{8,9},{9,10},{10,1... | collective-permute-start | bytes 18440 | tf_op jit(solution)/shard_map/ppermute | solution.py:226
  1.9 4.9 %collective-permute-start.1 = (bf16[8,3,128]{2,1,0:T(4,128)(2,1)S(1)}, bf16[8,3,128]{2,1,0:T(4,128)(2,1)S(1)}, u32[]{:S(2)}, u32[]{:S(2)}) collective-permute-start(bf16[8,3,128]{2,1,0:T(4,128)(2,1)S(1)} %get-tuple-element.31), channel_id=1, source_target_pairs={{1,0},{2,1},{3,2},{4,3},{5,4},{6,5},{7,6},{0,7},{9,8},{10,9},{11,1... | collective-permute-start | bytes 18440 | tf_op jit(solution)/shard_map/ppermute | solution.py:227
  6.9 7.1 %copy-start.8 = (s32[6144]{0:T(1024)S(1)}, s32[6144]{0:T(1024)}, u32[]{:S(2)}) copy-start(s32[6144]{0:T(1024)} %param.31) | copy-start | bytes 73732
  8.1 9.2 %collective-permute-start.3 = (bf16[3,400,128]{2,1,0:T(8,128)(2,1)S(1)}, bf16[3,400,128]{2,1,0:T(8,128)(2,1)S(1)}, u32[]{:S(2)}, u32[]{:S(2)}) collective-permute-start(bf16[3,400,128]{2,1,0:T(8,128)(2,1)S(1)} %get-tuple-element.35), channel_id=1, source_target_pairs={{8,16},{9,17},{10,18},{11,19},{12,20},{13,21},{14,22},{15,23},{16,... | collective-permute-start | bytes 921608 | tf_op jit(solution)/shard_map/ppermute | solution.py:249
  8.8 12.3 %collective-permute-start.2 = (bf16[3,400,128]{2,1,0:T(8,128)(2,1)S(1)}, bf16[3,400,128]{2,1,0:T(8,128)(2,1)S(1)}, u32[]{:S(2)}, u32[]{:S(2)}) collective-permute-start(bf16[3,400,128]{2,1,0:T(8,128)(2,1)S(1)} %get-tuple-element.36), channel_id=1, source_target_pairs={{0,8},{1,9},{2,10},{3,11},{4,12},{5,13},{6,14},{7,15},{8,0},{9,1},... | collective-permute-start | bytes 921608 | tf_op jit(solution)/shard_map/ppermute | solution.py:248
  14.0 2.4 %copy-start.4 = (s32[6144]{0:T(1024)}, s32[6144]{0:T(1024)S(1)}, u32[]{:S(2)}) copy-start(s32[6144]{0:T(1024)S(1)} %select_add_fusion.target) | copy-start | bytes 73732
  42.9 10.3 %copy-start = (f32[8,128,128]{2,1,0:T(8,128)S(1)}, f32[8,128,128]{2,1,0:T(8,128)}, u32[]{:S(2)}) copy-start(f32[8,128,128]{2,1,0:T(8,128)} %get-tuple-element.13) | copy-start | bytes 1572868
  54.0 1.4 collective-permute-start.4
  55.0 6.5 %copy-start.7 = (s32[6144]{0:T(1024)S(1)}, s32[6144]{0:T(1024)}, u32[]{:S(2)}) copy-start(s32[6144]{0:T(1024)} %param.32) | copy-start | bytes 73732
  55.0 6.5 %copy-start.10 = (f32[16]{0:T(128)S(1)}, f32[16]{0:T(128)}, u32[]{:S(2)}) copy-start(f32[16]{0:T(128)} %param.33) | copy-start | bytes 196
  55.5 4.4 %collective-permute-start.5 = (bf16[272,128]{1,0:T(8,128)(2,1)S(1)}, bf16[272,128]{1,0:T(8,128)(2,1)S(1)}, u32[]{:S(2)}, u32[]{:S(2)}) collective-permute-start(bf16[272,128]{1,0:T(8,128)(2,1)S(1)} %dynamic-slice_convert_fusion), channel_id=1, source_target_pairs={{0,2},{1,3},{2,0},{3,1},{4,6},{5,7},{6,4},{7,5},{8,10},{9,11},{10,... | collective-permute-start | bytes 208904 | tf_op jit(solution)/shard_map/ppermute | solution.py:205
  59.9 27.9 %collective-permute-start.6 = (bf16[136,128]{1,0:T(8,128)(2,1)S(1)}, bf16[136,128]{1,0:T(8,128)(2,1)S(1)}, u32[]{:S(2)}, u32[]{:S(2)}) collective-permute-start(bf16[136,128]{1,0:T(8,128)(2,1)S(1)} %dynamic-slice_convert_fusion.1), channel_id=1, source_target_pairs={{0,4},{1,5},{2,6},{3,7},{4,0},{5,1},{6,2},{7,3},{8,12},{9,13},{10,... | collective-permute-start | bytes 104456 | tf_op jit(solution)/shard_map/ppermute | solution.py:205
  87.7 29.2 %collective-permute-start.14 = (bf16[8192,128]{1,0:T(8,128)(2,1)}, bf16[8192,128]{1,0:T(8,128)(2,1)S(1)}, u32[]{:S(2)}, u32[]{:S(2)}) collective-permute-start(bf16[8192,128]{1,0:T(8,128)(2,1)} %get-tuple-element.18), channel_id=1, source_target_pairs={{0,1},{1,0},{2,3},{3,2},{4,5},{5,4},{6,7},{7,6},{8,9},{9,8},{10,11... | collective-permute-start | bytes 6291464 | tf_op jit(solution)/shard_map/ppermute | solution.py:205
  87.9 3.8 %collective-permute-start.7 = (bf16[68,128]{1,0:T(8,128)(2,1)S(1)}, bf16[68,128]{1,0:T(8,128)(2,1)S(1)}, u32[]{:S(2)}, u32[]{:S(2)}) collective-permute-start(bf16[68,128]{1,0:T(8,128)(2,1)S(1)} %dynamic-slice_convert_fusion.2), channel_id=1, source_target_pairs={{0,8},{8,0},{16,24},{24,16},{1,9},{9,1},{17,25},{25,17},{2,10},{10... | collective-permute-start | bytes 52232 | tf_op jit(solution)/shard_map/ppermute | solution.py:205
  91.7 4.6 %collective-permute-start.8 = (bf16[34,128]{1,0:T(8,128)(2,1)S(1)}, bf16[34,128]{1,0:T(8,128)(2,1)S(1)}, u32[]{:S(2)}, u32[]{:S(2)}) collective-permute-start(bf16[34,128]{1,0:T(8,128)(2,1)S(1)} %dynamic-slice_convert_fusion.3), channel_id=1, source_target_pairs={{0,16},{8,24},{16,0},{24,8},{1,17},{9,25},{17,1},{25,9},{2,18},{10... | collective-permute-start | bytes 26120 | tf_op jit(solution)/shard_map/ppermute | solution.py:205
  96.4 4.7 %collective-permute-start.9 = (bf16[34,128]{1,0:T(8,128)(2,1)S(1)}, bf16[34,128]{1,0:T(8,128)(2,1)S(1)}, u32[]{:S(2)}, u32[]{:S(2)}) collective-permute-start(bf16[34,128]{1,0:T(8,128)(2,1)S(1)} %add_convert_fusion), channel_id=1, source_target_pairs={{0,16},{8,24},{16,0},{24,8},{1,17},{9,25},{17,1},{25,9},{2,18},{10... | collective-permute-start | bytes 26120 | tf_op jit(solution)/shard_map/ppermute | solution.py:205
  101.1 3.8 %collective-permute-start.10 = (bf16[68,128]{1,0:T(8,128)(2,1)S(1)}, bf16[68,128]{1,0:T(8,128)(2,1)S(1)}, u32[]{:S(2)}, u32[]{:S(2)}) collective-permute-start(bf16[68,128]{1,0:T(8,128)(2,1)S(1)} %maximum_select_fusion.4), channel_id=1, source_target_pairs={{0,8},{8,0},{16,24},{24,16},{1,9},{9,1},{17,25},{25,17},{2,10},{10... | collective-permute-start | bytes 52232 | tf_op jit(solution)/shard_map/ppermute | solution.py:205
  104.9 4.0 %collective-permute-start.11 = (bf16[136,128]{1,0:T(8,128)(2,1)S(1)}, bf16[136,128]{1,0:T(8,128)(2,1)S(1)}, u32[]{:S(2)}, u32[]{:S(2)}) collective-permute-start(bf16[136,128]{1,0:T(8,128)(2,1)S(1)} %maximum_select_fusion.3), channel_id=1, source_target_pairs={{0,4},{1,5},{2,6},{3,7},{4,0},{5,1},{6,2},{7,3},{8,12},{9,13},{10,... | collective-permute-start | bytes 104456 | tf_op jit(solution)/shard_map/ppermute | solution.py:205
  108.9 4.4 %collective-permute-start.12 = (bf16[272,128]{1,0:T(8,128)(2,1)S(1)}, bf16[272,128]{1,0:T(8,128)(2,1)S(1)}, u32[]{:S(2)}, u32[]{:S(2)}) collective-permute-start(bf16[272,128]{1,0:T(8,128)(2,1)S(1)} %maximum_select_fusion.2), channel_id=1, source_target_pairs={{0,2},{1,3},{2,0},{3,1},{4,6},{5,7},{6,4},{7,5},{8,10},{9,11},{10,... | collective-permute-start | bytes 208904 | tf_op jit(solution)/shard_map/ppermute | solution.py:205
  113.3 1.4 collective-permute-start.13
  118.9 9.8 %collective-permute-start.19 = (bf16[1280,128]{1,0:T(8,128)(2,1)S(1)}, bf16[1280,128]{1,0:T(8,128)(2,1)S(1)}, u32[]{:S(2)}, u32[]{:S(2)}) collective-permute-start(bf16[1280,128]{1,0:T(8,128)(2,1)S(1)} %slice.337), channel_id=1, source_target_pairs={{0,4},{1,5},{2,6},{3,7},{4,0},{5,1},{6,2},{7,3},{8,12},{9,13},{10,... | collective-permute-start | bytes 983048 | tf_op jit(solution)/shard_map/ppermute | solution.py:205
  121.1 20.6 %collective-permute-start.23 = (bf16[1536,128]{1,0:T(8,128)(2,1)S(1)}, bf16[1536,128]{1,0:T(8,128)(2,1)S(1)}, u32[]{:S(2)}, u32[]{:S(2)}) collective-permute-start(bf16[1536,128]{1,0:T(8,128)(2,1)S(1)} %slice.336), channel_id=1, source_target_pairs={{0,16},{8,24},{16,0},{24,8},{1,17},{9,25},{17,1},{25,9},{2,18},{10... | collective-permute-start | bytes 1179656 | tf_op jit(solution)/shard_map/ppermute | solution.py:205
  124.1 10.7 %collective-permute-start.15 = (bf16[1280,128]{1,0:T(8,128)(2,1)S(1)}, bf16[1280,128]{1,0:T(8,128)(2,1)S(1)}, u32[]{:S(2)}, u32[]{:S(2)}) collective-permute-start(bf16[1280,128]{1,0:T(8,128)(2,1)S(1)} %slice.338), channel_id=1, source_target_pairs={{0,2},{1,3},{2,0},{3,1},{4,6},{5,7},{6,4},{7,5},{8,10},{9,11},{10,... | collective-permute-start | bytes 983048 | tf_op jit(solution)/shard_map/ppermute | solution.py:205
  128.9 13.6 %collective-permute-start.20 = (bf16[640,128]{1,0:T(8,128)(2,1)S(1)}, bf16[640,128]{1,0:T(8,128)(2,1)S(1)}, u32[]{:S(2)}, u32[]{:S(2)}) collective-permute-start(bf16[640,128]{1,0:T(8,128)(2,1)S(1)} %slice.340), channel_id=1, source_target_pairs={{0,2},{1,3},{2,0},{3,1},{4,6},{5,7},{6,4},{7,5},{8,10},{9,11},{10,... | collective-permute-start | bytes 491528 | tf_op jit(solution)/shard_map/ppermute | solution.py:205
  134.9 11.1 %collective-permute-start.16 = (bf16[640,128]{1,0:T(8,128)(2,1)S(1)}, bf16[640,128]{1,0:T(8,128)(2,1)S(1)}, u32[]{:S(2)}, u32[]{:S(2)}) collective-permute-start(bf16[640,128]{1,0:T(8,128)(2,1)S(1)} %slice.341), channel_id=1, source_target_pairs={{0,4},{1,5},{2,6},{3,7},{4,0},{5,1},{6,2},{7,3},{8,12},{9,13},{10,... | collective-permute-start | bytes 491528 | tf_op jit(solution)/shard_map/ppermute | solution.py:205
  141.7 13.3 %collective-permute-start.24 = (bf16[768,128]{1,0:T(8,128)(2,1)S(1)}, bf16[768,128]{1,0:T(8,128)(2,1)S(1)}, u32[]{:S(2)}, u32[]{:S(2)}) collective-permute-start(bf16[768,128]{1,0:T(8,128)(2,1)S(1)} %slice.339), channel_id=1, source_target_pairs={{0,8},{8,0},{16,24},{24,16},{1,9},{9,1},{17,25},{25,17},{2,10},{10... | collective-permute-start | bytes 589832 | tf_op jit(solution)/shard_map/ppermute | solution.py:205
  142.6 7.0 %collective-permute-start.21 = (bf16[320,128]{1,0:T(8,128)(2,1)S(1)}, bf16[320,128]{1,0:T(8,128)(2,1)S(1)}, u32[]{:S(2)}, u32[]{:S(2)}) collective-permute-start(bf16[320,128]{1,0:T(8,128)(2,1)S(1)} %slice.343), channel_id=1, source_target_pairs={{0,16},{8,24},{16,0},{24,8},{1,17},{9,25},{17,1},{25,9},{2,18},{10... | collective-permute-start | bytes 245768 | tf_op jit(solution)/shard_map/ppermute | solution.py:205
  146.1 8.5 %collective-permute-start.17 = (bf16[320,128]{1,0:T(8,128)(2,1)S(1)}, bf16[320,128]{1,0:T(8,128)(2,1)S(1)}, u32[]{:S(2)}, u32[]{:S(2)}) collective-permute-start(bf16[320,128]{1,0:T(8,128)(2,1)S(1)} %slice.344), channel_id=1, source_target_pairs={{0,16},{8,24},{16,0},{24,8},{1,17},{9,25},{17,1},{25,9},{2,18},{10... | collective-permute-start | bytes 245768 | tf_op jit(solution)/shard_map/ppermute | solution.py:205
  149.6 7.1 %collective-permute-start.22 = (bf16[160,128]{1,0:T(8,128)(2,1)S(1)}, bf16[160,128]{1,0:T(8,128)(2,1)S(1)}, u32[]{:S(2)}, u32[]{:S(2)}) collective-permute-start(bf16[160,128]{1,0:T(8,128)(2,1)S(1)} %slice.346), channel_id=1, source_target_pairs={{0,8},{8,0},{16,24},{24,16},{1,9},{9,1},{17,25},{25,17},{2,10},{10... | collective-permute-start | bytes 122888 | tf_op jit(solution)/shard_map/ppermute | solution.py:205
  154.6 5.9 %collective-permute-start.18 = (bf16[160,128]{1,0:T(8,128)(2,1)S(1)}, bf16[160,128]{1,0:T(8,128)(2,1)S(1)}, u32[]{:S(2)}, u32[]{:S(2)}) collective-permute-start(bf16[160,128]{1,0:T(8,128)(2,1)S(1)} %slice.347), channel_id=1, source_target_pairs={{0,8},{8,0},{16,24},{24,16},{1,9},{9,1},{17,25},{25,17},{2,10},{10... | collective-permute-start | bytes 122888 | tf_op jit(solution)/shard_map/ppermute | solution.py:205
  155.1 4.7 %collective-permute-start.25 = (bf16[384,128]{1,0:T(8,128)(2,1)S(1)}, bf16[384,128]{1,0:T(8,128)(2,1)S(1)}, u32[]{:S(2)}, u32[]{:S(2)}) collective-permute-start(bf16[384,128]{1,0:T(8,128)(2,1)S(1)} %slice.342), channel_id=1, source_target_pairs={{0,2},{1,3},{2,0},{3,1},{4,6},{5,7},{6,4},{7,5},{8,10},{9,11},{10,... | collective-permute-start | bytes 294920 | tf_op jit(solution)/shard_map/ppermute | solution.py:205
  159.9 4.2 %collective-permute-start.26 = (bf16[192,128]{1,0:T(8,128)(2,1)S(1)}, bf16[192,128]{1,0:T(8,128)(2,1)S(1)}, u32[]{:S(2)}, u32[]{:S(2)}) collective-permute-start(bf16[192,128]{1,0:T(8,128)(2,1)S(1)} %slice.345), channel_id=1, source_target_pairs={{0,4},{1,5},{2,6},{3,7},{4,0},{5,1},{6,2},{7,3},{8,12},{9,13},{10,... | collective-permute-start | bytes 147464 | tf_op jit(solution)/shard_map/ppermute | solution.py:205
  (6 other events, 8.9 us)

commit v2 on v1

v2 whole, which is shorter than its diff:
```python
import jax
import jax.numpy as jnp
from jax import lax
from jax.experimental import pallas as pl
from jax.experimental.pallas import tpu as pltpu
from jax.sharding import PartitionSpec as P

A_DEV = 512
PAD = 8
TAPS = 7
MARGIN = 3
BATCH = 32
gelu_scale = 0.7978845608028654
cubic_coef = 0.044715
f32 = jnp.float32
bf16 = jnp.bfloat16
shape = jax.ShapeDtypeStruct


def params():
    return pltpu.CompilerParams(vmem_limit_bytes=56 << 20)


def vmem():
    return pl.BlockSpec(memory_space=pltpu.VMEM)


def smem():
    return pl.BlockSpec(memory_space=pltpu.SMEM)


def conv_block(field, base, dw, dwb, rows, channels):
    sums = [jnp.broadcast_to(dwb[...], (8, channels)) for _ in range(rows)]
    for b in range(TAPS):
        weights = [
            jnp.broadcast_to(dw[pl.ds(a * TAPS + b, 1), :], (8, channels)) for a in range(TAPS)
        ]
        for h in range(rows + TAPS - 1):
            x = field(h, base + (PAD - MARGIN + b))
            for a in range(TAPS):
                if 0 <= h - a < rows:
                    sums[h - a] = sums[h - a] + weights[a] * x
    return sums


def fill_rows(padded, state, south, north):
    rows, cols, _ = state.shape
    inner = slice(PAD, PAD + cols)
    padded[0:MARGIN, inner, :] = south[...].astype(f32)
    padded[rows + MARGIN : rows + 2 * MARGIN, inner, :] = north[...].astype(f32)
    for r in range(rows):
        padded[r + MARGIN, inner, :] = state[r].astype(f32)


def conv_kernel(state, south, north, dw, dwb, conv, padded):
    rows, cols, channels = state.shape
    fill_rows(padded, state, south, north)

    def step_of(step, _):
        base = pl.multiple_of(step * 8, 8)
        field = lambda h, at: padded[h, pl.ds(at, 8), :]
        sums = conv_block(field, base, dw, dwb, rows, channels)
        for r in range(rows):
            conv[r, pl.ds(base, 8), :] = sums[r]
        return 0

    lax.fori_loop(1, cols // 8 - 1, step_of, 0)


def block_kernel(
    state, south, north, left, right, conv, forcing, cotangent, land, entry_weights,
    dw, dwb, gain, nbias, up, upb, down, downb, scale, up_t, down_t,
    result, terms, grad_conv, grads, field, edge, acc_up, acc_down,
):
    rows, cols, channels = state.shape
    wide = 16
    for side in range(2):
        own = slice(0, wide) if side == 0 else slice(cols - wide, cols)
        at = PAD if side == 0 else 0
        edge[side, 0:MARGIN, at : at + wide, :] = south[:, own, :].astype(f32)
        edge[side, rows + MARGIN : rows + 2 * MARGIN, at : at + wide, :] = north[:, own, :].astype(f32)
        for r in range(rows):
            edge[side, r + MARGIN, at : at + wide, :] = state[r, own, :].astype(f32)
        for h in range(rows + 2 * MARGIN):
            if side == 0:
                edge[side, h, PAD - MARGIN : PAD, :] = left[h].astype(f32)
            else:
                edge[side, h, wide : wide + MARGIN, :] = right[h].astype(f32)
        sums = conv_block(
            lambda h, at: edge[side, h, pl.ds(at, 8), :], 0, dw, dwb, rows, channels
        )
        out = slice(0, 8) if side == 0 else slice(cols - 8, cols)
        for r in range(rows):
            field[r, out, :] = sums[r]
    for r in range(rows):
        field[r, 8 : cols - 8, :] = conv[r, 8 : cols - 8, :]

    acc_up[...] = jnp.zeros_like(acc_up)
    acc_down[...] = jnp.zeros_like(acc_down)
    group = 2
    size = group * cols

    def column(ref, first):
        return jnp.concatenate(
            [
                jnp.broadcast_to(ref[pl.ds(first + k, 1), :].astype(f32), (channels, cols)).T
                for k in range(group)
            ],
            axis=0,
        )

    def mlp_step(step, _):
        first = step * group
        here = field[pl.ds(first, group)].reshape(size, channels)
        average = jnp.mean(here, axis=-1, keepdims=True)
        centred = here - average
        variance = jnp.mean(centred * centred, axis=-1, keepdims=True)
        inv_std = lax.rsqrt(variance + 1e-06)
        normed = centred * inv_std
        force = forcing[pl.ds(first, group)].reshape(size, channels).astype(f32)
        mixed = (normed * gain[...] + nbias[...] + force).astype(bf16)
        pre = jnp.dot(mixed, up[...], preferred_element_type=f32) + upb[...]
        square = pre * pre
        tanh_value = jnp.tanh(pre * (gelu_scale + gelu_scale * cubic_coef * square))
        half = 0.5 + 0.5 * tanh_value
        hidden = (pre * half).astype(bf16)
        slope = half + pre * (1.0 - tanh_value * tanh_value) * (
            0.5 * gelu_scale + 1.5 * gelu_scale * cubic_coef * square
        )
        projected = jnp.dot(hidden, down[...], preferred_element_type=f32) + downb[...]
        ocean = column(land, first)
        own = state[pl.ds(first, group)].reshape(size, channels).astype(f32)
        out = ocean * (own + scale[...] * projected)
        result[pl.ds(first, group)] = out.astype(bf16).reshape(group, cols, channels)
        cot = cotangent[pl.ds(first, group)].reshape(size, channels).astype(f32)
        grad_out = (ocean * scale[...] * cot).astype(bf16)
        grad_hidden = jnp.dot(grad_out, down_t[...], preferred_element_type=f32)
        grad_pre = (grad_hidden * slope).astype(bf16)
        gmix = jnp.dot(grad_pre, up_t[...], preferred_element_type=f32)
        at = pl.multiple_of(step * size, 8)
        for k in range(2):
            terms[pl.ds(k * rows * cols + at, size), :] = column(entry_weights.at[k], first) * gmix
        gained = gmix * gain[...]
        gconv = inv_std * (
            gained
            - jnp.mean(gained, axis=-1, keepdims=True)
            - normed * jnp.mean(gained * normed, axis=-1, keepdims=True)
        )
        grad_conv[pl.ds(first, group)] = gconv.reshape(group, cols, channels)
        contract = (((0,), (0,)), ((), ()))
        acc_up[...] += lax.dot_general(mixed, grad_pre, contract, preferred_element_type=f32)
        acc_down[...] += lax.dot_general(grad_out, hidden, contract, preferred_element_type=f32)
        return 0

    lax.fori_loop(0, rows // group, mlp_step, 0)
    blocks = up.shape[1] // channels
    for k in range(blocks):
        part = slice(k * channels, (k + 1) * channels)
        grads[k] = acc_up[:, part]
        grads[blocks + k] = acc_down[:, part].T


def conv_grad_kernel(state, south, north, left, right, grad_conv, out, padded):
    rows, cols, channels = grad_conv.shape
    height = rows + 2 * MARGIN
    fill_rows(padded, state, south, north)
    for h in range(height):
        padded[h, PAD - MARGIN : PAD, :] = left[h].astype(f32)
        padded[h, PAD + cols : PAD + cols + MARGIN, :] = right[h].astype(f32)
    out[...] = jnp.zeros_like(out)
    unroll = 2
    for b in range(TAPS):

        def step_of(step, sums):
            sums = list(sums)
            for u in range(unroll):
                base = pl.multiple_of((step * unroll + u) * 8, 8)
                gc = [grad_conv[r, pl.ds(base, 8), :] for r in range(rows)]
                for h in range(height):
                    x = padded[h, pl.ds(base + (PAD - MARGIN + b), 8), :]
                    for a in range(TAPS):
                        if 0 <= h - a < rows:
                            k = a * 2 + (h - a) % 2
                            sums[k] = sums[k] + gc[h - a] * x
            return tuple(sums)

        zero = jnp.zeros((8, channels), f32)
        sums = lax.fori_loop(0, cols // (8 * unroll), step_of, (zero,) * (2 * TAPS))
        for a in range(TAPS):
            total = sums[2 * a] + sums[2 * a + 1]
            out[pl.ds(a * TAPS + b, 1), :] = jnp.sum(total, axis=0, keepdims=True)


def table_kernel(keys, info, terms, out, *scratch):
    table = scratch[0] if scratch else out
    rows = out.shape[0] if scratch else out.shape[0] - 8
    shift = (terms.shape[0] - 1).bit_length()
    chunk = 512

    def clear(step, _):
        at = pl.multiple_of(step * chunk, chunk)
        table[pl.ds(at, chunk), :] = jnp.zeros((chunk, table.shape[1]), f32)
        return 0

    lax.fori_loop(0, rows // chunk, clear, 0)
    offset = info[0]
    batches = info[1]

    def entry(place):
        key = keys[place]
        return key >> shift, key & ((1 << shift) - 1)

    def add_batch(step, _):
        found = [entry(offset + step + k * batches) for k in range(BATCH)]
        sums = [table[pl.ds(t, 1), :] + terms[pl.ds(e, 1), :] for t, e in found]
        for (t, _), value in zip(found, sums):
            table[pl.ds(t, 1), :] = value
        return 0

    def add_one(step, _):
        t, e = entry(offset + step)
        table[pl.ds(t, 1), :] = table[pl.ds(t, 1), :] + terms[pl.ds(e, 1), :]
        return 0

    @pl.when(info[2] == 0)
    def _():
        lax.fori_loop(0, batches, add_batch, 0)

    @pl.when(info[2] != 0)
    def _():
        lax.fori_loop(0, batches * BATCH, add_one, 0)

    if scratch:

        def give(step, _):
            at = pl.multiple_of(step * chunk, chunk)
            out[pl.ds(at, chunk), :] = table[pl.ds(at, chunk), :].astype(out.dtype)
            return 0

        lax.fori_loop(0, rows // chunk, give, 0)


def swap_bit(array, bit):
    pairs = [(i, i ^ (1 << bit)) for i in range(lax.axis_size("lon"))]
    return lax.ppermute(array, "lon", pairs)


def after(array, *others):
    return lax.optimization_barrier((array,) + others)[0]


def on_device(
    state, forcing, cotangent, land_mask, dw_weight, dw_bias, norm_gain, norm_bias,
    up_weight, up_bias, down_weight, down_bias, layer_scale, owner, atmos_cell, weight_index,
    intersection_weights,
):
    rows, cols, channels = state.shape
    cells = rows * cols
    hid = up_weight.shape[1]
    lat_count = lax.axis_size("lat")
    lon_count = lax.axis_size("lon")
    lat = lax.axis_index("lat")
    lon = lax.axis_index("lon")
    lon_bits = lon_count.bit_length() - 1
    devices = lat_count * lon_count
    entries = owner.shape[0]
    fan = entries // cells

    low_rows = state[:MARGIN]
    high_rows = state[rows - MARGIN :]
    odd = lat % 2 == 1
    last = lat == lat_count - 1
    even_pairs, odd_pairs = [], []
    for l in range(lat_count):
        for j in range(lon_count):
            here = l * lon_count + j
            even_pairs.append((here, (l ^ 1) * lon_count + j))
            beyond = l + 1 if l % 2 else l - 1
            if l == lat_count - 1:
                odd_pairs.append((here, l * lon_count + lon_count - 1 - j))
            elif beyond >= 0:
                odd_pairs.append((here, beyond * lon_count + j))
    got_even = lax.ppermute(jnp.where(odd, low_rows, high_rows), ("lat", "lon"), even_pairs)
    got_odd = lax.ppermute(
        jnp.where(last, high_rows[::-1, ::-1], jnp.where(odd, high_rows, low_rows)),
        ("lat", "lon"),
        odd_pairs,
    )
    south = jnp.where(odd, got_even, got_odd)
    north = jnp.where(odd, got_odd, got_even)

    forward = [(i, (i + 1) % lon_count) for i in range(lon_count)]
    backward = [(t, s) for s, t in forward]
    column = lambda part: jnp.concatenate([south[:, part], state[:, part], north[:, part]], axis=0)
    left = lax.ppermute(column(slice(cols - MARGIN, cols)), "lon", forward)
    right = lax.ppermute(column(slice(0, MARGIN)), "lon", backward)

    owner_lat = owner[:, 0] // lon_count
    relative = (owner[:, 0] % lon_count) ^ lon
    rest = list(range(1, lon_bits))
    orders = [rest, rest[::-1]]
    width = A_DEV // 2
    half_rows = devices // 2 * A_DEV
    numbers = []
    for order in orders:
        number = jnp.zeros_like(relative)
        for bit in order:
            number = number * 2 + ((relative >> bit) & 1)
        numbers.append(number * lat_count + owner_lat)
    upper = (atmos_cell >= width).astype(jnp.int32)
    block = jnp.where(upper == 1, numbers[1], numbers[0])
    row = (relative & 1) * half_rows + upper * (half_rows // 2) + block * width
    row = row + atmos_cell - upper * width
    entry = jnp.arange(entries, dtype=jnp.int32)
    shift = (entries - 1).bit_length()
    keys = lax.sort((row << shift) + (entry % fan) * cells + entry // fan, is_stable=False)
    sorted_row = keys >> shift
    mine = sorted_row < half_rows
    least = 64
    shared = jnp.any(sorted_row[least:] == sorted_row[:-least]).astype(jnp.int32)
    kept = jnp.sum(mine.astype(jnp.int32))
    spare = jnp.full((least * BATCH,), half_rows << shift, jnp.int32)
    batches_of = lambda count: jnp.maximum((count + BATCH - 1) // BATCH, least)
    send_info = jnp.stack([kept, batches_of(entries - kept), shared])
    keep_info = jnp.stack([jnp.zeros_like(kept), batches_of(kept), shared])
    send_keys = jnp.concatenate([keys - (half_rows << shift), spare])
    keep_keys = jnp.concatenate([jnp.where(mine, keys, half_rows << shift), spare])
    index = weight_index.reshape(rows, cols, fan).transpose(2, 0, 1)
    entry_weights = jnp.zeros((fan, rows, cols), f32)
    for k in range(intersection_weights.shape[0]):
        entry_weights = jnp.where(index == k, intersection_weights[k], entry_weights)

    line = lambda v: v.reshape(1, -1)
    taps = dw_weight.reshape(-1, channels).astype(f32)
    conv = pl.pallas_call(
        conv_kernel,
        out_shape=shape((rows, cols, channels), f32),
        in_specs=[vmem()] * 5,
        out_specs=vmem(),
        scratch_shapes=[pltpu.VMEM((rows + 2 * MARGIN, cols + 2 * PAD, channels), f32)],
        compiler_params=params(),
        name="conv",
    )(state, south, north, taps, line(dw_bias))
    result, terms, grad_conv, grads = pl.pallas_call(
        block_kernel,
        out_shape=(
            shape((rows, cols, channels), bf16),
            shape((entries, channels), f32),
            shape((rows, cols, channels), f32),
            shape((2 * hid // channels, channels, channels), f32),
        ),
        in_specs=[vmem()] * 21,
        out_specs=[vmem()] * 4,
        scratch_shapes=[
            pltpu.VMEM((rows, cols, channels), f32),
            pltpu.VMEM((2, rows + 2 * MARGIN, 24, channels), f32),
            pltpu.VMEM((channels, hid), f32),
            pltpu.VMEM((channels, hid), f32),
        ],
        compiler_params=params(),
        name="block",
    )(
        state, south, north, left, right, conv, forcing, cotangent, land_mask, entry_weights,
        taps, line(dw_bias), line(norm_gain), line(norm_bias), up_weight, line(up_bias),
        down_weight, line(down_bias), line(layer_scale), up_weight.T, down_weight.T,
    )

    send = pl.pallas_call(
        table_kernel,
        out_shape=shape((half_rows, channels), bf16),
        in_specs=[smem(), smem(), vmem()],
        out_specs=vmem(),
        scratch_shapes=[pltpu.VMEM((half_rows + 8, channels), f32)],
        compiler_params=params(),
        name="send_table",
    )(send_keys, send_info, terms)
    got = swap_bit(send, 0)
    keep = pl.pallas_call(
        table_kernel,
        out_shape=shape((half_rows + 8, channels), f32),
        in_specs=[smem(), smem(), vmem()],
        out_specs=vmem(),
        compiler_params=params(),
        name="keep_table",
    )(keep_keys, keep_info, after(terms, send))

    middle = half_rows // 2
    parts = [
        keep[:middle] + got[:middle].astype(f32),
        keep[middle : 2 * middle] + got[middle:].astype(f32),
    ]
    for stage in range(len(rest)):
        for q, order in enumerate(orders):
            size = parts[q].shape[0] // 2
            arrived = swap_bit(parts[q][size:].astype(bf16), order[stage])
            parts[q] = parts[q][:size] + arrived.astype(f32)
    lined = jnp.concatenate([p.reshape(lat_count, width, channels) for p in parts], axis=1)
    bands = lax.all_to_all(lined.astype(bf16), "lat", split_axis=0, concat_axis=0, tiled=True)
    forcing_grad = jnp.sum(bands.astype(f32), axis=0)

    tap_count = dw_weight.shape[0] * dw_weight.shape[1]
    dw_rows = -(-tap_count // devices) * devices
    grad_dw = pl.pallas_call(
        conv_grad_kernel,
        out_shape=shape((dw_rows, channels), f32),
        in_specs=[vmem()] * 6,
        out_specs=vmem(),
        scratch_shapes=[pltpu.VMEM((rows + 2 * MARGIN, cols + 2 * PAD, channels), f32)],
        compiler_params=params(),
        name="conv_grad",
    )(state, south, north, left, right, after(grad_conv, keep))
    total = jnp.concatenate([grads.reshape(2 * hid, channels), grad_dw], axis=0).astype(bf16)
    total = total.reshape(devices, -1, channels)
    total = lax.all_to_all(total, ("lat", "lon"), split_axis=0, concat_axis=0, tiled=True)
    total = jnp.sum(total.astype(f32), axis=0, keepdims=True).astype(bf16)
    total = jnp.broadcast_to(total, (devices,) + total.shape[1:])
    total = lax.all_to_all(total, ("lat", "lon"), split_axis=0, concat_axis=0, tiled=True)
    scale = float(cells * devices) ** (-0.5)
    total = total.reshape(-1, channels).astype(f32) * scale
    grad_up = total[:hid].reshape(hid // channels, channels, channels)
    grad_up = grad_up.transpose(1, 0, 2).reshape(channels, hid)
    grad_down = total[hid : 2 * hid]
    grad_dw = total[2 * hid : 2 * hid + tap_count].reshape(dw_weight.shape)
    return (result, grad_dw, grad_up, grad_down, forcing_grad)


def solution(mesh):
    grid = P("lat", "lon", None)
    in_specs = (grid, grid, grid, P("lat", "lon")) + (P(),) * 9
    in_specs += (P(("lat", "lon"), None), P(("lat", "lon")), P(("lat", "lon")), P())
    out_specs = (grid, P(), P(), P(), P(("lat", "lon"), None))
    return jax.shard_map(
        on_device, mesh=mesh, in_specs=in_specs, out_specs=out_specs, check_vma=False
    )
```

time: 165 us -> 169 us (1.024)
  other arithmetic: 9.88 us -> 31.3 us
  waiting for transfers between devices: 49.1 us -> 28.8 us
  starting transfers between devices: 39.5 us -> 25.4 us
  local copies, waits for them, and re-layouts: 8.59 us -> 20.9 us
  Pallas kernels: 56.5 us -> 58.8 us
  between operations: 1.18 us -> 3.1 us
    ppermute x26 -> x8, waiting for transfers between devices: 45.2 us -> 11.7 us  [the longest x5 11.7 us: swap_bit(): return lax.ppermute(array, 'lon', pairs)]
    ppermute x26 -> x8, starting transfers between devices: 34.4 us -> 7.9 us  [the longest x5 4.49 us: swap_bit(): return lax.ppermute(array, 'lon', pairs)]
    all_to_all x0 -> x3, waiting for transfers between devices: none -> 17.2 us  [the longest x1 12.2 us: on_device(): lax.all_to_all(lined.astype(bf16), 'lat', split_axis=0, concat_axis=0, ti...]
    select_n x5 -> x3, other arithmetic: 0.15 us -> 11.9 us  [the longest x2 10.8 us: on_device(): jnp.where(index == k, intersection_weights[k], entry_weights)]
    all_to_all x0 -> x3, starting transfers between devices: none -> 11.6 us  [the longest x2 8.1 us: on_device(): lax.all_to_all(total, ('lat', 'lon'), split_axis=0, concat_axis=0, tiled=...]
    sort x0 -> x1, other arithmetic: none -> 5.58 us  [on_device(): lax.sort((row << shift) + entry % fan * cells + entry // fan, is_stable=F...]
    another operation x0 -> x6, other arithmetic: none -> 4.75 us
    eq x0 -> x4, local copies, waits for them, and re-layouts: none -> 4.43 us  [on_device(): index == k]
  transfers between devices with their start and end apart: 27 -> 12, of which waited for: 17 -> 4; matrix products, arithmetic and copies ran while one was open for 7% -> 25% of each run, Pallas kernels for 15% -> 19%
where the time goes in v2:
time: 169 us; the launch traced here: 168 us
  Pallas kernels  58.8 us (35%)
  other arithmetic  31.3 us (19%)
  waiting for transfers between devices  28.8 us (17%)
  starting transfers between devices  25.4 us (15%)
  local copies, waits for them, and re-layouts  20.9 us (12%)
  between operations  3.1 us (2%)
    pallas_call x1, Pallas kernels, on_device(): pl.pallas_call(table_kernel, out_shape=shape((half_rows, channels), bf16)...  13.7 us
    pallas_call x1, Pallas kernels, on_device(): pl.pallas_call(block_kernel, out_shape=(shape((rows, cols, channels), bf1...  13.3 us
    pallas_call x1, Pallas kernels, on_device(): pl.pallas_call(table_kernel, out_shape=shape((half_rows + 8, channels), f...  13.2 us
    all_to_all x1, waiting for transfers between devices, on_device(): lax.all_to_all(lined.astype(bf16), 'lat', split_axis=0, concat_axis=0, ti...  12.2 us
    ppermute x5, waiting for transfers between devices, swap_bit(): return lax.ppermute(array, 'lon', pairs)  11.7 us
    select_n x2, other arithmetic, on_device(): jnp.where(index == k, intersection_weights[k], entry_weights)  10.8 us
    pallas_call x1, Pallas kernels, on_device(): pl.pallas_call(conv_kernel, out_shape=shape((rows, cols, channels), f32),...  9.95 us
    pallas_call x1, Pallas kernels, on_device(): pl.pallas_call(conv_grad_kernel, out_shape=shape((dw_rows, channels), f32...  8.67 us
  transfers between devices with their start and end apart: 12, of which 4 were waited for; matrix products, arithmetic and copies ran while one was open for 25% of the time, Pallas kernels for 19%

profile of v2, /device:TPU:0, one launch (start us, length us, event | category | flops | bytes accessed | tf_op | source)
XLA Modules:
  0.0 168.3 jit_solution(2132922246463030562)
XLA Ops:
  0.7 1.0 slice.128
  2.0 1.1 select_select_fusion
  3.8 5.9 %collective-permute-start = (bf16[3,384,128]{2,1,0:T(8,128)(2,1)S(1)}, bf16[3,384,128]{2,1,0:T(8,128)(2,1)S(1)}, u32[]{:S(2)}, u32[]{:S(2)}) collective-permute-start(bf16[3,384,128]{2,1,0:T(8,128)(2,1)S(1)} %get-tuple-element.22), channel_id=1, source_target_pairs={{0,8},{1,9},{2,10},{3,11},{4,12},{5,13},{6,14},{7,15},{8,0},{9,1},... | collective-permute-start | bytes 884744 | tf_op jit(solution)/shard_map/ppermute | solution.py:283
  10.5 5.6 %sort.7 = s32[6144]{0:T(1024)S(1)} sort(s32[6144]{0:T(1024)S(1)} %fusion.5), dimensions={0}, to_apply=%region_0.1 | sort | flops 79872 | bytes 49152 | tf_op jit(solution)/shard_map/sort | solution.py:316
  18.3 8.8 %select_select_fusion.1 = f32[6144]{0:T(1024)S(1)} fusion(s32[6144]{0:T(1024)S(1)} %copy-done.9, f32[]{:T(128)} %bitcast.4, f32[]{:T(128)} %bitcast.5, f32[]{:T(128)} %bitcast.6, f32[]{:T(128)} %bitcast.7, f32[]{:T(128)} %bitcast.8, f32[]{:T(128)} %bitcast.9, f32[]{:T(128)} %bitcast.10, f32[]{:T(128)} %bitcast.11, f32[]{:T(128)} %bitcast.12, f32[]{:T(128)} %bitcast.13, ...), kind=kLoop, calls=%fused_computation.37 | loop fusion | flops 172032 | bytes 49208 | tf_op jit(solution)/shard_map/jit(_where)/select_n | solution.py:331
  28.5 1.7 %eq.203 = pred[8,384,2]{2,1,0:T(8,128)(4,1)S(1)} reshape(pred[6144]{0:T(1024)(128)(4,1)S(1)} %get-tuple-element.35) | data formatting | bytes 12288 | tf_op jit(solution)/shard_map/eq | solution.py:331
  30.8 1.7 %eq.207 = pred[8,384,2]{2,1,0:T(8,128)(4,1)S(1)} reshape(pred[6144]{0:T(1024)(128)(4,1)S(1)} %get-tuple-element.36) | data formatting | bytes 12288 | tf_op jit(solution)/shard_map/eq | solution.py:331
  33.0 1.5 reshape.139
  35.0 1.9 %bitcast_select_fusion.entry_weights = f32[2,8,384]{2,1,0:T(8,128)} fusion(pred[8,384,2]{1,0,2:T(8,128)(4,1)S(1)} %copy.26, f32[8,384,2]{1,0,2:T(8,128)S(1)} %copy.27, pred[8,384,2]{1,0,2:T(8,128)(4,1)S(1)} %copy.25, f32[]{:T(128)} %bitcast.3, f32[]{:T(128)} %bitcast.2), kind=kLoop, calls=%fused_computation.36 | loop fusion | flops 12288 | bytes 61448 | tf_op jit(solution)/shard_map/jit(_where)/select_n | solution.py:331
  37.2 2.7 %collective-permute-start.3 = (bf16[14,3,128]{2,1,0:T(4,128)(2,1)S(1)}, bf16[14,3,128]{2,1,0:T(4,128)(2,1)S(1)}, u32[]{:S(2)}, u32[]{:S(2)}) collective-permute-start(bf16[14,3,128]{2,1,0:T(4,128)(2,1)S(1)} %pad_maximum_fusion.3), channel_id=1, source_target_pairs={{1,0},{2,1},{3,2},{4,3},{5,4},{6,5},{7,6},{0,7},{9,8},{10,9},{11,1... | collective-permute-start | bytes 32264 | tf_op jit(solution)/shard_map/ppermute | solution.py:296
  39.8 1.4 add_add_fusion.1.info
  44.0 9.9 %conv.1 = f32[8,384,128]{2,1,0:T(8,128)} custom-call(bf16[8,384,128]{2,1,0:T(8,128)(2,1)} %state.5, bf16[3,384,128]{2,1,0:T(8,128)(2,1)} %copy-done.2, bf16[3,384,128]{2,1,0:T(8,128)(2,1)} %copy-done.1, f32[49,128]{1,0:T(8,128)} %reshape.114.dw, f32[1,128]{1,0:T(1,128)} %bitcast.52), custom_call_target="tpu_custom_call" | custom-call | tf_op jit(solution)/shard_map/conv/pallas_call | solution.py:335
  54.5 13.3 %block.1 = (bf16[8,384,128]{2,1,0:T(8,128)(2,1)}, f32[6144,128]{1,0:T(8,128)}, f32[8,384,128]{2,1,0:T(8,128)}, f32[8,128,128]{2,1,0:T(8,128)}) custom-call(bf16[8,384,128]{2,1,0:T(8,128)(2,1)} %state.5, bf16[3,384,128]{2,1,0:T(8,128)(2,1)} %copy-done.2, bf16[3,384,128]{2,1,0:T(8,128)(2,1)} %copy-done.1, bf16[14,3,128]{2,1,0:T(4,128)(2,1)} %copy-done.10, ...), custom_call_target="tpu_custom_call" | custom-call | tf_op jit(solution)/shard_map/block/pallas_call | solution.py:344
  67.9 13.7 %send_table.1 = bf16[8192,128]{1,0:T(8,128)(2,1)} custom-call(s32[8192]{0:T(1024)} %concatenate.23.keys, s32[3]{0:T(128)} %add_add_fusion.1.info, f32[6144,128]{1,0:T(8,128)} %get-tuple-element.15.terms), custom_call_target="tpu_custom_call" | custom-call | tf_op jit(solution)/shard_map/send_table/pallas_call | solution.py:368
  83.5 13.2 %keep_table.1 = f32[8200,128]{1,0:T(8,128)} custom-call(s32[8192]{0:T(1024)} %concatenate.22.keys, s32[3]{0:T(128)} %add_add_fusion.info, f32[6144,128]{1,0:T(8,128)} %get-tuple-element.15.terms), custom_call_target="tpu_custom_call" | custom-call | tf_op jit(solution)/shard_map/keep_table/pallas_call | solution.py:378
  96.7 3.2 %slice_add_fusion.1 = (f32[4096,128]{1,0:T(8,128)S(1)}, f32[4096,128]{1,0:T(8,128)S(1)}) fusion(f32[8200,128]{1,0:T(8,128)} %keep_table.1, bf16[8192,128]{1,0:T(8,128)(2,1)} %collective-permute-done.4), kind=kLoop, calls=%fused_computation.1 | loop fusion | flops 2097152 | bytes 10485760 | tf_op jit(solution)/shard_map/add | solution.py:389
  99.9 1.3 copy-done
  101.3 1.6 collective-permute-start.7
  102.9 8.7 %conv_grad.1 = f32[64,128]{1,0:T(8,128)} custom-call(bf16[8,384,128]{2,1,0:T(8,128)(2,1)} %state.5, bf16[3,384,128]{2,1,0:T(8,128)(2,1)} %copy-done.2, bf16[3,384,128]{2,1,0:T(8,128)(2,1)} %copy-done.1, bf16[14,3,128]{2,1,0:T(4,128)(2,1)} %copy-done.10, bf16[14,3,128]{2,1,0:T(4,128)(2,1)} %copy-done.11, f32[8,384,128]{2,1,0:T(8,128)} %get-tuple-element.16.grad_conv), custom_call_target="tpu_custom_call" | custom-call | tf_op jit(solution)/shard_map/conv_grad/pallas_call | solution.py:403
  114.6 4.5 %all-to-all-start = ((bf16[32,34,128]{2,1,0:T(8,128)(2,1)}), bf16[32,34,128]{2,1,0:T(8,128)(2,1)S(1)}, u32[]{:S(2)}, u32[]{:S(2)}) async-start(bf16[32,34,128]{2,1,0:T(8,128)(2,1)} %convert_element_type.58), calls=%async_computation | async-start | bytes 655360 | tf_op jit(solution)/shard_map/all_to_all | solution.py:414
  119.1 1.4 slice_add_fusion.2
  121.3 1.8 %collective-permute-start.8 = (bf16[1024,128]{1,0:T(8,128)(2,1)}, bf16[1024,128]{1,0:T(8,128)(2,1)}, u32[]{:S(2)}, u32[]{:S(2)}) collective-permute-start(bf16[1024,128]{1,0:T(8,128)(2,1)} %slice.217), channel_id=1, source_target_pairs={{0,2},{1,3},{2,0},{3,1},{4,6},{5,7},{6,4},{7,5},{8,10},{9,11},{10,... | collective-permute-start | bytes 786440 | tf_op jit(solution)/shard_map/ppermute | solution.py:245
  123.0 7.4 %collective-permute-done.5 = bf16[2048,128]{1,0:T(8,128)(2,1)} collective-permute-done((bf16[2048,128]{1,0:T(8,128)(2,1)}, bf16[2048,128]{1,0:T(8,128)(2,1)}, u32[]{:S(2)}, u32[]{:S(2)}) %collective-permute-start.5) | collective-permute-done | bytes 524320 | tf_op jit(solution)/shard_map/ppermute | solution.py:245
  130.5 1.1 slice_add_fusion.3
  131.6 1.0 copy-done.3
  134.1 3.6 %all-to-all-start.1 = ((bf16[32,34,128]{2,1,0:T(8,128)(2,1)}), bf16[32,34,128]{2,1,0:T(8,128)(2,1)S(1)}, u32[]{:S(2)}, u32[]{:S(2)}) async-start(bf16[32,34,128]{2,1,0:T(8,128)(2,1)} %broadcast_in_dim.81), calls=%async_computation.1 | async-start | bytes 655360 | tf_op jit(solution)/shard_map/all_to_all | solution.py:417
  137.7 1.0 fusion
  138.7 4.2 %collective-permute-done.6 = bf16[1024,128]{1,0:T(8,128)(2,1)} collective-permute-done((bf16[1024,128]{1,0:T(8,128)(2,1)S(1)}, bf16[1024,128]{1,0:T(8,128)(2,1)}, u32[]{:S(2)}, u32[]{:S(2)}) %collective-permute-start.6) | collective-permute-done | bytes 262176 | tf_op jit(solution)/shard_map/ppermute | solution.py:245
  142.9 1.0 fusion.1
  144.7 4.9 %all-to-all-done.1 = bf16[32,34,128]{2,1,0:T(8,128)(2,1)S(1)} async-done(((bf16[32,34,128]{2,1,0:T(8,128)(2,1)}), bf16[32,34,128]{2,1,0:T(8,128)(2,1)S(1)}, u32[]{:S(2)}, u32[]{:S(2)}) %all-to-all-start.1) | async-done | bytes 278560 | tf_op jit(solution)/shard_map/all_to_all | solution.py:417
  149.7 3.5 %all-to-all-start.2 = ((bf16[4,512,128]{2,1,0:T(8,128)(2,1)}), bf16[4,512,128]{2,1,0:T(8,128)(2,1)S(1)}, u32[]{:S(2)}, u32[]{:S(2)}) async-start(bf16[4,512,128]{2,1,0:T(8,128)(2,1)} %pad_maximum_fusion), calls=%async_computation.2 | async-start | bytes 1048576 | tf_op jit(solution)/shard_map/all_to_all | solution.py:398
  155.3 12.2 %all-to-all-done.2 = bf16[4,512,128]{2,1,0:T(8,128)(2,1)S(1)} async-done(((bf16[4,512,128]{2,1,0:T(8,128)(2,1)}), bf16[4,512,128]{2,1,0:T(8,128)(2,1)S(1)}, u32[]{:S(2)}, u32[]{:S(2)}) %all-to-all-start.2) | async-done | bytes 524320 | tf_op jit(solution)/shard_map/all_to_all | solution.py:398
  (79 shorter events, 19.2 us)
Async XLA Ops:
  0.6 9.8 %copy-start.12 = (s32[6144]{0:T(1024)S(1)}, s32[6144]{0:T(1024)}, u32[]{:S(2)}) copy-start(s32[6144]{0:T(1024)} %param.31) | copy-start | bytes 73732
  0.6 9.8 %copy-start.13 = (s32[6144,1]{0,1:T(1,128)S(1)}, s32[6144,1]{0,1:T(1,128)}, u32[]{:S(2)}) copy-start(s32[6144,1]{0,1:T(1,128)} %param.30) | copy-start | bytes 73732
  0.7 16.9 %copy-start.8 = (f32[16]{0:T(128)S(1)}, f32[16]{0:T(128)}, u32[]{:S(2)}) copy-start(f32[16]{0:T(128)} %param.33) | copy-start | bytes 196
  0.7 17.6 %copy-start.9 = (s32[6144]{0:T(1024)S(1)}, s32[6144]{0:T(1024)}, u32[]{:S(2)}) copy-start(s32[6144]{0:T(1024)} %param.32) | copy-start | bytes 73732
  3.1 33.8 %collective-permute-start.1 = (bf16[3,384,128]{2,1,0:T(8,128)(2,1)S(1)}, bf16[3,384,128]{2,1,0:T(8,128)(2,1)S(1)}, u32[]{:S(2)}, u32[]{:S(2)}) collective-permute-start(bf16[3,384,128]{2,1,0:T(8,128)(2,1)S(1)} %get-tuple-element.21), channel_id=1, source_target_pairs={{8,16},{9,17},{10,18},{11,19},{12,20},{13,21},{14,22},{15,23},{16,... | collective-permute-start | bytes 884744 | tf_op jit(solution)/shard_map/ppermute | solution.py:284
  3.8 33.1 %collective-permute-start = (bf16[3,384,128]{2,1,0:T(8,128)(2,1)S(1)}, bf16[3,384,128]{2,1,0:T(8,128)(2,1)S(1)}, u32[]{:S(2)}, u32[]{:S(2)}) collective-permute-start(bf16[3,384,128]{2,1,0:T(8,128)(2,1)S(1)} %get-tuple-element.22), channel_id=1, source_target_pairs={{0,8},{1,9},{2,10},{3,11},{4,12},{5,13},{6,14},{7,15},{8,0},{9,1},... | collective-permute-start | bytes 884744 | tf_op jit(solution)/shard_map/ppermute | solution.py:283
  33.0 8.2 %copy-start.14 = (bf16[7,7,128]{2,1,0:T(8,128)(2,1)S(1)}, bf16[7,7,128]{2,1,0:T(8,128)(2,1)}, u32[]{:S(2)}) copy-start(bf16[7,7,128]{2,1,0:T(8,128)(2,1)} %param.21) | copy-start | bytes 37636
  33.0 8.8 %copy-start.5 = (bf16[128,512]{1,0:T(8,128)(2,1)S(1)}, bf16[128,512]{1,0:T(8,128)(2,1)}, u32[]{:S(2)}) copy-start(bf16[128,512]{1,0:T(8,128)(2,1)} %up.1) | copy-start | bytes 393220
  33.0 9.6 %copy-start.6 = (bf16[512,128]{1,0:T(8,128)(2,1)S(1)}, bf16[512,128]{1,0:T(8,128)(2,1)}, u32[]{:S(2)}) copy-start(bf16[512,128]{1,0:T(8,128)(2,1)} %down.1) | copy-start | bytes 393220
  37.0 7.0 %copy-start.1 = (bf16[3,384,128]{2,1,0:T(8,128)(2,1)}, bf16[3,384,128]{2,1,0:T(8,128)(2,1)S(1)}, u32[]{:S(2)}) copy-start(bf16[3,384,128]{2,1,0:T(8,128)(2,1)S(1)} %get-tuple-element.23.north) | copy-start | bytes 884740
  37.0 7.0 %copy-start.2 = (bf16[3,384,128]{2,1,0:T(8,128)(2,1)}, bf16[3,384,128]{2,1,0:T(8,128)(2,1)S(1)}, u32[]{:S(2)}) copy-start(bf16[3,384,128]{2,1,0:T(8,128)(2,1)S(1)} %get-tuple-element.24.south) | copy-start | bytes 884740
  37.1 16.9 %collective-permute-start.2 = (bf16[14,3,128]{2,1,0:T(4,128)(2,1)S(1)}, bf16[14,3,128]{2,1,0:T(4,128)(2,1)S(1)}, u32[]{:S(2)}, u32[]{:S(2)}) collective-permute-start(bf16[14,3,128]{2,1,0:T(4,128)(2,1)S(1)} %pad_maximum_fusion.2), channel_id=1, source_target_pairs={{0,1},{1,2},{2,3},{3,4},{4,5},{5,6},{6,7},{7,0},{8,9},{9,10},{10,1... | collective-permute-start | bytes 32264 | tf_op jit(solution)/shard_map/ppermute | solution.py:295
  37.2 16.8 %collective-permute-start.3 = (bf16[14,3,128]{2,1,0:T(4,128)(2,1)S(1)}, bf16[14,3,128]{2,1,0:T(4,128)(2,1)S(1)}, u32[]{:S(2)}, u32[]{:S(2)}) collective-permute-start(bf16[14,3,128]{2,1,0:T(4,128)(2,1)S(1)} %pad_maximum_fusion.3), channel_id=1, source_target_pairs={{1,0},{2,1},{3,2},{4,3},{5,4},{6,5},{7,6},{0,7},{9,8},{10,9},{11,1... | collective-permute-start | bytes 32264 | tf_op jit(solution)/shard_map/ppermute | solution.py:296
  53.9 0.6 copy-start.10
  53.9 0.6 copy-start.11
  81.5 15.1 %collective-permute-start.4 = (bf16[8192,128]{1,0:T(8,128)(2,1)}, bf16[8192,128]{1,0:T(8,128)(2,1)}, u32[]{:S(2)}, u32[]{:S(2)}) collective-permute-start(bf16[8192,128]{1,0:T(8,128)(2,1)} %send_table.1), channel_id=1, source_target_pairs={{0,1},{1,0},{2,3},{3,2},{4,5},{5,4},{6,7},{7,6},{8,9},{9,8},{10,11... | collective-permute-start | bytes 6291464 | tf_op jit(solution)/shard_map/ppermute | solution.py:245
  96.7 6.2 %copy-start.7 = (f32[8,128,128]{2,1,0:T(8,128)S(1)}, f32[8,128,128]{2,1,0:T(8,128)}, u32[]{:S(2)}) copy-start(f32[8,128,128]{2,1,0:T(8,128)} %get-tuple-element.12) | copy-start | bytes 1572868
  99.9 1.3 copy-start
  101.3 17.8 %collective-permute-start.7 = (bf16[2048,128]{1,0:T(8,128)(2,1)S(1)}, bf16[2048,128]{1,0:T(8,128)(2,1)}, u32[]{:S(2)}, u32[]{:S(2)}) collective-permute-start(bf16[2048,128]{1,0:T(8,128)(2,1)S(1)} %slice.215), channel_id=1, source_target_pairs={{0,4},{1,5},{2,6},{3,7},{4,0},{5,1},{6,2},{7,3},{8,12},{9,13},{10,... | collective-permute-start | bytes 1572872 | tf_op jit(solution)/shard_map/ppermute | solution.py:245
  113.2 17.3 %collective-permute-start.5 = (bf16[2048,128]{1,0:T(8,128)(2,1)}, bf16[2048,128]{1,0:T(8,128)(2,1)}, u32[]{:S(2)}, u32[]{:S(2)}) collective-permute-start(bf16[2048,128]{1,0:T(8,128)(2,1)} %slice.216), channel_id=1, source_target_pairs={{0,2},{1,3},{2,0},{3,1},{4,6},{5,7},{6,4},{7,5},{8,10},{9,11},{10,... | collective-permute-start | bytes 1572872 | tf_op jit(solution)/shard_map/ppermute | solution.py:245
  114.6 18.6 %all-to-all-start = ((bf16[32,34,128]{2,1,0:T(8,128)(2,1)}), bf16[32,34,128]{2,1,0:T(8,128)(2,1)S(1)}, u32[]{:S(2)}, u32[]{:S(2)}) async-start(bf16[32,34,128]{2,1,0:T(8,128)(2,1)} %convert_element_type.58), calls=%async_computation | async-start | bytes 655360 | tf_op jit(solution)/shard_map/all_to_all | solution.py:414
  121.3 16.4 %collective-permute-start.8 = (bf16[1024,128]{1,0:T(8,128)(2,1)}, bf16[1024,128]{1,0:T(8,128)(2,1)}, u32[]{:S(2)}, u32[]{:S(2)}) collective-permute-start(bf16[1024,128]{1,0:T(8,128)(2,1)} %slice.217), channel_id=1, source_target_pairs={{0,2},{1,3},{2,0},{3,1},{4,6},{5,7},{6,4},{7,5},{8,10},{9,11},{10,... | collective-permute-start | bytes 786440 | tf_op jit(solution)/shard_map/ppermute | solution.py:245
  131.6 1.0 copy-start.3
  132.7 10.2 %copy-start.4 = (f32[2048,128]{1,0:T(8,128)S(1)}, f32[2048,128]{1,0:T(8,128)}, u32[]{:S(2)}) copy-start(f32[2048,128]{1,0:T(8,128)} %copy-done.3) | copy-start | bytes 3145732
  132.7 10.2 %collective-permute-start.6 = (bf16[1024,128]{1,0:T(8,128)(2,1)S(1)}, bf16[1024,128]{1,0:T(8,128)(2,1)}, u32[]{:S(2)}, u32[]{:S(2)}) collective-permute-start(bf16[1024,128]{1,0:T(8,128)(2,1)S(1)} %slice.218), channel_id=1, source_target_pairs={{0,4},{1,5},{2,6},{3,7},{4,0},{5,1},{6,2},{7,3},{8,12},{9,13},{10,... | collective-permute-start | bytes 786440 | tf_op jit(solution)/shard_map/ppermute | solution.py:245
  134.1 15.6 %all-to-all-start.1 = ((bf16[32,34,128]{2,1,0:T(8,128)(2,1)}), bf16[32,34,128]{2,1,0:T(8,128)(2,1)S(1)}, u32[]{:S(2)}, u32[]{:S(2)}) async-start(bf16[32,34,128]{2,1,0:T(8,128)(2,1)} %broadcast_in_dim.81), calls=%async_computation.1 | async-start | bytes 655360 | tf_op jit(solution)/shard_map/all_to_all | solution.py:417
  149.7 17.9 %all-to-all-start.2 = ((bf16[4,512,128]{2,1,0:T(8,128)(2,1)}), bf16[4,512,128]{2,1,0:T(8,128)(2,1)S(1)}, u32[]{:S(2)}, u32[]{:S(2)}) async-start(bf16[4,512,128]{2,1,0:T(8,128)(2,1)} %pad_maximum_fusion), calls=%async_computation.2 | async-start | bytes 1048576 | tf_op jit(solution)/shard_map/all_to_all | solution.py:398

commit v3 on v2

--- a/solution.py
+++ b/solution.py
@@ -19,6 +19,10 @@
 
 def params():
     return pltpu.CompilerParams(vmem_limit_bytes=56 << 20)
+
+
+def cost(microseconds):
+    return pl.CostEstimate(flops=int(microseconds * 1e9), bytes_accessed=0, transcendentals=0)
 
 
 def vmem():
@@ -68,9 +72,9 @@
 
 
 def block_kernel(
-    state, south, north, left, right, conv, forcing, cotangent, land, entry_weights,
+    state, south, north, left, right, conv, forcing, cotangent, land, weight_index, weight_table,
     dw, dwb, gain, nbias, up, upb, down, downb, scale, up_t, down_t,
-    result, terms, grad_conv, grads, field, edge, acc_up, acc_down,
+    result, terms, grad_conv, grads, field, edge, acc_up, acc_down, entry_weights, spread,
 ):
     rows, cols, channels = state.shape
     wide = 16
@@ -95,16 +99,24 @@
     for r in range(rows):
         field[r, 8 : cols - 8, :] = conv[r, 8 : cols - 8, :]
 
+    index = weight_index[...]
+    looked_up = jnp.zeros(index.shape, f32)
+    for k in range(weight_table.shape[0]):
+        looked_up = jnp.where(index == k, weight_table[k], looked_up)
+    entry_weights[...] = looked_up
     acc_up[...] = jnp.zeros_like(acc_up)
     acc_down[...] = jnp.zeros_like(acc_down)
     group = 2
     size = group * cols
-
-    def column(ref, first):
+    fan = terms.shape[0] // (rows * cols)
+    lines = fan * size // channels
+
+    def column(ref, first, count):
+        width = ref.shape[1]
         return jnp.concatenate(
             [
-                jnp.broadcast_to(ref[pl.ds(first + k, 1), :].astype(f32), (channels, cols)).T
-                for k in range(group)
+                jnp.broadcast_to(ref[pl.ds(first + k, 1), :].astype(f32), (channels, width)).T
+                for k in range(count)
             ],
             axis=0,
         )
@@ -128,7 +140,7 @@
             0.5 * gelu_scale + 1.5 * gelu_scale * cubic_coef * square
         )
         projected = jnp.dot(hidden, down[...], preferred_element_type=f32) + downb[...]
-        ocean = column(land, first)
+        ocean = column(land, first, group)
         own = state[pl.ds(first, group)].reshape(size, channels).astype(f32)
         out = ocean * (own + scale[...] * projected)
         result[pl.ds(first, group)] = out.astype(bf16).reshape(group, cols, channels)
@@ -138,8 +150,10 @@
         grad_pre = (grad_hidden * slope).astype(bf16)
         gmix = jnp.dot(grad_pre, up_t[...], preferred_element_type=f32)
         at = pl.multiple_of(step * size, 8)
-        for k in range(2):
-            terms[pl.ds(k * rows * cols + at, size), :] = column(entry_weights.at[k], first) * gmix
+        spread[...] = column(entry_weights, step * lines, lines)
+        for k in range(fan):
+            weights = spread[pl.ds(k, size, stride=fan), :]
+            terms[pl.ds(k * rows * cols + at, size), :] = weights * gmix
         gained = gmix * gain[...]
         gconv = inv_std * (
             gained
@@ -191,35 +205,27 @@
             out[pl.ds(a * TAPS + b, 1), :] = jnp.sum(total, axis=0, keepdims=True)
 
 
-def table_kernel(keys, info, terms, out, *scratch):
-    table = scratch[0] if scratch else out
-    rows = out.shape[0] if scratch else out.shape[0] - 8
-    shift = (terms.shape[0] - 1).bit_length()
-    chunk = 512
-
-    def clear(step, _):
-        at = pl.multiple_of(step * chunk, chunk)
-        table[pl.ds(at, chunk), :] = jnp.zeros((chunk, table.shape[1]), f32)
-        return 0
-
-    lax.fori_loop(0, rows // chunk, clear, 0)
+def table_kernel(rows, names, info, terms, zeros, table, sem):
+    clear = pltpu.make_async_copy(zeros, table, sem)
+    clear.start()
+    clear.wait()
     offset = info[0]
     batches = info[1]
 
-    def entry(place):
-        key = keys[place]
-        return key >> shift, key & ((1 << shift) - 1)
-
     def add_batch(step, _):
-        found = [entry(offset + step + k * batches) for k in range(BATCH)]
-        sums = [table[pl.ds(t, 1), :] + terms[pl.ds(e, 1), :] for t, e in found]
+        place = offset + step
+        found = []
+        for _ in range(BATCH):
+            found.append((rows[place], names[place]))
+            place = place + batches
+        sums = [table[t] + terms[e] for t, e in found]
         for (t, _), value in zip(found, sums):
-            table[pl.ds(t, 1), :] = value
+            table[t] = value
         return 0
 
     def add_one(step, _):
-        t, e = entry(offset + step)
-        table[pl.ds(t, 1), :] = table[pl.ds(t, 1), :] + terms[pl.ds(e, 1), :]
+        t = rows[offset + step]
+        table[t] = table[t] + terms[names[offset + step]]
         return 0
 
     @pl.when(info[2] == 0)
@@ -229,15 +235,6 @@
     @pl.when(info[2] != 0)
     def _():
         lax.fori_loop(0, batches * BATCH, add_one, 0)
-
-    if scratch:
-
-        def give(step, _):
-            at = pl.multiple_of(step * chunk, chunk)
-            out[pl.ds(at, chunk), :] = table[pl.ds(at, chunk), :].astype(out.dtype)
-            return 0
-
-        lax.fori_loop(0, rows // chunk, give, 0)
 
 
 def swap_bit(array, bit):
@@ -313,22 +310,21 @@
     row = row + atmos_cell - upper * width
     entry = jnp.arange(entries, dtype=jnp.int32)
     shift = (entries - 1).bit_length()
-    keys = lax.sort((row << shift) + (entry % fan) * cells + entry // fan, is_stable=False)
+    least = 64
+    spare = jnp.full((least * BATCH,), 2 * half_rows << shift, jnp.int32)
+    keys = (row << shift) + (entry % fan) * cells + entry // fan
+    keys = lax.sort(jnp.concatenate([keys, spare]), is_stable=False)
     sorted_row = keys >> shift
+    names = keys & ((1 << shift) - 1)
     mine = sorted_row < half_rows
-    least = 64
-    shared = jnp.any(sorted_row[least:] == sorted_row[:-least]).astype(jnp.int32)
+    send_rows = jnp.where(mine, 0, sorted_row - half_rows)
+    keep_rows = jnp.where(mine, sorted_row, half_rows)
+    same = sorted_row[least:entries] == sorted_row[: entries - least]
+    shared = jnp.max(same.astype(jnp.int32))
     kept = jnp.sum(mine.astype(jnp.int32))
-    spare = jnp.full((least * BATCH,), half_rows << shift, jnp.int32)
     batches_of = lambda count: jnp.maximum((count + BATCH - 1) // BATCH, least)
     send_info = jnp.stack([kept, batches_of(entries - kept), shared])
     keep_info = jnp.stack([jnp.zeros_like(kept), batches_of(kept), shared])
-    send_keys = jnp.concatenate([keys - (half_rows << shift), spare])
-    keep_keys = jnp.concatenate([jnp.where(mine, keys, half_rows << shift), spare])
-    index = weight_index.reshape(rows, cols, fan).transpose(2, 0, 1)
-    entry_weights = jnp.zeros((fan, rows, cols), f32)
-    for k in range(intersection_weights.shape[0]):
-        entry_weights = jnp.where(index == k, intersection_weights[k], entry_weights)
 
     line = lambda v: v.reshape(1, -1)
     taps = dw_weight.reshape(-1, channels).astype(f32)
@@ -339,6 +335,7 @@
         out_specs=vmem(),
         scratch_shapes=[pltpu.VMEM((rows + 2 * MARGIN, cols + 2 * PAD, channels), f32)],
         compiler_params=params(),
+        cost_estimate=cost(10),
         name="conv",
     )(state, south, north, taps, line(dw_bias))
     result, terms, grad_conv, grads = pl.pallas_call(
@@ -349,40 +346,43 @@
             shape((rows, cols, channels), f32),
             shape((2 * hid // channels, channels, channels), f32),
         ),
-        in_specs=[vmem()] * 21,
+        in_specs=[vmem()] * 10 + [smem()] + [vmem()] * 11,
         out_specs=[vmem()] * 4,
         scratch_shapes=[
             pltpu.VMEM((rows, cols, channels), f32),
             pltpu.VMEM((2, rows + 2 * MARGIN, 24, channels), f32),
             pltpu.VMEM((channels, hid), f32),
             pltpu.VMEM((channels, hid), f32),
+            pltpu.VMEM((entries // channels, channels), f32),
+            pltpu.VMEM((2 * fan * cols, channels), f32),
         ],
         compiler_params=params(),
+        cost_estimate=cost(13),
         name="block",
     )(
-        state, south, north, left, right, conv, forcing, cotangent, land_mask, entry_weights,
-        taps, line(dw_bias), line(norm_gain), line(norm_bias), up_weight, line(up_bias),
+        state, south, north, left, right, conv, forcing, cotangent, land_mask,
+        weight_index.reshape(-1, channels), intersection_weights, taps, line(dw_bias), line(norm_gain), line(norm_bias), up_weight, line(up_bias),
         down_weight, line(down_bias), line(layer_scale), up_weight.T, down_weight.T,
     )
 
-    send = pl.pallas_call(
-        table_kernel,
-        out_shape=shape((half_rows, channels), bf16),
-        in_specs=[smem(), smem(), vmem()],
-        out_specs=vmem(),
-        scratch_shapes=[pltpu.VMEM((half_rows + 8, channels), f32)],
-        compiler_params=params(),
-        name="send_table",
-    )(send_keys, send_info, terms)
+    zeros = jnp.zeros((half_rows + 8, 1, channels), f32)
+
+    def table(name, place_rows, info, of_terms):
+        return pl.pallas_call(
+            table_kernel,
+            out_shape=shape(zeros.shape, f32),
+            in_specs=[smem()] * 3 + [vmem(), pl.BlockSpec(memory_space=pl.ANY)],
+            out_specs=vmem(),
+            scratch_shapes=[pltpu.SemaphoreType.DMA],
+            compiler_params=params(),
+            cost_estimate=cost(6),
+            name=name,
+        )(place_rows, names, info, of_terms, zeros).reshape(-1, channels)
+
+    terms = terms.reshape(entries, 1, channels)
+    send = table("send_table", send_rows, send_info, terms)[:half_rows].astype(bf16)
     got = swap_bit(send, 0)
-    keep = pl.pallas_call(
-        table_kernel,
-        out_shape=shape((half_rows + 8, channels), f32),
-        in_specs=[smem(), smem(), vmem()],
-        out_specs=vmem(),
-        compiler_params=params(),
-        name="keep_table",
-    )(keep_keys, keep_info, after(terms, send))
+    keep = table("keep_table", keep_rows, keep_info, after(terms, send))
 
     middle = half_rows // 2
     parts = [
@@ -407,6 +407,7 @@
         out_specs=vmem(),
         scratch_shapes=[pltpu.VMEM((rows + 2 * MARGIN, cols + 2 * PAD, channels), f32)],
         compiler_params=params(),
+        cost_estimate=cost(9),
         name="conv_grad",
     )(state, south, north, left, right, after(grad_conv, keep))
     total = jnp.concatenate([grads.reshape(2 * hid, channels), grad_dw], axis=0).astype(bf16)

time: 169 us -> 164 us (0.970)
  other arithmetic: 31.3 us -> 19.9 us
  Pallas kernels: 58.8 us -> 65.1 us
    select_n x2 -> x1, other arithmetic: 10.8 us -> 1.27 us  [on_device(): send_rows = jnp.where(mine, 0, sorted_row - half_rows)]
    pallas_call x2, Pallas kernels: 26.9 us -> 33.1 us  [table(): pl.pallas_call(table_kernel, out_shape=shape(zeros.shape, f32), in_specs=...]
    eq x4 -> x0, local copies, waits for them, and re-layouts: 4.43 us -> none  [on_device(): index == k]
    broadcast_in_dim x0 -> x1, local copies, waits for them, and re-layouts: none -> 3.06 us  [on_device(): zeros = jnp.zeros((half_rows + 8, 1, channels), f32)]
    all_to_all x2, waiting for transfers between devices: 4.91 us -> 7.51 us  [on_device(): lax.all_to_all(total, ('lat', 'lon'), split_axis=0, concat_axis=0, tiled=...]
    convert_element_type x0 -> x1, local copies, waits for them, and re-layouts: none -> 2.39 us  [on_device(): table('send_table', send_rows, send_info, terms)[:half_rows].astype(bf16)]
    select_n x2 -> x0, local copies, waits for them, and re-layouts: 2.01 us -> none  [on_device(): jnp.where(index == k, intersection_weights[k], entry_weights)]
    ppermute x5, waiting for transfers between devices: 11.7 us -> 9.92 us  [swap_bit(): return lax.ppermute(array, 'lon', pairs)]
  transfers between devices with their start and end apart: 12 -> 12, of which waited for: 4 -> 4; matrix products, arithmetic and copies ran while one was open for 25% -> 16% of each run, Pallas kernels for 19% -> 22%
where the time goes in v3:
time: 164 us; the launch traced here: 162 us
  Pallas kernels  65.1 us (40%)
  waiting for transfers between devices  29.7 us (18%)
  starting transfers between devices  24.6 us (15%)
  local copies, waits for them, and re-layouts  20.5 us (12%)
  other arithmetic  19.9 us (12%)
  between operations  2.32 us (1%)
    pallas_call x2, Pallas kernels, table(): pl.pallas_call(table_kernel, out_shape=shape(zeros.shape, f32), in_specs=...  33.1 us
    pallas_call x1, Pallas kernels, on_device(): pl.pallas_call(block_kernel, out_shape=(shape((rows, cols, channels), bf1...  13.4 us
    all_to_all x1, waiting for transfers between devices, on_device(): lax.all_to_all(lined.astype(bf16), 'lat', split_axis=0, concat_axis=0, ti...  12.2 us
    ppermute x5, waiting for transfers between devices, swap_bit(): return lax.ppermute(array, 'lon', pairs)  9.92 us
    pallas_call x1, Pallas kernels, on_device(): pl.pallas_call(conv_kernel, out_shape=shape((rows, cols, channels), f32),...  9.9 us
    pallas_call x1, Pallas kernels, on_device(): pl.pallas_call(conv_grad_kernel, out_shape=shape((dw_rows, channels), f32...  8.67 us
    all_to_all x2, waiting for transfers between devices, on_device(): lax.all_to_all(total, ('lat', 'lon'), split_axis=0, concat_axis=0, tiled=...  7.51 us
    all_to_all x2, starting transfers between devices, on_device(): lax.all_to_all(total, ('lat', 'lon'), split_axis=0, concat_axis=0, tiled=...  7.43 us
  transfers between devices with their start and end apart: 12, of which 4 were waited for; matrix products, arithmetic and copies ran while one was open for 16% of the time, Pallas kernels for 22%

profile of v3, /device:TPU:0, one launch (start us, length us, event | category | flops | bytes accessed | tf_op | source)
XLA Modules:
  0.0 162.1 jit_solution(17364854247605895872)
XLA Ops:
  0.7 1.1 slice.91
  2.1 1.1 select_select_fusion
  3.9 5.9 %collective-permute-start = (bf16[3,384,128]{2,1,0:T(8,128)(2,1)S(1)}, bf16[3,384,128]{2,1,0:T(8,128)(2,1)S(1)}, u32[]{:S(2)}, u32[]{:S(2)}) collective-permute-start(bf16[3,384,128]{2,1,0:T(8,128)(2,1)S(1)} %get-tuple-element.20), channel_id=1, source_target_pairs={{0,8},{1,9},{2,10},{3,11},{4,12},{5,13},{6,14},{7,15},{8,0},{9,1},... | collective-permute-start | bytes 884744 | tf_op jit(solution)/shard_map/ppermute | solution.py:280
  9.9 5.6 %sort.7 = s32[8192]{0:T(1024)S(1)} sort(s32[8192]{0:T(1024)S(1)} %concatenate.20), dimensions={0}, to_apply=%region_1.2 | sort | flops 106496 | bytes 65536 | tf_op jit(solution)/shard_map/sort | solution.py:316
  15.5 1.3 add_select_fusion.4
  20.9 1.9 %add_add_fusion = (s32[3]{0:T(128)}, s32[3]{0:T(128)}) fusion(s32[1]{0:T(128)} %bitcast.13, s32[1]{0:T(128)} %constant.123.clone.1, s32[1]{0:T(128)} %bitcast.14, s32[1]{0:T(128)} %bitcast.17, s32[1]{0:T(128)} %bitcast.16), kind=kLoop, calls=%fused_computation.61 | loop fusion | flops 12 | bytes 44 | tf_op jit(solution)/shard_map/stack | solution.py:327
  23.8 2.7 %collective-permute-start.3 = (bf16[14,3,128]{2,1,0:T(4,128)(2,1)S(1)}, bf16[14,3,128]{2,1,0:T(4,128)(2,1)S(1)}, u32[]{:S(2)}, u32[]{:S(2)}) collective-permute-start(bf16[14,3,128]{2,1,0:T(4,128)(2,1)S(1)} %pad_maximum_fusion.3), channel_id=1, source_target_pairs={{1,0},{2,1},{3,2},{4,3},{5,4},{6,5},{7,6},{0,7},{9,8},{10,9},{11,1... | collective-permute-start | bytes 32264 | tf_op jit(solution)/shard_map/ppermute | solution.py:293
  26.5 9.9 %conv.1 = f32[8,384,128]{2,1,0:T(8,128)} custom-call(bf16[8,384,128]{2,1,0:T(8,128)(2,1)} %state.5, bf16[3,384,128]{2,1,0:T(8,128)(2,1)} %copy-done.5, bf16[3,384,128]{2,1,0:T(8,128)(2,1)} %copy-done.4, f32[49,128]{1,0:T(8,128)} %reshape.90.dw, f32[1,128]{1,0:T(1,128)} %bitcast.47), custom_call_target="tpu_custom_call" | custom-call | flops 10000000000 | tf_op jit(solution)/shard_map/conv/pallas_call | solution.py:331
  37.0 13.4 %block.1 = (bf16[8,384,128]{2,1,0:T(8,128)(2,1)}, f32[6144,128]{1,0:T(8,128)}, f32[8,384,128]{2,1,0:T(8,128)}, f32[8,128,128]{2,1,0:T(8,128)}) custom-call(bf16[8,384,128]{2,1,0:T(8,128)(2,1)} %state.5, bf16[3,384,128]{2,1,0:T(8,128)(2,1)} %copy-done.5, bf16[3,384,128]{2,1,0:T(8,128)(2,1)} %copy-done.4, bf16[14,3,128]{2,1,0:T(4,128)(2,1)} %copy-done.11, ...), custom_call_target="tpu_custom_call" | custom-call | flops 12999999488 | tf_op jit(solution)/shard_map/block/pallas_call | solution.py:341
  50.5 3.1 %broadcast_in_dim.18.zeros = f32[8200,1,128]{2,1,0:T(1,128)} broadcast(f32[]{:T(128)} %constant.130.clone.1), dimensions={} | broadcast | bytes 4198404 | tf_op jit(solution)/shard_map/broadcast_in_dim | solution.py:368
  53.5 16.8 %send_table.1 = f32[8200,1,128]{2,1,0:T(1,128)} custom-call(s32[8192]{0:T(1024)} %get-tuple-element.29.rows, s32[8192]{0:T(1024)} %get-tuple-element.32.names, s32[3]{0:T(128)} %get-tuple-element.37.info, f32[6144,1,128]{2,1,0:T(1,128)} %bitcast.53, f32[8200,1,128]{2,1,0:T(1,128)} %broadcast_in_dim.18.zeros), custom_call_target="tpu_custom_call" | custom-call | flops 6000000000 | tf_op jit(solution)/shard_map/send_table/pallas_call | solution.py:371
  70.4 2.4 %fusion = bf16[8192,128]{1,0:T(8,128)(2,1)S(1)} fusion(f32[8200,1,128]{2,0,1:T(8,128)} %bitcast.40), kind=kLoop, calls=%fused_computation.1 | loop fusion | bytes 4194304 | tf_op jit(solution)/shard_map/convert_element_type | solution.py:383
  72.9 16.3 %keep_table.1 = f32[8200,1,128]{2,1,0:T(1,128)} custom-call(s32[8192]{0:T(1024)} %get-tuple-element.31.rows, s32[8192]{0:T(1024)} %get-tuple-element.32.names, s32[3]{0:T(128)} %get-tuple-element.36.info, f32[6144,1,128]{2,1,0:T(1,128)} %bitcast.54, f32[8200,1,128]{2,1,0:T(1,128)} %broadcast_in_dim.18.zeros), custom_call_target="tpu_custom_call" | custom-call | flops 6000000000 | tf_op jit(solution)/shard_map/keep_table/pallas_call | solution.py:371
  89.2 2.4 %slice.134 = f32[4096,1,128]{2,1,0:T(1,128)S(1)} slice(f32[8200,1,128]{2,1,0:T(1,128)} %keep_table.1), slice={[4096:8192], [0:1], [0:128]} | slice | bytes 4194304 | tf_op jit(solution)/shard_map/slice | solution.py:390
  91.6 2.0 %fusion.1 = (f32[4096,128]{1,0:T(8,128)S(1)}, f32[4096,128]{1,0:T(8,128)S(1)}) fusion(f32[8200,1,128]{2,0,1:T(8,128)} %bitcast.35, bf16[8192,128]{1,0:T(8,128)(2,1)S(1)} %collective-permute-done.4, f32[4096,128]{1,0:T(8,128)S(1)} %bitcast.34), kind=kLoop, calls=%fused_computation.3 | loop fusion | flops 2097152 | bytes 10485760 | tf_op jit(solution)/shard_map/add | solution.py:389
  93.5 1.3 copy-done
  94.9 1.6 collective-permute-start.7
  96.5 8.7 %conv_grad.1 = f32[64,128]{1,0:T(8,128)} custom-call(bf16[8,384,128]{2,1,0:T(8,128)(2,1)} %state.5, bf16[3,384,128]{2,1,0:T(8,128)(2,1)} %copy-done.5, bf16[3,384,128]{2,1,0:T(8,128)(2,1)} %copy-done.4, bf16[14,3,128]{2,1,0:T(4,128)(2,1)} %copy-done.11, bf16[14,3,128]{2,1,0:T(4,128)(2,1)} %copy-done.12, f32[8,384,128]{2,1,0:T(8,128)} %get-tuple-element.12.grad_conv), custom_call_target="tpu_custom_call" | custom-call | flops 8999999488 | tf_op jit(solution)/shard_map/conv_grad/pallas_call | solution.py:403
  106.0 0.9 slice.171
  108.2 4.1 %all-to-all-start = ((bf16[32,34,128]{2,1,0:T(8,128)(2,1)}), bf16[32,34,128]{2,1,0:T(8,128)(2,1)S(1)}, u32[]{:S(2)}, u32[]{:S(2)}) async-start(bf16[32,34,128]{2,1,0:T(8,128)(2,1)} %convert_element_type.62), calls=%async_computation | async-start | bytes 655360 | tf_op jit(solution)/shard_map/all_to_all | solution.py:415
  112.3 1.4 slice_add_fusion
  114.5 1.8 %collective-permute-start.8 = (bf16[1024,128]{1,0:T(8,128)(2,1)}, bf16[1024,128]{1,0:T(8,128)(2,1)}, u32[]{:S(2)}, u32[]{:S(2)}) collective-permute-start(bf16[1024,128]{1,0:T(8,128)(2,1)} %slice.172), channel_id=1, source_target_pairs={{0,2},{1,3},{2,0},{3,1},{4,6},{5,7},{6,4},{7,5},{8,10},{9,11},{10,... | collective-permute-start | bytes 786440 | tf_op jit(solution)/shard_map/ppermute | solution.py:242
  116.3 8.3 %collective-permute-done.5 = bf16[2048,128]{1,0:T(8,128)(2,1)} collective-permute-done((bf16[2048,128]{1,0:T(8,128)(2,1)}, bf16[2048,128]{1,0:T(8,128)(2,1)}, u32[]{:S(2)}, u32[]{:S(2)}) %collective-permute-start.5) | collective-permute-done | bytes 524320 | tf_op jit(solution)/shard_map/ppermute | solution.py:242
  124.6 1.1 slice_add_fusion.1
  125.7 1.0 copy-done.1
  128.0 3.4 %all-to-all-start.1 = ((bf16[32,34,128]{2,1,0:T(8,128)(2,1)}), bf16[32,34,128]{2,1,0:T(8,128)(2,1)S(1)}, u32[]{:S(2)}, u32[]{:S(2)}) async-start(bf16[32,34,128]{2,1,0:T(8,128)(2,1)} %broadcast_in_dim.16), calls=%async_computation.1 | async-start | bytes 655360 | tf_op jit(solution)/shard_map/all_to_all | solution.py:418
  131.4 1.0 fusion.2
  132.4 1.6 collective-permute-done.6
  134.0 1.0 fusion.3
  135.9 7.5 %all-to-all-done.1 = bf16[32,34,128]{2,1,0:T(8,128)(2,1)S(1)} async-done(((bf16[32,34,128]{2,1,0:T(8,128)(2,1)}), bf16[32,34,128]{2,1,0:T(8,128)(2,1)S(1)}, u32[]{:S(2)}, u32[]{:S(2)}) %all-to-all-start.1) | async-done | bytes 278560 | tf_op jit(solution)/shard_map/all_to_all | solution.py:418
  143.4 3.5 %all-to-all-start.2 = ((bf16[4,512,128]{2,1,0:T(8,128)(2,1)}), bf16[4,512,128]{2,1,0:T(8,128)(2,1)S(1)}, u32[]{:S(2)}, u32[]{:S(2)}) async-start(bf16[4,512,128]{2,1,0:T(8,128)(2,1)} %pad_maximum_fusion), calls=%async_computation.2 | async-start | bytes 1048576 | tf_op jit(solution)/shard_map/all_to_all | solution.py:398
  149.1 12.2 %all-to-all-done.2 = bf16[4,512,128]{2,1,0:T(8,128)(2,1)S(1)} async-done(((bf16[4,512,128]{2,1,0:T(8,128)(2,1)}), bf16[4,512,128]{2,1,0:T(8,128)(2,1)S(1)}, u32[]{:S(2)}, u32[]{:S(2)}) %all-to-all-start.2) | async-done | bytes 524320 | tf_op jit(solution)/shard_map/all_to_all | solution.py:398
  (66 shorter events, 13.6 us)
Async XLA Ops:
  0.6 9.2 %copy-start.8 = (s32[6144]{0:T(1024)S(1)}, s32[6144]{0:T(1024)}, u32[]{:S(2)}) copy-start(s32[6144]{0:T(1024)} %param.31) | copy-start | bytes 73732
  0.6 9.2 %copy-start.9 = (s32[6144,1]{0,1:T(1,128)S(1)}, s32[6144,1]{0,1:T(1,128)}, u32[]{:S(2)}) copy-start(s32[6144,1]{0,1:T(1,128)} %param.30) | copy-start | bytes 73732
  0.7 17.4 %copy-start.10 = (bf16[7,7,128]{2,1,0:T(8,128)(2,1)S(1)}, bf16[7,7,128]{2,1,0:T(8,128)(2,1)}, u32[]{:S(2)}) copy-start(bf16[7,7,128]{2,1,0:T(8,128)(2,1)} %param.21) | copy-start | bytes 37636
  0.7 18.7 %copy-start.6 = (bf16[128,512]{1,0:T(8,128)(2,1)S(1)}, bf16[128,512]{1,0:T(8,128)(2,1)}, u32[]{:S(2)}) copy-start(bf16[128,512]{1,0:T(8,128)(2,1)} %up.1) | copy-start | bytes 393220
  0.7 19.5 %copy-start.7 = (bf16[512,128]{1,0:T(8,128)(2,1)S(1)}, bf16[512,128]{1,0:T(8,128)(2,1)}, u32[]{:S(2)}) copy-start(bf16[512,128]{1,0:T(8,128)(2,1)} %down.1) | copy-start | bytes 393220
  3.2 20.4 %collective-permute-start.1 = (bf16[3,384,128]{2,1,0:T(8,128)(2,1)S(1)}, bf16[3,384,128]{2,1,0:T(8,128)(2,1)S(1)}, u32[]{:S(2)}, u32[]{:S(2)}) collective-permute-start(bf16[3,384,128]{2,1,0:T(8,128)(2,1)S(1)} %get-tuple-element.19), channel_id=1, source_target_pairs={{8,16},{9,17},{10,18},{11,19},{12,20},{13,21},{14,22},{15,23},{16,... | collective-permute-start | bytes 884744 | tf_op jit(solution)/shard_map/ppermute | solution.py:281
  3.9 19.7 %collective-permute-start = (bf16[3,384,128]{2,1,0:T(8,128)(2,1)S(1)}, bf16[3,384,128]{2,1,0:T(8,128)(2,1)S(1)}, u32[]{:S(2)}, u32[]{:S(2)}) collective-permute-start(bf16[3,384,128]{2,1,0:T(8,128)(2,1)S(1)} %get-tuple-element.20), channel_id=1, source_target_pairs={{0,8},{1,9},{2,10},{3,11},{4,12},{5,13},{6,14},{7,15},{8,0},{9,1},... | collective-permute-start | bytes 884744 | tf_op jit(solution)/shard_map/ppermute | solution.py:280
  23.7 2.8 %copy-start.4 = (bf16[3,384,128]{2,1,0:T(8,128)(2,1)}, bf16[3,384,128]{2,1,0:T(8,128)(2,1)S(1)}, u32[]{:S(2)}) copy-start(bf16[3,384,128]{2,1,0:T(8,128)(2,1)S(1)} %get-tuple-element.21.north) | copy-start | bytes 884740
  23.7 2.8 %copy-start.5 = (bf16[3,384,128]{2,1,0:T(8,128)(2,1)}, bf16[3,384,128]{2,1,0:T(8,128)(2,1)S(1)}, u32[]{:S(2)}) copy-start(bf16[3,384,128]{2,1,0:T(8,128)(2,1)S(1)} %get-tuple-element.22.south) | copy-start | bytes 884740
  23.8 12.7 %collective-permute-start.2 = (bf16[14,3,128]{2,1,0:T(4,128)(2,1)S(1)}, bf16[14,3,128]{2,1,0:T(4,128)(2,1)S(1)}, u32[]{:S(2)}, u32[]{:S(2)}) collective-permute-start(bf16[14,3,128]{2,1,0:T(4,128)(2,1)S(1)} %pad_maximum_fusion.2), channel_id=1, source_target_pairs={{0,1},{1,2},{2,3},{3,4},{4,5},{5,6},{6,7},{7,0},{8,9},{9,10},{10,1... | collective-permute-start | bytes 32264 | tf_op jit(solution)/shard_map/ppermute | solution.py:292
  23.8 12.6 %collective-permute-start.3 = (bf16[14,3,128]{2,1,0:T(4,128)(2,1)S(1)}, bf16[14,3,128]{2,1,0:T(4,128)(2,1)S(1)}, u32[]{:S(2)}, u32[]{:S(2)}) collective-permute-start(bf16[14,3,128]{2,1,0:T(4,128)(2,1)S(1)} %pad_maximum_fusion.3), channel_id=1, source_target_pairs={{1,0},{2,1},{3,2},{4,3},{5,4},{6,5},{7,6},{0,7},{9,8},{10,9},{11,1... | collective-permute-start | bytes 32264 | tf_op jit(solution)/shard_map/ppermute | solution.py:293
  36.4 0.6 copy-start.11
  36.4 0.6 copy-start.12
  72.8 18.8 %collective-permute-start.4 = (bf16[8192,128]{1,0:T(8,128)(2,1)S(1)}, bf16[8192,128]{1,0:T(8,128)(2,1)S(1)}, u32[]{:S(2)}, u32[]{:S(2)}) collective-permute-start(bf16[8192,128]{1,0:T(8,128)(2,1)S(1)} %fusion), channel_id=1, source_target_pairs={{0,1},{1,0},{2,3},{3,2},{4,5},{5,4},{6,7},{7,6},{8,9},{9,8},{10,11... | collective-permute-start | bytes 6291464 | tf_op jit(solution)/shard_map/ppermute | solution.py:242
  93.5 1.3 copy-start
  94.9 11.1 %copy-start.3 = (f32[8,128,128]{2,1,0:T(8,128)S(1)}, f32[8,128,128]{2,1,0:T(8,128)}, u32[]{:S(2)}) copy-start(f32[8,128,128]{2,1,0:T(8,128)} %get-tuple-element.11) | copy-start | bytes 1572868
  94.9 17.4 %collective-permute-start.7 = (bf16[2048,128]{1,0:T(8,128)(2,1)S(1)}, bf16[2048,128]{1,0:T(8,128)(2,1)}, u32[]{:S(2)}, u32[]{:S(2)}) collective-permute-start(bf16[2048,128]{1,0:T(8,128)(2,1)S(1)} %slice.170), channel_id=1, source_target_pairs={{0,4},{1,5},{2,6},{3,7},{4,0},{5,1},{6,2},{7,3},{8,12},{9,13},{10,... | collective-permute-start | bytes 1572872 | tf_op jit(solution)/shard_map/ppermute | solution.py:242
  106.9 17.7 %collective-permute-start.5 = (bf16[2048,128]{1,0:T(8,128)(2,1)}, bf16[2048,128]{1,0:T(8,128)(2,1)}, u32[]{:S(2)}, u32[]{:S(2)}) collective-permute-start(bf16[2048,128]{1,0:T(8,128)(2,1)} %slice.171), channel_id=1, source_target_pairs={{0,2},{1,3},{2,0},{3,1},{4,6},{5,7},{6,4},{7,5},{8,10},{9,11},{10,... | collective-permute-start | bytes 1572872 | tf_op jit(solution)/shard_map/ppermute | solution.py:242
  108.2 18.9 %all-to-all-start = ((bf16[32,34,128]{2,1,0:T(8,128)(2,1)}), bf16[32,34,128]{2,1,0:T(8,128)(2,1)S(1)}, u32[]{:S(2)}, u32[]{:S(2)}) async-start(bf16[32,34,128]{2,1,0:T(8,128)(2,1)} %convert_element_type.62), calls=%async_computation | async-start | bytes 655360 | tf_op jit(solution)/shard_map/all_to_all | solution.py:415
  114.5 16.9 %collective-permute-start.8 = (bf16[1024,128]{1,0:T(8,128)(2,1)}, bf16[1024,128]{1,0:T(8,128)(2,1)}, u32[]{:S(2)}, u32[]{:S(2)}) collective-permute-start(bf16[1024,128]{1,0:T(8,128)(2,1)} %slice.172), channel_id=1, source_target_pairs={{0,2},{1,3},{2,0},{3,1},{4,6},{5,7},{6,4},{7,5},{8,10},{9,11},{10,... | collective-permute-start | bytes 786440 | tf_op jit(solution)/shard_map/ppermute | solution.py:242
  125.7 1.0 copy-start.1
  126.7 7.3 %copy-start.2 = (f32[2048,128]{1,0:T(8,128)S(1)}, f32[2048,128]{1,0:T(8,128)}, u32[]{:S(2)}) copy-start(f32[2048,128]{1,0:T(8,128)} %copy-done.1) | copy-start | bytes 3145732
  126.8 7.3 %collective-permute-start.6 = (bf16[1024,128]{1,0:T(8,128)(2,1)S(1)}, bf16[1024,128]{1,0:T(8,128)(2,1)}, u32[]{:S(2)}, u32[]{:S(2)}) collective-permute-start(bf16[1024,128]{1,0:T(8,128)(2,1)S(1)} %slice.173), channel_id=1, source_target_pairs={{0,4},{1,5},{2,6},{3,7},{4,0},{5,1},{6,2},{7,3},{8,12},{9,13},{10,... | collective-permute-start | bytes 786440 | tf_op jit(solution)/shard_map/ppermute | solution.py:242
  128.0 15.4 %all-to-all-start.1 = ((bf16[32,34,128]{2,1,0:T(8,128)(2,1)}), bf16[32,34,128]{2,1,0:T(8,128)(2,1)S(1)}, u32[]{:S(2)}, u32[]{:S(2)}) async-start(bf16[32,34,128]{2,1,0:T(8,128)(2,1)} %broadcast_in_dim.16), calls=%async_computation.1 | async-start | bytes 655360 | tf_op jit(solution)/shard_map/all_to_all | solution.py:418
  143.4 17.9 %all-to-all-start.2 = ((bf16[4,512,128]{2,1,0:T(8,128)(2,1)}), bf16[4,512,128]{2,1,0:T(8,128)(2,1)S(1)}, u32[]{:S(2)}, u32[]{:S(2)}) async-start(bf16[4,512,128]{2,1,0:T(8,128)(2,1)} %pad_maximum_fusion), calls=%async_computation.2 | async-start | bytes 1048576 | tf_op jit(solution)/shard_map/all_to_all | solution.py:398

commit v4 on v3

--- a/solution.py
+++ b/solution.py
@@ -9,7 +9,7 @@
 PAD = 8
 TAPS = 7
 MARGIN = 3
-BATCH = 32
+GROUP = 256
 gelu_scale = 0.7978845608028654
 cubic_coef = 0.044715
 f32 = jnp.float32
@@ -205,36 +205,93 @@
             out[pl.ds(a * TAPS + b, 1), :] = jnp.sum(total, axis=0, keepdims=True)
 
 
-def table_kernel(rows, names, info, terms, zeros, table, sem):
-    clear = pltpu.make_async_copy(zeros, table, sem)
-    clear.start()
-    clear.wait()
-    offset = info[0]
-    batches = info[1]
-
-    def add_batch(step, _):
-        place = offset + step
-        found = []
-        for _ in range(BATCH):
-            found.append((rows[place], names[place]))
-            place = place + batches
-        sums = [table[t] + terms[e] for t, e in found]
-        for (t, _), value in zip(found, sums):
-            table[t] = value
+def first_at_least(keys, bound):
+    def step_of(_, ends):
+        low, high = ends
+        middle = (low + high) // 2
+        below = keys[middle] < bound
+        open_ = low < high
+        return (
+            jnp.where(open_ & below, middle + 1, low),
+            jnp.where(open_ & ~below, middle, high),
+        )
+
+    steps = keys.shape[0].bit_length()
+    return lax.fori_loop(0, steps, step_of, (jnp.int32(0), jnp.int32(keys.shape[0])))[0]
+
+
+def add_entries(keys, key_lines, terms, table, block, first_group, groups):
+    shift = (terms.shape[0] - 1).bit_length()
+    size = block.shape[0]
+    group_shift = shift + GROUP.bit_length() - 1
+    begin = first_at_least(keys, first_group << group_shift)
+    end = first_at_least(keys, (first_group + groups) << group_shift)
+
+    def step_of(step, _):
+        base = step * size
+        for k in range(size):
+            name = keys[base + k] & ((1 << shift) - 1)
+            block[pl.ds(k, 1), :] = terms[pl.ds(name, 1), :]
+        values = block[...].astype(bf16)
+        rows = key_lines[pl.ds(step, 1), :] >> shift
+        low = jnp.maximum(keys[base] >> group_shift, first_group)
+        high = jnp.minimum(keys[base + size - 1] >> group_shift, first_group + groups - 1)
+
+        def add_group(group, _):
+            local = jnp.broadcast_to(rows - group * GROUP, (GROUP, size))
+            hit = local == lax.broadcasted_iota(jnp.int32, (GROUP, size), 0)
+            one_hot = jnp.where(hit, 1.0, 0.0).astype(bf16)
+            at = pl.ds(pl.multiple_of((group - first_group) * GROUP, GROUP), GROUP)
+            table[at, :] += jnp.dot(one_hot, values, preferred_element_type=f32)
+            return 0
+
+        lax.fori_loop(low, high + 1, add_group, 0)
         return 0
 
-    def add_one(step, _):
-        t = rows[offset + step]
-        table[t] = table[t] + terms[names[offset + step]]
+    lax.fori_loop(begin // size, (end + size - 1) // size, step_of, 0)
+
+
+def in_chunks(rows, body):
+    chunk = 512
+
+    def step_of(step, _):
+        body(pl.ds(pl.multiple_of(step * chunk, chunk), chunk))
         return 0
 
-    @pl.when(info[2] == 0)
-    def _():
-        lax.fori_loop(0, batches, add_batch, 0)
-
-    @pl.when(info[2] != 0)
-    def _():
-        lax.fori_loop(0, batches * BATCH, add_one, 0)
+    lax.fori_loop(0, rows // chunk, step_of, 0)
+
+
+def send_kernel(keys, key_lines, terms, out, table, block):
+    rows = table.shape[0]
+
+    def clear(at):
+        table[at, :] = jnp.zeros((at.size, table.shape[1]), f32)
+
+    def give(at):
+        out[at, :] = table[at, :].astype(bf16)
+
+    in_chunks(rows, clear)
+    add_entries(keys, key_lines, terms, table, block, rows // GROUP, rows // GROUP)
+    in_chunks(rows, give)
+
+
+def keep_kernel(keys, key_lines, terms, got, kept, send_a, send_b, table, block):
+    rows = table.shape[0]
+
+    def fill(at):
+        table[at, :] = got[at, :].astype(f32)
+
+    in_chunks(rows, fill)
+    add_entries(keys, key_lines, terms, table, block, 0, rows // GROUP)
+    quarter = rows // 4
+    for part, send in enumerate((send_a, send_b)):
+        lower = part * 2 * quarter
+
+        def give(at):
+            kept[part, at, :] = table[pl.ds(lower + at.start, at.size), :]
+            send[at, :] = table[pl.ds(lower + quarter + at.start, at.size), :].astype(bf16)
+
+        in_chunks(quarter, give)
 
 
 def swap_bit(array, bit):
@@ -292,7 +349,7 @@
     left = lax.ppermute(column(slice(cols - MARGIN, cols)), "lon", forward)
     right = lax.ppermute(column(slice(0, MARGIN)), "lon", backward)
 
-    owner_lat = owner[:, 0] // lon_count
+    lat_relative = (owner[:, 0] // lon_count) ^ lat
     relative = (owner[:, 0] % lon_count) ^ lon
     rest = list(range(1, lon_bits))
     orders = [rest, rest[::-1]]
@@ -303,28 +360,16 @@
         number = jnp.zeros_like(relative)
         for bit in order:
             number = number * 2 + ((relative >> bit) & 1)
-        numbers.append(number * lat_count + owner_lat)
+        numbers.append(number * lat_count + lat_relative)
     upper = (atmos_cell >= width).astype(jnp.int32)
     block = jnp.where(upper == 1, numbers[1], numbers[0])
     row = (relative & 1) * half_rows + upper * (half_rows // 2) + block * width
     row = row + atmos_cell - upper * width
     entry = jnp.arange(entries, dtype=jnp.int32)
     shift = (entries - 1).bit_length()
-    least = 64
-    spare = jnp.full((least * BATCH,), 2 * half_rows << shift, jnp.int32)
     keys = (row << shift) + (entry % fan) * cells + entry // fan
-    keys = lax.sort(jnp.concatenate([keys, spare]), is_stable=False)
-    sorted_row = keys >> shift
-    names = keys & ((1 << shift) - 1)
-    mine = sorted_row < half_rows
-    send_rows = jnp.where(mine, 0, sorted_row - half_rows)
-    keep_rows = jnp.where(mine, sorted_row, half_rows)
-    same = sorted_row[least:entries] == sorted_row[: entries - least]
-    shared = jnp.max(same.astype(jnp.int32))
-    kept = jnp.sum(mine.astype(jnp.int32))
-    batches_of = lambda count: jnp.maximum((count + BATCH - 1) // BATCH, least)
-    send_info = jnp.stack([kept, batches_of(entries - kept), shared])
-    keep_info = jnp.stack([jnp.zeros_like(kept), batches_of(kept), shared])
+    keys = lax.sort(keys, is_stable=False)
+    key_lines = keys.reshape(-1, channels)
 
     line = lambda v: v.reshape(1, -1)
     taps = dw_weight.reshape(-1, channels).astype(f32)
@@ -365,38 +410,18 @@
         down_weight, line(down_bias), line(layer_scale), up_weight.T, down_weight.T,
     )
 
-    zeros = jnp.zeros((half_rows + 8, 1, channels), f32)
-
-    def table(name, place_rows, info, of_terms):
-        return pl.pallas_call(
-            table_kernel,
-            out_shape=shape(zeros.shape, f32),
-            in_specs=[smem()] * 3 + [vmem(), pl.BlockSpec(memory_space=pl.ANY)],
-            out_specs=vmem(),
-            scratch_shapes=[pltpu.SemaphoreType.DMA],
-            compiler_params=params(),
-            cost_estimate=cost(6),
-            name=name,
-        )(place_rows, names, info, of_terms, zeros).reshape(-1, channels)
-
-    terms = terms.reshape(entries, 1, channels)
-    send = table("send_table", send_rows, send_info, terms)[:half_rows].astype(bf16)
+    block = pltpu.VMEM((channels, channels), f32)
+    send = pl.pallas_call(
+        send_kernel,
+        out_shape=shape((half_rows, channels), bf16),
+        in_specs=[smem(), vmem(), vmem()],
+        out_specs=vmem(),
+        scratch_shapes=[pltpu.VMEM((half_rows, channels), f32), block],
+        compiler_params=params(),
+        cost_estimate=cost(6),
+        name="send_table",
+    )(keys, key_lines, terms)
     got = swap_bit(send, 0)
-    keep = table("keep_table", keep_rows, keep_info, after(terms, send))
-
-    middle = half_rows // 2
-    parts = [
-        keep[:middle] + got[:middle].astype(f32),
-        keep[middle : 2 * middle] + got[middle:].astype(f32),
-    ]
-    for stage in range(len(rest)):
-        for q, order in enumerate(orders):
-            size = parts[q].shape[0] // 2
-            arrived = swap_bit(parts[q][size:].astype(bf16), order[stage])
-            parts[q] = parts[q][:size] + arrived.astype(f32)
-    lined = jnp.concatenate([p.reshape(lat_count, width, channels) for p in parts], axis=1)
-    bands = lax.all_to_all(lined.astype(bf16), "lat", split_axis=0, concat_axis=0, tiled=True)
-    forcing_grad = jnp.sum(bands.astype(f32), axis=0)
 
     tap_count = dw_weight.shape[0] * dw_weight.shape[1]
     dw_rows = -(-tap_count // devices) * devices
@@ -409,7 +434,42 @@
         compiler_params=params(),
         cost_estimate=cost(9),
         name="conv_grad",
-    )(state, south, north, left, right, after(grad_conv, keep))
+    )(state, south, north, left, right, after(grad_conv, send))
+
+    quarter = half_rows // 4
+    kept, send_a, send_b = pl.pallas_call(
+        keep_kernel,
+        out_shape=(
+            shape((2, quarter, channels), f32),
+            shape((quarter, channels), bf16),
+            shape((quarter, channels), bf16),
+        ),
+        in_specs=[smem(), vmem(), vmem(), vmem()],
+        out_specs=[vmem()] * 3,
+        scratch_shapes=[pltpu.VMEM((half_rows, channels), f32), block],
+        compiler_params=params(),
+        cost_estimate=cost(7),
+        name="keep_table",
+    )(keys, key_lines, after(terms, grad_dw), got)
+
+    sends = [send_a, send_b]
+    kept = [kept[0], kept[1]]
+    for stage in range(len(rest)):
+        arrived = [swap_bit(sends[q], orders[q][stage]) for q in range(2)]
+        if stage + 1 < len(rest):
+            size = kept[0].shape[0] // 2
+            for q in range(2):
+                sends[q] = (kept[q][size:] + arrived[q][size:].astype(f32)).astype(bf16)
+                kept[q] = kept[q][:size] + arrived[q][:size].astype(f32)
+        else:
+            kept = [kept[q] + arrived[q].astype(f32) for q in range(2)]
+    lined = jnp.concatenate([p.reshape(lat_count, width, channels) for p in kept], axis=1)
+    forcing_grad = lined[0]
+    for distance in range(1, lat_count):
+        pairs = [(i, i ^ distance) for i in range(lat_count)]
+        arrived = lax.ppermute(lined[distance].astype(bf16), "lat", pairs)
+        forcing_grad = forcing_grad + arrived.astype(f32)
+
     total = jnp.concatenate([grads.reshape(2 * hid, channels), grad_dw], axis=0).astype(bf16)
     total = total.reshape(devices, -1, channels)
     total = lax.all_to_all(total, ("lat", "lon"), split_axis=0, concat_axis=0, tiled=True)

time: 164 us -> 146 us (0.89)
  local copies, waits for them, and re-layouts: 20.5 us -> 9.98 us
  other arithmetic: 19.9 us -> 13.1 us
    all_to_all x1 -> x0, waiting for transfers between devices: 12.2 us -> none  [on_device(): lax.all_to_all(lined.astype(bf16), 'lat', split_axis=0, concat_axis=0, ti...]
    ppermute x0 -> x3, waiting for transfers between devices: none -> 8.44 us  [on_device(): arrived = lax.ppermute(lined[distance].astype(bf16), 'lat', pairs)]
    ppermute x5, waiting for transfers between devices: 9.92 us -> 17.9 us  [swap_bit(): return lax.ppermute(array, 'lon', pairs)]
    another operation x5 -> x3, other arithmetic: 4.74 us -> 0.11 us
    slice x5 -> x0, local copies, waits for them, and re-layouts: 4.04 us -> none  [the longest x1 2.38 us: on_device(): keep[middle:2 * middle] + got[middle:].astype(f32)]
    ppermute x0 -> x3, starting transfers between devices: none -> 3.85 us  [on_device(): arrived = lax.ppermute(lined[distance].astype(bf16), 'lat', pairs)]
    all_to_all x1 -> x0, starting transfers between devices: 3.47 us -> none  [on_device(): lax.all_to_all(lined.astype(bf16), 'lat', split_axis=0, concat_axis=0, ti...]
    all_to_all x2, waiting for transfers between devices: 7.51 us -> 4.21 us  [on_device(): lax.all_to_all(total, ('lat', 'lon'), split_axis=0, concat_axis=0, tiled=...]
  transfers between devices with their start and end apart: 12 -> 14, of which waited for: 4 -> 7; matrix products, arithmetic and copies ran while one was open for 16% -> 11% of each run, Pallas kernels for 22% -> 13%
where the time goes in v4:
time: 146 us; the launch traced here: 145 us
  Pallas kernels  65.5 us (45%)
  waiting for transfers between devices  30.5 us (21%)
  starting transfers between devices  25.3 us (17%)
  other arithmetic  13.1 us (9%)
  local copies, waits for them, and re-layouts  9.98 us (7%)
    ppermute x5, waiting for transfers between devices, swap_bit(): return lax.ppermute(array, 'lon', pairs)  17.9 us
    pallas_call x1, Pallas kernels, on_device(): pl.pallas_call(keep_kernel, out_shape=(shape((2, quarter, channels), f32)...  17.7 us
    pallas_call x1, Pallas kernels, on_device(): pl.pallas_call(send_kernel, out_shape=shape((half_rows, channels), bf16),...  15.7 us
    pallas_call x1, Pallas kernels, on_device(): pl.pallas_call(block_kernel, out_shape=(shape((rows, cols, channels), bf1...  13.5 us
    pallas_call x1, Pallas kernels, on_device(): pl.pallas_call(conv_kernel, out_shape=shape((rows, cols, channels), f32),...  9.91 us
    pallas_call x1, Pallas kernels, on_device(): pl.pallas_call(conv_grad_kernel, out_shape=shape((dw_rows, channels), f32...  8.67 us
    ppermute x3, waiting for transfers between devices, on_device(): arrived = lax.ppermute(lined[distance].astype(bf16), 'lat', pairs)  8.44 us
    all_to_all x2, starting transfers between devices, on_device(): lax.all_to_all(total, ('lat', 'lon'), split_axis=0, concat_axis=0, tiled=...  7.07 us
  transfers between devices with their start and end apart: 14, of which 7 were waited for; matrix products, arithmetic and copies ran while one was open for 11% of the time, Pallas kernels for 13%

profile of v4, /device:TPU:0, one launch (start us, length us, event | category | flops | bytes accessed | tf_op | source)
XLA Modules:
  0.0 145.3 jit_solution(10811300109480066779)
XLA Ops:
  0.7 1.1 slice.91
  2.1 1.1 select_select_fusion
  3.9 5.9 %collective-permute-start = (bf16[3,384,128]{2,1,0:T(8,128)(2,1)S(1)}, bf16[3,384,128]{2,1,0:T(8,128)(2,1)S(1)}, u32[]{:S(2)}, u32[]{:S(2)}) collective-permute-start(bf16[3,384,128]{2,1,0:T(8,128)(2,1)S(1)} %get-tuple-element.28), channel_id=1, source_target_pairs={{0,8},{1,9},{2,10},{3,11},{4,12},{5,13},{6,14},{7,15},{8,0},{9,1},... | collective-permute-start | bytes 884744 | tf_op jit(solution)/shard_map/ppermute | solution.py:337
  9.9 6.2 %sort.7.keys = s32[6144]{0:T(1024)} sort(s32[6144]{0:T(1024)S(1)} %fusion.14), dimensions={0}, to_apply=%region_0.1 | sort | flops 79872 | bytes 49152 | tf_op jit(solution)/shard_map/sort | solution.py:371
  17.4 0.8 copy.26
  19.2 2.7 %collective-permute-start.3 = (bf16[14,3,128]{2,1,0:T(4,128)(2,1)S(1)}, bf16[14,3,128]{2,1,0:T(4,128)(2,1)S(1)}, u32[]{:S(2)}, u32[]{:S(2)}) collective-permute-start(bf16[14,3,128]{2,1,0:T(4,128)(2,1)S(1)} %pad_maximum_fusion.3), channel_id=1, source_target_pairs={{1,0},{2,1},{3,2},{4,3},{5,4},{6,5},{7,6},{0,7},{9,8},{10,9},{11,1... | collective-permute-start | bytes 32264 | tf_op jit(solution)/shard_map/ppermute | solution.py:350
  21.9 9.9 %conv.1 = f32[8,384,128]{2,1,0:T(8,128)} custom-call(bf16[8,384,128]{2,1,0:T(8,128)(2,1)} %state.5, bf16[3,384,128]{2,1,0:T(8,128)(2,1)} %copy-done.3, bf16[3,384,128]{2,1,0:T(8,128)(2,1)} %copy-done.2, f32[49,128]{1,0:T(8,128)} %reshape.89.dw, f32[1,128]{1,0:T(1,128)} %bitcast.65), custom_call_target="tpu_custom_call" | custom-call | flops 10000000000 | tf_op jit(solution)/shard_map/conv/pallas_call | solution.py:376
  32.4 13.5 %block.1 = (bf16[8,384,128]{2,1,0:T(8,128)(2,1)}, f32[6144,128]{1,0:T(8,128)}, f32[8,384,128]{2,1,0:T(8,128)}, f32[8,128,128]{2,1,0:T(8,128)}) custom-call(bf16[8,384,128]{2,1,0:T(8,128)(2,1)} %state.5, bf16[3,384,128]{2,1,0:T(8,128)(2,1)} %copy-done.3, bf16[3,384,128]{2,1,0:T(8,128)(2,1)} %copy-done.2, bf16[14,3,128]{2,1,0:T(4,128)(2,1)} %copy-done.11, ...), custom_call_target="tpu_custom_call" | custom-call | flops 12999999488 | tf_op jit(solution)/shard_map/block/pallas_call | solution.py:386
  45.9 15.7 %send_table.1 = bf16[8192,128]{1,0:T(8,128)(2,1)} custom-call(s32[6144]{0:T(1024)} %sort.7.keys, s32[48,128]{1,0:T(8,128)} %bitcast.60, f32[6144,128]{1,0:T(8,128)} %get-tuple-element.19.terms), custom_call_target="tpu_custom_call" | custom-call | flops 6000000000 | tf_op jit(solution)/shard_map/send_table/pallas_call | solution.py:414
  61.5 8.7 %conv_grad.1 = f32[64,128]{1,0:T(8,128)} custom-call(bf16[8,384,128]{2,1,0:T(8,128)(2,1)} %state.5, bf16[3,384,128]{2,1,0:T(8,128)(2,1)} %copy-done.3, bf16[3,384,128]{2,1,0:T(8,128)(2,1)} %copy-done.2, bf16[14,3,128]{2,1,0:T(4,128)(2,1)} %copy-done.11, bf16[14,3,128]{2,1,0:T(4,128)(2,1)} %copy-done.12, f32[8,384,128]{2,1,0:T(8,128)} %get-tuple-element.18.grad_conv), custom_call_target="tpu_custom_call" | custom-call | flops 8999999488 | tf_op jit(solution)/shard_map/conv_grad/pallas_call | solution.py:428
  70.2 1.3 copy-done.10
  71.5 17.7 %keep_table.1 = (f32[2,2048,128]{2,1,0:T(8,128)}, bf16[2048,128]{1,0:T(8,128)(2,1)}, bf16[2048,128]{1,0:T(8,128)(2,1)}) custom-call(s32[6144]{0:T(1024)} %sort.7.keys, s32[48,128]{1,0:T(8,128)} %bitcast.61, f32[6144,128]{1,0:T(8,128)} %get-tuple-element.19.terms, bf16[8192,128]{1,0:T(8,128)(2,1)} %copy-done.10), custom_call_target="tpu_custom_call" | custom-call | flops 7000000000 | tf_op jit(solution)/shard_map/keep_table/pallas_call | solution.py:440
  89.3 1.5 %collective-permute-start.7 = (bf16[2048,128]{1,0:T(8,128)(2,1)}, bf16[2048,128]{1,0:T(8,128)(2,1)}, u32[]{:S(2)}, u32[]{:S(2)}) collective-permute-start(bf16[2048,128]{1,0:T(8,128)(2,1)} %get-tuple-element.22), channel_id=1, source_target_pairs={{0,4},{1,5},{2,6},{3,7},{4,0},{5,1},{6,2},{7,3},{8,12},{9,13},{10,... | collective-permute-start | bytes 1572872 | tf_op jit(solution)/shard_map/ppermute | solution.py:299
  90.8 0.8 convert_element_type.72
  91.7 3.1 %all-to-all-start = ((bf16[32,34,128]{2,1,0:T(8,128)(2,1)}), bf16[32,34,128]{2,1,0:T(8,128)(2,1)S(1)}, u32[]{:S(2)}, u32[]{:S(2)}) async-start(bf16[32,34,128]{2,1,0:T(8,128)(2,1)} %convert_element_type.72), calls=%async_computation | async-start | bytes 655360 | tf_op jit(solution)/shard_map/all_to_all | solution.py:475
  94.8 1.8 %collective-permute-start.5 = (bf16[2048,128]{1,0:T(8,128)(2,1)}, bf16[2048,128]{1,0:T(8,128)(2,1)S(1)}, u32[]{:S(2)}, u32[]{:S(2)}) collective-permute-start(bf16[2048,128]{1,0:T(8,128)(2,1)} %get-tuple-element.21), channel_id=1, source_target_pairs={{0,2},{1,3},{2,0},{3,1},{4,6},{5,7},{6,4},{7,5},{8,10},{9,11},{10,... | collective-permute-start | bytes 1572872 | tf_op jit(solution)/shard_map/ppermute | solution.py:299
  96.6 10.9 %collective-permute-done.7 = bf16[2048,128]{1,0:T(8,128)(2,1)} collective-permute-done((bf16[2048,128]{1,0:T(8,128)(2,1)}, bf16[2048,128]{1,0:T(8,128)(2,1)}, u32[]{:S(2)}, u32[]{:S(2)}) %collective-permute-start.7) | collective-permute-done | bytes 524320 | tf_op jit(solution)/shard_map/ppermute | solution.py:299
  107.5 1.7 %fusion.1 = bf16[1024,128]{1,0:T(8,128)(2,1)} fusion(f32[2,2048,128]{2,1,0:T(8,128)S(1)} %copy-done, bf16[2048,128]{1,0:T(8,128)(2,1)} %collective-permute-done.7), kind=kLoop, calls=%fused_computation.6 | loop fusion | flops 393216 | bytes 1048576 | tf_op jit(solution)/shard_map/convert_element_type | solution.py:462
  109.5 0.8 broadcast_in_dim.2
  110.3 4.0 %all-to-all-start.1 = ((bf16[32,34,128]{2,1,0:T(8,128)(2,1)}), bf16[32,34,128]{2,1,0:T(8,128)(2,1)S(1)}, u32[]{:S(2)}, u32[]{:S(2)}) async-start(bf16[32,34,128]{2,1,0:T(8,128)(2,1)} %broadcast_in_dim.2), calls=%async_computation.1 | async-start | bytes 655360 | tf_op jit(solution)/shard_map/all_to_all | solution.py:478
  114.3 4.5 %collective-permute-done.8 = bf16[1024,128]{1,0:T(8,128)(2,1)} collective-permute-done((bf16[1024,128]{1,0:T(8,128)(2,1)}, bf16[1024,128]{1,0:T(8,128)(2,1)}, u32[]{:S(2)}, u32[]{:S(2)}) %collective-permute-start.8) | collective-permute-done | bytes 262176 | tf_op jit(solution)/shard_map/ppermute | solution.py:299
  118.8 1.9 %fusion.2 = (f32[1024,128]{1,0:T(8,128)S(1)}, bf16[1024,128]{1,0:T(8,128)(2,1)}) fusion(bf16[1024,128]{1,0:T(8,128)(2,1)} %collective-permute-done.8, f32[2,2048,128]{2,1,0:T(8,128)S(1)} %copy-done, bf16[2048,128]{1,0:T(8,128)(2,1)} %collective-permute-done.7, bf16[2048,128]{1,0:T(8,128)(2,1)S(1)} %collective-permute-done.5), kind=kLoop, calls=%fused_computation.8 | loop fusion | flops 917504 | bytes 2621440 | tf_op jit(solution)/shard_map/add | solution.py:465
  120.6 1.4 collective-permute-start.6
  122.1 4.2 %all-to-all-done.1 = bf16[32,34,128]{2,1,0:T(8,128)(2,1)S(1)} async-done(((bf16[32,34,128]{2,1,0:T(8,128)(2,1)}), bf16[32,34,128]{2,1,0:T(8,128)(2,1)S(1)}, u32[]{:S(2)}, u32[]{:S(2)}) %all-to-all-start.1) | async-done | bytes 278560 | tf_op jit(solution)/shard_map/all_to_all | solution.py:478
  126.4 2.5 %collective-permute-done.6 = bf16[1024,128]{1,0:T(8,128)(2,1)S(1)} collective-permute-done((bf16[1024,128]{1,0:T(8,128)(2,1)}, bf16[1024,128]{1,0:T(8,128)(2,1)S(1)}, u32[]{:S(2)}, u32[]{:S(2)}) %collective-permute-start.6) | collective-permute-done | bytes 262176 | tf_op jit(solution)/shard_map/ppermute | solution.py:299
  128.9 1.1 fusion.4
  130.1 1.7 %collective-permute-start.9 = (bf16[512,128]{1,0:T(8,128)(2,1)S(1)}, bf16[512,128]{1,0:T(8,128)(2,1)S(1)}, u32[]{:S(2)}, u32[]{:S(2)}) collective-permute-start(bf16[512,128]{1,0:T(8,128)(2,1)S(1)} %get-tuple-element.33), channel_id=1, source_target_pairs={{0,8},{8,0},{16,24},{24,16},{1,9},{9,1},{17,25},{25,17},{2,10},{10... | collective-permute-start | bytes 393224 | tf_op jit(solution)/shard_map/ppermute | solution.py:470
  131.9 2.1 %collective-permute-start.11 = (bf16[512,128]{1,0:T(8,128)(2,1)S(1)}, bf16[512,128]{1,0:T(8,128)(2,1)S(1)}, u32[]{:S(2)}, u32[]{:S(2)}) collective-permute-start(bf16[512,128]{1,0:T(8,128)(2,1)S(1)} %get-tuple-element.34), channel_id=1, source_target_pairs={{0,24},{8,16},{16,8},{24,0},{1,25},{9,17},{17,9},{25,1},{2,26},{10... | collective-permute-start | bytes 393224 | tf_op jit(solution)/shard_map/ppermute | solution.py:470
  136.1 0.9 collective-permute-done.9
  136.9 3.3 %collective-permute-done.11 = bf16[512,128]{1,0:T(8,128)(2,1)S(1)} collective-permute-done((bf16[512,128]{1,0:T(8,128)(2,1)S(1)}, bf16[512,128]{1,0:T(8,128)(2,1)S(1)}, u32[]{:S(2)}, u32[]{:S(2)}) %collective-permute-start.11) | collective-permute-done | bytes 131104 | tf_op jit(solution)/shard_map/ppermute | solution.py:470
  140.2 4.2 %collective-permute-done.10 = bf16[512,128]{1,0:T(8,128)(2,1)S(1)} collective-permute-done((bf16[512,128]{1,0:T(8,128)(2,1)S(1)}, bf16[512,128]{1,0:T(8,128)(2,1)S(1)}, u32[]{:S(2)}, u32[]{:S(2)}) %collective-permute-start.10) | collective-permute-done | bytes 131104 | tf_op jit(solution)/shard_map/ppermute | solution.py:470
  144.5 0.8 fusion.9
  (58 shorter events, 6.7 us)
Async XLA Ops:
  0.6 9.2 %copy-start.7 = (s32[6144]{0:T(1024)S(1)}, s32[6144]{0:T(1024)}, u32[]{:S(2)}) copy-start(s32[6144]{0:T(1024)} %param.31) | copy-start | bytes 73732
  0.6 9.2 %copy-start.8 = (s32[6144,1]{0,1:T(1,128)S(1)}, s32[6144,1]{0,1:T(1,128)}, u32[]{:S(2)}) copy-start(s32[6144,1]{0,1:T(1,128)} %param.30) | copy-start | bytes 73732
  0.7 15.4 %copy-start.9 = (bf16[7,7,128]{2,1,0:T(8,128)(2,1)S(1)}, bf16[7,7,128]{2,1,0:T(8,128)(2,1)}, u32[]{:S(2)}) copy-start(bf16[7,7,128]{2,1,0:T(8,128)(2,1)} %param.21) | copy-start | bytes 37636
  0.7 16.0 %copy-start.4 = (bf16[128,512]{1,0:T(8,128)(2,1)S(1)}, bf16[128,512]{1,0:T(8,128)(2,1)}, u32[]{:S(2)}) copy-start(bf16[128,512]{1,0:T(8,128)(2,1)} %up.1) | copy-start | bytes 393220
  0.7 16.8 %copy-start.5 = (bf16[512,128]{1,0:T(8,128)(2,1)S(1)}, bf16[512,128]{1,0:T(8,128)(2,1)}, u32[]{:S(2)}) copy-start(bf16[512,128]{1,0:T(8,128)(2,1)} %down.1) | copy-start | bytes 393220
  3.2 15.7 %collective-permute-start.1 = (bf16[3,384,128]{2,1,0:T(8,128)(2,1)S(1)}, bf16[3,384,128]{2,1,0:T(8,128)(2,1)S(1)}, u32[]{:S(2)}, u32[]{:S(2)}) collective-permute-start(bf16[3,384,128]{2,1,0:T(8,128)(2,1)S(1)} %get-tuple-element.27), channel_id=1, source_target_pairs={{8,16},{9,17},{10,18},{11,19},{12,20},{13,21},{14,22},{15,23},{16,... | collective-permute-start | bytes 884744 | tf_op jit(solution)/shard_map/ppermute | solution.py:338
  3.9 15.1 %collective-permute-start = (bf16[3,384,128]{2,1,0:T(8,128)(2,1)S(1)}, bf16[3,384,128]{2,1,0:T(8,128)(2,1)S(1)}, u32[]{:S(2)}, u32[]{:S(2)}) collective-permute-start(bf16[3,384,128]{2,1,0:T(8,128)(2,1)S(1)} %get-tuple-element.28), channel_id=1, source_target_pairs={{0,8},{1,9},{2,10},{3,11},{4,12},{5,13},{6,14},{7,15},{8,0},{9,1},... | collective-permute-start | bytes 884744 | tf_op jit(solution)/shard_map/ppermute | solution.py:337
  19.0 2.8 %copy-start.2 = (bf16[3,384,128]{2,1,0:T(8,128)(2,1)}, bf16[3,384,128]{2,1,0:T(8,128)(2,1)S(1)}, u32[]{:S(2)}) copy-start(bf16[3,384,128]{2,1,0:T(8,128)(2,1)S(1)} %get-tuple-element.29.north) | copy-start | bytes 884740
  19.0 2.8 %copy-start.3 = (bf16[3,384,128]{2,1,0:T(8,128)(2,1)}, bf16[3,384,128]{2,1,0:T(8,128)(2,1)S(1)}, u32[]{:S(2)}) copy-start(bf16[3,384,128]{2,1,0:T(8,128)(2,1)S(1)} %get-tuple-element.30.south) | copy-start | bytes 884740
  19.1 12.7 %collective-permute-start.2 = (bf16[14,3,128]{2,1,0:T(4,128)(2,1)S(1)}, bf16[14,3,128]{2,1,0:T(4,128)(2,1)S(1)}, u32[]{:S(2)}, u32[]{:S(2)}) collective-permute-start(bf16[14,3,128]{2,1,0:T(4,128)(2,1)S(1)} %pad_maximum_fusion.2), channel_id=1, source_target_pairs={{0,1},{1,2},{2,3},{3,4},{4,5},{5,6},{6,7},{7,0},{8,9},{9,10},{10,1... | collective-permute-start | bytes 32264 | tf_op jit(solution)/shard_map/ppermute | solution.py:349
  19.2 12.6 %collective-permute-start.3 = (bf16[14,3,128]{2,1,0:T(4,128)(2,1)S(1)}, bf16[14,3,128]{2,1,0:T(4,128)(2,1)S(1)}, u32[]{:S(2)}, u32[]{:S(2)}) collective-permute-start(bf16[14,3,128]{2,1,0:T(4,128)(2,1)S(1)} %pad_maximum_fusion.3), channel_id=1, source_target_pairs={{1,0},{2,1},{3,2},{4,3},{5,4},{6,5},{7,6},{0,7},{9,8},{10,9},{11,1... | collective-permute-start | bytes 32264 | tf_op jit(solution)/shard_map/ppermute | solution.py:350
  31.8 0.6 copy-start.11
  31.8 0.6 copy-start.12
  61.5 8.7 %collective-permute-start.4 = (bf16[8192,128]{1,0:T(8,128)(2,1)}, bf16[8192,128]{1,0:T(8,128)(2,1)S(1)}, u32[]{:S(2)}, u32[]{:S(2)}) collective-permute-start(bf16[8192,128]{1,0:T(8,128)(2,1)} %send_table.1), channel_id=1, source_target_pairs={{0,1},{1,0},{2,3},{3,2},{4,5},{5,4},{6,7},{7,6},{8,9},{9,8},{10,11... | collective-permute-start | bytes 6291464 | tf_op jit(solution)/shard_map/ppermute | solution.py:299
  70.2 20.6 %copy-start.6 = (f32[64,128]{1,0:T(8,128)S(1)}, f32[64,128]{1,0:T(8,128)}, u32[]{:S(2)}) copy-start(f32[64,128]{1,0:T(8,128)} %conv_grad.1) | copy-start | bytes 98308
  70.2 20.6 %copy-start.1 = (f32[8,128,128]{2,1,0:T(8,128)S(1)}, f32[8,128,128]{2,1,0:T(8,128)}, u32[]{:S(2)}) copy-start(f32[8,128,128]{2,1,0:T(8,128)} %get-tuple-element.15) | copy-start | bytes 1572868
  70.2 1.3 copy-start.10
  89.3 18.2 %copy-start = (f32[2,2048,128]{2,1,0:T(8,128)S(1)}, f32[2,2048,128]{2,1,0:T(8,128)}, u32[]{:S(2)}) copy-start(f32[2,2048,128]{2,1,0:T(8,128)} %get-tuple-element.20) | copy-start | bytes 6291460
  89.3 18.2 %collective-permute-start.7 = (bf16[2048,128]{1,0:T(8,128)(2,1)}, bf16[2048,128]{1,0:T(8,128)(2,1)}, u32[]{:S(2)}, u32[]{:S(2)}) collective-permute-start(bf16[2048,128]{1,0:T(8,128)(2,1)} %get-tuple-element.22), channel_id=1, source_target_pairs={{0,4},{1,5},{2,6},{3,7},{4,0},{5,1},{6,2},{7,3},{8,12},{9,13},{10,... | collective-permute-start | bytes 1572872 | tf_op jit(solution)/shard_map/ppermute | solution.py:299
  91.7 17.8 %all-to-all-start = ((bf16[32,34,128]{2,1,0:T(8,128)(2,1)}), bf16[32,34,128]{2,1,0:T(8,128)(2,1)S(1)}, u32[]{:S(2)}, u32[]{:S(2)}) async-start(bf16[32,34,128]{2,1,0:T(8,128)(2,1)} %convert_element_type.72), calls=%async_computation | async-start | bytes 655360 | tf_op jit(solution)/shard_map/all_to_all | solution.py:475
  94.8 19.5 %collective-permute-start.5 = (bf16[2048,128]{1,0:T(8,128)(2,1)}, bf16[2048,128]{1,0:T(8,128)(2,1)S(1)}, u32[]{:S(2)}, u32[]{:S(2)}) collective-permute-start(bf16[2048,128]{1,0:T(8,128)(2,1)} %get-tuple-element.21), channel_id=1, source_target_pairs={{0,2},{1,3},{2,0},{3,1},{4,6},{5,7},{6,4},{7,5},{8,10},{9,11},{10,... | collective-permute-start | bytes 1572872 | tf_op jit(solution)/shard_map/ppermute | solution.py:299
  109.2 9.6 %collective-permute-start.8 = (bf16[1024,128]{1,0:T(8,128)(2,1)}, bf16[1024,128]{1,0:T(8,128)(2,1)}, u32[]{:S(2)}, u32[]{:S(2)}) collective-permute-start(bf16[1024,128]{1,0:T(8,128)(2,1)} %fusion.1), channel_id=1, source_target_pairs={{0,2},{1,3},{2,0},{3,1},{4,6},{5,7},{6,4},{7,5},{8,10},{9,11},{10,... | collective-permute-start | bytes 786440 | tf_op jit(solution)/shard_map/ppermute | solution.py:299
  110.3 16.0 %all-to-all-start.1 = ((bf16[32,34,128]{2,1,0:T(8,128)(2,1)}), bf16[32,34,128]{2,1,0:T(8,128)(2,1)S(1)}, u32[]{:S(2)}, u32[]{:S(2)}) async-start(bf16[32,34,128]{2,1,0:T(8,128)(2,1)} %broadcast_in_dim.2), calls=%async_computation.1 | async-start | bytes 655360 | tf_op jit(solution)/shard_map/all_to_all | solution.py:478
  120.6 8.3 %collective-permute-start.6 = (bf16[1024,128]{1,0:T(8,128)(2,1)}, bf16[1024,128]{1,0:T(8,128)(2,1)S(1)}, u32[]{:S(2)}, u32[]{:S(2)}) collective-permute-start(bf16[1024,128]{1,0:T(8,128)(2,1)} %get-tuple-element.24), channel_id=1, source_target_pairs={{0,4},{1,5},{2,6},{3,7},{4,0},{5,1},{6,2},{7,3},{8,12},{9,13},{10,... | collective-permute-start | bytes 786440 | tf_op jit(solution)/shard_map/ppermute | solution.py:299
  130.1 6.8 %collective-permute-start.9 = (bf16[512,128]{1,0:T(8,128)(2,1)S(1)}, bf16[512,128]{1,0:T(8,128)(2,1)S(1)}, u32[]{:S(2)}, u32[]{:S(2)}) collective-permute-start(bf16[512,128]{1,0:T(8,128)(2,1)S(1)} %get-tuple-element.33), channel_id=1, source_target_pairs={{0,8},{8,0},{16,24},{24,16},{1,9},{9,1},{17,25},{25,17},{2,10},{10... | collective-permute-start | bytes 393224 | tf_op jit(solution)/shard_map/ppermute | solution.py:470
  131.9 8.4 %collective-permute-start.11 = (bf16[512,128]{1,0:T(8,128)(2,1)S(1)}, bf16[512,128]{1,0:T(8,128)(2,1)S(1)}, u32[]{:S(2)}, u32[]{:S(2)}) collective-permute-start(bf16[512,128]{1,0:T(8,128)(2,1)S(1)} %get-tuple-element.34), channel_id=1, source_target_pairs={{0,24},{8,16},{16,8},{24,0},{1,25},{9,17},{17,9},{25,1},{2,26},{10... | collective-permute-start | bytes 393224 | tf_op jit(solution)/shard_map/ppermute | solution.py:470
  134.0 10.5 %collective-permute-start.10 = (bf16[512,128]{1,0:T(8,128)(2,1)S(1)}, bf16[512,128]{1,0:T(8,128)(2,1)S(1)}, u32[]{:S(2)}, u32[]{:S(2)}) collective-permute-start(bf16[512,128]{1,0:T(8,128)(2,1)S(1)} %get-tuple-element.35), channel_id=1, source_target_pairs={{0,16},{8,24},{16,0},{24,8},{1,17},{9,25},{17,1},{25,9},{2,18},{10... | collective-permute-start | bytes 393224 | tf_op jit(solution)/shard_map/ppermute | solution.py:470

commit v5 on v3

--- a/solution.py
+++ b/solution.py
@@ -1,3 +1,5 @@
+import functools
+
 import jax
 import jax.numpy as jnp
 from jax import lax
@@ -9,7 +11,8 @@
 PAD = 8
 TAPS = 7
 MARGIN = 3
-BATCH = 32
+BATCH = 16
+BATCHES = 2
 gelu_scale = 0.7978845608028654
 cubic_coef = 0.044715
 f32 = jnp.float32
@@ -17,8 +20,8 @@
 shape = jax.ShapeDtypeStruct
 
 
-def params():
-    return pltpu.CompilerParams(vmem_limit_bytes=56 << 20)
+def params(mebibytes=40):
+    return pltpu.CompilerParams(vmem_limit_bytes=mebibytes << 20)
 
 
 def cost(microseconds):
@@ -29,8 +32,22 @@
     return pl.BlockSpec(memory_space=pltpu.VMEM)
 
 
+def anywhere():
+    return pl.BlockSpec(memory_space=pl.ANY)
+
+
 def smem():
     return pl.BlockSpec(memory_space=pltpu.SMEM)
+
+
+def in_chunks(rows, body):
+    chunk = 512
+
+    def step_of(step, _):
+        body(pl.ds(pl.multiple_of(step * chunk, chunk), chunk))
+        return 0
+
+    lax.fori_loop(0, rows // chunk, step_of, 0)
 
 
 def conv_block(field, base, dw, dwb, rows, channels):
@@ -73,10 +90,17 @@
 
 def block_kernel(
     state, south, north, left, right, conv, forcing, cotangent, land, weight_index, weight_table,
-    dw, dwb, gain, nbias, up, upb, down, downb, scale, up_t, down_t,
-    result, terms, grad_conv, grads, field, edge, acc_up, acc_down, entry_weights, spread,
+    target_list, clash_list, dw, dwb, gain, nbias, up, upb, down, downb, scale, up_t, down_t,
+    result, keep_0, keep_1, keep_2, keep_3, send, grad_conv, grads,
+    field, edge, acc_up, acc_down, entry_weights, spread, terms, table, targets, clash, sems,
 ):
     rows, cols, channels = state.shape
+    scalar_copies = [
+        pltpu.make_async_copy(target_list, targets, sems.at[0]),
+        pltpu.make_async_copy(clash_list, clash, sems.at[1]),
+    ]
+    for copy in scalar_copies:
+        copy.start()
     wide = 16
     for side in range(2):
         own = slice(0, wide) if side == 0 else slice(cols - wide, cols)
@@ -99,6 +123,10 @@
     for r in range(rows):
         field[r, 8 : cols - 8, :] = conv[r, 8 : cols - 8, :]
 
+    def clear(at):
+        table[at, :] = jnp.zeros((at.size, channels), f32)
+
+    in_chunks(table.shape[0], clear)
     index = weight_index[...]
     looked_up = jnp.zeros(index.shape, f32)
     for k in range(weight_table.shape[0]):
@@ -108,7 +136,7 @@
     acc_down[...] = jnp.zeros_like(acc_down)
     group = 2
     size = group * cols
-    fan = terms.shape[0] // (rows * cols)
+    fan = terms.shape[0] // size
     lines = fan * size // channels
 
     def column(ref, first, count):
@@ -149,11 +177,10 @@
         grad_hidden = jnp.dot(grad_out, down_t[...], preferred_element_type=f32)
         grad_pre = (grad_hidden * slope).astype(bf16)
         gmix = jnp.dot(grad_pre, up_t[...], preferred_element_type=f32)
-        at = pl.multiple_of(step * size, 8)
         spread[...] = column(entry_weights, step * lines, lines)
         for k in range(fan):
             weights = spread[pl.ds(k, size, stride=fan), :]
-            terms[pl.ds(k * rows * cols + at, size), :] = weights * gmix
+            terms[pl.ds(k * size, size), :] = weights * gmix
         gained = gmix * gain[...]
         gconv = inv_std * (
             gained
@@ -164,14 +191,96 @@
         contract = (((0,), (0,)), ((), ()))
         acc_up[...] += lax.dot_general(mixed, grad_pre, contract, preferred_element_type=f32)
         acc_down[...] += lax.dot_general(grad_out, hidden, contract, preferred_element_type=f32)
+
+        @pl.when(step == 0)
+        def _():
+            for copy in scalar_copies:
+                copy.wait()
+
+        unit = BATCH * BATCHES
+        units = fan * size // unit
+
+        def add_unit(index, _):
+            first_cell = index * (unit // fan)
+            first_entry = step * (fan * size) + index * unit
+
+            def entry(k):
+                cell = first_cell + k // fan
+                return targets[first_entry + k], terms[pl.ds((k % fan) * size + cell, 1), :]
+
+            clashing = clash[first_entry]
+
+            @pl.when(clashing == 0)
+            def _():
+                for batch in range(BATCHES):
+                    found = [entry(batch * BATCH + k) for k in range(BATCH)]
+                    sums = [table[pl.ds(t, 1), :] + v for t, v in found]
+                    for (t, _), value in zip(found, sums):
+                        table[pl.ds(t, 1), :] = value
+
+            @pl.when(clashing != 0)
+            def _():
+                for k in range(unit):
+                    t, v = entry(k)
+                    table[pl.ds(t, 1), :] = table[pl.ds(t, 1), :] + v
+
+            return 0
+
+        lax.fori_loop(0, units, add_unit, 0)
         return 0
 
     lax.fori_loop(0, rows // group, mlp_step, 0)
+    half = table.shape[0] // 2
+
+    keep_copies = [
+        pltpu.make_async_copy(table.at[pl.ds(k * (half // 4), half // 4)], keep, sems.at[2 + k])
+        for k, keep in enumerate((keep_0, keep_1, keep_2, keep_3))
+    ]
+    for copy in keep_copies:
+        copy.start()
+
+    def give(at):
+        send[at, :] = table[pl.ds(half + at.start, at.size), :].astype(bf16)
+
+    in_chunks(half, give)
     blocks = up.shape[1] // channels
     for k in range(blocks):
         part = slice(k * channels, (k + 1) * channels)
         grads[k] = acc_up[:, part]
         grads[blocks + k] = acc_down[:, part].T
+    for copy in keep_copies:
+        copy.wait()
+
+
+def target_kernel(lat_count, lon_count, orders, owner, cell, targets, clash):
+    lat, lon = lax.axis_index("lat"), lax.axis_index("lon")
+    lon_bits = lon_count.bit_length() - 1
+    half_rows = lat_count * lon_count // 2 * A_DEV
+    width = A_DEV // 2
+    device = owner[...]
+    at_lat = (device >> lon_bits) ^ lat
+    at_lon = (device & (lon_count - 1)) ^ lon
+    numbers = []
+    for order in orders:
+        number = jnp.zeros_like(device)
+        for bit in order:
+            number = number * 2 + ((at_lon >> bit) & 1)
+        numbers.append(number * lat_count + at_lat)
+    upper = (cell[...] >= width).astype(jnp.int32)
+    block = jnp.where(upper == 1, numbers[1], numbers[0])
+    row = (at_lon & 1) * half_rows + upper * (half_rows // 2) + block * width
+    row = row + cell[...] - upper * width
+    targets[...] = row
+    lane = lax.broadcasted_iota(jnp.int32, row.shape, 1)
+    twice = jnp.zeros_like(row)
+    for distance in range(1, BATCH):
+        same = (row == pltpu.roll(row, distance, 1)) & (lane % BATCH >= distance)
+        twice = jnp.where(same, 1, twice)
+    distance = 1
+    while distance < BATCH * BATCHES:
+        twice = jnp.maximum(twice, pltpu.roll(twice, row.shape[1] - distance, 1))
+        distance *= 2
+    clash[...] = twice
 
 
 def conv_grad_kernel(state, south, north, left, right, grad_conv, out, padded):
@@ -203,38 +312,6 @@
         for a in range(TAPS):
             total = sums[2 * a] + sums[2 * a + 1]
             out[pl.ds(a * TAPS + b, 1), :] = jnp.sum(total, axis=0, keepdims=True)
-
-
-def table_kernel(rows, names, info, terms, zeros, table, sem):
-    clear = pltpu.make_async_copy(zeros, table, sem)
-    clear.start()
-    clear.wait()
-    offset = info[0]
-    batches = info[1]
-
-    def add_batch(step, _):
-        place = offset + step
-        found = []
-        for _ in range(BATCH):
-            found.append((rows[place], names[place]))
-            place = place + batches
-        sums = [table[t] + terms[e] for t, e in found]
-        for (t, _), value in zip(found, sums):
-            table[t] = value
-        return 0
-
-    def add_one(step, _):
-        t = rows[offset + step]
-        table[t] = table[t] + terms[names[offset + step]]
-        return 0
-
-    @pl.when(info[2] == 0)
-    def _():
-        lax.fori_loop(0, batches, add_batch, 0)
-
-    @pl.when(info[2] != 0)
-    def _():
-        lax.fori_loop(0, batches * BATCH, add_one, 0)
 
 
 def swap_bit(array, bit):
@@ -292,39 +369,19 @@
     left = lax.ppermute(column(slice(cols - MARGIN, cols)), "lon", forward)
     right = lax.ppermute(column(slice(0, MARGIN)), "lon", backward)
 
-    owner_lat = owner[:, 0] // lon_count
-    relative = (owner[:, 0] % lon_count) ^ lon
     rest = list(range(1, lon_bits))
     orders = [rest, rest[::-1]]
     width = A_DEV // 2
     half_rows = devices // 2 * A_DEV
-    numbers = []
-    for order in orders:
-        number = jnp.zeros_like(relative)
-        for bit in order:
-            number = number * 2 + ((relative >> bit) & 1)
-        numbers.append(number * lat_count + owner_lat)
-    upper = (atmos_cell >= width).astype(jnp.int32)
-    block = jnp.where(upper == 1, numbers[1], numbers[0])
-    row = (relative & 1) * half_rows + upper * (half_rows // 2) + block * width
-    row = row + atmos_cell - upper * width
-    entry = jnp.arange(entries, dtype=jnp.int32)
-    shift = (entries - 1).bit_length()
-    least = 64
-    spare = jnp.full((least * BATCH,), 2 * half_rows << shift, jnp.int32)
-    keys = (row << shift) + (entry % fan) * cells + entry // fan
-    keys = lax.sort(jnp.concatenate([keys, spare]), is_stable=False)
-    sorted_row = keys >> shift
-    names = keys & ((1 << shift) - 1)
-    mine = sorted_row < half_rows
-    send_rows = jnp.where(mine, 0, sorted_row - half_rows)
-    keep_rows = jnp.where(mine, sorted_row, half_rows)
-    same = sorted_row[least:entries] == sorted_row[: entries - least]
-    shared = jnp.max(same.astype(jnp.int32))
-    kept = jnp.sum(mine.astype(jnp.int32))
-    batches_of = lambda count: jnp.maximum((count + BATCH - 1) // BATCH, least)
-    send_info = jnp.stack([kept, batches_of(entries - kept), shared])
-    keep_info = jnp.stack([jnp.zeros_like(kept), batches_of(kept), shared])
+    lines = (entries // channels, channels)
+    targets, clash = pl.pallas_call(
+        functools.partial(target_kernel, lat_count, lon_count, orders),
+        out_shape=(shape(lines, jnp.int32),) * 2,
+        in_specs=[vmem()] * 2,
+        out_specs=[vmem()] * 2,
+        cost_estimate=cost(1),
+        name="targets",
+    )(owner.reshape(lines), atmos_cell.reshape(lines))
 
     line = lambda v: v.reshape(1, -1)
     taps = dw_weight.reshape(-1, channels).astype(f32)
@@ -338,16 +395,18 @@
         cost_estimate=cost(10),
         name="conv",
     )(state, south, north, taps, line(dw_bias))
-    result, terms, grad_conv, grads = pl.pallas_call(
+    quarter = shape((half_rows // 4, channels), f32)
+    result, *keep, send, grad_conv, grads = pl.pallas_call(
         block_kernel,
         out_shape=(
             shape((rows, cols, channels), bf16),
-            shape((entries, channels), f32),
+            *(quarter,) * 4,
+            shape((half_rows, channels), bf16),
             shape((rows, cols, channels), f32),
             shape((2 * hid // channels, channels, channels), f32),
         ),
-        in_specs=[vmem()] * 10 + [smem()] + [vmem()] * 11,
-        out_specs=[vmem()] * 4,
+        in_specs=[vmem()] * 10 + [smem()] + [anywhere()] * 2 + [vmem()] * 11,
+        out_specs=[vmem()] + [anywhere()] * 4 + [vmem()] * 3,
         scratch_shapes=[
             pltpu.VMEM((rows, cols, channels), f32),
             pltpu.VMEM((2, rows + 2 * MARGIN, 24, channels), f32),
@@ -355,48 +414,23 @@
             pltpu.VMEM((channels, hid), f32),
             pltpu.VMEM((entries // channels, channels), f32),
             pltpu.VMEM((2 * fan * cols, channels), f32),
+            pltpu.VMEM((2 * fan * cols, channels), f32),
+            pltpu.VMEM((2 * half_rows, channels), f32),
+            pltpu.SMEM((entries,), jnp.int32),
+            pltpu.SMEM((entries,), jnp.int32),
+            pltpu.SemaphoreType.DMA((6,)),
         ],
-        compiler_params=params(),
-        cost_estimate=cost(13),
+        compiler_params=params(min(60, 28 + (half_rows * channels * 10 >> 20))),
+        cost_estimate=cost(28),
         name="block",
     )(
         state, south, north, left, right, conv, forcing, cotangent, land_mask,
-        weight_index.reshape(-1, channels), intersection_weights, taps, line(dw_bias), line(norm_gain), line(norm_bias), up_weight, line(up_bias),
+        weight_index.reshape(-1, channels), intersection_weights,
+        targets.reshape(-1), clash.reshape(-1), taps, line(dw_bias), line(norm_gain), line(norm_bias), up_weight, line(up_bias),
         down_weight, line(down_bias), line(layer_scale), up_weight.T, down_weight.T,
     )
 
-    zeros = jnp.zeros((half_rows + 8, 1, channels), f32)
-
-    def table(name, place_rows, info, of_terms):
-        return pl.pallas_call(
-            table_kernel,
-            out_shape=shape(zeros.shape, f32),
-            in_specs=[smem()] * 3 + [vmem(), pl.BlockSpec(memory_space=pl.ANY)],
-            out_specs=vmem(),
-            scratch_shapes=[pltpu.SemaphoreType.DMA],
-            compiler_params=params(),
-            cost_estimate=cost(6),
-            name=name,
-        )(place_rows, names, info, of_terms, zeros).reshape(-1, channels)
-
-    terms = terms.reshape(entries, 1, channels)
-    send = table("send_table", send_rows, send_info, terms)[:half_rows].astype(bf16)
     got = swap_bit(send, 0)
-    keep = table("keep_table", keep_rows, keep_info, after(terms, send))
-
-    middle = half_rows // 2
-    parts = [
-        keep[:middle] + got[:middle].astype(f32),
-        keep[middle : 2 * middle] + got[middle:].astype(f32),
-    ]
-    for stage in range(len(rest)):
-        for q, order in enumerate(orders):
-            size = parts[q].shape[0] // 2
-            arrived = swap_bit(parts[q][size:].astype(bf16), order[stage])
-            parts[q] = parts[q][:size] + arrived.astype(f32)
-    lined = jnp.concatenate([p.reshape(lat_count, width, channels) for p in parts], axis=1)
-    bands = lax.all_to_all(lined.astype(bf16), "lat", split_axis=0, concat_axis=0, tiled=True)
-    forcing_grad = jnp.sum(bands.astype(f32), axis=0)
 
     tap_count = dw_weight.shape[0] * dw_weight.shape[1]
     dw_rows = -(-tap_count // devices) * devices
@@ -409,7 +443,29 @@
         compiler_params=params(),
         cost_estimate=cost(9),
         name="conv_grad",
-    )(state, south, north, left, right, after(grad_conv, keep))
+    )(state, south, north, left, right, after(grad_conv, send))
+
+    size = half_rows // 4
+    got = after(got, grad_dw)
+    merged = [keep[k] + got[k * size : (k + 1) * size].astype(f32) for k in range(4)]
+    kept = [merged[0], merged[2]]
+    sends = [merged[1].astype(bf16), merged[3].astype(bf16)]
+    for stage in range(len(rest)):
+        arrived = [swap_bit(sends[q], orders[q][stage]) for q in range(2)]
+        if stage + 1 < len(rest):
+            size = kept[0].shape[0] // 2
+            for q in range(2):
+                sends[q] = (kept[q][size:] + arrived[q][size:].astype(f32)).astype(bf16)
+                kept[q] = kept[q][:size] + arrived[q][:size].astype(f32)
+        else:
+            kept = [kept[q] + arrived[q].astype(f32) for q in range(2)]
+    lined = jnp.concatenate([p.reshape(lat_count, width, channels) for p in kept], axis=1)
+    forcing_grad = lined[0]
+    for distance in range(1, lat_count):
+        pairs = [(i, i ^ distance) for i in range(lat_count)]
+        arrived = lax.ppermute(lined[distance].astype(bf16), "lat", pairs)
+        forcing_grad = forcing_grad + arrived.astype(f32)
+
     total = jnp.concatenate([grads.reshape(2 * hid, channels), grad_dw], axis=0).astype(bf16)
     total = total.reshape(devices, -1, channels)
     total = lax.all_to_all(total, ("lat", "lon"), split_axis=0, concat_axis=0, tiled=True)

time: 164 us -> 126 us (0.77)
  Pallas kernels: 65.1 us -> 41.1 us
  local copies, waits for them, and re-layouts: 20.5 us -> 7.73 us
  other arithmetic: 19.9 us -> 11 us
  waiting for transfers between devices: 29.7 us -> 34.7 us
  starting transfers between devices: 24.6 us -> 29.2 us
    pallas_call x2 -> x1, Pallas kernels: 33.1 us -> 1.9 us  [on_device(): pl.pallas_call(functools.partial(target_kernel, lat_count, lon_count, ord...]
    all_to_all x1 -> x0, waiting for transfers between devices: 12.2 us -> none  [on_device(): lax.all_to_all(lined.astype(bf16), 'lat', split_axis=0, concat_axis=0, ti...]
    pallas_call x1, Pallas kernels: 13.4 us -> 25.3 us  [on_device(): pl.pallas_call(block_kernel, out_shape=(shape((rows, cols, channels), bf1...]
    ppermute x0 -> x3, waiting for transfers between devices: none -> 8.29 us  [on_device(): arrived = lax.ppermute(lined[distance].astype(bf16), 'lat', pairs)]
    convert_element_type x0 -> x3, other arithmetic: none -> 6.76 us  [the longest x1 3.73 us: on_device(): sends = [merged[1].astype(bf16), merged[3].astype(bf16)]]
    sort x1 -> x0, other arithmetic: 5.59 us -> none  [on_device(): keys = lax.sort(jnp.concatenate([keys, spare]), is_stable=False)]
    another operation x5 -> x3, other arithmetic: 4.74 us -> 0.11 us
    ppermute x0 -> x3, starting transfers between devices: none -> 4.26 us  [on_device(): arrived = lax.ppermute(lined[distance].astype(bf16), 'lat', pairs)]
  transfers between devices with their start and end apart: 12 -> 14, of which waited for: 4 -> 10; matrix products, arithmetic and copies ran while one was open for 16% -> 11% of each run, Pallas kernels for 22% -> 13%
where the time goes in v5:
time: 126 us; the launch traced here: 125 us
  Pallas kernels  41.1 us (33%)
  waiting for transfers between devices  34.7 us (28%)
  starting transfers between devices  29.2 us (23%)
  other arithmetic  11 us (9%)
  local copies, waits for them, and re-layouts  7.73 us (6%)
    pallas_call x1, Pallas kernels, on_device(): pl.pallas_call(block_kernel, out_shape=(shape((rows, cols, channels), bf1...  25.3 us
    ppermute x5, waiting for transfers between devices, swap_bit(): return lax.ppermute(array, 'lon', pairs)  12.9 us
    all_to_all x2, waiting for transfers between devices, on_device(): lax.all_to_all(total, ('lat', 'lon'), split_axis=0, concat_axis=0, tiled=...  9.7 us
    all_to_all x2, starting transfers between devices, on_device(): lax.all_to_all(total, ('lat', 'lon'), split_axis=0, concat_axis=0, tiled=...  8.32 us
    ppermute x3, waiting for transfers between devices, on_device(): arrived = lax.ppermute(lined[distance].astype(bf16), 'lat', pairs)  8.29 us
    pallas_call x1, Pallas kernels, on_device(): pl.pallas_call(conv_kernel, out_shape=shape((rows, cols, channels), f32),...  7.73 us
    ppermute x5, starting transfers between devices, swap_bit(): return lax.ppermute(array, 'lon', pairs)  7.28 us
    pallas_call x1, Pallas kernels, on_device(): pl.pallas_call(conv_grad_kernel, out_shape=shape((dw_rows, channels), f32...  6.17 us
  transfers between devices with their start and end apart: 14, of which 10 were waited for; matrix products, arithmetic and copies ran while one was open for 11% of the time, Pallas kernels for 13%

profile of v5, /device:TPU:0, one launch (start us, length us, event | category | flops | bytes accessed | tf_op | source)
XLA Modules:
  0.0 124.8 jit_solution(5030843549923115433)
XLA Ops:
  0.7 1.0 slice.85
  2.1 1.1 select_select_fusion
  3.9 5.9 %collective-permute-start = (bf16[3,384,128]{2,1,0:T(8,128)(2,1)S(1)}, bf16[3,384,128]{2,1,0:T(8,128)(2,1)S(1)}, u32[]{:S(2)}, u32[]{:S(2)}) collective-permute-start(bf16[3,384,128]{2,1,0:T(8,128)(2,1)S(1)} %get-tuple-element.36), channel_id=1, source_target_pairs={{0,8},{1,9},{2,10},{3,11},{4,12},{5,13},{6,14},{7,15},{8,0},{9,1},... | collective-permute-start | bytes 884744 | tf_op jit(solution)/shard_map/ppermute | solution.py:357
  10.7 1.9 %targets.1 = (s32[48,128]{1,0:T(8,128)}, s32[48,128]{1,0:T(8,128)}) custom-call(s32[48,128]{1,0:T(8,128)} %bitcast.56, s32[48,128]{1,0:T(8,128)} %bitcast.57), custom_call_target="tpu_custom_call" | custom-call | flops 1000000000 | tf_op jit(solution)/shard_map/targets/pallas_call | solution.py:377
  12.7 3.8 %collective-permute-done = bf16[3,384,128]{2,1,0:T(8,128)(2,1)S(1)} collective-permute-done((bf16[3,384,128]{2,1,0:T(8,128)(2,1)S(1)}, bf16[3,384,128]{2,1,0:T(8,128)(2,1)S(1)}, u32[]{:S(2)}, u32[]{:S(2)}) %collective-permute-start) | collective-permute-done | bytes 294944 | tf_op jit(solution)/shard_map/ppermute | solution.py:357
  16.7 2.7 %collective-permute-start.3 = (bf16[14,3,128]{2,1,0:T(4,128)(2,1)S(1)}, bf16[14,3,128]{2,1,0:T(4,128)(2,1)S(1)}, u32[]{:S(2)}, u32[]{:S(2)}) collective-permute-start(bf16[14,3,128]{2,1,0:T(4,128)(2,1)S(1)} %pad_maximum_fusion.3), channel_id=1, source_target_pairs={{1,0},{2,1},{3,2},{4,3},{5,4},{6,5},{7,6},{0,7},{9,8},{10,9},{11,1... | collective-permute-start | bytes 32264 | tf_op jit(solution)/shard_map/ppermute | solution.py:370
  19.5 7.7 %conv.1 = f32[8,384,128]{2,1,0:T(8,128)S(1)} custom-call(bf16[8,384,128]{2,1,0:T(8,128)(2,1)S(1)} %copy-done.1, bf16[3,384,128]{2,1,0:T(8,128)(2,1)S(1)} %get-tuple-element.38.south, bf16[3,384,128]{2,1,0:T(8,128)(2,1)S(1)} %get-tuple-element.37.north, f32[49,128]{1,0:T(8,128)S(1)} %reshape.97.dw, f32[1,128]{1,0:T(1,128)S(1)} %bitcast.41), custom_call_target="tpu_custom_call" | custom-call | flops 10000000000 | tf_op jit(solution)/shard_map/conv/pallas_call | solution.py:388
  28.1 25.3 %block.1 = (bf16[8,384,128]{2,1,0:T(8,128)(2,1)}, f32[2048,128]{1,0:T(8,128)S(1)}, f32[2048,128]{1,0:T(8,128)S(1)}, f32[2048,128]{1,0:T(8,128)S(1)}, f32[2048,12...) custom-call(bf16[8,384,128]{2,1,0:T(8,128)(2,1)S(1)} %copy-done.2, ...), custom_call_target="tpu_custom_call" | custom-call | flops 28000000000 | tf_op jit(solution)/shard_map/block/pallas_call | solution.py:399
  53.5 6.2 %conv_grad.1 = f32[64,128]{1,0:T(8,128)S(1)} custom-call(bf16[8,384,128]{2,1,0:T(8,128)(2,1)S(1)} %copy-done.2, bf16[3,384,128]{2,1,0:T(8,128)(2,1)S(1)} %get-tuple-element.38.south, bf16[3,384,128]{2,1,0:T(8,128)(2,1)S(1)} %get-tuple-element.37.north, bf16[14,3,128]{2,1,0:T(4,128)(2,1)S(1)} %collective-permute-done.2.left, ...), custom_call_target="tpu_custom_call" | custom-call | flops 8999999488 | tf_op jit(solution)/shard_map/conv_grad/pallas_call | solution.py:437
  59.8 0.8 convert_element_type.86
  60.6 5.7 %all-to-all-start = ((bf16[32,34,128]{2,1,0:T(8,128)(2,1)}), bf16[32,34,128]{2,1,0:T(8,128)(2,1)S(1)}, u32[]{:S(2)}, u32[]{:S(2)}) async-start(bf16[32,34,128]{2,1,0:T(8,128)(2,1)} %convert_element_type.86), calls=%async_computation | async-start | bytes 655360 | tf_op jit(solution)/shard_map/all_to_all | solution.py:471
  66.3 3.7 %add_convert_fusion = (bf16[2048,128]{1,0:T(8,128)(2,1)}, f32[2048,128]{1,0:T(8,128)}, bf16[2048,128]{1,0:T(8,128)(2,1)}, f32[2048,128]{1,0:T(8,128)}) fusion(f32[2048,128]{1,0:T(8,128)} %copy-done, bf16[8192,128]{1,0:T(8,128)(2,1)} %collective-permute-done.4, f32[2048,128]{1,0:T(8,128)S(1)} %get-tuple-element.27, f32[2048,128]{1,0:T(8,128)S(1)} %get-tuple-element.26, ...), kind=kLoop, calls=%fused_computation.4 | loop fusion | flops 2621440 | bytes 9437184 | tf_op jit(solution)/shard_map/convert_element_type | solution.py:452
  70.1 1.8 %collective-permute-start.7 = (bf16[2048,128]{1,0:T(8,128)(2,1)}, bf16[2048,128]{1,0:T(8,128)(2,1)S(1)}, u32[]{:S(2)}, u32[]{:S(2)}) collective-permute-start(bf16[2048,128]{1,0:T(8,128)(2,1)} %get-tuple-element.29), channel_id=1, source_target_pairs={{0,4},{1,5},{2,6},{3,7},{4,0},{5,1},{6,2},{7,3},{8,12},{9,13},{10,... | collective-permute-start | bytes 1572872 | tf_op jit(solution)/shard_map/ppermute | solution.py:319
  71.8 6.5 %all-to-all-done = bf16[32,34,128]{2,1,0:T(8,128)(2,1)S(1)} async-done(((bf16[32,34,128]{2,1,0:T(8,128)(2,1)}), bf16[32,34,128]{2,1,0:T(8,128)(2,1)S(1)}, u32[]{:S(2)}, u32[]{:S(2)}) %all-to-all-start) | async-done | bytes 278560 | tf_op jit(solution)/shard_map/all_to_all | solution.py:471
  79.2 2.6 %all-to-all-start.1 = ((bf16[32,34,128]{2,1,0:T(8,128)(2,1)}), bf16[32,34,128]{2,1,0:T(8,128)(2,1)S(1)}, u32[]{:S(2)}, u32[]{:S(2)}) async-start(bf16[32,34,128]{2,1,0:T(8,128)(2,1)} %broadcast_in_dim.2), calls=%async_computation.1 | async-start | bytes 655360 | tf_op jit(solution)/shard_map/all_to_all | solution.py:474
  81.8 1.7 %collective-permute-start.5 = (bf16[2048,128]{1,0:T(8,128)(2,1)}, bf16[2048,128]{1,0:T(8,128)(2,1)}, u32[]{:S(2)}, u32[]{:S(2)}) collective-permute-start(bf16[2048,128]{1,0:T(8,128)(2,1)} %get-tuple-element.31), channel_id=1, source_target_pairs={{0,2},{1,3},{2,0},{3,1},{4,6},{5,7},{6,4},{7,5},{8,10},{9,11},{10,... | collective-permute-start | bytes 1572872 | tf_op jit(solution)/shard_map/ppermute | solution.py:319
  83.5 2.9 %collective-permute-done.7 = bf16[2048,128]{1,0:T(8,128)(2,1)S(1)} collective-permute-done((bf16[2048,128]{1,0:T(8,128)(2,1)}, bf16[2048,128]{1,0:T(8,128)(2,1)S(1)}, u32[]{:S(2)}, u32[]{:S(2)}) %collective-permute-start.7) | collective-permute-done | bytes 524320 | tf_op jit(solution)/shard_map/ppermute | solution.py:319
  86.4 2.0 %fusion.1 = bf16[1024,128]{1,0:T(8,128)(2,1)} fusion(f32[2048,128]{1,0:T(8,128)} %get-tuple-element.30, bf16[2048,128]{1,0:T(8,128)(2,1)S(1)} %collective-permute-done.7), kind=kLoop, calls=%fused_computation.10 | loop fusion | flops 393216 | bytes 1048576 | tf_op jit(solution)/shard_map/convert_element_type | solution.py:458
  88.4 2.1 %collective-permute-start.8 = (bf16[1024,128]{1,0:T(8,128)(2,1)}, bf16[1024,128]{1,0:T(8,128)(2,1)S(1)}, u32[]{:S(2)}, u32[]{:S(2)}) collective-permute-start(bf16[1024,128]{1,0:T(8,128)(2,1)} %fusion.1), channel_id=1, source_target_pairs={{0,2},{1,3},{2,0},{3,1},{4,6},{5,7},{6,4},{7,5},{8,10},{9,11},{10,... | collective-permute-start | bytes 786440 | tf_op jit(solution)/shard_map/ppermute | solution.py:319
  90.6 3.2 %all-to-all-done.1 = bf16[32,34,128]{2,1,0:T(8,128)(2,1)S(1)} async-done(((bf16[32,34,128]{2,1,0:T(8,128)(2,1)}), bf16[32,34,128]{2,1,0:T(8,128)(2,1)S(1)}, u32[]{:S(2)}, u32[]{:S(2)}) %all-to-all-start.1) | async-done | bytes 278560 | tf_op jit(solution)/shard_map/all_to_all | solution.py:474
  93.8 0.9 mul.11
  94.7 5.2 %collective-permute-done.5 = bf16[2048,128]{1,0:T(8,128)(2,1)} collective-permute-done((bf16[2048,128]{1,0:T(8,128)(2,1)}, bf16[2048,128]{1,0:T(8,128)(2,1)}, u32[]{:S(2)}, u32[]{:S(2)}) %collective-permute-start.5) | collective-permute-done | bytes 524320 | tf_op jit(solution)/shard_map/ppermute | solution.py:319
  99.8 1.0 fusion.3
  100.8 1.6 %collective-permute-start.6 = (bf16[1024,128]{1,0:T(8,128)(2,1)S(1)}, bf16[1024,128]{1,0:T(8,128)(2,1)S(1)}, u32[]{:S(2)}, u32[]{:S(2)}) collective-permute-start(bf16[1024,128]{1,0:T(8,128)(2,1)S(1)} %fusion.3), channel_id=1, source_target_pairs={{0,4},{1,5},{2,6},{3,7},{4,0},{5,1},{6,2},{7,3},{8,12},{9,13},{10,... | collective-permute-start | bytes 786440 | tf_op jit(solution)/shard_map/ppermute | solution.py:319
  102.5 2.4 %collective-permute-done.8 = bf16[1024,128]{1,0:T(8,128)(2,1)S(1)} collective-permute-done((bf16[1024,128]{1,0:T(8,128)(2,1)}, bf16[1024,128]{1,0:T(8,128)(2,1)S(1)}, u32[]{:S(2)}, u32[]{:S(2)}) %collective-permute-start.8) | collective-permute-done | bytes 262176 | tf_op jit(solution)/shard_map/ppermute | solution.py:319
  104.9 1.0 fusion.2
  105.9 2.4 %collective-permute-done.6 = bf16[1024,128]{1,0:T(8,128)(2,1)S(1)} collective-permute-done((bf16[1024,128]{1,0:T(8,128)(2,1)S(1)}, bf16[1024,128]{1,0:T(8,128)(2,1)S(1)}, u32[]{:S(2)}, u32[]{:S(2)}) %collective-permute-start.6) | collective-permute-done | bytes 262176 | tf_op jit(solution)/shard_map/ppermute | solution.py:319
  108.3 1.0 fusion.4
  109.4 1.7 %collective-permute-start.9 = (bf16[512,128]{1,0:T(8,128)(2,1)S(1)}, bf16[512,128]{1,0:T(8,128)(2,1)S(1)}, u32[]{:S(2)}, u32[]{:S(2)}) collective-permute-start(bf16[512,128]{1,0:T(8,128)(2,1)S(1)} %get-tuple-element.41), channel_id=1, source_target_pairs={{0,8},{8,0},{16,24},{24,16},{1,9},{9,1},{17,25},{25,17},{2,10},{10... | collective-permute-start | bytes 393224 | tf_op jit(solution)/shard_map/ppermute | solution.py:466
  111.1 2.5 %collective-permute-start.11 = (bf16[512,128]{1,0:T(8,128)(2,1)S(1)}, bf16[512,128]{1,0:T(8,128)(2,1)S(1)}, u32[]{:S(2)}, u32[]{:S(2)}) collective-permute-start(bf16[512,128]{1,0:T(8,128)(2,1)S(1)} %get-tuple-element.42), channel_id=1, source_target_pairs={{0,24},{8,16},{16,8},{24,0},{1,25},{9,17},{17,9},{25,1},{2,26},{10... | collective-permute-start | bytes 393224 | tf_op jit(solution)/shard_map/ppermute | solution.py:466
  116.1 3.7 %collective-permute-done.11 = bf16[512,128]{1,0:T(8,128)(2,1)S(1)} collective-permute-done((bf16[512,128]{1,0:T(8,128)(2,1)S(1)}, bf16[512,128]{1,0:T(8,128)(2,1)S(1)}, u32[]{:S(2)}, u32[]{:S(2)}) %collective-permute-start.11) | collective-permute-done | bytes 131104 | tf_op jit(solution)/shard_map/ppermute | solution.py:466
  119.8 4.3 %collective-permute-done.10 = bf16[512,128]{1,0:T(8,128)(2,1)S(1)} collective-permute-done((bf16[512,128]{1,0:T(8,128)(2,1)S(1)}, bf16[512,128]{1,0:T(8,128)(2,1)S(1)}, u32[]{:S(2)}, u32[]{:S(2)}) %collective-permute-start.10) | collective-permute-done | bytes 131104 | tf_op jit(solution)/shard_map/ppermute | solution.py:466
  (84 shorter events, 7.3 us)
Async XLA Ops:
  0.6 9.1 %copy-start.25 = (bf16[7,7,128]{2,1,0:T(8,128)(2,1)S(1)}, bf16[7,7,128]{2,1,0:T(8,128)(2,1)}, u32[]{:S(2)}) copy-start(bf16[7,7,128]{2,1,0:T(8,128)(2,1)} %param.21) | copy-start | bytes 37636
  0.6 9.1 %copy-start.3 = (bf16[128,512]{1,0:T(8,128)(2,1)S(1)}, bf16[128,512]{1,0:T(8,128)(2,1)}, u32[]{:S(2)}) copy-start(bf16[128,512]{1,0:T(8,128)(2,1)} %up.1) | copy-start | bytes 393220
  0.7 9.3 %copy-start.4 = (bf16[512,128]{1,0:T(8,128)(2,1)S(1)}, bf16[512,128]{1,0:T(8,128)(2,1)}, u32[]{:S(2)}) copy-start(bf16[512,128]{1,0:T(8,128)(2,1)} %down.1) | copy-start | bytes 393220
  3.2 9.5 %collective-permute-start.1 = (bf16[3,384,128]{2,1,0:T(8,128)(2,1)S(1)}, bf16[3,384,128]{2,1,0:T(8,128)(2,1)S(1)}, u32[]{:S(2)}, u32[]{:S(2)}) collective-permute-start(bf16[3,384,128]{2,1,0:T(8,128)(2,1)S(1)} %get-tuple-element.35), channel_id=1, source_target_pairs={{8,16},{9,17},{10,18},{11,19},{12,20},{13,21},{14,22},{15,23},{16,... | collective-permute-start | bytes 884744 | tf_op jit(solution)/shard_map/ppermute | solution.py:358
  3.9 12.6 %collective-permute-start = (bf16[3,384,128]{2,1,0:T(8,128)(2,1)S(1)}, bf16[3,384,128]{2,1,0:T(8,128)(2,1)S(1)}, u32[]{:S(2)}, u32[]{:S(2)}) collective-permute-start(bf16[3,384,128]{2,1,0:T(8,128)(2,1)S(1)} %get-tuple-element.36), channel_id=1, source_target_pairs={{0,8},{1,9},{2,10},{3,11},{4,12},{5,13},{6,14},{7,15},{8,0},{9,1},... | collective-permute-start | bytes 884744 | tf_op jit(solution)/shard_map/ppermute | solution.py:357
  9.8 9.6 %copy-start.6 = (f32[49,128]{1,0:T(8,128)}, f32[49,128]{1,0:T(8,128)S(1)}, u32[]{:S(2)}) copy-start(f32[49,128]{1,0:T(8,128)S(1)} %reshape.97.dw) | copy-start | bytes 75268
  10.7 8.6 %copy-start.13 = (f32[128]{0:T(128)S(1)}, f32[128]{0:T(128)}, u32[]{:S(2)}) copy-start(f32[128]{0:T(128)} %param.22) | copy-start | bytes 1540
  16.6 10.7 %collective-permute-start.2 = (bf16[14,3,128]{2,1,0:T(4,128)(2,1)S(1)}, bf16[14,3,128]{2,1,0:T(4,128)(2,1)S(1)}, u32[]{:S(2)}, u32[]{:S(2)}) collective-permute-start(bf16[14,3,128]{2,1,0:T(4,128)(2,1)S(1)} %pad_maximum_fusion.2), channel_id=1, source_target_pairs={{0,1},{1,2},{2,3},{3,4},{4,5},{5,6},{6,7},{7,0},{8,9},{9,10},{10,1... | collective-permute-start | bytes 32264 | tf_op jit(solution)/shard_map/ppermute | solution.py:369
  16.7 10.6 %collective-permute-start.3 = (bf16[14,3,128]{2,1,0:T(4,128)(2,1)S(1)}, bf16[14,3,128]{2,1,0:T(4,128)(2,1)S(1)}, u32[]{:S(2)}, u32[]{:S(2)}) collective-permute-start(bf16[14,3,128]{2,1,0:T(4,128)(2,1)S(1)} %pad_maximum_fusion.3), channel_id=1, source_target_pairs={{1,0},{2,1},{3,2},{4,3},{5,4},{6,5},{7,6},{0,7},{9,8},{10,9},{11,1... | collective-permute-start | bytes 32264 | tf_op jit(solution)/shard_map/ppermute | solution.py:370
  19.3 7.9 %copy-start.2 = (bf16[8,384,128]{2,1,0:T(8,128)(2,1)S(1)}, bf16[8,384,128]{2,1,0:T(8,128)(2,1)}, u32[]{:S(2)}) copy-start(bf16[8,384,128]{2,1,0:T(8,128)(2,1)} %state.5) | copy-start | bytes 2359300
  19.4 7.9 %copy-start.5 = (bf16[512,128]{0,1:T(8,128)(2,1)S(1)}, bf16[512,128]{0,1:T(8,128)(2,1)}, u32[]{:S(2)}) copy-start(bf16[512,128]{0,1:T(8,128)(2,1)} %copy.26) | copy-start | bytes 393220
  19.4 7.9 %copy-start.8 = (bf16[8,384,128]{2,1,0:T(8,128)(2,1)S(1)}, bf16[8,384,128]{2,1,0:T(8,128)(2,1)}, u32[]{:S(2)}) copy-start(bf16[8,384,128]{2,1,0:T(8,128)(2,1)} %forcing.1) | copy-start | bytes 2359300
  19.4 7.9 %copy-start.9 = (bf16[8,384,128]{2,1,0:T(8,128)(2,1)S(1)}, bf16[8,384,128]{2,1,0:T(8,128)(2,1)}, u32[]{:S(2)}) copy-start(bf16[8,384,128]{2,1,0:T(8,128)(2,1)} %cotangent.1) | copy-start | bytes 2359300
  19.4 7.9 %copy-start.10 = (s32[6144]{0:T(1024)S(1)}, s32[6144]{0:T(1024)}, u32[]{:S(2)}) copy-start(s32[6144]{0:T(1024)} %param.32) | copy-start | bytes 73732
  19.4 7.9 %copy-start.11 = (s32[8,384]{1,0:T(8,128)S(1)}, s32[8,384]{1,0:T(8,128)}, u32[]{:S(2)}) copy-start(s32[8,384]{1,0:T(8,128)} %land.1) | copy-start | bytes 36868
  19.4 7.9 %copy-start.12 = (f32[512]{0:T(512)S(1)}, f32[512]{0:T(512)}, u32[]{:S(2)}) copy-start(f32[512]{0:T(512)} %param.26) | copy-start | bytes 6148
  19.4 7.9 %copy-start.14 = (f32[16]{0:T(128)S(1)}, f32[16]{0:T(128)}, u32[]{:S(2)}) copy-start(f32[16]{0:T(128)} %weight_table.1) | copy-start | bytes 196
  19.4 7.9 %copy-start.15 = (f32[128]{0:T(128)S(1)}, f32[128]{0:T(128)}, u32[]{:S(2)}) copy-start(f32[128]{0:T(128)} %param.23) | copy-start | bytes 1540
  19.4 7.9 %copy-start.16 = (f32[128]{0:T(128)S(1)}, f32[128]{0:T(128)}, u32[]{:S(2)}) copy-start(f32[128]{0:T(128)} %param.24) | copy-start | bytes 1540
  19.5 7.9 %copy-start.17 = (f32[128]{0:T(128)S(1)}, f32[128]{0:T(128)}, u32[]{:S(2)}) copy-start(f32[128]{0:T(128)} %param.28) | copy-start | bytes 1540
  53.4 12.9 %collective-permute-start.4 = (bf16[8192,128]{1,0:T(8,128)(2,1)}, bf16[8192,128]{1,0:T(8,128)(2,1)}, u32[]{:S(2)}, u32[]{:S(2)}) collective-permute-start(bf16[8192,128]{1,0:T(8,128)(2,1)} %get-tuple-element.22), channel_id=1, source_target_pairs={{0,1},{1,0},{2,3},{3,2},{4,5},{5,4},{6,7},{7,6},{8,9},{9,8},{10,11... | collective-permute-start | bytes 6291464 | tf_op jit(solution)/shard_map/ppermute | solution.py:319
  60.6 17.7 %all-to-all-start = ((bf16[32,34,128]{2,1,0:T(8,128)(2,1)}), bf16[32,34,128]{2,1,0:T(8,128)(2,1)S(1)}, u32[]{:S(2)}, u32[]{:S(2)}) async-start(bf16[32,34,128]{2,1,0:T(8,128)(2,1)} %convert_element_type.86), calls=%async_computation | async-start | bytes 655360 | tf_op jit(solution)/shard_map/all_to_all | solution.py:471
  70.1 16.3 %collective-permute-start.7 = (bf16[2048,128]{1,0:T(8,128)(2,1)}, bf16[2048,128]{1,0:T(8,128)(2,1)S(1)}, u32[]{:S(2)}, u32[]{:S(2)}) collective-permute-start(bf16[2048,128]{1,0:T(8,128)(2,1)} %get-tuple-element.29), channel_id=1, source_target_pairs={{0,4},{1,5},{2,6},{3,7},{4,0},{5,1},{6,2},{7,3},{8,12},{9,13},{10,... | collective-permute-start | bytes 1572872 | tf_op jit(solution)/shard_map/ppermute | solution.py:319
  78.4 21.4 %copy-start.21 = (f32[2048,128]{1,0:T(8,128)S(1)}, f32[2048,128]{1,0:T(8,128)}, u32[]{:S(2)}) copy-start(f32[2048,128]{1,0:T(8,128)} %get-tuple-element.32) | copy-start | bytes 3145732
  79.2 14.6 %all-to-all-start.1 = ((bf16[32,34,128]{2,1,0:T(8,128)(2,1)}), bf16[32,34,128]{2,1,0:T(8,128)(2,1)S(1)}, u32[]{:S(2)}, u32[]{:S(2)}) async-start(bf16[32,34,128]{2,1,0:T(8,128)(2,1)} %broadcast_in_dim.2), calls=%async_computation.1 | async-start | bytes 655360 | tf_op jit(solution)/shard_map/all_to_all | solution.py:474
  81.8 18.1 %collective-permute-start.5 = (bf16[2048,128]{1,0:T(8,128)(2,1)}, bf16[2048,128]{1,0:T(8,128)(2,1)}, u32[]{:S(2)}, u32[]{:S(2)}) collective-permute-start(bf16[2048,128]{1,0:T(8,128)(2,1)} %get-tuple-element.31), channel_id=1, source_target_pairs={{0,2},{1,3},{2,0},{3,1},{4,6},{5,7},{6,4},{7,5},{8,10},{9,11},{10,... | collective-permute-start | bytes 1572872 | tf_op jit(solution)/shard_map/ppermute | solution.py:319
  86.4 18.5 %copy-start.22 = (f32[2048,128]{1,0:T(8,128)S(1)}, f32[2048,128]{1,0:T(8,128)}, u32[]{:S(2)}) copy-start(f32[2048,128]{1,0:T(8,128)} %get-tuple-element.30) | copy-start | bytes 3145732
  88.4 16.4 %collective-permute-start.8 = (bf16[1024,128]{1,0:T(8,128)(2,1)}, bf16[1024,128]{1,0:T(8,128)(2,1)S(1)}, u32[]{:S(2)}, u32[]{:S(2)}) collective-permute-start(bf16[1024,128]{1,0:T(8,128)(2,1)} %fusion.1), channel_id=1, source_target_pairs={{0,2},{1,3},{2,0},{3,1},{4,6},{5,7},{6,4},{7,5},{8,10},{9,11},{10,... | collective-permute-start | bytes 786440 | tf_op jit(solution)/shard_map/ppermute | solution.py:319
  100.8 7.4 %collective-permute-start.6 = (bf16[1024,128]{1,0:T(8,128)(2,1)S(1)}, bf16[1024,128]{1,0:T(8,128)(2,1)S(1)}, u32[]{:S(2)}, u32[]{:S(2)}) collective-permute-start(bf16[1024,128]{1,0:T(8,128)(2,1)S(1)} %fusion.3), channel_id=1, source_target_pairs={{0,4},{1,5},{2,6},{3,7},{4,0},{5,1},{6,2},{7,3},{8,12},{9,13},{10,... | collective-permute-start | bytes 786440 | tf_op jit(solution)/shard_map/ppermute | solution.py:319
  109.4 6.6 %collective-permute-start.9 = (bf16[512,128]{1,0:T(8,128)(2,1)S(1)}, bf16[512,128]{1,0:T(8,128)(2,1)S(1)}, u32[]{:S(2)}, u32[]{:S(2)}) collective-permute-start(bf16[512,128]{1,0:T(8,128)(2,1)S(1)} %get-tuple-element.41), channel_id=1, source_target_pairs={{0,8},{8,0},{16,24},{24,16},{1,9},{9,1},{17,25},{25,17},{2,10},{10... | collective-permute-start | bytes 393224 | tf_op jit(solution)/shard_map/ppermute | solution.py:466
  111.1 8.7 %collective-permute-start.11 = (bf16[512,128]{1,0:T(8,128)(2,1)S(1)}, bf16[512,128]{1,0:T(8,128)(2,1)S(1)}, u32[]{:S(2)}, u32[]{:S(2)}) collective-permute-start(bf16[512,128]{1,0:T(8,128)(2,1)S(1)} %get-tuple-element.42), channel_id=1, source_target_pairs={{0,24},{8,16},{16,8},{24,0},{1,25},{9,17},{17,9},{25,1},{2,26},{10... | collective-permute-start | bytes 393224 | tf_op jit(solution)/shard_map/ppermute | solution.py:466
  113.6 10.5 %collective-permute-start.10 = (bf16[512,128]{1,0:T(8,128)(2,1)S(1)}, bf16[512,128]{1,0:T(8,128)(2,1)S(1)}, u32[]{:S(2)}, u32[]{:S(2)}) collective-permute-start(bf16[512,128]{1,0:T(8,128)(2,1)S(1)} %get-tuple-element.43), channel_id=1, source_target_pairs={{0,16},{8,24},{16,0},{24,8},{1,17},{9,25},{17,1},{25,9},{2,18},{10... | collective-permute-start | bytes 393224 | tf_op jit(solution)/shard_map/ppermute | solution.py:466
  (9 other events, 51.3 us)

commit v6 on v5

--- a/solution.py
+++ b/solution.py
@@ -50,18 +50,81 @@
     lax.fori_loop(0, rows // chunk, step_of, 0)
 
 
-def conv_block(field, base, dw, dwb, rows, channels):
-    sums = [jnp.broadcast_to(dwb[...], (8, channels)) for _ in range(rows)]
+def conv_sums(field, base, dw, starts, lines, rows):
+    sums = dict(zip(rows, starts))
     for b in range(TAPS):
         weights = [
-            jnp.broadcast_to(dw[pl.ds(a * TAPS + b, 1), :], (8, channels)) for a in range(TAPS)
+            jnp.broadcast_to(dw[pl.ds(a * TAPS + b, 1), :], (8, dw.shape[1])) for a in range(TAPS)
         ]
-        for h in range(rows + TAPS - 1):
+        for h in lines:
             x = field(h, base + (PAD - MARGIN + b))
             for a in range(TAPS):
-                if 0 <= h - a < rows:
+                if h - a in sums:
                     sums[h - a] = sums[h - a] + weights[a] * x
-    return sums
+    return [sums[r] for r in rows]
+
+
+def edge_kernel(state, even, odd, *, bands):
+    rows, cols, channels = state.shape
+    lat = lax.axis_index("lat")
+
+    @pl.when(lat % 2 == 1)
+    def _():
+        even[...] = state[0:MARGIN]
+        odd[...] = state[rows - MARGIN : rows]
+
+    @pl.when(lat % 2 == 0)
+    def _():
+        even[...] = state[rows - MARGIN : rows]
+        odd[...] = state[0:MARGIN]
+
+    @pl.when(lat == bands - 1)
+    def _():
+        column = lax.broadcasted_iota(jnp.int32, (cols, cols), 1)
+        line = lax.broadcasted_iota(jnp.int32, (cols, cols), 0)
+        reverse = jnp.where(line + column == cols - 1, 1.0, 0.0).astype(bf16)
+        for m in range(MARGIN):
+            turned = jnp.dot(reverse, state[rows - 1 - m], preferred_element_type=f32)
+            odd[m] = turned.astype(bf16)
+
+
+def inner_conv_kernel(state, dw, dwb, conv, padded):
+    rows, cols, channels = state.shape
+    for r in range(rows):
+        padded[r, PAD : PAD + cols, :] = state[r].astype(f32)
+
+    def step_of(step, _):
+        base = pl.multiple_of(step * 8, 8)
+        field = lambda h, at: padded[h - MARGIN, pl.ds(at, 8), :]
+        bias = jnp.broadcast_to(dwb[...], (8, channels))
+        lines = range(MARGIN, rows + MARGIN)
+        sums = conv_sums(field, base, dw, [bias] * rows, lines, list(range(rows)))
+        for r in range(rows):
+            conv[r, pl.ds(base, 8), :] = sums[r]
+        return 0
+
+    lax.fori_loop(1, cols // 8 - 1, step_of, 0)
+
+
+def halo_conv_kernel(south, north, dw, conv, padded, *, rows):
+    _, cols, channels = south.shape
+    padded[0:MARGIN, PAD : PAD + cols, :] = south[...].astype(f32)
+    padded[MARGIN : 2 * MARGIN, PAD : PAD + cols, :] = north[...].astype(f32)
+
+    def step_of(step, _):
+        base = pl.multiple_of(step * 8, 8)
+        zero = jnp.zeros((8, channels), f32)
+        for side in range(2):
+            first = 0 if side == 0 else rows + MARGIN
+            field = lambda h, at: padded[h - first + side * MARGIN, pl.ds(at, 8), :]
+            out = [k if side == 0 else rows - MARGIN + k for k in range(MARGIN)]
+            lines = range(first, first + MARGIN)
+            sums = conv_sums(field, base, dw, [zero] * MARGIN, lines, out)
+            for k in range(MARGIN):
+                conv[side * MARGIN + k, pl.ds(base, 8), :] = sums[k]
+        return 0
+
+    lax.fori_loop(1, cols // 8 - 1, step_of, 0)
 
 
 def fill_rows(padded, state, south, north):
@@ -73,23 +136,8 @@
         padded[r + MARGIN, inner, :] = state[r].astype(f32)
 
 
-def conv_kernel(state, south, north, dw, dwb, conv, padded):
-    rows, cols, channels = state.shape
-    fill_rows(padded, state, south, north)
-
-    def step_of(step, _):
-        base = pl.multiple_of(step * 8, 8)
-        field = lambda h, at: padded[h, pl.ds(at, 8), :]
-        sums = conv_block(field, base, dw, dwb, rows, channels)
-        for r in range(rows):
-            conv[r, pl.ds(base, 8), :] = sums[r]
-        return 0
-
-    lax.fori_loop(1, cols // 8 - 1, step_of, 0)
-
-
 def block_kernel(
-    state, south, north, left, right, conv, forcing, cotangent, land, weight_index, weight_table,
+    state, south, north, left, right, conv, halo, forcing, cotangent, land, weight_index, weight_table,
     target_list, clash_list, dw, dwb, gain, nbias, up, upb, down, downb, scale, up_t, down_t,
     result, keep_0, keep_1, keep_2, keep_3, send, grad_conv, grads,
     field, edge, acc_up, acc_down, entry_weights, spread, terms, table, targets, clash, sems,
@@ -114,14 +162,21 @@
                 edge[side, h, PAD - MARGIN : PAD, :] = left[h].astype(f32)
             else:
                 edge[side, h, wide : wide + MARGIN, :] = right[h].astype(f32)
-        sums = conv_block(
-            lambda h, at: edge[side, h, pl.ds(at, 8), :], 0, dw, dwb, rows, channels
-        )
+        bias = jnp.broadcast_to(dwb[...], (8, channels))
+        lines = range(rows + 2 * MARGIN)
+        at_edge = lambda h, at: edge[side, h, pl.ds(at, 8), :]
+        sums = conv_sums(at_edge, 0, dw, [bias] * rows, lines, list(range(rows)))
         out = slice(0, 8) if side == 0 else slice(cols - 8, cols)
         for r in range(rows):
             field[r, out, :] = sums[r]
+    inner = slice(8, cols - 8)
     for r in range(rows):
-        field[r, 8 : cols - 8, :] = conv[r, 8 : cols - 8, :]
+        here = conv[r, inner, :]
+        if r < MARGIN:
+            here = here + halo[r, inner, :]
+        if r >= rows - MARGIN:
+            here = here + halo[r - rows + 2 * MARGIN, inner, :]
+        field[r, inner, :] = here
 
     def clear(at):
         table[at, :] = jnp.zeros((at.size, channels), f32)
@@ -340,10 +395,7 @@
     entries = owner.shape[0]
     fan = entries // cells
 
-    low_rows = state[:MARGIN]
-    high_rows = state[rows - MARGIN :]
     odd = lat % 2 == 1
-    last = lat == lat_count - 1
     even_pairs, odd_pairs = [], []
     for l in range(lat_count):
         for j in range(lon_count):
@@ -354,12 +406,17 @@
                 odd_pairs.append((here, l * lon_count + lon_count - 1 - j))
             elif beyond >= 0:
                 odd_pairs.append((here, beyond * lon_count + j))
-    got_even = lax.ppermute(jnp.where(odd, low_rows, high_rows), ("lat", "lon"), even_pairs)
-    got_odd = lax.ppermute(
-        jnp.where(last, high_rows[::-1, ::-1], jnp.where(odd, high_rows, low_rows)),
-        ("lat", "lon"),
-        odd_pairs,
-    )
+    edge_rows = shape((MARGIN, cols, channels), bf16)
+    for_even, for_odd = pl.pallas_call(
+        functools.partial(edge_kernel, bands=lat_count),
+        out_shape=(edge_rows, edge_rows),
+        in_specs=[vmem()],
+        out_specs=[vmem()] * 2,
+        cost_estimate=cost(1),
+        name="edges",
+    )(state)
+    got_even = lax.ppermute(for_even, ("lat", "lon"), even_pairs)
+    got_odd = lax.ppermute(for_odd, ("lat", "lon"), odd_pairs)
     south = jnp.where(odd, got_even, got_odd)
     north = jnp.where(odd, got_odd, got_even)
 
@@ -386,15 +443,25 @@
     line = lambda v: v.reshape(1, -1)
     taps = dw_weight.reshape(-1, channels).astype(f32)
     conv = pl.pallas_call(
-        conv_kernel,
+        inner_conv_kernel,
         out_shape=shape((rows, cols, channels), f32),
-        in_specs=[vmem()] * 5,
+        in_specs=[vmem()] * 3,
         out_specs=vmem(),
-        scratch_shapes=[pltpu.VMEM((rows + 2 * MARGIN, cols + 2 * PAD, channels), f32)],
+        scratch_shapes=[pltpu.VMEM((rows, cols + 2 * PAD, channels), f32)],
         compiler_params=params(),
-        cost_estimate=cost(10),
-        name="conv",
-    )(state, south, north, taps, line(dw_bias))
+        cost_estimate=cost(7),
+        name="inner_conv",
+    )(after(state, for_even), taps, line(dw_bias))
+    halo = pl.pallas_call(
+        functools.partial(halo_conv_kernel, rows=rows),
+        out_shape=shape((2 * MARGIN, cols, channels), f32),
+        in_specs=[vmem()] * 3,
+        out_specs=vmem(),
+        scratch_shapes=[pltpu.VMEM((2 * MARGIN, cols + 2 * PAD, channels), f32)],
+        compiler_params=params(),
+        cost_estimate=cost(2),
+        name="halo_conv",
+    )(south, north, taps)
     quarter = shape((half_rows // 4, channels), f32)
     result, *keep, send, grad_conv, grads = pl.pallas_call(
         block_kernel,
@@ -405,7 +472,7 @@
             shape((rows, cols, channels), f32),
             shape((2 * hid // channels, channels, channels), f32),
         ),
-        in_specs=[vmem()] * 10 + [smem()] + [anywhere()] * 2 + [vmem()] * 11,
+        in_specs=[vmem()] * 11 + [smem()] + [anywhere()] * 2 + [vmem()] * 11,
         out_specs=[vmem()] + [anywhere()] * 4 + [vmem()] * 3,
         scratch_shapes=[
             pltpu.VMEM((rows, cols, channels), f32),
@@ -424,7 +491,7 @@
         cost_estimate=cost(28),
         name="block",
     )(
-        state, south, north, left, right, conv, forcing, cotangent, land_mask,
+        state, south, north, left, right, conv, halo, forcing, cotangent, land_mask,
         weight_index.reshape(-1, channels), intersection_weights,
         targets.reshape(-1), clash.reshape(-1), taps, line(dw_bias), line(norm_gain), line(norm_bias), up_weight, line(up_bias),
         down_weight, line(down_bias), line(layer_scale), up_weight.T, down_weight.T,
@@ -447,26 +514,32 @@
 
     size = half_rows // 4
     got = after(got, grad_dw)
-    merged = [keep[k] + got[k * size : (k + 1) * size].astype(f32) for k in range(4)]
-    kept = [merged[0], merged[2]]
-    sends = [merged[1].astype(bf16), merged[3].astype(bf16)]
+    slices = [(keep[k], got[k * size : (k + 1) * size]) for k in range(4)]
+    add = lambda summands: functools.reduce(lambda x, y: x + y.astype(f32), summands)
+    sends = [add(slices[1]).astype(bf16), add(slices[3]).astype(bf16)]
+    first_sends = sends
+    held = [list(slices[0]), list(slices[2])]
     for stage in range(len(rest)):
         arrived = [swap_bit(sends[q], orders[q][stage]) for q in range(2)]
+        arrived = lax.optimization_barrier(tuple(arrived))
+        for q in range(2):
+            held[q].append(arrived[q])
         if stage + 1 < len(rest):
-            size = kept[0].shape[0] // 2
-            for q in range(2):
-                sends[q] = (kept[q][size:] + arrived[q][size:].astype(f32)).astype(bf16)
-                kept[q] = kept[q][:size] + arrived[q][:size].astype(f32)
-        else:
-            kept = [kept[q] + arrived[q].astype(f32) for q in range(2)]
-    lined = jnp.concatenate([p.reshape(lat_count, width, channels) for p in kept], axis=1)
-    forcing_grad = lined[0]
+            size //= 2
+            sends = [add([h[size : 2 * size] for h in held[q]]).astype(bf16) for q in range(2)]
+            held = [[h[:size] for h in held[q]] for q in range(2)]
+    def for_band(distance):
+        at = slice(distance * width, (distance + 1) * width)
+        return jnp.concatenate([add([h[at] for h in held[q]]) for q in range(2)], axis=0)
+
+    forcing_grad = for_band(0)
     for distance in range(1, lat_count):
         pairs = [(i, i ^ distance) for i in range(lat_count)]
-        arrived = lax.ppermute(lined[distance].astype(bf16), "lat", pairs)
+        arrived = lax.ppermute(for_band(distance).astype(bf16), "lat", pairs)
         forcing_grad = forcing_grad + arrived.astype(f32)
 
     total = jnp.concatenate([grads.reshape(2 * hid, channels), grad_dw], axis=0).astype(bf16)
+    total = after(total, *first_sends)
     total = total.reshape(devices, -1, channels)
     total = lax.all_to_all(total, ("lat", "lon"), split_axis=0, concat_axis=0, tiled=True)
     total = jnp.sum(total.astype(f32), axis=0, keepdims=True).astype(bf16)

time: 126 us -> 107 us (0.85)
  waiting for transfers between devices: 34.7 us -> 23.4 us
  other arithmetic: 11 us -> 7.08 us
  local copies, waits for them, and re-layouts: 7.73 us -> 5.49 us
    all_to_all x2, waiting for transfers between devices: 9.7 us -> 0.01 us  [on_device(): lax.all_to_all(total, ('lat', 'lon'), split_axis=0, concat_axis=0, tiled=...]
    convert_element_type x3 -> x2, other arithmetic: 6.76 us -> 3.63 us  [the longest x1 2.1 us: on_device(): add([h[size:2 * size] for h in held[q]]).astype(bf16)]
    another operation x3 -> x4, other arithmetic: 0.11 us -> 2.43 us
    ppermute x5, waiting for transfers between devices: 12.9 us -> 10.6 us  [swap_bit(): return lax.ppermute(array, 'lon', pairs)]
    add x2 -> x0, other arithmetic: 2.04 us -> none  [on_device(): kept = [kept[q] + arrived[q].astype(f32) for q in range(2)]]
    ppermute x5, starting transfers between devices: 7.28 us -> 5.76 us  [swap_bit(): return lax.ppermute(array, 'lon', pairs)]
    pallas_call x1 -> x3, Pallas kernels: 7.73 us -> 8.91 us  [the longest x1 5.04 us: on_device(): pl.pallas_call(inner_conv_kernel, out_shape=shape((rows, cols, channels),...]
  transfers between devices with their start and end apart: 14 -> 14, of which waited for: 10 -> 3; matrix products, arithmetic and copies ran while one was open for 11% -> 7% of each run, Pallas kernels for 13% -> 14%
where the time goes in v6:
time: 107 us
  Pallas kernels  41.5 us (39%)
  starting transfers between devices  28.3 us (26%)
  waiting for transfers between devices  23.4 us (22%)
  other arithmetic  7.08 us (7%)
  local copies, waits for them, and re-layouts  5.49 us (5%)
  between operations  1.16 us (1%)
    pallas_call x1, Pallas kernels, on_device(): pl.pallas_call(block_kernel, out_shape=(shape((rows, cols, channels), bf1...  24.5 us
    ppermute x3, waiting for transfers between devices, on_device(): arrived = lax.ppermute(for_band(distance).astype(bf16), 'lat', pairs)  12.8 us
    ppermute x5, waiting for transfers between devices, swap_bit(): return lax.ppermute(array, 'lon', pairs)  10.6 us
    all_to_all x2, starting transfers between devices, on_device(): lax.all_to_all(total, ('lat', 'lon'), split_axis=0, concat_axis=0, tiled=...  8.78 us
    pallas_call x1, Pallas kernels, on_device(): pl.pallas_call(conv_grad_kernel, out_shape=shape((dw_rows, channels), f32...  6.17 us
    ppermute x1, starting transfers between devices, on_device(): got_even = lax.ppermute(for_even, ('lat', 'lon'), even_pairs)  5.89 us
    ppermute x5, starting transfers between devices, swap_bit(): return lax.ppermute(array, 'lon', pairs)  5.76 us
    pallas_call x1, Pallas kernels, on_device(): pl.pallas_call(inner_conv_kernel, out_shape=shape((rows, cols, channels),...  5.04 us
  transfers between devices with their start and end apart: 14, of which 3 were waited for; matrix products, arithmetic and copies ran while one was open for 7% of the time, Pallas kernels for 14%

profile of v6, /device:TPU:0, one launch (start us, length us, event | category | flops | bytes accessed | tf_op | source)
XLA Modules:
  0.0 106.9 jit_solution(2334605704489862095)
XLA Ops:
  0.7 2.1 %edges.1 = (bf16[3,384,128]{2,1,0:T(8,128)(2,1)}, bf16[3,384,128]{2,1,0:T(8,128)(2,1)}) custom-call(bf16[8,384,128]{2,1,0:T(8,128)(2,1)} %state.6), custom_call_target="tpu_custom_call" | custom-call | flops 1000000000 | tf_op jit(solution)/shard_map/edges/pallas_call | solution.py:410
  2.8 0.7 collective-permute-start.1
  3.4 5.9 %collective-permute-start = (bf16[3,384,128]{2,1,0:T(8,128)(2,1)}, bf16[3,384,128]{2,1,0:T(8,128)(2,1)S(1)}, u32[]{:S(2)}, u32[]{:S(2)}) collective-permute-start(bf16[3,384,128]{2,1,0:T(8,128)(2,1)} %get-tuple-element.25), channel_id=1, source_target_pairs={{0,8},{1,9},{2,10},{3,11},{4,12},{5,13},{6,14},{7,15},{8,0},{9,1},... | collective-permute-start | bytes 884744 | tf_op jit(solution)/shard_map/ppermute | solution.py:418
  9.6 5.0 %inner_conv.1.conv = f32[8,384,128]{2,1,0:T(8,128)S(1)} custom-call(bf16[8,384,128]{2,1,0:T(8,128)(2,1)S(1)} %copy-done.2, f32[49,128]{1,0:T(8,128)S(1)} %reshape.87.dw, f32[1,128]{1,0:T(1,128)S(1)} %bitcast.25), custom_call_target="tpu_custom_call" | custom-call | flops 7000000000 | tf_op jit(solution)/shard_map/inner_conv/pallas_call | solution.py:445
  14.7 1.2 %copy-done.16 = f32[8,384,128]{2,1,0:T(8,128)} copy-done((f32[8,384,128]{2,1,0:T(8,128)}, f32[8,384,128]{2,1,0:T(8,128)S(1)}, u32[]{:S(2)}) %copy-start.16) | copy-done | bytes 1572888
  15.8 1.9 %targets.1 = (s32[48,128]{1,0:T(8,128)}, s32[48,128]{1,0:T(8,128)}) custom-call(s32[48,128]{1,0:T(8,128)} %bitcast.36, s32[48,128]{1,0:T(8,128)} %bitcast.37), custom_call_target="tpu_custom_call" | custom-call | flops 1000000000 | tf_op jit(solution)/shard_map/targets/pallas_call | solution.py:434
  18.1 2.7 %collective-permute-start.3 = (bf16[14,3,128]{2,1,0:T(4,128)(2,1)S(1)}, bf16[14,3,128]{2,1,0:T(4,128)(2,1)S(1)}, u32[]{:S(2)}, u32[]{:S(2)}) collective-permute-start(bf16[14,3,128]{2,1,0:T(4,128)(2,1)S(1)} %pad_maximum_fusion.5), channel_id=1, source_target_pairs={{1,0},{2,1},{3,2},{4,3},{5,4},{6,5},{7,6},{0,7},{9,8},{10,9},{11,1... | collective-permute-start | bytes 32264 | tf_op jit(solution)/shard_map/ppermute | solution.py:427
  20.8 1.8 %halo_conv.1.halo = f32[6,384,128]{2,1,0:T(8,128)S(1)} custom-call(bf16[3,384,128]{2,1,0:T(8,128)(2,1)S(1)} %get-tuple-element.60.south, bf16[3,384,128]{2,1,0:T(8,128)(2,1)S(1)} %get-tuple-element.59.north, f32[49,128]{1,0:T(8,128)S(1)} %reshape.87.dw), custom_call_target="tpu_custom_call" | custom-call | flops 2000000000 | tf_op jit(solution)/shard_map/halo_conv/pallas_call | solution.py:455
  22.7 24.5 %block.1 = (bf16[8,384,128]{2,1,0:T(8,128)(2,1)}, f32[2048,128]{1,0:T(8,128)S(1)}, f32[2048,128]{1,0:T(8,128)S(1)}, f32[2048,128]{1,0:T(8,128)S(1)}, f32[2048,12...) custom-call(bf16[8,384,128]{2,1,0:T(8,128)(2,1)S(1)} %copy-done.2, ...), custom_call_target="tpu_custom_call" | custom-call | flops 28000000000 | tf_op jit(solution)/shard_map/block/pallas_call | solution.py:466
  47.3 0.2 collective-permute-start.4
  47.5 6.2 %conv_grad.1 = f32[64,128]{1,0:T(8,128)S(1)} custom-call(bf16[8,384,128]{2,1,0:T(8,128)(2,1)S(1)} %copy-done.2, bf16[3,384,128]{2,1,0:T(8,128)(2,1)S(1)} %get-tuple-element.60.south, bf16[3,384,128]{2,1,0:T(8,128)(2,1)S(1)} %get-tuple-element.59.north, bf16[14,3,128]{2,1,0:T(4,128)(2,1)S(1)} %collective-permute-done.2.left, ...), custom_call_target="tpu_custom_call" | custom-call | flops 8999999488 | tf_op jit(solution)/shard_map/conv_grad/pallas_call | solution.py:504
  53.7 1.5 %add_convert_fusion = (bf16[2048,128]{1,0:T(8,128)(2,1)}, bf16[2048,128]{1,0:T(8,128)(2,1)}) fusion(f32[2048,128]{1,0:T(8,128)S(1)} %get-tuple-element.37, bf16[8192,128]{1,0:T(8,128)(2,1)S(1)} %collective-permute-done.4, f32[2048,128]{1,0:T(8,128)S(1)} %get-tuple-element.35), kind=kLoop, calls=%fused_computation | loop fusion | flops 1572864 | bytes 4194304 | tf_op jit(solution)/shard_map/convert_element_type | solution.py:519
  55.5 1.7 %collective-permute-start.6 = (bf16[2048,128]{1,0:T(8,128)(2,1)}, bf16[2048,128]{1,0:T(8,128)(2,1)}, u32[]{:S(2)}, u32[]{:S(2)}) collective-permute-start(bf16[2048,128]{1,0:T(8,128)(2,1)} %get-tuple-element.55), channel_id=1, source_target_pairs={{0,4},{1,5},{2,6},{3,7},{4,0},{5,1},{6,2},{7,3},{8,12},{9,13},{10,... | collective-permute-start | bytes 1572872 | tf_op jit(solution)/shard_map/ppermute | solution.py:374
  57.2 1.2 %collective-permute-start.5 = (bf16[2048,128]{1,0:T(8,128)(2,1)}, bf16[2048,128]{1,0:T(8,128)(2,1)}, u32[]{:S(2)}, u32[]{:S(2)}) collective-permute-start(bf16[2048,128]{1,0:T(8,128)(2,1)} %get-tuple-element.56), channel_id=1, source_target_pairs={{0,2},{1,3},{2,0},{3,1},{4,6},{5,7},{6,4},{7,5},{8,10},{9,11},{10,... | collective-permute-start | bytes 1572872 | tf_op jit(solution)/shard_map/ppermute | solution.py:374
  58.5 0.8 reshape.83
  59.4 4.5 %all-to-all-start = ((bf16[32,34,128]{2,1,0:T(8,128)(2,1)}), bf16[32,34,128]{2,1,0:T(8,128)(2,1)S(1)}, u32[]{:S(2)}, u32[]{:S(2)}) async-start(bf16[32,34,128]{2,1,0:T(8,128)(2,1)} %reshape.83), calls=%async_computation | async-start | bytes 655360 | tf_op jit(solution)/shard_map/all_to_all | solution.py:544
  63.8 7.9 %collective-permute-done.6 = bf16[2048,128]{1,0:T(8,128)(2,1)} collective-permute-done((bf16[2048,128]{1,0:T(8,128)(2,1)}, bf16[2048,128]{1,0:T(8,128)(2,1)}, u32[]{:S(2)}, u32[]{:S(2)}) %collective-permute-start.6) | collective-permute-done | bytes 524320 | tf_op jit(solution)/shard_map/ppermute | solution.py:374
  71.7 2.6 %collective-permute-done.5 = bf16[2048,128]{1,0:T(8,128)(2,1)} collective-permute-done((bf16[2048,128]{1,0:T(8,128)(2,1)}, bf16[2048,128]{1,0:T(8,128)(2,1)}, u32[]{:S(2)}, u32[]{:S(2)}) %collective-permute-start.5) | collective-permute-done | bytes 524320 | tf_op jit(solution)/shard_map/ppermute | solution.py:374
  74.4 2.1 %add_convert_fusion.2 = (bf16[1024,128]{1,0:T(8,128)(2,1)}, bf16[1024,128]{1,0:T(8,128)(2,1)S(1)}) fusion(f32[2048,128]{1,0:T(8,128)S(1)} %get-tuple-element.41, bf16[2048,128]{1,0:T(8,128)(2,1)} %collective-permute-done.6, bf16[8192,128]{1,0:T(8,128)(2,1)} %copy-done.18, bf16[2048,128]{1,0:T(8,128)(2,1)} %collective-permute-done.5, ...), kind=kLoop, calls=%fused_computation.3 | loop fusion | flops 1310720 | bytes 2621440 | tf_op jit(solution)/shard_map/convert_element_type | solution.py:529
  76.5 0.8 collective-permute-start.8
  77.3 1.7 %collective-permute-start.7 = (bf16[1024,128]{1,0:T(8,128)(2,1)S(1)}, bf16[1024,128]{1,0:T(8,128)(2,1)S(1)}, u32[]{:S(2)}, u32[]{:S(2)}) collective-permute-start(bf16[1024,128]{1,0:T(8,128)(2,1)S(1)} %get-tuple-element.54), channel_id=1, source_target_pairs={{0,4},{1,5},{2,6},{3,7},{4,0},{5,1},{6,2},{7,3},{8,12},{9,13},{10,... | collective-permute-start | bytes 786440 | tf_op jit(solution)/shard_map/ppermute | solution.py:374
  79.1 0.8 broadcast_in_dim.2
  79.9 4.3 %all-to-all-start.1 = ((bf16[32,34,128]{2,1,0:T(8,128)(2,1)}), bf16[32,34,128]{2,1,0:T(8,128)(2,1)S(1)}, u32[]{:S(2)}, u32[]{:S(2)}) async-start(bf16[32,34,128]{2,1,0:T(8,128)(2,1)} %broadcast_in_dim.2), calls=%async_computation.1 | async-start | bytes 655360 | tf_op jit(solution)/shard_map/all_to_all | solution.py:547
  84.2 1.2 %add_convert_fusion.8 = (bf16[256,128]{1,0:T(8,128)(2,1)S(1)}, bf16[256,128]{1,0:T(8,128)(2,1)S(1)}, bf16[256,128]{1,0:T(8,128)(2,1)S(1)}, f32[256,128]{1,0:T(8,128)S(1)}) fusion(f32[2048,128]{1,0:T(8,128)S(1)} %get-tuple-element.41, bf16[1024,128]{1,0:T(8,128)(2,1)S(1)} %collective-permute-done.8, bf16[2048,128]{1,0:T(8,128)(2,1)} %collective-permute-done.6, ...), kind=kLoop, calls=%fused_computation.19 | loop fusion | flops 884736 | bytes 1638400 | tf_op jit(solution)/shard_map/convert.7
  85.4 1.2 %add_convert_fusion.9 = (bf16[256,128]{1,0:T(8,128)(2,1)S(1)}, bf16[256,128]{1,0:T(8,128)(2,1)S(1)}, bf16[256,128]{1,0:T(8,128)(2,1)S(1)}, f32[256,128]{1,0:T(8,128)S(1)}) fusion(f32[2048,128]{1,0:T(8,128)S(1)} %get-tuple-element.39, bf16[1024,128]{1,0:T(8,128)(2,1)S(1)} %collective-permute-done.7, bf16[2048,128]{1,0:T(8,128)(2,1)} %collective-permute-done.5, ...), kind=kLoop, calls=%fused_computation.20 | loop fusion | flops 884736 | bytes 1638400 | tf_op jit(solution)/shard_map/convert.6
  86.6 3.2 %collective-permute-start.10 = (bf16[512,128]{1,0:T(8,128)(2,1)S(1)}, bf16[512,128]{1,0:T(8,128)(2,1)S(1)}, u32[]{:S(2)}, u32[]{:S(2)}) collective-permute-start(bf16[512,128]{1,0:T(8,128)(2,1)S(1)} %pad_maximum_fusion.2), channel_id=1, source_target_pairs={{0,16},{8,24},{16,0},{24,8},{1,17},{9,25},{17,1},{25,9},{2,18},{10... | collective-permute-start | bytes 393224 | tf_op jit(solution)/shard_map/ppermute | solution.py:538
  89.8 1.1 %collective-permute-start.11 = (bf16[512,128]{1,0:T(8,128)(2,1)S(1)}, bf16[512,128]{1,0:T(8,128)(2,1)S(1)}, u32[]{:S(2)}, u32[]{:S(2)}) collective-permute-start(bf16[512,128]{1,0:T(8,128)(2,1)S(1)} %pad_maximum_fusion.3), channel_id=1, source_target_pairs={{0,24},{8,16},{16,8},{24,0},{1,25},{9,17},{17,9},{25,1},{2,26},{10... | collective-permute-start | bytes 393224 | tf_op jit(solution)/shard_map/ppermute | solution.py:538
  91.1 12.8 %collective-permute-done.10 = bf16[512,128]{1,0:T(8,128)(2,1)S(1)} collective-permute-done((bf16[512,128]{1,0:T(8,128)(2,1)S(1)}, bf16[512,128]{1,0:T(8,128)(2,1)S(1)}, u32[]{:S(2)}, u32[]{:S(2)}) %collective-permute-start.10) | collective-permute-done | bytes 131104 | tf_op jit(solution)/shard_map/ppermute | solution.py:538
  103.9 0.8 fusion.1
  104.8 0.7 fusion.3
  105.5 0.7 copy.30
  106.3 0.6 reshape.84
  (70 shorter events, 1.2 us)
Async XLA Ops:
  0.6 9.0 %copy-start.2 = (bf16[8,384,128]{2,1,0:T(8,128)(2,1)S(1)}, bf16[8,384,128]{2,1,0:T(8,128)(2,1)}, u32[]{:S(2)}) copy-start(bf16[8,384,128]{2,1,0:T(8,128)(2,1)} %state.6) | copy-start | bytes 2359300
  0.6 8.7 %copy-start.19 = (bf16[7,7,128]{2,1,0:T(8,128)(2,1)S(1)}, bf16[7,7,128]{2,1,0:T(8,128)(2,1)}, u32[]{:S(2)}) copy-start(bf16[7,7,128]{2,1,0:T(8,128)(2,1)} %param.21) | copy-start | bytes 37636
  0.7 8.7 %copy-start = (bf16[128,512]{1,0:T(8,128)(2,1)S(1)}, bf16[128,512]{1,0:T(8,128)(2,1)}, u32[]{:S(2)}) copy-start(bf16[128,512]{1,0:T(8,128)(2,1)} %up.1) | copy-start | bytes 393220
  0.7 8.8 %copy-start.1 = (bf16[512,128]{1,0:T(8,128)(2,1)S(1)}, bf16[512,128]{1,0:T(8,128)(2,1)}, u32[]{:S(2)}) copy-start(bf16[512,128]{1,0:T(8,128)(2,1)} %down.1) | copy-start | bytes 393220
  0.7 8.9 %copy-start.8 = (f32[128]{0:T(128)S(1)}, f32[128]{0:T(128)}, u32[]{:S(2)}) copy-start(f32[128]{0:T(128)} %param.22) | copy-start | bytes 1540
  2.8 15.0 %collective-permute-start.1 = (bf16[3,384,128]{2,1,0:T(8,128)(2,1)}, bf16[3,384,128]{2,1,0:T(8,128)(2,1)S(1)}, u32[]{:S(2)}, u32[]{:S(2)}) collective-permute-start(bf16[3,384,128]{2,1,0:T(8,128)(2,1)} %get-tuple-element.26), channel_id=1, source_target_pairs={{8,16},{9,17},{10,18},{11,19},{12,20},{13,21},{14,22},{15,23},{16,... | collective-permute-start | bytes 884744 | tf_op jit(solution)/shard_map/ppermute | solution.py:419
  3.4 14.3 %collective-permute-start = (bf16[3,384,128]{2,1,0:T(8,128)(2,1)}, bf16[3,384,128]{2,1,0:T(8,128)(2,1)S(1)}, u32[]{:S(2)}, u32[]{:S(2)}) collective-permute-start(bf16[3,384,128]{2,1,0:T(8,128)(2,1)} %get-tuple-element.25), channel_id=1, source_target_pairs={{0,8},{1,9},{2,10},{3,11},{4,12},{5,13},{6,14},{7,15},{8,0},{9,1},... | collective-permute-start | bytes 884744 | tf_op jit(solution)/shard_map/ppermute | solution.py:418
  17.9 4.7 %collective-permute-start.2 = (bf16[14,3,128]{2,1,0:T(4,128)(2,1)S(1)}, bf16[14,3,128]{2,1,0:T(4,128)(2,1)S(1)}, u32[]{:S(2)}, u32[]{:S(2)}) collective-permute-start(bf16[14,3,128]{2,1,0:T(4,128)(2,1)S(1)} %pad_maximum_fusion.4), channel_id=1, source_target_pairs={{0,1},{1,2},{2,3},{3,4},{4,5},{5,6},{6,7},{7,0},{8,9},{9,10},{10,1... | collective-permute-start | bytes 32264 | tf_op jit(solution)/shard_map/ppermute | solution.py:426
  18.0 4.7 %copy-start.3 = (bf16[8,384,128]{2,1,0:T(8,128)(2,1)S(1)}, bf16[8,384,128]{2,1,0:T(8,128)(2,1)}, u32[]{:S(2)}) copy-start(bf16[8,384,128]{2,1,0:T(8,128)(2,1)} %forcing.1) | copy-start | bytes 2359300
  18.0 4.7 %copy-start.4 = (bf16[8,384,128]{2,1,0:T(8,128)(2,1)S(1)}, bf16[8,384,128]{2,1,0:T(8,128)(2,1)}, u32[]{:S(2)}) copy-start(bf16[8,384,128]{2,1,0:T(8,128)(2,1)} %cotangent.1) | copy-start | bytes 2359300
  18.0 4.7 %copy-start.5 = (s32[6144]{0:T(1024)S(1)}, s32[6144]{0:T(1024)}, u32[]{:S(2)}) copy-start(s32[6144]{0:T(1024)} %param.32) | copy-start | bytes 73732
  18.0 4.7 %copy-start.6 = (s32[8,384]{1,0:T(8,128)S(1)}, s32[8,384]{1,0:T(8,128)}, u32[]{:S(2)}) copy-start(s32[8,384]{1,0:T(8,128)} %land.1) | copy-start | bytes 36868
  18.0 4.7 %copy-start.7 = (f32[512]{0:T(512)S(1)}, f32[512]{0:T(512)}, u32[]{:S(2)}) copy-start(f32[512]{0:T(512)} %param.26) | copy-start | bytes 6148
  18.0 4.7 %copy-start.9 = (f32[16]{0:T(128)S(1)}, f32[16]{0:T(128)}, u32[]{:S(2)}) copy-start(f32[16]{0:T(128)} %weight_table.1) | copy-start | bytes 196
  18.0 4.6 %copy-start.10 = (f32[128]{0:T(128)S(1)}, f32[128]{0:T(128)}, u32[]{:S(2)}) copy-start(f32[128]{0:T(128)} %param.23) | copy-start | bytes 1540
  18.0 4.6 %copy-start.11 = (f32[128]{0:T(128)S(1)}, f32[128]{0:T(128)}, u32[]{:S(2)}) copy-start(f32[128]{0:T(128)} %param.24) | copy-start | bytes 1540
  18.1 4.6 %copy-start.12 = (f32[128]{0:T(128)S(1)}, f32[128]{0:T(128)}, u32[]{:S(2)}) copy-start(f32[128]{0:T(128)} %param.28) | copy-start | bytes 1540
  18.1 4.6 %copy-start.13 = (f32[128]{0:T(128)S(1)}, f32[128]{0:T(128)}, u32[]{:S(2)}) copy-start(f32[128]{0:T(128)} %param.29) | copy-start | bytes 1540
  18.1 4.6 %copy-start.14 = (s32[48,128]{1,0:T(8,128)S(1)}, s32[48,128]{1,0:T(8,128)}, u32[]{:S(2)}) copy-start(s32[48,128]{1,0:T(8,128)} %get-tuple-element.28) | copy-start | bytes 73732
  18.1 4.6 %copy-start.15 = (s32[48,128]{1,0:T(8,128)S(1)}, s32[48,128]{1,0:T(8,128)}, u32[]{:S(2)}) copy-start(s32[48,128]{1,0:T(8,128)} %get-tuple-element.29) | copy-start | bytes 73732
  18.1 4.6 %copy-start.17 = (f32[8,384,128]{2,1,0:T(8,128)S(1)}, f32[8,384,128]{2,1,0:T(8,128)}, u32[]{:S(2)}) copy-start(f32[8,384,128]{2,1,0:T(8,128)} %copy-done.16) | copy-start | bytes 4718596
  18.1 4.5 %collective-permute-start.3 = (bf16[14,3,128]{2,1,0:T(4,128)(2,1)S(1)}, bf16[14,3,128]{2,1,0:T(4,128)(2,1)S(1)}, u32[]{:S(2)}, u32[]{:S(2)}) collective-permute-start(bf16[14,3,128]{2,1,0:T(4,128)(2,1)S(1)} %pad_maximum_fusion.5), channel_id=1, source_target_pairs={{1,0},{2,1},{3,2},{4,3},{5,4},{6,5},{7,6},{0,7},{9,8},{10,9},{11,1... | collective-permute-start | bytes 32264 | tf_op jit(solution)/shard_map/ppermute | solution.py:427
  47.3 6.4 %collective-permute-start.4 = (bf16[8192,128]{1,0:T(8,128)(2,1)S(1)}, bf16[8192,128]{1,0:T(8,128)(2,1)S(1)}, u32[]{:S(2)}, u32[]{:S(2)}) collective-permute-start(bf16[8192,128]{1,0:T(8,128)(2,1)S(1)} %get-tuple-element.33), channel_id=1, source_target_pairs={{0,1},{1,0},{2,3},{3,2},{4,5},{5,4},{6,7},{7,6},{8,9},{9,8},{10,11... | collective-permute-start | bytes 6291464 | tf_op jit(solution)/shard_map/ppermute | solution.py:374
  55.5 16.2 %collective-permute-start.6 = (bf16[2048,128]{1,0:T(8,128)(2,1)}, bf16[2048,128]{1,0:T(8,128)(2,1)}, u32[]{:S(2)}, u32[]{:S(2)}) collective-permute-start(bf16[2048,128]{1,0:T(8,128)(2,1)} %get-tuple-element.55), channel_id=1, source_target_pairs={{0,4},{1,5},{2,6},{3,7},{4,0},{5,1},{6,2},{7,3},{8,12},{9,13},{10,... | collective-permute-start | bytes 1572872 | tf_op jit(solution)/shard_map/ppermute | solution.py:374
  57.2 17.1 %collective-permute-start.5 = (bf16[2048,128]{1,0:T(8,128)(2,1)}, bf16[2048,128]{1,0:T(8,128)(2,1)}, u32[]{:S(2)}, u32[]{:S(2)}) collective-permute-start(bf16[2048,128]{1,0:T(8,128)(2,1)} %get-tuple-element.56), channel_id=1, source_target_pairs={{0,2},{1,3},{2,0},{3,1},{4,6},{5,7},{6,4},{7,5},{8,10},{9,11},{10,... | collective-permute-start | bytes 1572872 | tf_op jit(solution)/shard_map/ppermute | solution.py:374
  59.4 19.6 %all-to-all-start = ((bf16[32,34,128]{2,1,0:T(8,128)(2,1)}), bf16[32,34,128]{2,1,0:T(8,128)(2,1)S(1)}, u32[]{:S(2)}, u32[]{:S(2)}) async-start(bf16[32,34,128]{2,1,0:T(8,128)(2,1)} %reshape.83), calls=%async_computation | async-start | bytes 655360 | tf_op jit(solution)/shard_map/all_to_all | solution.py:544
  76.5 7.7 %collective-permute-start.8 = (bf16[1024,128]{1,0:T(8,128)(2,1)}, bf16[1024,128]{1,0:T(8,128)(2,1)S(1)}, u32[]{:S(2)}, u32[]{:S(2)}) collective-permute-start(bf16[1024,128]{1,0:T(8,128)(2,1)} %get-tuple-element.53), channel_id=1, source_target_pairs={{0,2},{1,3},{2,0},{3,1},{4,6},{5,7},{6,4},{7,5},{8,10},{9,11},{10,... | collective-permute-start | bytes 786440 | tf_op jit(solution)/shard_map/ppermute | solution.py:374
  77.3 7.0 %collective-permute-start.7 = (bf16[1024,128]{1,0:T(8,128)(2,1)S(1)}, bf16[1024,128]{1,0:T(8,128)(2,1)S(1)}, u32[]{:S(2)}, u32[]{:S(2)}) collective-permute-start(bf16[1024,128]{1,0:T(8,128)(2,1)S(1)} %get-tuple-element.54), channel_id=1, source_target_pairs={{0,4},{1,5},{2,6},{3,7},{4,0},{5,1},{6,2},{7,3},{8,12},{9,13},{10,... | collective-permute-start | bytes 786440 | tf_op jit(solution)/shard_map/ppermute | solution.py:374
  79.9 24.8 %all-to-all-start.1 = ((bf16[32,34,128]{2,1,0:T(8,128)(2,1)}), bf16[32,34,128]{2,1,0:T(8,128)(2,1)S(1)}, u32[]{:S(2)}, u32[]{:S(2)}) async-start(bf16[32,34,128]{2,1,0:T(8,128)(2,1)} %broadcast_in_dim.2), calls=%async_computation.1 | async-start | bytes 655360 | tf_op jit(solution)/shard_map/all_to_all | solution.py:547
  86.6 17.3 %collective-permute-start.10 = (bf16[512,128]{1,0:T(8,128)(2,1)S(1)}, bf16[512,128]{1,0:T(8,128)(2,1)S(1)}, u32[]{:S(2)}, u32[]{:S(2)}) collective-permute-start(bf16[512,128]{1,0:T(8,128)(2,1)S(1)} %pad_maximum_fusion.2), channel_id=1, source_target_pairs={{0,16},{8,24},{16,0},{24,8},{1,17},{9,25},{17,1},{25,9},{2,18},{10... | collective-permute-start | bytes 393224 | tf_op jit(solution)/shard_map/ppermute | solution.py:538
  89.8 14.1 %collective-permute-start.11 = (bf16[512,128]{1,0:T(8,128)(2,1)S(1)}, bf16[512,128]{1,0:T(8,128)(2,1)S(1)}, u32[]{:S(2)}, u32[]{:S(2)}) collective-permute-start(bf16[512,128]{1,0:T(8,128)(2,1)S(1)} %pad_maximum_fusion.3), channel_id=1, source_target_pairs={{0,24},{8,16},{16,8},{24,0},{1,25},{9,17},{17,9},{25,1},{2,26},{10... | collective-permute-start | bytes 393224 | tf_op jit(solution)/shard_map/ppermute | solution.py:538
  90.9 13.0 %collective-permute-start.9 = (bf16[512,128]{1,0:T(8,128)(2,1)S(1)}, bf16[512,128]{1,0:T(8,128)(2,1)S(1)}, u32[]{:S(2)}, u32[]{:S(2)}) collective-permute-start(bf16[512,128]{1,0:T(8,128)(2,1)S(1)} %pad_maximum_fusion.1), channel_id=1, source_target_pairs={{0,8},{8,0},{16,24},{24,16},{1,9},{9,1},{17,25},{25,17},{2,10},{10... | collective-permute-start | bytes 393224 | tf_op jit(solution)/shard_map/ppermute | solution.py:538
  (2 other events, 2.9 us)

commit v7 on v6

--- a/solution.py
+++ b/solution.py
@@ -11,8 +11,8 @@
 PAD = 8
 TAPS = 7
 MARGIN = 3
-BATCH = 16
-BATCHES = 2
+BATCH = 32
+SMALL = 8
 gelu_scale = 0.7978845608028654
 cubic_coef = 0.044715
 f32 = jnp.float32
@@ -88,8 +88,11 @@
             odd[m] = turned.astype(bf16)
 
 
-def inner_conv_kernel(state, dw, dwb, conv, padded):
+def inner_conv_kernel(
+    lat_count, lon_count, orders, state, dw, dwb, owner, cell, conv, targets, clash, padded
+):
     rows, cols, channels = state.shape
+    find_targets(lat_count, lon_count, orders, owner, cell, targets, clash)
     for r in range(rows):
         padded[r, PAD : PAD + cols, :] = state[r].astype(f32)
 
@@ -252,32 +255,28 @@
             for copy in scalar_copies:
                 copy.wait()
 
-        unit = BATCH * BATCHES
-        units = fan * size // unit
+        units = fan * size // BATCH
 
         def add_unit(index, _):
-            first_cell = index * (unit // fan)
-            first_entry = step * (fan * size) + index * unit
-
-            def entry(k):
-                cell = first_cell + k // fan
-                return targets[first_entry + k], terms[pl.ds((k % fan) * size + cell, 1), :]
+            first_cell = index * (BATCH // fan)
+            first_entry = step * (fan * size) + index * BATCH
+
+            def add_batch(first, count):
+                found = []
+                for k in range(first, first + count):
+                    value = terms[pl.ds((k % fan) * size + first_cell + k // fan, 1), :]
+                    found.append((targets[first_entry + k], value))
+                sums = [table[pl.ds(t, 1), :] + v for t, v in found]
+                for (t, _), value in zip(found, sums):
+                    table[pl.ds(t, 1), :] = value
 
             clashing = clash[first_entry]
-
-            @pl.when(clashing == 0)
-            def _():
-                for batch in range(BATCHES):
-                    found = [entry(batch * BATCH + k) for k in range(BATCH)]
-                    sums = [table[pl.ds(t, 1), :] + v for t, v in found]
-                    for (t, _), value in zip(found, sums):
-                        table[pl.ds(t, 1), :] = value
-
-            @pl.when(clashing != 0)
-            def _():
-                for k in range(unit):
-                    t, v = entry(k)
-                    table[pl.ds(t, 1), :] = table[pl.ds(t, 1), :] + v
+            for level, count in enumerate((BATCH, SMALL, 1)):
+
+                @pl.when(clashing == level)
+                def _():
+                    for first in range(0, BATCH, count):
+                        add_batch(first, count)
 
             return 0
 
@@ -307,7 +306,7 @@
         copy.wait()
 
 
-def target_kernel(lat_count, lon_count, orders, owner, cell, targets, clash):
+def find_targets(lat_count, lon_count, orders, owner, cell, targets, clash):
     lat, lon = lax.axis_index("lat"), lax.axis_index("lon")
     lon_bits = lon_count.bit_length() - 1
     half_rows = lat_count * lon_count // 2 * A_DEV
@@ -328,11 +327,13 @@
     targets[...] = row
     lane = lax.broadcasted_iota(jnp.int32, row.shape, 1)
     twice = jnp.zeros_like(row)
-    for distance in range(1, BATCH):
-        same = (row == pltpu.roll(row, distance, 1)) & (lane % BATCH >= distance)
-        twice = jnp.where(same, 1, twice)
+    for distance in range(BATCH - 1, 0, -1):
+        same = row == pltpu.roll(row, distance, 1)
+        twice = jnp.where(same & (lane % BATCH >= distance), jnp.maximum(twice, 1), twice)
+        if distance < SMALL:
+            twice = jnp.where(same & (lane % SMALL >= distance), 2, twice)
     distance = 1
-    while distance < BATCH * BATCHES:
+    while distance < BATCH:
         twice = jnp.maximum(twice, pltpu.roll(twice, row.shape[1] - distance, 1))
         distance *= 2
     clash[...] = twice
@@ -402,10 +403,10 @@
             here = l * lon_count + j
             even_pairs.append((here, (l ^ 1) * lon_count + j))
             beyond = l + 1 if l % 2 else l - 1
-            if l == lat_count - 1:
+            if 0 <= beyond < lat_count:
+                odd_pairs.append((here, beyond * lon_count + j))
+            else:
                 odd_pairs.append((here, l * lon_count + lon_count - 1 - j))
-            elif beyond >= 0:
-                odd_pairs.append((here, beyond * lon_count + j))
     edge_rows = shape((MARGIN, cols, channels), bf16)
     for_even, for_odd = pl.pallas_call(
         functools.partial(edge_kernel, bands=lat_count),
@@ -417,7 +418,7 @@
     )(state)
     got_even = lax.ppermute(for_even, ("lat", "lon"), even_pairs)
     got_odd = lax.ppermute(for_odd, ("lat", "lon"), odd_pairs)
-    south = jnp.where(odd, got_even, got_odd)
+    south = jnp.where(odd, got_even, jnp.where(lat == 0, jnp.zeros_like(got_odd), got_odd))
     north = jnp.where(odd, got_odd, got_even)
 
     forward = [(i, (i + 1) % lon_count) for i in range(lon_count)]
@@ -431,27 +432,20 @@
     width = A_DEV // 2
     half_rows = devices // 2 * A_DEV
     lines = (entries // channels, channels)
-    targets, clash = pl.pallas_call(
-        functools.partial(target_kernel, lat_count, lon_count, orders),
-        out_shape=(shape(lines, jnp.int32),) * 2,
-        in_specs=[vmem()] * 2,
-        out_specs=[vmem()] * 2,
-        cost_estimate=cost(1),
-        name="targets",
-    )(owner.reshape(lines), atmos_cell.reshape(lines))
-
     line = lambda v: v.reshape(1, -1)
     taps = dw_weight.reshape(-1, channels).astype(f32)
-    conv = pl.pallas_call(
-        inner_conv_kernel,
-        out_shape=shape((rows, cols, channels), f32),
-        in_specs=[vmem()] * 3,
-        out_specs=vmem(),
+    conv, targets, clash = pl.pallas_call(
+        functools.partial(inner_conv_kernel, lat_count, lon_count, orders),
+        out_shape=(shape((rows, cols, channels), f32),) + (shape(lines, jnp.int32),) * 2,
+        in_specs=[vmem()] * 5,
+        out_specs=[vmem()] * 3,
         scratch_shapes=[pltpu.VMEM((rows, cols + 2 * PAD, channels), f32)],
         compiler_params=params(),
         cost_estimate=cost(7),
         name="inner_conv",
-    )(after(state, for_even), taps, line(dw_bias))
+    )(
+        after(state, for_even), taps, line(dw_bias), owner.reshape(lines), atmos_cell.reshape(lines)
+    )
     halo = pl.pallas_call(
         functools.partial(halo_conv_kernel, rows=rows),
         out_shape=shape((2 * MARGIN, cols, channels), f32),
@@ -533,10 +527,10 @@
         return jnp.concatenate([add([h[at] for h in held[q]]) for q in range(2)], axis=0)
 
     forcing_grad = for_band(0)
+    from_bands = []
     for distance in range(1, lat_count):
         pairs = [(i, i ^ distance) for i in range(lat_count)]
-        arrived = lax.ppermute(for_band(distance).astype(bf16), "lat", pairs)
-        forcing_grad = forcing_grad + arrived.astype(f32)
+        from_bands.append(lax.ppermute(for_band(distance).astype(bf16), "lat", pairs))
 
     total = jnp.concatenate([grads.reshape(2 * hid, channels), grad_dw], axis=0).astype(bf16)
     total = after(total, *first_sends)
@@ -551,6 +545,10 @@
     grad_up = grad_up.transpose(1, 0, 2).reshape(channels, hid)
     grad_down = total[hid : 2 * hid]
     grad_dw = total[2 * hid : 2 * hid + tap_count].reshape(dw_weight.shape)
+    arrived, grad_dw, grad_up, grad_down = lax.optimization_barrier(
+        (from_bands, grad_dw, grad_up, grad_down)
+    )
+    forcing_grad = add([forcing_grad] + list(arrived))
     return (result, grad_dw, grad_up, grad_down, forcing_grad)
 
 

time: 107 us -> 107 us (level)
  Pallas kernels: 41.5 us -> 44.9 us
  waiting for transfers between devices: 23.4 us -> 21.3 us
    ppermute x3, waiting for transfers between devices: 12.8 us -> 5.71 us  [on_device(): lax.ppermute(for_band(distance).astype(bf16), 'lat', pairs)]
    all_to_all x2, waiting for transfers between devices: 0.01 us -> 4.75 us  [on_device(): lax.all_to_all(total, ('lat', 'lon'), split_axis=0, concat_axis=0, tiled=...]
    pallas_call x1, Pallas kernels: 24.5 us -> 29.3 us  [on_device(): pl.pallas_call(block_kernel, out_shape=(shape((rows, cols, channels), bf1...]
    ppermute x1, starting transfers between devices: 5.89 us -> 1.27 us  [on_device(): got_even = lax.ppermute(for_even, ('lat', 'lon'), even_pairs)]
    ppermute x1, starting transfers between devices: 0.67 us -> 3.33 us  [on_device(): got_odd = lax.ppermute(for_odd, ('lat', 'lon'), odd_pairs)]
    another operation x4 -> x2, other arithmetic: 2.43 us -> 0.04 us
    add x1 -> x3, other arithmetic: 0.77 us -> 3.13 us  [on_device(): x + y.astype(f32)]
    ppermute x1, waiting for transfers between devices: 0.01 us -> 1.41 us  [on_device(): got_even = lax.ppermute(for_even, ('lat', 'lon'), even_pairs)]
  transfers between devices with their start and end apart: 14 -> 14, of which waited for: 3 -> 5; matrix products, arithmetic and copies ran while one was open for 7% -> 7% of each run, Pallas kernels for 14% -> 13%
where the time goes in v7:
time: 107 us
  Pallas kernels  44.9 us (42%)
  starting transfers between devices  27.5 us (26%)
  waiting for transfers between devices  21.3 us (20%)
  other arithmetic  6.31 us (6%)
  local copies, waits for them, and re-layouts  5.49 us (5%)
  between operations  1.15 us (1%)
    pallas_call x1, Pallas kernels, on_device(): pl.pallas_call(block_kernel, out_shape=(shape((rows, cols, channels), bf1...  29.3 us
    all_to_all x2, starting transfers between devices, on_device(): lax.all_to_all(total, ('lat', 'lon'), split_axis=0, concat_axis=0, tiled=...  10.2 us
    ppermute x5, waiting for transfers between devices, swap_bit(): return lax.ppermute(array, 'lon', pairs)  9.41 us
    pallas_call x1, Pallas kernels, on_device(): pl.pallas_call(conv_grad_kernel, out_shape=shape((dw_rows, channels), f32...  6.17 us
    ppermute x3, waiting for transfers between devices, on_device(): lax.ppermute(for_band(distance).astype(bf16), 'lat', pairs)  5.71 us
    pallas_call x1, Pallas kernels, on_device(): pl.pallas_call(functools.partial(inner_conv_kernel, lat_count, lon_count,...  5.57 us
    ppermute x5, starting transfers between devices, swap_bit(): return lax.ppermute(array, 'lon', pairs)  5.44 us
    all_to_all x2, waiting for transfers between devices, on_device(): lax.all_to_all(total, ('lat', 'lon'), split_axis=0, concat_axis=0, tiled=...  4.75 us
  transfers between devices with their start and end apart: 14, of which 5 were waited for; matrix products, arithmetic and copies ran while one was open for 7% of the time, Pallas kernels for 13%

profile of v7, /device:TPU:0, one launch (start us, length us, event | category | flops | bytes accessed | tf_op | source)
XLA Modules:
  0.0 106.6 jit_solution(12557385202458159359)
XLA Ops:
  0.7 2.1 %edges.1 = (bf16[3,384,128]{2,1,0:T(8,128)(2,1)}, bf16[3,384,128]{2,1,0:T(8,128)(2,1)}) custom-call(bf16[8,384,128]{2,1,0:T(8,128)(2,1)} %state.6), custom_call_target="tpu_custom_call" | custom-call | flops 1000000000 | tf_op jit(solution)/shard_map/edges/pallas_call | solution.py:411
  2.7 3.3 %collective-permute-start.1 = (bf16[3,384,128]{2,1,0:T(8,128)(2,1)}, bf16[3,384,128]{2,1,0:T(8,128)(2,1)S(1)}, u32[]{:S(2)}, u32[]{:S(2)}) collective-permute-start(bf16[3,384,128]{2,1,0:T(8,128)(2,1)} %get-tuple-element.33), channel_id=1, source_target_pairs={{0,7},{1,6},{2,5},{3,4},{4,3},{5,2},{6,1},{7,0},{8,16},{9,17},{10,... | collective-permute-start | bytes 884744 | tf_op jit(solution)/shard_map/ppermute | solution.py:420
  6.1 1.3 %collective-permute-start = (bf16[3,384,128]{2,1,0:T(8,128)(2,1)}, bf16[3,384,128]{2,1,0:T(8,128)(2,1)S(1)}, u32[]{:S(2)}, u32[]{:S(2)}) collective-permute-start(bf16[3,384,128]{2,1,0:T(8,128)(2,1)} %get-tuple-element.32), channel_id=1, source_target_pairs={{0,8},{1,9},{2,10},{3,11},{4,12},{5,13},{6,14},{7,15},{8,0},{9,1},... | collective-permute-start | bytes 884744 | tf_op jit(solution)/shard_map/ppermute | solution.py:419
  7.4 5.6 %inner_conv.1 = (f32[8,384,128]{2,1,0:T(8,128)S(1)}, s32[48,128]{1,0:T(8,128)S(1)}, s32[48,128]{1,0:T(8,128)S(1)}) custom-call(bf16[8,384,128]{2,1,0:T(8,128)(2,1)S(1)} %copy-done.2, f32[49,128]{1,0:T(8,128)S(1)} %reshape.87.dw, f32[1,128]{1,0:T(1,128)S(1)} %bitcast.27, s32[48,128]{1,0:T(8,128)S(1)} %bitcast.23, s32[48,128]{1,0:T(8,128)S(1)} %bitcast.24), custom_call_target="tpu_custom_call" | custom-call | flops 7000000000 | tf_op jit(solution)/shard_map/inner_conv/pallas_call | solution.py:437
  13.0 1.2 %copy-done.16 = f32[8,384,128]{2,1,0:T(8,128)} copy-done((f32[8,384,128]{2,1,0:T(8,128)}, f32[8,384,128]{2,1,0:T(8,128)S(1)}, u32[]{:S(2)}) %copy-start.16) | copy-done | bytes 1572888
  14.5 1.4 %collective-permute-done = bf16[3,384,128]{2,1,0:T(8,128)(2,1)S(1)} collective-permute-done((bf16[3,384,128]{2,1,0:T(8,128)(2,1)}, bf16[3,384,128]{2,1,0:T(8,128)(2,1)S(1)}, u32[]{:S(2)}, u32[]{:S(2)}) %collective-permute-start) | collective-permute-done | bytes 294944 | tf_op jit(solution)/shard_map/ppermute | solution.py:419
  16.2 2.7 %collective-permute-start.3 = (bf16[14,3,128]{2,1,0:T(4,128)(2,1)S(1)}, bf16[14,3,128]{2,1,0:T(4,128)(2,1)S(1)}, u32[]{:S(2)}, u32[]{:S(2)}) collective-permute-start(bf16[14,3,128]{2,1,0:T(4,128)(2,1)S(1)} %pad_maximum_fusion.5), channel_id=1, source_target_pairs={{1,0},{2,1},{3,2},{4,3},{5,4},{6,5},{7,6},{0,7},{9,8},{10,9},{11,1... | collective-permute-start | bytes 32264 | tf_op jit(solution)/shard_map/ppermute | solution.py:428
  18.9 1.8 %halo_conv.1.halo = f32[6,384,128]{2,1,0:T(8,128)S(1)} custom-call(bf16[3,384,128]{2,1,0:T(8,128)(2,1)S(1)} %get-tuple-element.74.south, bf16[3,384,128]{2,1,0:T(8,128)(2,1)S(1)} %get-tuple-element.73.north, f32[49,128]{1,0:T(8,128)S(1)} %reshape.87.dw), custom_call_target="tpu_custom_call" | custom-call | flops 2000000000 | tf_op jit(solution)/shard_map/halo_conv/pallas_call | solution.py:449
  20.8 29.3 %block.1 = (bf16[8,384,128]{2,1,0:T(8,128)(2,1)}, f32[2048,128]{1,0:T(8,128)S(1)}, f32[2048,128]{1,0:T(8,128)S(1)}, f32[2048,128]{1,0:T(8,128)S(1)}, f32[2048,12...) custom-call(bf16[8,384,128]{2,1,0:T(8,128)(2,1)S(1)} %copy-done.2, ...), custom_call_target="tpu_custom_call" | custom-call | flops 28000000000 | tf_op jit(solution)/shard_map/block/pallas_call | solution.py:460
  50.2 6.2 %conv_grad.1 = f32[64,128]{1,0:T(8,128)S(1)} custom-call(bf16[8,384,128]{2,1,0:T(8,128)(2,1)S(1)} %copy-done.2, bf16[3,384,128]{2,1,0:T(8,128)(2,1)S(1)} %get-tuple-element.74.south, bf16[3,384,128]{2,1,0:T(8,128)(2,1)S(1)} %get-tuple-element.73.north, bf16[14,3,128]{2,1,0:T(4,128)(2,1)S(1)} %collective-permute-done.2.left, ...), custom_call_target="tpu_custom_call" | custom-call | flops 8999999488 | tf_op jit(solution)/shard_map/conv_grad/pallas_call | solution.py:498
  56.4 1.5 %add_convert_fusion = (bf16[2048,128]{1,0:T(8,128)(2,1)}, bf16[2048,128]{1,0:T(8,128)(2,1)}) fusion(f32[2048,128]{1,0:T(8,128)S(1)} %get-tuple-element.45, bf16[8192,128]{1,0:T(8,128)(2,1)S(1)} %collective-permute-done.4, f32[2048,128]{1,0:T(8,128)S(1)} %get-tuple-element.44), kind=kLoop, calls=%fused_computation | loop fusion | flops 1572864 | bytes 4194304 | tf_op jit(solution)/shard_map/convert_element_type | solution.py:513
  58.1 0.3 collective-permute-start.6
  58.4 2.6 %collective-permute-start.5 = (bf16[2048,128]{1,0:T(8,128)(2,1)}, bf16[2048,128]{1,0:T(8,128)(2,1)}, u32[]{:S(2)}, u32[]{:S(2)}) collective-permute-start(bf16[2048,128]{1,0:T(8,128)(2,1)} %get-tuple-element.70), channel_id=1, source_target_pairs={{0,2},{1,3},{2,0},{3,1},{4,6},{5,7},{6,4},{7,5},{8,10},{9,11},{10,... | collective-permute-start | bytes 1572872 | tf_op jit(solution)/shard_map/ppermute | solution.py:375
  61.1 0.8 reshape.83
  61.9 4.5 %all-to-all-start = ((bf16[32,34,128]{2,1,0:T(8,128)(2,1)}), bf16[32,34,128]{2,1,0:T(8,128)(2,1)S(1)}, u32[]{:S(2)}, u32[]{:S(2)}) async-start(bf16[32,34,128]{2,1,0:T(8,128)(2,1)} %reshape.83), calls=%async_computation | async-start | bytes 655360 | tf_op jit(solution)/shard_map/all_to_all | solution.py:538
  66.4 8.3 %collective-permute-done.6 = bf16[2048,128]{1,0:T(8,128)(2,1)} collective-permute-done((bf16[2048,128]{1,0:T(8,128)(2,1)}, bf16[2048,128]{1,0:T(8,128)(2,1)}, u32[]{:S(2)}, u32[]{:S(2)}) %collective-permute-start.6) | collective-permute-done | bytes 524320 | tf_op jit(solution)/shard_map/ppermute | solution.py:375
  74.6 1.1 %collective-permute-done.5 = bf16[2048,128]{1,0:T(8,128)(2,1)} collective-permute-done((bf16[2048,128]{1,0:T(8,128)(2,1)}, bf16[2048,128]{1,0:T(8,128)(2,1)}, u32[]{:S(2)}, u32[]{:S(2)}) %collective-permute-start.5) | collective-permute-done | bytes 524320 | tf_op jit(solution)/shard_map/ppermute | solution.py:375
  75.8 1.4 %add_convert_fusion.2 = (bf16[1024,128]{1,0:T(8,128)(2,1)S(1)}, bf16[1024,128]{1,0:T(8,128)(2,1)S(1)}) fusion(f32[2048,128]{1,0:T(8,128)S(1)} %get-tuple-element.47, bf16[2048,128]{1,0:T(8,128)(2,1)} %collective-permute-done.6, bf16[8192,128]{1,0:T(8,128)(2,1)} %copy-done.18, bf16[2048,128]{1,0:T(8,128)(2,1)} %collective-permute-done.5, ...), kind=kLoop, calls=%fused_computation.3 | loop fusion | flops 1310720 | bytes 2621440 | tf_op jit(solution)/shard_map/convert_element_type | solution.py:523
  77.1 2.0 %collective-permute-start.8 = (bf16[1024,128]{1,0:T(8,128)(2,1)S(1)}, bf16[1024,128]{1,0:T(8,128)(2,1)S(1)}, u32[]{:S(2)}, u32[]{:S(2)}) collective-permute-start(bf16[1024,128]{1,0:T(8,128)(2,1)S(1)} %get-tuple-element.67), channel_id=1, source_target_pairs={{0,2},{1,3},{2,0},{3,1},{4,6},{5,7},{6,4},{7,5},{8,10},{9,11},{10,... | collective-permute-start | bytes 786440 | tf_op jit(solution)/shard_map/ppermute | solution.py:375
  79.1 0.5 collective-permute-start.7
  79.7 0.8 broadcast_in_dim.10
  80.5 5.7 %all-to-all-start.1 = ((bf16[32,34,128]{2,1,0:T(8,128)(2,1)}), bf16[32,34,128]{2,1,0:T(8,128)(2,1)S(1)}, u32[]{:S(2)}, u32[]{:S(2)}) async-start(bf16[32,34,128]{2,1,0:T(8,128)(2,1)} %broadcast_in_dim.10), calls=%async_computation.1 | async-start | bytes 655360 | tf_op jit(solution)/shard_map/all_to_all | solution.py:541
  86.2 1.2 %convert_add_fusion = (f32[256,128]{1,0:T(8,128)S(1)}, bf16[256,128]{1,0:T(8,128)(2,1)S(1)}, bf16[256,128]{1,0:T(8,128)(2,1)S(1)}, bf16[256,128]{1,0:T(8,128)(2,1)S(1)}) fusion(f32[2048,128]{1,0:T(8,128)S(1)} %get-tuple-element.47, bf16[1024,128]{1,0:T(8,128)(2,1)S(1)} %collective-permute-done.8, bf16[2048,128]{1,0:T(8,128)(2,1)} %collective-permute-done.6, ...), kind=kLoop, calls=%fused_computation.15 | loop fusion | flops 884736 | bytes 1638400 | tf_op jit(solution)/shard_map/add | solution.py:512
  87.4 1.2 %convert_add_fusion.1 = (f32[256,128]{1,0:T(8,128)S(1)}, bf16[256,128]{1,0:T(8,128)(2,1)S(1)}, bf16[256,128]{1,0:T(8,128)(2,1)S(1)}, bf16[256,128]{1,0:T(8,128)(2,1)S(1)}) fusion(f32[2048,128]{1,0:T(8,128)S(1)} %get-tuple-element.39, bf16[1024,128]{1,0:T(8,128)(2,1)S(1)} %collective-permute-done.7, bf16[2048,128]{1,0:T(8,128)(2,1)} %collective-permute-done.5, ...), kind=kLoop, calls=%fused_computation.16 | loop fusion | flops 884736 | bytes 1638400 | tf_op jit(solution)/shard_map/add | solution.py:512
  88.6 1.8 %collective-permute-start.9 = (bf16[512,128]{1,0:T(8,128)(2,1)S(1)}, bf16[512,128]{1,0:T(8,128)(2,1)S(1)}, u32[]{:S(2)}, u32[]{:S(2)}) collective-permute-start(bf16[512,128]{1,0:T(8,128)(2,1)S(1)} %pad_maximum_fusion.1), channel_id=1, source_target_pairs={{0,8},{8,0},{16,24},{24,16},{1,9},{9,1},{17,25},{25,17},{2,10},{10... | collective-permute-start | bytes 393224 | tf_op jit(solution)/shard_map/ppermute | solution.py:533
  90.4 2.5 %collective-permute-start.10 = (bf16[512,128]{1,0:T(8,128)(2,1)S(1)}, bf16[512,128]{1,0:T(8,128)(2,1)S(1)}, u32[]{:S(2)}, u32[]{:S(2)}) collective-permute-start(bf16[512,128]{1,0:T(8,128)(2,1)S(1)} %pad_maximum_fusion.2), channel_id=1, source_target_pairs={{0,16},{8,24},{16,0},{24,8},{1,17},{9,25},{17,1},{25,9},{2,18},{10... | collective-permute-start | bytes 393224 | tf_op jit(solution)/shard_map/ppermute | solution.py:533
  93.2 4.8 %all-to-all-done.1 = bf16[32,34,128]{2,1,0:T(8,128)(2,1)S(1)} async-done(((bf16[32,34,128]{2,1,0:T(8,128)(2,1)}), bf16[32,34,128]{2,1,0:T(8,128)(2,1)S(1)}, u32[]{:S(2)}, u32[]{:S(2)}) %all-to-all-start.1) | async-done | bytes 278560 | tf_op jit(solution)/shard_map/all_to_all | solution.py:541
  98.1 0.7 fusion.3
  98.8 0.7 copy.30
  99.5 0.6 reshape.84
  100.2 5.7 %collective-permute-done.10 = bf16[512,128]{1,0:T(8,128)(2,1)S(1)} collective-permute-done((bf16[512,128]{1,0:T(8,128)(2,1)S(1)}, bf16[512,128]{1,0:T(8,128)(2,1)S(1)}, u32[]{:S(2)}, u32[]{:S(2)}) %collective-permute-start.10) | collective-permute-done | bytes 131104 | tf_op jit(solution)/shard_map/ppermute | solution.py:533
  105.9 0.8 fusion.1
  (69 shorter events, 1.3 us)
Async XLA Ops:
  0.6 6.7 %copy-start.2 = (bf16[8,384,128]{2,1,0:T(8,128)(2,1)S(1)}, bf16[8,384,128]{2,1,0:T(8,128)(2,1)}, u32[]{:S(2)}) copy-start(bf16[8,384,128]{2,1,0:T(8,128)(2,1)} %state.6) | copy-start | bytes 2359300
  0.6 6.7 %copy-start.19 = (bf16[7,7,128]{2,1,0:T(8,128)(2,1)S(1)}, bf16[7,7,128]{2,1,0:T(8,128)(2,1)}, u32[]{:S(2)}) copy-start(bf16[7,7,128]{2,1,0:T(8,128)(2,1)} %param.21) | copy-start | bytes 37636
  0.7 6.7 %copy-start.6 = (s32[6144]{0:T(1024)S(1)}, s32[6144]{0:T(1024)}, u32[]{:S(2)}) copy-start(s32[6144]{0:T(1024)} %param.31) | copy-start | bytes 73732
  0.7 6.7 %copy-start.5 = (s32[6144,1]{0,1:T(1,128)S(1)}, s32[6144,1]{0,1:T(1,128)}, u32[]{:S(2)}) copy-start(s32[6144,1]{0,1:T(1,128)} %param.30) | copy-start | bytes 73732
  0.7 6.7 %copy-start.10 = (f32[128]{0:T(128)S(1)}, f32[128]{0:T(128)}, u32[]{:S(2)}) copy-start(f32[128]{0:T(128)} %param.22) | copy-start | bytes 1540
  2.7 11.7 %collective-permute-start.1 = (bf16[3,384,128]{2,1,0:T(8,128)(2,1)}, bf16[3,384,128]{2,1,0:T(8,128)(2,1)S(1)}, u32[]{:S(2)}, u32[]{:S(2)}) collective-permute-start(bf16[3,384,128]{2,1,0:T(8,128)(2,1)} %get-tuple-element.33), channel_id=1, source_target_pairs={{0,7},{1,6},{2,5},{3,4},{4,3},{5,2},{6,1},{7,0},{8,16},{9,17},{10,... | collective-permute-start | bytes 884744 | tf_op jit(solution)/shard_map/ppermute | solution.py:420
  6.1 9.8 %collective-permute-start = (bf16[3,384,128]{2,1,0:T(8,128)(2,1)}, bf16[3,384,128]{2,1,0:T(8,128)(2,1)S(1)}, u32[]{:S(2)}, u32[]{:S(2)}) collective-permute-start(bf16[3,384,128]{2,1,0:T(8,128)(2,1)} %get-tuple-element.32), channel_id=1, source_target_pairs={{0,8},{1,9},{2,10},{3,11},{4,12},{5,13},{6,14},{7,15},{8,0},{9,1},... | collective-permute-start | bytes 884744 | tf_op jit(solution)/shard_map/ppermute | solution.py:419
  7.4 6.8 %copy-start = (bf16[128,512]{1,0:T(8,128)(2,1)S(1)}, bf16[128,512]{1,0:T(8,128)(2,1)}, u32[]{:S(2)}) copy-start(bf16[128,512]{1,0:T(8,128)(2,1)} %up.1) | copy-start | bytes 393220
  7.4 6.9 %copy-start.1 = (bf16[512,128]{1,0:T(8,128)(2,1)S(1)}, bf16[512,128]{1,0:T(8,128)(2,1)}, u32[]{:S(2)}) copy-start(bf16[512,128]{1,0:T(8,128)(2,1)} %down.1) | copy-start | bytes 393220
  16.0 4.7 %collective-permute-start.2 = (bf16[14,3,128]{2,1,0:T(4,128)(2,1)S(1)}, bf16[14,3,128]{2,1,0:T(4,128)(2,1)S(1)}, u32[]{:S(2)}, u32[]{:S(2)}) collective-permute-start(bf16[14,3,128]{2,1,0:T(4,128)(2,1)S(1)} %pad_maximum_fusion.4), channel_id=1, source_target_pairs={{0,1},{1,2},{2,3},{3,4},{4,5},{5,6},{6,7},{7,0},{8,9},{9,10},{10,1... | collective-permute-start | bytes 32264 | tf_op jit(solution)/shard_map/ppermute | solution.py:427
  16.0 4.6 %copy-start.3 = (bf16[8,384,128]{2,1,0:T(8,128)(2,1)S(1)}, bf16[8,384,128]{2,1,0:T(8,128)(2,1)}, u32[]{:S(2)}) copy-start(bf16[8,384,128]{2,1,0:T(8,128)(2,1)} %forcing.1) | copy-start | bytes 2359300
  16.1 4.6 %copy-start.4 = (bf16[8,384,128]{2,1,0:T(8,128)(2,1)S(1)}, bf16[8,384,128]{2,1,0:T(8,128)(2,1)}, u32[]{:S(2)}) copy-start(bf16[8,384,128]{2,1,0:T(8,128)(2,1)} %cotangent.1) | copy-start | bytes 2359300
  16.1 4.6 %copy-start.7 = (s32[6144]{0:T(1024)S(1)}, s32[6144]{0:T(1024)}, u32[]{:S(2)}) copy-start(s32[6144]{0:T(1024)} %param.32) | copy-start | bytes 73732
  16.1 4.6 %copy-start.8 = (s32[8,384]{1,0:T(8,128)S(1)}, s32[8,384]{1,0:T(8,128)}, u32[]{:S(2)}) copy-start(s32[8,384]{1,0:T(8,128)} %land.1) | copy-start | bytes 36868
  16.1 4.6 %copy-start.9 = (f32[512]{0:T(512)S(1)}, f32[512]{0:T(512)}, u32[]{:S(2)}) copy-start(f32[512]{0:T(512)} %param.26) | copy-start | bytes 6148
  16.1 4.6 %copy-start.11 = (f32[16]{0:T(128)S(1)}, f32[16]{0:T(128)}, u32[]{:S(2)}) copy-start(f32[16]{0:T(128)} %weight_table.1) | copy-start | bytes 196
  16.1 4.6 %copy-start.12 = (f32[128]{0:T(128)S(1)}, f32[128]{0:T(128)}, u32[]{:S(2)}) copy-start(f32[128]{0:T(128)} %param.23) | copy-start | bytes 1540
  16.1 4.6 %copy-start.13 = (f32[128]{0:T(128)S(1)}, f32[128]{0:T(128)}, u32[]{:S(2)}) copy-start(f32[128]{0:T(128)} %param.24) | copy-start | bytes 1540
  16.1 4.6 %copy-start.14 = (f32[128]{0:T(128)S(1)}, f32[128]{0:T(128)}, u32[]{:S(2)}) copy-start(f32[128]{0:T(128)} %param.28) | copy-start | bytes 1540
  16.2 4.6 %copy-start.15 = (f32[128]{0:T(128)S(1)}, f32[128]{0:T(128)}, u32[]{:S(2)}) copy-start(f32[128]{0:T(128)} %param.29) | copy-start | bytes 1540
  16.2 4.6 %copy-start.17 = (f32[8,384,128]{2,1,0:T(8,128)S(1)}, f32[8,384,128]{2,1,0:T(8,128)}, u32[]{:S(2)}) copy-start(f32[8,384,128]{2,1,0:T(8,128)} %copy-done.16) | copy-start | bytes 4718596
  16.2 4.5 %collective-permute-start.3 = (bf16[14,3,128]{2,1,0:T(4,128)(2,1)S(1)}, bf16[14,3,128]{2,1,0:T(4,128)(2,1)S(1)}, u32[]{:S(2)}, u32[]{:S(2)}) collective-permute-start(bf16[14,3,128]{2,1,0:T(4,128)(2,1)S(1)} %pad_maximum_fusion.5), channel_id=1, source_target_pairs={{1,0},{2,1},{3,2},{4,3},{5,4},{6,5},{7,6},{0,7},{9,8},{10,9},{11,1... | collective-permute-start | bytes 32264 | tf_op jit(solution)/shard_map/ppermute | solution.py:428
  50.1 6.3 %collective-permute-start.4 = (bf16[8192,128]{1,0:T(8,128)(2,1)S(1)}, bf16[8192,128]{1,0:T(8,128)(2,1)S(1)}, u32[]{:S(2)}, u32[]{:S(2)}) collective-permute-start(bf16[8192,128]{1,0:T(8,128)(2,1)S(1)} %get-tuple-element.40), channel_id=1, source_target_pairs={{0,1},{1,0},{2,3},{3,2},{4,5},{5,4},{6,7},{7,6},{8,9},{9,8},{10,11... | collective-permute-start | bytes 6291464 | tf_op jit(solution)/shard_map/ppermute | solution.py:375
  58.1 16.5 %collective-permute-start.6 = (bf16[2048,128]{1,0:T(8,128)(2,1)}, bf16[2048,128]{1,0:T(8,128)(2,1)}, u32[]{:S(2)}, u32[]{:S(2)}) collective-permute-start(bf16[2048,128]{1,0:T(8,128)(2,1)} %get-tuple-element.69), channel_id=1, source_target_pairs={{0,4},{1,5},{2,6},{3,7},{4,0},{5,1},{6,2},{7,3},{8,12},{9,13},{10,... | collective-permute-start | bytes 1572872 | tf_op jit(solution)/shard_map/ppermute | solution.py:375
  58.4 17.4 %collective-permute-start.5 = (bf16[2048,128]{1,0:T(8,128)(2,1)}, bf16[2048,128]{1,0:T(8,128)(2,1)}, u32[]{:S(2)}, u32[]{:S(2)}) collective-permute-start(bf16[2048,128]{1,0:T(8,128)(2,1)} %get-tuple-element.70), channel_id=1, source_target_pairs={{0,2},{1,3},{2,0},{3,1},{4,6},{5,7},{6,4},{7,5},{8,10},{9,11},{10,... | collective-permute-start | bytes 1572872 | tf_op jit(solution)/shard_map/ppermute | solution.py:375
  61.9 17.7 %all-to-all-start = ((bf16[32,34,128]{2,1,0:T(8,128)(2,1)}), bf16[32,34,128]{2,1,0:T(8,128)(2,1)S(1)}, u32[]{:S(2)}, u32[]{:S(2)}) async-start(bf16[32,34,128]{2,1,0:T(8,128)(2,1)} %reshape.83), calls=%async_computation | async-start | bytes 655360 | tf_op jit(solution)/shard_map/all_to_all | solution.py:538
  77.1 9.0 %collective-permute-start.8 = (bf16[1024,128]{1,0:T(8,128)(2,1)S(1)}, bf16[1024,128]{1,0:T(8,128)(2,1)S(1)}, u32[]{:S(2)}, u32[]{:S(2)}) collective-permute-start(bf16[1024,128]{1,0:T(8,128)(2,1)S(1)} %get-tuple-element.67), channel_id=1, source_target_pairs={{0,2},{1,3},{2,0},{3,1},{4,6},{5,7},{6,4},{7,5},{8,10},{9,11},{10,... | collective-permute-start | bytes 786440 | tf_op jit(solution)/shard_map/ppermute | solution.py:375
  79.1 7.1 %collective-permute-start.7 = (bf16[1024,128]{1,0:T(8,128)(2,1)S(1)}, bf16[1024,128]{1,0:T(8,128)(2,1)S(1)}, u32[]{:S(2)}, u32[]{:S(2)}) collective-permute-start(bf16[1024,128]{1,0:T(8,128)(2,1)S(1)} %get-tuple-element.68), channel_id=1, source_target_pairs={{0,4},{1,5},{2,6},{3,7},{4,0},{5,1},{6,2},{7,3},{8,12},{9,13},{10,... | collective-permute-start | bytes 786440 | tf_op jit(solution)/shard_map/ppermute | solution.py:375
  80.5 17.5 %all-to-all-start.1 = ((bf16[32,34,128]{2,1,0:T(8,128)(2,1)}), bf16[32,34,128]{2,1,0:T(8,128)(2,1)S(1)}, u32[]{:S(2)}, u32[]{:S(2)}) async-start(bf16[32,34,128]{2,1,0:T(8,128)(2,1)} %broadcast_in_dim.10), calls=%async_computation.1 | async-start | bytes 655360 | tf_op jit(solution)/shard_map/all_to_all | solution.py:541
  88.6 11.6 %collective-permute-start.9 = (bf16[512,128]{1,0:T(8,128)(2,1)S(1)}, bf16[512,128]{1,0:T(8,128)(2,1)S(1)}, u32[]{:S(2)}, u32[]{:S(2)}) collective-permute-start(bf16[512,128]{1,0:T(8,128)(2,1)S(1)} %pad_maximum_fusion.1), channel_id=1, source_target_pairs={{0,8},{8,0},{16,24},{24,16},{1,9},{9,1},{17,25},{25,17},{2,10},{10... | collective-permute-start | bytes 393224 | tf_op jit(solution)/shard_map/ppermute | solution.py:533
  90.4 15.4 %collective-permute-start.10 = (bf16[512,128]{1,0:T(8,128)(2,1)S(1)}, bf16[512,128]{1,0:T(8,128)(2,1)S(1)}, u32[]{:S(2)}, u32[]{:S(2)}) collective-permute-start(bf16[512,128]{1,0:T(8,128)(2,1)S(1)} %pad_maximum_fusion.2), channel_id=1, source_target_pairs={{0,16},{8,24},{16,0},{24,8},{1,17},{9,25},{17,1},{25,9},{2,18},{10... | collective-permute-start | bytes 393224 | tf_op jit(solution)/shard_map/ppermute | solution.py:533
  93.0 12.9 %collective-permute-start.11 = (bf16[512,128]{1,0:T(8,128)(2,1)S(1)}, bf16[512,128]{1,0:T(8,128)(2,1)S(1)}, u32[]{:S(2)}, u32[]{:S(2)}) collective-permute-start(bf16[512,128]{1,0:T(8,128)(2,1)S(1)} %pad_maximum_fusion.3), channel_id=1, source_target_pairs={{0,24},{8,16},{16,8},{24,0},{1,25},{9,17},{17,9},{25,1},{2,26},{10... | collective-permute-start | bytes 393224 | tf_op jit(solution)/shard_map/ppermute | solution.py:533
  (2 other events, 2.9 us)

commit v8 on v7

--- a/solution.py
+++ b/solution.py
@@ -11,7 +11,8 @@
 PAD = 8
 TAPS = 7
 MARGIN = 3
-BATCH = 32
+BATCH = 16
+BATCHES = 2
 SMALL = 8
 gelu_scale = 0.7978845608028654
 cubic_coef = 0.044715
@@ -255,11 +256,12 @@
             for copy in scalar_copies:
                 copy.wait()
 
-        units = fan * size // BATCH
+        unit = BATCH * BATCHES
+        units = fan * size // unit
 
         def add_unit(index, _):
-            first_cell = index * (BATCH // fan)
-            first_entry = step * (fan * size) + index * BATCH
+            first_cell = index * (unit // fan)
+            first_entry = step * (fan * size) + index * unit
 
             def add_batch(first, count):
                 found = []
@@ -275,7 +277,7 @@
 
                 @pl.when(clashing == level)
                 def _():
-                    for first in range(0, BATCH, count):
+                    for first in range(0, unit, count):
                         add_batch(first, count)
 
             return 0
@@ -333,7 +335,7 @@
         if distance < SMALL:
             twice = jnp.where(same & (lane % SMALL >= distance), 2, twice)
     distance = 1
-    while distance < BATCH:
+    while distance < BATCH * BATCHES:
         twice = jnp.maximum(twice, pltpu.roll(twice, row.shape[1] - distance, 1))
         distance *= 2
     clash[...] = twice
@@ -534,11 +536,12 @@
 
     total = jnp.concatenate([grads.reshape(2 * hid, channels), grad_dw], axis=0).astype(bf16)
     total = after(total, *first_sends)
-    total = total.reshape(devices, -1, channels)
-    total = lax.all_to_all(total, ("lat", "lon"), split_axis=0, concat_axis=0, tiled=True)
-    total = jnp.sum(total.astype(f32), axis=0, keepdims=True).astype(bf16)
-    total = jnp.broadcast_to(total, (devices,) + total.shape[1:])
-    total = lax.all_to_all(total, ("lat", "lon"), split_axis=0, concat_axis=0, tiled=True)
+    total = total.reshape(lon_count, -1, channels)
+    exchange = functools.partial(lax.all_to_all, split_axis=0, concat_axis=0, tiled=True)
+    spread = lambda x, count: jnp.broadcast_to(x, (count,) + x.shape)
+    total = jnp.sum(exchange(total, "lon").astype(f32), axis=0).astype(bf16)
+    total = jnp.sum(exchange(spread(total, lat_count), "lat").astype(f32), axis=0).astype(bf16)
+    total = exchange(spread(total, lon_count), "lon")
     scale = float(cells * devices) ** (-0.5)
     total = total.reshape(-1, channels).astype(f32) * scale
     grad_up = total[:hid].reshape(hid // channels, channels, channels)

time: 107 us -> 118 us (1.10)
  blocking collectives: 0 us -> 27.2 us
  waiting for transfers between devices: 21.3 us -> 15.1 us
  starting transfers between devices: 27.5 us -> 21.9 us
  Pallas kernels: 44.9 us -> 40.2 us
    all_to_all x0 -> x2, blocking collectives: none -> 27.2 us  [the longest x1 15.6 us: on_device(): total = jnp.sum(exchange(total, 'lon').astype(f32), axis=0).astype(bf16)]
    all_to_all x2 -> x1, starting transfers between devices: 10.2 us -> 3.42 us  [on_device(): total = exchange(spread(total, lon_count), 'lon')]
    pallas_call x1, Pallas kernels: 29.3 us -> 24.7 us  [on_device(): pl.pallas_call(block_kernel, out_shape=(shape((rows, cols, channels), bf1...]
    ppermute x5, waiting for transfers between devices: 9.41 us -> 5.13 us  [swap_bit(): return lax.ppermute(array, 'lon', pairs)]
    all_to_all x2 -> x1, waiting for transfers between devices: 4.75 us -> 2.02 us  [on_device(): total = exchange(spread(total, lon_count), 'lon')]
  transfers between devices with their start and end apart: 14 -> 13, of which waited for: 5 -> 5; matrix products, arithmetic and copies ran while one was open for 7% -> 5% of each run, Pallas kernels for 13% -> 11%
where the time goes in v8:
time: 118 us; the launch traced here: 117 us
  Pallas kernels  40.2 us (34%)
  blocking collectives  27.2 us (23%)
  starting transfers between devices  21.9 us (19%)
  waiting for transfers between devices  15.1 us (13%)
  other arithmetic  6.79 us (6%)
  local copies, waits for them, and re-layouts  4.6 us (4%)
    pallas_call x1, Pallas kernels, on_device(): pl.pallas_call(block_kernel, out_shape=(shape((rows, cols, channels), bf1...  24.7 us
    all_to_all x1, blocking collectives, on_device(): total = jnp.sum(exchange(total, 'lon').astype(f32), axis=0).astype(bf16)  15.6 us
    all_to_all x1, blocking collectives, on_device(): exchange(spread(total, lat_count), 'lat').astype(f32)  11.7 us
    ppermute x5, starting transfers between devices, swap_bit(): return lax.ppermute(array, 'lon', pairs)  6.59 us
    ppermute x3, waiting for transfers between devices, on_device(): lax.ppermute(for_band(distance).astype(bf16), 'lat', pairs)  6.47 us
    pallas_call x1, Pallas kernels, on_device(): pl.pallas_call(conv_grad_kernel, out_shape=shape((dw_rows, channels), f32...  6.17 us
    pallas_call x1, Pallas kernels, on_device(): pl.pallas_call(functools.partial(inner_conv_kernel, lat_count, lon_count,...  5.47 us
    ppermute x5, waiting for transfers between devices, swap_bit(): return lax.ppermute(array, 'lon', pairs)  5.13 us
  transfers between devices with their start and end apart: 13, of which 5 were waited for; matrix products, arithmetic and copies ran while one was open for 5% of the time, Pallas kernels for 11%

profile of v8, /device:TPU:0, one launch (start us, length us, event | category | flops | bytes accessed | tf_op | source)
XLA Modules:
  0.0 117.0 jit_solution(17817229308116981385)
XLA Ops:
  0.7 2.0 %edges.1 = (bf16[3,384,128]{2,1,0:T(8,128)(2,1)}, bf16[3,384,128]{2,1,0:T(8,128)(2,1)}) custom-call(bf16[8,384,128]{2,1,0:T(8,128)(2,1)} %state.6), custom_call_target="tpu_custom_call" | custom-call | flops 1000000000 | tf_op jit(solution)/shard_map/edges/pallas_call | solution.py:413
  2.7 3.3 %collective-permute-start.1 = (bf16[3,384,128]{2,1,0:T(8,128)(2,1)}, bf16[3,384,128]{2,1,0:T(8,128)(2,1)S(1)}, u32[]{:S(2)}, u32[]{:S(2)}) collective-permute-start(bf16[3,384,128]{2,1,0:T(8,128)(2,1)} %get-tuple-element.33), channel_id=1, source_target_pairs={{0,7},{1,6},{2,5},{3,4},{4,3},{5,2},{6,1},{7,0},{8,16},{9,17},{10,... | collective-permute-start | bytes 884744 | tf_op jit(solution)/shard_map/ppermute | solution.py:422
  6.1 1.3 %collective-permute-start = (bf16[3,384,128]{2,1,0:T(8,128)(2,1)}, bf16[3,384,128]{2,1,0:T(8,128)(2,1)S(1)}, u32[]{:S(2)}, u32[]{:S(2)}) collective-permute-start(bf16[3,384,128]{2,1,0:T(8,128)(2,1)} %get-tuple-element.32), channel_id=1, source_target_pairs={{0,8},{1,9},{2,10},{3,11},{4,12},{5,13},{6,14},{7,15},{8,0},{9,1},... | collective-permute-start | bytes 884744 | tf_op jit(solution)/shard_map/ppermute | solution.py:421
  7.4 5.5 %inner_conv.1 = (f32[8,384,128]{2,1,0:T(8,128)S(1)}, s32[48,128]{1,0:T(8,128)S(1)}, s32[48,128]{1,0:T(8,128)S(1)}) custom-call(bf16[8,384,128]{2,1,0:T(8,128)(2,1)S(1)} %copy-done.2, f32[49,128]{1,0:T(8,128)S(1)} %reshape.83.dw, f32[1,128]{1,0:T(1,128)S(1)} %bitcast.29, s32[48,128]{1,0:T(8,128)S(1)} %bitcast.25, s32[48,128]{1,0:T(8,128)S(1)} %bitcast.26), custom_call_target="tpu_custom_call" | custom-call | flops 7000000000 | tf_op jit(solution)/shard_map/inner_conv/pallas_call | solution.py:439
  12.9 1.2 %copy-done.16 = f32[8,384,128]{2,1,0:T(8,128)} copy-done((f32[8,384,128]{2,1,0:T(8,128)}, f32[8,384,128]{2,1,0:T(8,128)S(1)}, u32[]{:S(2)}) %copy-start.16) | copy-done | bytes 1572888
  14.4 1.5 %collective-permute-done = bf16[3,384,128]{2,1,0:T(8,128)(2,1)S(1)} collective-permute-done((bf16[3,384,128]{2,1,0:T(8,128)(2,1)}, bf16[3,384,128]{2,1,0:T(8,128)(2,1)S(1)}, u32[]{:S(2)}, u32[]{:S(2)}) %collective-permute-start) | collective-permute-done | bytes 294944 | tf_op jit(solution)/shard_map/ppermute | solution.py:421
  16.2 2.7 %collective-permute-start.3 = (bf16[14,3,128]{2,1,0:T(4,128)(2,1)S(1)}, bf16[14,3,128]{2,1,0:T(4,128)(2,1)S(1)}, u32[]{:S(2)}, u32[]{:S(2)}) collective-permute-start(bf16[14,3,128]{2,1,0:T(4,128)(2,1)S(1)} %pad_maximum_fusion.5), channel_id=1, source_target_pairs={{1,0},{2,1},{3,2},{4,3},{5,4},{6,5},{7,6},{0,7},{9,8},{10,9},{11,1... | collective-permute-start | bytes 32264 | tf_op jit(solution)/shard_map/ppermute | solution.py:430
  18.8 1.8 %halo_conv.1.halo = f32[6,384,128]{2,1,0:T(8,128)S(1)} custom-call(bf16[3,384,128]{2,1,0:T(8,128)(2,1)S(1)} %get-tuple-element.74.south, bf16[3,384,128]{2,1,0:T(8,128)(2,1)S(1)} %get-tuple-element.73.north, f32[49,128]{1,0:T(8,128)S(1)} %reshape.83.dw), custom_call_target="tpu_custom_call" | custom-call | flops 2000000000 | tf_op jit(solution)/shard_map/halo_conv/pallas_call | solution.py:451
  20.8 24.7 %block.1 = (bf16[8,384,128]{2,1,0:T(8,128)(2,1)}, f32[2048,128]{1,0:T(8,128)S(1)}, f32[2048,128]{1,0:T(8,128)S(1)}, f32[2048,128]{1,0:T(8,128)S(1)}, f32[2048,12...) custom-call(bf16[8,384,128]{2,1,0:T(8,128)(2,1)S(1)} %copy-done.2, ...), custom_call_target="tpu_custom_call" | custom-call | flops 28000000000 | tf_op jit(solution)/shard_map/block/pallas_call | solution.py:462
  45.6 6.2 %conv_grad.1 = f32[64,128]{1,0:T(8,128)S(1)} custom-call(bf16[8,384,128]{2,1,0:T(8,128)(2,1)S(1)} %copy-done.2, bf16[3,384,128]{2,1,0:T(8,128)(2,1)S(1)} %get-tuple-element.74.south, bf16[3,384,128]{2,1,0:T(8,128)(2,1)S(1)} %get-tuple-element.73.north, bf16[14,3,128]{2,1,0:T(4,128)(2,1)S(1)} %collective-permute-done.2.left, ...), custom_call_target="tpu_custom_call" | custom-call | flops 8999999488 | tf_op jit(solution)/shard_map/conv_grad/pallas_call | solution.py:500
  51.9 1.4 %add_convert_fusion = (bf16[2048,128]{1,0:T(8,128)(2,1)}, bf16[2048,128]{1,0:T(8,128)(2,1)}) fusion(f32[2048,128]{1,0:T(8,128)S(1)} %get-tuple-element.45, bf16[8192,128]{1,0:T(8,128)(2,1)S(1)} %collective-permute-done.4, f32[2048,128]{1,0:T(8,128)S(1)} %get-tuple-element.44), kind=kLoop, calls=%fused_computation | loop fusion | flops 1572864 | bytes 4194304 | tf_op jit(solution)/shard_map/convert_element_type | solution.py:515
  54.0 2.6 %collective-permute-start.5 = (bf16[2048,128]{1,0:T(8,128)(2,1)}, bf16[2048,128]{1,0:T(8,128)(2,1)S(1)}, u32[]{:S(2)}, u32[]{:S(2)}) collective-permute-start(bf16[2048,128]{1,0:T(8,128)(2,1)} %get-tuple-element.70), channel_id=1, source_target_pairs={{0,2},{1,3},{2,0},{3,1},{4,6},{5,7},{6,4},{7,5},{8,10},{9,11},{10,... | collective-permute-start | bytes 1572872 | tf_op jit(solution)/shard_map/ppermute | solution.py:377
  56.6 15.6 %all_to_all.15 = bf16[8,136,128]{2,1,0:T(8,128)(2,1)S(1)} all-to-all(bf16[8,136,128]{2,1,0:T(8,128)(2,1)S(1)} %bitcast.39), channel_id=1, replica_groups=mesh['lat'=4,'lon'=8] {'lon'}, dimensions={0} | all-to-all | bytes 557056 | tf_op jit(solution)/shard_map/all_to_all | solution.py:542
  72.3 11.7 %all_to_all.16 = bf16[4,136,128]{2,1,0:T(8,128)(2,1)S(1)} all-to-all(bf16[4,136,128]{2,1,0:T(8,128)(2,1)S(1)} %broadcast_in_dim.10), channel_id=1, replica_groups=mesh['lat'=4,'lon'=8] {'lat'}, dimensions={0} | all-to-all | bytes 278528 | tf_op jit(solution)/shard_map/all_to_all | solution.py:543
  84.0 0.7 broadcast_in_dim.11
  84.7 3.4 %all-to-all-start.2 = ((bf16[8,136,128]{2,1,0:T(8,128)(2,1)}), bf16[8,136,128]{2,1,0:T(8,128)(2,1)S(1)}, u32[]{:S(2)}, u32[]{:S(2)}) async-start(bf16[8,136,128]{2,1,0:T(8,128)(2,1)} %broadcast_in_dim.11), calls=%async_computation.2 | async-start | bytes 557056 | tf_op jit(solution)/shard_map/all_to_all | solution.py:544
  88.2 2.1 %add_convert_fusion.2 = (bf16[1024,128]{1,0:T(8,128)(2,1)}, bf16[1024,128]{1,0:T(8,128)(2,1)}) fusion(f32[2048,128]{1,0:T(8,128)S(1)} %get-tuple-element.47, bf16[2048,128]{1,0:T(8,128)(2,1)} %collective-permute-done.6, bf16[8192,128]{1,0:T(8,128)(2,1)} %copy-done.18, bf16[2048,128]{1,0:T(8,128)(2,1)S(1)} %collective-permute-done.5, ...), kind=kLoop, calls=%fused_computation.3 | loop fusion | flops 1310720 | bytes 2621440 | tf_op jit(solution)/shard_map/convert_element_type | solution.py:525
  90.2 1.9 %collective-permute-start.8 = (bf16[1024,128]{1,0:T(8,128)(2,1)}, bf16[1024,128]{1,0:T(8,128)(2,1)S(1)}, u32[]{:S(2)}, u32[]{:S(2)}) collective-permute-start(bf16[1024,128]{1,0:T(8,128)(2,1)} %get-tuple-element.67), channel_id=1, source_target_pairs={{0,2},{1,3},{2,0},{3,1},{4,6},{5,7},{6,4},{7,5},{8,10},{9,11},{10,... | collective-permute-start | bytes 786440 | tf_op jit(solution)/shard_map/ppermute | solution.py:377
  92.2 1.5 %collective-permute-start.7 = (bf16[1024,128]{1,0:T(8,128)(2,1)}, bf16[1024,128]{1,0:T(8,128)(2,1)S(1)}, u32[]{:S(2)}, u32[]{:S(2)}) collective-permute-start(bf16[1024,128]{1,0:T(8,128)(2,1)} %get-tuple-element.68), channel_id=1, source_target_pairs={{0,4},{1,5},{2,6},{3,7},{4,0},{5,1},{6,2},{7,3},{8,12},{9,13},{10,... | collective-permute-start | bytes 786440 | tf_op jit(solution)/shard_map/ppermute | solution.py:377
  93.6 2.0 %all-to-all-done.2 = bf16[8,136,128]{2,1,0:T(8,128)(2,1)S(1)} async-done(((bf16[8,136,128]{2,1,0:T(8,128)(2,1)}), bf16[8,136,128]{2,1,0:T(8,128)(2,1)S(1)}, u32[]{:S(2)}, u32[]{:S(2)}) %all-to-all-start.2) | async-done | bytes 278560 | tf_op jit(solution)/shard_map/all_to_all | solution.py:544
  95.7 4.2 %collective-permute-done.8 = bf16[1024,128]{1,0:T(8,128)(2,1)S(1)} collective-permute-done((bf16[1024,128]{1,0:T(8,128)(2,1)}, bf16[1024,128]{1,0:T(8,128)(2,1)S(1)}, u32[]{:S(2)}, u32[]{:S(2)}) %collective-permute-start.8) | collective-permute-done | bytes 262176 | tf_op jit(solution)/shard_map/ppermute | solution.py:377
  99.9 0.9 collective-permute-done.7
  100.8 1.2 %convert_add_fusion = (f32[256,128]{1,0:T(8,128)S(1)}, bf16[256,128]{1,0:T(8,128)(2,1)S(1)}, bf16[256,128]{1,0:T(8,128)(2,1)S(1)}, bf16[256,128]{1,0:T(8,128)(2,1)S(1)}) fusion(f32[2048,128]{1,0:T(8,128)S(1)} %get-tuple-element.47, bf16[1024,128]{1,0:T(8,128)(2,1)S(1)} %collective-permute-done.8, bf16[2048,128]{1,0:T(8,128)(2,1)} %collective-permute-done.6, ...), kind=kLoop, calls=%fused_computation.15 | loop fusion | flops 884736 | bytes 1638400 | tf_op jit(solution)/shard_map/add | solution.py:514
  102.0 1.1 convert_add_fusion.1
  103.1 0.7 collective-permute-start.9
  103.8 1.2 %collective-permute-start.10 = (bf16[512,128]{1,0:T(8,128)(2,1)S(1)}, bf16[512,128]{1,0:T(8,128)(2,1)S(1)}, u32[]{:S(2)}, u32[]{:S(2)}) collective-permute-start(bf16[512,128]{1,0:T(8,128)(2,1)S(1)} %pad_maximum_fusion.2), channel_id=1, source_target_pairs={{0,16},{8,24},{16,0},{24,8},{1,17},{9,25},{17,1},{25,9},{2,18},{10... | collective-permute-start | bytes 393224 | tf_op jit(solution)/shard_map/ppermute | solution.py:535
  105.0 2.7 %collective-permute-start.11 = (bf16[512,128]{1,0:T(8,128)(2,1)S(1)}, bf16[512,128]{1,0:T(8,128)(2,1)S(1)}, u32[]{:S(2)}, u32[]{:S(2)}) collective-permute-start(bf16[512,128]{1,0:T(8,128)(2,1)S(1)} %pad_maximum_fusion.3), channel_id=1, source_target_pairs={{0,24},{8,16},{16,8},{24,0},{1,25},{9,17},{17,9},{25,1},{2,26},{10... | collective-permute-start | bytes 393224 | tf_op jit(solution)/shard_map/ppermute | solution.py:535
  107.7 0.7 fusion.3
  108.4 0.7 copy.30
  109.2 0.6 reshape.80
  109.8 6.5 %collective-permute-done.10 = bf16[512,128]{1,0:T(8,128)(2,1)S(1)} collective-permute-done((bf16[512,128]{1,0:T(8,128)(2,1)S(1)}, bf16[512,128]{1,0:T(8,128)(2,1)S(1)}, u32[]{:S(2)}, u32[]{:S(2)}) %collective-permute-start.10) | collective-permute-done | bytes 131104 | tf_op jit(solution)/shard_map/ppermute | solution.py:535
  116.3 0.8 fusion.1
  (69 shorter events, 1.5 us)
Async XLA Ops:
  0.6 6.7 %copy-start.2 = (bf16[8,384,128]{2,1,0:T(8,128)(2,1)S(1)}, bf16[8,384,128]{2,1,0:T(8,128)(2,1)}, u32[]{:S(2)}) copy-start(bf16[8,384,128]{2,1,0:T(8,128)(2,1)} %state.6) | copy-start | bytes 2359300
  0.6 6.7 %copy-start.19 = (bf16[7,7,128]{2,1,0:T(8,128)(2,1)S(1)}, bf16[7,7,128]{2,1,0:T(8,128)(2,1)}, u32[]{:S(2)}) copy-start(bf16[7,7,128]{2,1,0:T(8,128)(2,1)} %param.21) | copy-start | bytes 37636
  0.7 6.7 %copy-start.6 = (s32[6144]{0:T(1024)S(1)}, s32[6144]{0:T(1024)}, u32[]{:S(2)}) copy-start(s32[6144]{0:T(1024)} %param.31) | copy-start | bytes 73732
  0.7 6.7 %copy-start.5 = (s32[6144,1]{0,1:T(1,128)S(1)}, s32[6144,1]{0,1:T(1,128)}, u32[]{:S(2)}) copy-start(s32[6144,1]{0,1:T(1,128)} %param.30) | copy-start | bytes 73732
  0.7 6.7 %copy-start.10 = (f32[128]{0:T(128)S(1)}, f32[128]{0:T(128)}, u32[]{:S(2)}) copy-start(f32[128]{0:T(128)} %param.22) | copy-start | bytes 1540
  2.7 11.6 %collective-permute-start.1 = (bf16[3,384,128]{2,1,0:T(8,128)(2,1)}, bf16[3,384,128]{2,1,0:T(8,128)(2,1)S(1)}, u32[]{:S(2)}, u32[]{:S(2)}) collective-permute-start(bf16[3,384,128]{2,1,0:T(8,128)(2,1)} %get-tuple-element.33), channel_id=1, source_target_pairs={{0,7},{1,6},{2,5},{3,4},{4,3},{5,2},{6,1},{7,0},{8,16},{9,17},{10,... | collective-permute-start | bytes 884744 | tf_op jit(solution)/shard_map/ppermute | solution.py:422
  6.1 9.8 %collective-permute-start = (bf16[3,384,128]{2,1,0:T(8,128)(2,1)}, bf16[3,384,128]{2,1,0:T(8,128)(2,1)S(1)}, u32[]{:S(2)}, u32[]{:S(2)}) collective-permute-start(bf16[3,384,128]{2,1,0:T(8,128)(2,1)} %get-tuple-element.32), channel_id=1, source_target_pairs={{0,8},{1,9},{2,10},{3,11},{4,12},{5,13},{6,14},{7,15},{8,0},{9,1},... | collective-permute-start | bytes 884744 | tf_op jit(solution)/shard_map/ppermute | solution.py:421
  7.4 6.7 %copy-start = (bf16[128,512]{1,0:T(8,128)(2,1)S(1)}, bf16[128,512]{1,0:T(8,128)(2,1)}, u32[]{:S(2)}) copy-start(bf16[128,512]{1,0:T(8,128)(2,1)} %up.1) | copy-start | bytes 393220
  7.4 6.8 %copy-start.1 = (bf16[512,128]{1,0:T(8,128)(2,1)S(1)}, bf16[512,128]{1,0:T(8,128)(2,1)}, u32[]{:S(2)}) copy-start(bf16[512,128]{1,0:T(8,128)(2,1)} %down.1) | copy-start | bytes 393220
  15.9 4.7 %collective-permute-start.2 = (bf16[14,3,128]{2,1,0:T(4,128)(2,1)S(1)}, bf16[14,3,128]{2,1,0:T(4,128)(2,1)S(1)}, u32[]{:S(2)}, u32[]{:S(2)}) collective-permute-start(bf16[14,3,128]{2,1,0:T(4,128)(2,1)S(1)} %pad_maximum_fusion.4), channel_id=1, source_target_pairs={{0,1},{1,2},{2,3},{3,4},{4,5},{5,6},{6,7},{7,0},{8,9},{9,10},{10,1... | collective-permute-start | bytes 32264 | tf_op jit(solution)/shard_map/ppermute | solution.py:429
  16.0 4.6 %copy-start.3 = (bf16[8,384,128]{2,1,0:T(8,128)(2,1)S(1)}, bf16[8,384,128]{2,1,0:T(8,128)(2,1)}, u32[]{:S(2)}) copy-start(bf16[8,384,128]{2,1,0:T(8,128)(2,1)} %forcing.1) | copy-start | bytes 2359300
  16.1 4.6 %copy-start.4 = (bf16[8,384,128]{2,1,0:T(8,128)(2,1)S(1)}, bf16[8,384,128]{2,1,0:T(8,128)(2,1)}, u32[]{:S(2)}) copy-start(bf16[8,384,128]{2,1,0:T(8,128)(2,1)} %cotangent.1) | copy-start | bytes 2359300
  16.1 4.6 %copy-start.7 = (s32[6144]{0:T(1024)S(1)}, s32[6144]{0:T(1024)}, u32[]{:S(2)}) copy-start(s32[6144]{0:T(1024)} %param.32) | copy-start | bytes 73732
  16.1 4.6 %copy-start.8 = (s32[8,384]{1,0:T(8,128)S(1)}, s32[8,384]{1,0:T(8,128)}, u32[]{:S(2)}) copy-start(s32[8,384]{1,0:T(8,128)} %land.1) | copy-start | bytes 36868
  16.1 4.6 %copy-start.9 = (f32[512]{0:T(512)S(1)}, f32[512]{0:T(512)}, u32[]{:S(2)}) copy-start(f32[512]{0:T(512)} %param.26) | copy-start | bytes 6148
  16.1 4.6 %copy-start.11 = (f32[16]{0:T(128)S(1)}, f32[16]{0:T(128)}, u32[]{:S(2)}) copy-start(f32[16]{0:T(128)} %weight_table.1) | copy-start | bytes 196
  16.1 4.6 %copy-start.12 = (f32[128]{0:T(128)S(1)}, f32[128]{0:T(128)}, u32[]{:S(2)}) copy-start(f32[128]{0:T(128)} %param.23) | copy-start | bytes 1540
  16.1 4.6 %copy-start.13 = (f32[128]{0:T(128)S(1)}, f32[128]{0:T(128)}, u32[]{:S(2)}) copy-start(f32[128]{0:T(128)} %param.24) | copy-start | bytes 1540
  16.1 4.6 %copy-start.14 = (f32[128]{0:T(128)S(1)}, f32[128]{0:T(128)}, u32[]{:S(2)}) copy-start(f32[128]{0:T(128)} %param.28) | copy-start | bytes 1540
  16.1 4.6 %copy-start.15 = (f32[128]{0:T(128)S(1)}, f32[128]{0:T(128)}, u32[]{:S(2)}) copy-start(f32[128]{0:T(128)} %param.29) | copy-start | bytes 1540
  16.2 4.6 %copy-start.17 = (f32[8,384,128]{2,1,0:T(8,128)S(1)}, f32[8,384,128]{2,1,0:T(8,128)}, u32[]{:S(2)}) copy-start(f32[8,384,128]{2,1,0:T(8,128)} %copy-done.16) | copy-start | bytes 4718596
  16.2 4.5 %collective-permute-start.3 = (bf16[14,3,128]{2,1,0:T(4,128)(2,1)S(1)}, bf16[14,3,128]{2,1,0:T(4,128)(2,1)S(1)}, u32[]{:S(2)}, u32[]{:S(2)}) collective-permute-start(bf16[14,3,128]{2,1,0:T(4,128)(2,1)S(1)} %pad_maximum_fusion.5), channel_id=1, source_target_pairs={{1,0},{2,1},{3,2},{4,3},{5,4},{6,5},{7,6},{0,7},{9,8},{10,9},{11,1... | collective-permute-start | bytes 32264 | tf_op jit(solution)/shard_map/ppermute | solution.py:430
  45.5 6.3 %collective-permute-start.4 = (bf16[8192,128]{1,0:T(8,128)(2,1)S(1)}, bf16[8192,128]{1,0:T(8,128)(2,1)S(1)}, u32[]{:S(2)}, u32[]{:S(2)}) collective-permute-start(bf16[8192,128]{1,0:T(8,128)(2,1)S(1)} %get-tuple-element.40), channel_id=1, source_target_pairs={{0,1},{1,0},{2,3},{3,2},{4,5},{5,4},{6,7},{7,6},{8,9},{9,8},{10,11... | collective-permute-start | bytes 6291464 | tf_op jit(solution)/shard_map/ppermute | solution.py:377
  51.9 1.7 %copy-start.18 = (bf16[8192,128]{1,0:T(8,128)(2,1)}, bf16[8192,128]{1,0:T(8,128)(2,1)S(1)}, u32[]{:S(2)}) copy-start(bf16[8192,128]{1,0:T(8,128)(2,1)S(1)} %collective-permute-done.4) | copy-start | bytes 6291460
  53.5 34.6 %collective-permute-start.6 = (bf16[2048,128]{1,0:T(8,128)(2,1)}, bf16[2048,128]{1,0:T(8,128)(2,1)}, u32[]{:S(2)}, u32[]{:S(2)}) collective-permute-start(bf16[2048,128]{1,0:T(8,128)(2,1)} %get-tuple-element.69), channel_id=1, source_target_pairs={{0,4},{1,5},{2,6},{3,7},{4,0},{5,1},{6,2},{7,3},{8,12},{9,13},{10,... | collective-permute-start | bytes 1572872 | tf_op jit(solution)/shard_map/ppermute | solution.py:377
  54.0 34.1 %collective-permute-start.5 = (bf16[2048,128]{1,0:T(8,128)(2,1)}, bf16[2048,128]{1,0:T(8,128)(2,1)S(1)}, u32[]{:S(2)}, u32[]{:S(2)}) collective-permute-start(bf16[2048,128]{1,0:T(8,128)(2,1)} %get-tuple-element.70), channel_id=1, source_target_pairs={{0,2},{1,3},{2,0},{3,1},{4,6},{5,7},{6,4},{7,5},{8,10},{9,11},{10,... | collective-permute-start | bytes 1572872 | tf_op jit(solution)/shard_map/ppermute | solution.py:377
  84.7 10.9 %all-to-all-start.2 = ((bf16[8,136,128]{2,1,0:T(8,128)(2,1)}), bf16[8,136,128]{2,1,0:T(8,128)(2,1)S(1)}, u32[]{:S(2)}, u32[]{:S(2)}) async-start(bf16[8,136,128]{2,1,0:T(8,128)(2,1)} %broadcast_in_dim.11), calls=%async_computation.2 | async-start | bytes 557056 | tf_op jit(solution)/shard_map/all_to_all | solution.py:544
  90.2 9.7 %collective-permute-start.8 = (bf16[1024,128]{1,0:T(8,128)(2,1)}, bf16[1024,128]{1,0:T(8,128)(2,1)S(1)}, u32[]{:S(2)}, u32[]{:S(2)}) collective-permute-start(bf16[1024,128]{1,0:T(8,128)(2,1)} %get-tuple-element.67), channel_id=1, source_target_pairs={{0,2},{1,3},{2,0},{3,1},{4,6},{5,7},{6,4},{7,5},{8,10},{9,11},{10,... | collective-permute-start | bytes 786440 | tf_op jit(solution)/shard_map/ppermute | solution.py:377
  92.2 8.7 %collective-permute-start.7 = (bf16[1024,128]{1,0:T(8,128)(2,1)}, bf16[1024,128]{1,0:T(8,128)(2,1)S(1)}, u32[]{:S(2)}, u32[]{:S(2)}) collective-permute-start(bf16[1024,128]{1,0:T(8,128)(2,1)} %get-tuple-element.68), channel_id=1, source_target_pairs={{0,4},{1,5},{2,6},{3,7},{4,0},{5,1},{6,2},{7,3},{8,12},{9,13},{10,... | collective-permute-start | bytes 786440 | tf_op jit(solution)/shard_map/ppermute | solution.py:377
  103.1 6.7 %collective-permute-start.9 = (bf16[512,128]{1,0:T(8,128)(2,1)S(1)}, bf16[512,128]{1,0:T(8,128)(2,1)S(1)}, u32[]{:S(2)}, u32[]{:S(2)}) collective-permute-start(bf16[512,128]{1,0:T(8,128)(2,1)S(1)} %pad_maximum_fusion.1), channel_id=1, source_target_pairs={{0,8},{8,0},{16,24},{24,16},{1,9},{9,1},{17,25},{25,17},{2,10},{10... | collective-permute-start | bytes 393224 | tf_op jit(solution)/shard_map/ppermute | solution.py:535
  103.8 12.5 %collective-permute-start.10 = (bf16[512,128]{1,0:T(8,128)(2,1)S(1)}, bf16[512,128]{1,0:T(8,128)(2,1)S(1)}, u32[]{:S(2)}, u32[]{:S(2)}) collective-permute-start(bf16[512,128]{1,0:T(8,128)(2,1)S(1)} %pad_maximum_fusion.2), channel_id=1, source_target_pairs={{0,16},{8,24},{16,0},{24,8},{1,17},{9,25},{17,1},{25,9},{2,18},{10... | collective-permute-start | bytes 393224 | tf_op jit(solution)/shard_map/ppermute | solution.py:535
  105.0 11.2 %collective-permute-start.11 = (bf16[512,128]{1,0:T(8,128)(2,1)S(1)}, bf16[512,128]{1,0:T(8,128)(2,1)S(1)}, u32[]{:S(2)}, u32[]{:S(2)}) collective-permute-start(bf16[512,128]{1,0:T(8,128)(2,1)S(1)} %pad_maximum_fusion.3), channel_id=1, source_target_pairs={{0,24},{8,16},{16,8},{24,0},{1,25},{9,17},{17,9},{25,1},{2,26},{10... | collective-permute-start | bytes 393224 | tf_op jit(solution)/shard_map/ppermute | solution.py:535
  (1 other events, 1.2 us)

commit v9 on v8

--- a/solution.py
+++ b/solution.py
@@ -14,6 +14,7 @@
 BATCH = 16
 BATCHES = 2
 SMALL = 8
+GROUP = 1
 gelu_scale = 0.7978845608028654
 cubic_coef = 0.044715
 f32 = jnp.float32
@@ -193,7 +194,7 @@
     entry_weights[...] = looked_up
     acc_up[...] = jnp.zeros_like(acc_up)
     acc_down[...] = jnp.zeros_like(acc_down)
-    group = 2
+    group = GROUP
     size = group * cols
     fan = terms.shape[0] // size
     lines = fan * size // channels
@@ -476,8 +477,8 @@
             pltpu.VMEM((channels, hid), f32),
             pltpu.VMEM((channels, hid), f32),
             pltpu.VMEM((entries // channels, channels), f32),
-            pltpu.VMEM((2 * fan * cols, channels), f32),
-            pltpu.VMEM((2 * fan * cols, channels), f32),
+            pltpu.VMEM((GROUP * fan * cols, channels), f32),
+            pltpu.VMEM((GROUP * fan * cols, channels), f32),
             pltpu.VMEM((2 * half_rows, channels), f32),
             pltpu.SMEM((entries,), jnp.int32),
             pltpu.SMEM((entries,), jnp.int32),
@@ -512,36 +513,41 @@
     got = after(got, grad_dw)
     slices = [(keep[k], got[k * size : (k + 1) * size]) for k in range(4)]
     add = lambda summands: functools.reduce(lambda x, y: x + y.astype(f32), summands)
+    exchange = functools.partial(lax.all_to_all, split_axis=0, concat_axis=0, tiled=True)
+    spread = lambda x, count: jnp.broadcast_to(x, (count,) + x.shape)
+    total = jnp.concatenate([grads.reshape(2 * hid, channels), grad_dw], axis=0).astype(bf16)
+    sum_first = lambda x: jnp.sum(x.astype(f32), axis=0).astype(bf16)
+    side_steps = [
+        lambda x: sum_first(exchange(x.reshape(lon_count, -1, channels), "lon")),
+        lambda x: sum_first(exchange(spread(x, lat_count), "lat")),
+    ]
     sends = [add(slices[1]).astype(bf16), add(slices[3]).astype(bf16)]
-    first_sends = sends
     held = [list(slices[0]), list(slices[2])]
     for stage in range(len(rest)):
         arrived = [swap_bit(sends[q], orders[q][stage]) for q in range(2)]
-        arrived = lax.optimization_barrier(tuple(arrived))
+        if stage < len(side_steps):
+            total = side_steps[stage](after(total, *sends))
+        *arrived, total = lax.optimization_barrier((*arrived, total))
         for q in range(2):
             held[q].append(arrived[q])
         if stage + 1 < len(rest):
             size //= 2
             sends = [add([h[size : 2 * size] for h in held[q]]).astype(bf16) for q in range(2)]
             held = [[h[:size] for h in held[q]] for q in range(2)]
+    for step in side_steps[len(rest) :]:
+        total = step(total)
+
     def for_band(distance):
         at = slice(distance * width, (distance + 1) * width)
         return jnp.concatenate([add([h[at] for h in held[q]]) for q in range(2)], axis=0)
 
     forcing_grad = for_band(0)
-    from_bands = []
-    for distance in range(1, lat_count):
-        pairs = [(i, i ^ distance) for i in range(lat_count)]
-        from_bands.append(lax.ppermute(for_band(distance).astype(bf16), "lat", pairs))
-
-    total = jnp.concatenate([grads.reshape(2 * hid, channels), grad_dw], axis=0).astype(bf16)
-    total = after(total, *first_sends)
-    total = total.reshape(lon_count, -1, channels)
-    exchange = functools.partial(lax.all_to_all, split_axis=0, concat_axis=0, tiled=True)
-    spread = lambda x, count: jnp.broadcast_to(x, (count,) + x.shape)
-    total = jnp.sum(exchange(total, "lon").astype(f32), axis=0).astype(bf16)
-    total = jnp.sum(exchange(spread(total, lat_count), "lat").astype(f32), axis=0).astype(bf16)
-    total = exchange(spread(total, lon_count), "lon")
+    sends = [for_band(distance).astype(bf16) for distance in range(1, lat_count)]
+    from_bands = [
+        lax.ppermute(sends[distance - 1], "lat", [(i, i ^ distance) for i in range(lat_count)])
+        for distance in range(1, lat_count)
+    ]
+    total = exchange(spread(after(total, *sends), lon_count), "lon")
     scale = float(cells * devices) ** (-0.5)
     total = total.reshape(-1, channels).astype(f32) * scale
     grad_up = total[:hid].reshape(hid // channels, channels, channels)

time: 118 us -> 110 us (0.932)
  waiting for transfers between devices: 15.1 us -> 8.51 us
    ppermute x5, waiting for transfers between devices: 5.13 us -> 0.01 us  [swap_bit(): return lax.ppermute(array, 'lon', pairs)]
    ppermute x3, waiting for transfers between devices: 6.47 us -> 4.41 us  [on_device(): lax.ppermute(sends[distance - 1], 'lat', [(i, i ^ distance) for i in rang...]
  transfers between devices with their start and end apart: 13 -> 13, of which waited for: 5 -> 3; matrix products, arithmetic and copies ran while one was open for 5% -> 2% of each run, Pallas kernels for 11% -> 12%
where the time goes in v9:
time: 110 us; the launch traced here: 109 us
  Pallas kernels  40.4 us (37%)
  blocking collectives  27.1 us (25%)
  starting transfers between devices  21.2 us (19%)
  waiting for transfers between devices  8.51 us (8%)
  other arithmetic  6.22 us (6%)
  local copies, waits for them, and re-layouts  4.61 us (4%)
  between operations  1.17 us (1%)
    pallas_call x1, Pallas kernels, on_device(): pl.pallas_call(block_kernel, out_shape=(shape((rows, cols, channels), bf1...  25 us
    all_to_all x1, blocking collectives, on_device(): exchange(x.reshape(lon_count, -1, channels), 'lon')  15.4 us
    all_to_all x1, blocking collectives, on_device(): exchange(spread(x, lat_count), 'lat')  11.7 us
    pallas_call x1, Pallas kernels, on_device(): pl.pallas_call(conv_grad_kernel, out_shape=shape((dw_rows, channels), f32...  6.17 us
    ppermute x5, starting transfers between devices, swap_bit(): return lax.ppermute(array, 'lon', pairs)  6.01 us
    pallas_call x1, Pallas kernels, on_device(): pl.pallas_call(functools.partial(inner_conv_kernel, lat_count, lon_count,...  5.47 us
    ppermute x3, starting transfers between devices, on_device(): lax.ppermute(sends[distance - 1], 'lat', [(i, i ^ distance) for i in rang...  4.45 us
    ppermute x3, waiting for transfers between devices, on_device(): lax.ppermute(sends[distance - 1], 'lat', [(i, i ^ distance) for i in rang...  4.41 us
  transfers between devices with their start and end apart: 13, of which 3 were waited for; matrix products, arithmetic and copies ran while one was open for 2% of the time, Pallas kernels for 12%

profile of v9, /device:TPU:0, one launch (start us, length us, event | category | flops | bytes accessed | tf_op | source)
XLA Modules:
  0.0 109.3 jit_solution(342689510670315123)
XLA Ops:
  0.7 2.0 %edges.1 = (bf16[3,384,128]{2,1,0:T(8,128)(2,1)}, bf16[3,384,128]{2,1,0:T(8,128)(2,1)}) custom-call(bf16[8,384,128]{2,1,0:T(8,128)(2,1)} %state.6), custom_call_target="tpu_custom_call" | custom-call | flops 1000000000 | tf_op jit(solution)/shard_map/edges/pallas_call | solution.py:414
  2.7 3.3 %collective-permute-start.1 = (bf16[3,384,128]{2,1,0:T(8,128)(2,1)}, bf16[3,384,128]{2,1,0:T(8,128)(2,1)S(1)}, u32[]{:S(2)}, u32[]{:S(2)}) collective-permute-start(bf16[3,384,128]{2,1,0:T(8,128)(2,1)} %get-tuple-element.37), channel_id=1, source_target_pairs={{0,7},{1,6},{2,5},{3,4},{4,3},{5,2},{6,1},{7,0},{8,16},{9,17},{10,... | collective-permute-start | bytes 884744 | tf_op jit(solution)/shard_map/ppermute | solution.py:423
  6.1 1.3 %collective-permute-start = (bf16[3,384,128]{2,1,0:T(8,128)(2,1)}, bf16[3,384,128]{2,1,0:T(8,128)(2,1)S(1)}, u32[]{:S(2)}, u32[]{:S(2)}) collective-permute-start(bf16[3,384,128]{2,1,0:T(8,128)(2,1)} %get-tuple-element.36), channel_id=1, source_target_pairs={{0,8},{1,9},{2,10},{3,11},{4,12},{5,13},{6,14},{7,15},{8,0},{9,1},... | collective-permute-start | bytes 884744 | tf_op jit(solution)/shard_map/ppermute | solution.py:422
  7.4 5.5 %inner_conv.1 = (f32[8,384,128]{2,1,0:T(8,128)S(1)}, s32[48,128]{1,0:T(8,128)S(1)}, s32[48,128]{1,0:T(8,128)S(1)}) custom-call(bf16[8,384,128]{2,1,0:T(8,128)(2,1)S(1)} %copy-done.2, f32[49,128]{1,0:T(8,128)S(1)} %reshape.83.dw, f32[1,128]{1,0:T(1,128)S(1)} %bitcast.29, s32[48,128]{1,0:T(8,128)S(1)} %bitcast.25, s32[48,128]{1,0:T(8,128)S(1)} %bitcast.26), custom_call_target="tpu_custom_call" | custom-call | flops 7000000000 | tf_op jit(solution)/shard_map/inner_conv/pallas_call | solution.py:440
  12.9 1.2 %copy-done.16 = f32[8,384,128]{2,1,0:T(8,128)} copy-done((f32[8,384,128]{2,1,0:T(8,128)}, f32[8,384,128]{2,1,0:T(8,128)S(1)}, u32[]{:S(2)}) %copy-start.16) | copy-done | bytes 1572888
  14.4 1.5 %collective-permute-done = bf16[3,384,128]{2,1,0:T(8,128)(2,1)S(1)} collective-permute-done((bf16[3,384,128]{2,1,0:T(8,128)(2,1)}, bf16[3,384,128]{2,1,0:T(8,128)(2,1)S(1)}, u32[]{:S(2)}, u32[]{:S(2)}) %collective-permute-start) | collective-permute-done | bytes 294944 | tf_op jit(solution)/shard_map/ppermute | solution.py:422
  16.2 2.7 %collective-permute-start.3 = (bf16[14,3,128]{2,1,0:T(4,128)(2,1)S(1)}, bf16[14,3,128]{2,1,0:T(4,128)(2,1)S(1)}, u32[]{:S(2)}, u32[]{:S(2)}) collective-permute-start(bf16[14,3,128]{2,1,0:T(4,128)(2,1)S(1)} %pad_maximum_fusion.5), channel_id=1, source_target_pairs={{1,0},{2,1},{3,2},{4,3},{5,4},{6,5},{7,6},{0,7},{9,8},{10,9},{11,1... | collective-permute-start | bytes 32264 | tf_op jit(solution)/shard_map/ppermute | solution.py:431
  18.8 1.8 %halo_conv.1.halo = f32[6,384,128]{2,1,0:T(8,128)S(1)} custom-call(bf16[3,384,128]{2,1,0:T(8,128)(2,1)S(1)} %get-tuple-element.82.south, bf16[3,384,128]{2,1,0:T(8,128)(2,1)S(1)} %get-tuple-element.81.north, f32[49,128]{1,0:T(8,128)S(1)} %reshape.83.dw), custom_call_target="tpu_custom_call" | custom-call | flops 2000000000 | tf_op jit(solution)/shard_map/halo_conv/pallas_call | solution.py:452
  20.8 25.0 %block.1 = (bf16[8,384,128]{2,1,0:T(8,128)(2,1)}, f32[2048,128]{1,0:T(8,128)S(1)}, f32[2048,128]{1,0:T(8,128)S(1)}, f32[2048,128]{1,0:T(8,128)S(1)}, f32[2048,12...) custom-call(bf16[8,384,128]{2,1,0:T(8,128)(2,1)S(1)} %copy-done.2, ...), custom_call_target="tpu_custom_call" | custom-call | flops 28000000000 | tf_op jit(solution)/shard_map/block/pallas_call | solution.py:463
  45.8 6.2 %conv_grad.1 = f32[64,128]{1,0:T(8,128)S(1)} custom-call(bf16[8,384,128]{2,1,0:T(8,128)(2,1)S(1)} %copy-done.2, bf16[3,384,128]{2,1,0:T(8,128)(2,1)S(1)} %get-tuple-element.82.south, bf16[3,384,128]{2,1,0:T(8,128)(2,1)S(1)} %get-tuple-element.81.north, bf16[14,3,128]{2,1,0:T(4,128)(2,1)S(1)} %collective-permute-done.2.left, ...), custom_call_target="tpu_custom_call" | custom-call | flops 8999999488 | tf_op jit(solution)/shard_map/conv_grad/pallas_call | solution.py:501
  52.0 1.4 %add_convert_fusion = (bf16[2048,128]{1,0:T(8,128)(2,1)}, bf16[2048,128]{1,0:T(8,128)(2,1)}) fusion(f32[2048,128]{1,0:T(8,128)S(1)} %get-tuple-element.49, bf16[8192,128]{1,0:T(8,128)(2,1)S(1)} %collective-permute-done.4, f32[2048,128]{1,0:T(8,128)S(1)} %get-tuple-element.48), kind=kLoop, calls=%fused_computation | loop fusion | flops 1572864 | bytes 4194304 | tf_op jit(solution)/shard_map/convert_element_type | solution.py:524
  53.5 0.2 copy-done.18
  53.7 0.5 collective-permute-start.6
  54.2 2.7 %collective-permute-start.5 = (bf16[2048,128]{1,0:T(8,128)(2,1)}, bf16[2048,128]{1,0:T(8,128)(2,1)}, u32[]{:S(2)}, u32[]{:S(2)}) collective-permute-start(bf16[2048,128]{1,0:T(8,128)(2,1)} %get-tuple-element.78), channel_id=1, source_target_pairs={{0,2},{1,3},{2,0},{3,1},{4,6},{5,7},{6,4},{7,5},{8,10},{9,11},{10,... | collective-permute-start | bytes 1572872 | tf_op jit(solution)/shard_map/ppermute | solution.py:378
  56.9 15.4 %all_to_all.15 = bf16[8,136,128]{2,1,0:T(8,128)(2,1)S(1)} all-to-all(bf16[8,136,128]{2,1,0:T(8,128)(2,1)S(1)} %bitcast.39), channel_id=1, replica_groups=mesh['lat'=4,'lon'=8] {'lon'}, dimensions={0} | all-to-all | bytes 557056 | tf_op jit(solution)/shard_map/all_to_all | solution.py:521
  72.4 1.4 %add_convert_fusion.2 = (bf16[1024,128]{1,0:T(8,128)(2,1)S(1)}, bf16[1024,128]{1,0:T(8,128)(2,1)S(1)}) fusion(f32[2048,128]{1,0:T(8,128)S(1)} %get-tuple-element.53, bf16[2048,128]{1,0:T(8,128)(2,1)} %collective-permute-done.6, bf16[8192,128]{1,0:T(8,128)(2,1)} %copy-done.18, bf16[2048,128]{1,0:T(8,128)(2,1)} %collective-permute-done.5, ...), kind=kLoop, calls=%fused_computation.3 | loop fusion | flops 1310720 | bytes 2621440 | tf_op jit(solution)/shard_map/convert_element_type | solution.py:535
  73.8 1.3 %collective-permute-start.8 = (bf16[1024,128]{1,0:T(8,128)(2,1)S(1)}, bf16[1024,128]{1,0:T(8,128)(2,1)S(1)}, u32[]{:S(2)}, u32[]{:S(2)}) collective-permute-start(bf16[1024,128]{1,0:T(8,128)(2,1)S(1)} %get-tuple-element.75), channel_id=1, source_target_pairs={{0,2},{1,3},{2,0},{3,1},{4,6},{5,7},{6,4},{7,5},{8,10},{9,11},{10,... | collective-permute-start | bytes 786440 | tf_op jit(solution)/shard_map/ppermute | solution.py:378
  75.1 1.4 %collective-permute-start.7 = (bf16[1024,128]{1,0:T(8,128)(2,1)S(1)}, bf16[1024,128]{1,0:T(8,128)(2,1)S(1)}, u32[]{:S(2)}, u32[]{:S(2)}) collective-permute-start(bf16[1024,128]{1,0:T(8,128)(2,1)S(1)} %get-tuple-element.76), channel_id=1, source_target_pairs={{0,4},{1,5},{2,6},{3,7},{4,0},{5,1},{6,2},{7,3},{8,12},{9,13},{10,... | collective-permute-start | bytes 786440 | tf_op jit(solution)/shard_map/ppermute | solution.py:378
  76.6 11.7 %all_to_all.16 = bf16[4,136,128]{2,1,0:T(8,128)(2,1)S(1)} all-to-all(bf16[4,136,128]{2,1,0:T(8,128)(2,1)S(1)} %broadcast_in_dim.10), channel_id=1, replica_groups=mesh['lat'=4,'lon'=8] {'lat'}, dimensions={0} | all-to-all | bytes 278528 | tf_op jit(solution)/shard_map/all_to_all | solution.py:522
  88.3 1.2 %convert_add_fusion = (f32[256,128]{1,0:T(8,128)S(1)}, bf16[256,128]{1,0:T(8,128)(2,1)S(1)}, bf16[256,128]{1,0:T(8,128)(2,1)S(1)}, bf16[256,128]{1,0:T(8,128)(2,1)S(1)}) fusion(f32[2048,128]{1,0:T(8,128)S(1)} %get-tuple-element.53, bf16[1024,128]{1,0:T(8,128)(2,1)S(1)} %collective-permute-done.8, bf16[2048,128]{1,0:T(8,128)(2,1)} %collective-permute-done.6, ...), kind=kLoop, calls=%fused_computation.15 | loop fusion | flops 884736 | bytes 1638400 | tf_op jit(solution)/shard_map/add | solution.py:515
  89.5 1.2 %convert_add_fusion.1 = (f32[256,128]{1,0:T(8,128)S(1)}, bf16[256,128]{1,0:T(8,128)(2,1)S(1)}, bf16[256,128]{1,0:T(8,128)(2,1)S(1)}, bf16[256,128]{1,0:T(8,128)(2,1)S(1)}) fusion(f32[2048,128]{1,0:T(8,128)S(1)} %get-tuple-element.43, bf16[1024,128]{1,0:T(8,128)(2,1)S(1)} %collective-permute-done.7, bf16[2048,128]{1,0:T(8,128)(2,1)} %collective-permute-done.5, ...), kind=kLoop, calls=%fused_computation.16 | loop fusion | flops 884736 | bytes 1638400 | tf_op jit(solution)/shard_map/add | solution.py:515
  90.7 0.7 broadcast_in_dim.11
  91.5 3.4 %all-to-all-start.2 = ((bf16[8,136,128]{2,1,0:T(8,128)(2,1)}), bf16[8,136,128]{2,1,0:T(8,128)(2,1)S(1)}, u32[]{:S(2)}, u32[]{:S(2)}) async-start(bf16[8,136,128]{2,1,0:T(8,128)(2,1)} %broadcast_in_dim.11), calls=%async_computation.2 | async-start | bytes 557056 | tf_op jit(solution)/shard_map/all_to_all | solution.py:550
  94.9 0.7 collective-permute-start.9
  95.6 0.7 collective-permute-start.10
  96.3 3.1 %collective-permute-start.11 = (bf16[512,128]{1,0:T(8,128)(2,1)S(1)}, bf16[512,128]{1,0:T(8,128)(2,1)S(1)}, u32[]{:S(2)}, u32[]{:S(2)}) collective-permute-start(bf16[512,128]{1,0:T(8,128)(2,1)S(1)} %pad_maximum_fusion.3), channel_id=1, source_target_pairs={{0,24},{8,16},{16,8},{24,0},{1,25},{9,17},{17,9},{25,1},{2,26},{10... | collective-permute-start | bytes 393224 | tf_op jit(solution)/shard_map/ppermute | solution.py:547
  99.4 2.6 %all-to-all-done.2 = bf16[8,136,128]{2,1,0:T(8,128)(2,1)S(1)} async-done(((bf16[8,136,128]{2,1,0:T(8,128)(2,1)}), bf16[8,136,128]{2,1,0:T(8,128)(2,1)S(1)}, u32[]{:S(2)}, u32[]{:S(2)}) %all-to-all-start.2) | async-done | bytes 278560 | tf_op jit(solution)/shard_map/all_to_all | solution.py:550
  102.0 0.7 fusion.3
  102.8 0.7 copy.30
  103.5 0.6 reshape.80
  104.1 4.4 %collective-permute-done.10 = bf16[512,128]{1,0:T(8,128)(2,1)S(1)} collective-permute-done((bf16[512,128]{1,0:T(8,128)(2,1)S(1)}, bf16[512,128]{1,0:T(8,128)(2,1)S(1)}, u32[]{:S(2)}, u32[]{:S(2)}) %collective-permute-start.10) | collective-permute-done | bytes 131104 | tf_op jit(solution)/shard_map/ppermute | solution.py:547
  108.5 0.8 fusion.1
  (69 shorter events, 0.8 us)
Async XLA Ops:
  0.6 6.7 %copy-start.2 = (bf16[8,384,128]{2,1,0:T(8,128)(2,1)S(1)}, bf16[8,384,128]{2,1,0:T(8,128)(2,1)}, u32[]{:S(2)}) copy-start(bf16[8,384,128]{2,1,0:T(8,128)(2,1)} %state.6) | copy-start | bytes 2359300
  0.6 6.7 %copy-start.19 = (bf16[7,7,128]{2,1,0:T(8,128)(2,1)S(1)}, bf16[7,7,128]{2,1,0:T(8,128)(2,1)}, u32[]{:S(2)}) copy-start(bf16[7,7,128]{2,1,0:T(8,128)(2,1)} %param.21) | copy-start | bytes 37636
  0.7 6.7 %copy-start.6 = (s32[6144]{0:T(1024)S(1)}, s32[6144]{0:T(1024)}, u32[]{:S(2)}) copy-start(s32[6144]{0:T(1024)} %param.31) | copy-start | bytes 73732
  0.7 6.7 %copy-start.5 = (s32[6144,1]{0,1:T(1,128)S(1)}, s32[6144,1]{0,1:T(1,128)}, u32[]{:S(2)}) copy-start(s32[6144,1]{0,1:T(1,128)} %param.30) | copy-start | bytes 73732
  0.7 6.7 %copy-start.10 = (f32[128]{0:T(128)S(1)}, f32[128]{0:T(128)}, u32[]{:S(2)}) copy-start(f32[128]{0:T(128)} %param.22) | copy-start | bytes 1540
  2.7 11.6 %collective-permute-start.1 = (bf16[3,384,128]{2,1,0:T(8,128)(2,1)}, bf16[3,384,128]{2,1,0:T(8,128)(2,1)S(1)}, u32[]{:S(2)}, u32[]{:S(2)}) collective-permute-start(bf16[3,384,128]{2,1,0:T(8,128)(2,1)} %get-tuple-element.37), channel_id=1, source_target_pairs={{0,7},{1,6},{2,5},{3,4},{4,3},{5,2},{6,1},{7,0},{8,16},{9,17},{10,... | collective-permute-start | bytes 884744 | tf_op jit(solution)/shard_map/ppermute | solution.py:423
  6.1 9.8 %collective-permute-start = (bf16[3,384,128]{2,1,0:T(8,128)(2,1)}, bf16[3,384,128]{2,1,0:T(8,128)(2,1)S(1)}, u32[]{:S(2)}, u32[]{:S(2)}) collective-permute-start(bf16[3,384,128]{2,1,0:T(8,128)(2,1)} %get-tuple-element.36), channel_id=1, source_target_pairs={{0,8},{1,9},{2,10},{3,11},{4,12},{5,13},{6,14},{7,15},{8,0},{9,1},... | collective-permute-start | bytes 884744 | tf_op jit(solution)/shard_map/ppermute | solution.py:422
  7.4 6.7 %copy-start = (bf16[128,512]{1,0:T(8,128)(2,1)S(1)}, bf16[128,512]{1,0:T(8,128)(2,1)}, u32[]{:S(2)}) copy-start(bf16[128,512]{1,0:T(8,128)(2,1)} %up.1) | copy-start | bytes 393220
  7.4 6.8 %copy-start.1 = (bf16[512,128]{1,0:T(8,128)(2,1)S(1)}, bf16[512,128]{1,0:T(8,128)(2,1)}, u32[]{:S(2)}) copy-start(bf16[512,128]{1,0:T(8,128)(2,1)} %down.1) | copy-start | bytes 393220
  15.9 4.7 %collective-permute-start.2 = (bf16[14,3,128]{2,1,0:T(4,128)(2,1)S(1)}, bf16[14,3,128]{2,1,0:T(4,128)(2,1)S(1)}, u32[]{:S(2)}, u32[]{:S(2)}) collective-permute-start(bf16[14,3,128]{2,1,0:T(4,128)(2,1)S(1)} %pad_maximum_fusion.4), channel_id=1, source_target_pairs={{0,1},{1,2},{2,3},{3,4},{4,5},{5,6},{6,7},{7,0},{8,9},{9,10},{10,1... | collective-permute-start | bytes 32264 | tf_op jit(solution)/shard_map/ppermute | solution.py:430
  16.0 4.6 %copy-start.3 = (bf16[8,384,128]{2,1,0:T(8,128)(2,1)S(1)}, bf16[8,384,128]{2,1,0:T(8,128)(2,1)}, u32[]{:S(2)}) copy-start(bf16[8,384,128]{2,1,0:T(8,128)(2,1)} %forcing.1) | copy-start | bytes 2359300
  16.1 4.6 %copy-start.4 = (bf16[8,384,128]{2,1,0:T(8,128)(2,1)S(1)}, bf16[8,384,128]{2,1,0:T(8,128)(2,1)}, u32[]{:S(2)}) copy-start(bf16[8,384,128]{2,1,0:T(8,128)(2,1)} %cotangent.1) | copy-start | bytes 2359300
  16.1 4.6 %copy-start.7 = (s32[6144]{0:T(1024)S(1)}, s32[6144]{0:T(1024)}, u32[]{:S(2)}) copy-start(s32[6144]{0:T(1024)} %param.32) | copy-start | bytes 73732
  16.1 4.6 %copy-start.8 = (s32[8,384]{1,0:T(8,128)S(1)}, s32[8,384]{1,0:T(8,128)}, u32[]{:S(2)}) copy-start(s32[8,384]{1,0:T(8,128)} %land.1) | copy-start | bytes 36868
  16.1 4.6 %copy-start.9 = (f32[512]{0:T(512)S(1)}, f32[512]{0:T(512)}, u32[]{:S(2)}) copy-start(f32[512]{0:T(512)} %param.26) | copy-start | bytes 6148
  16.1 4.6 %copy-start.11 = (f32[16]{0:T(128)S(1)}, f32[16]{0:T(128)}, u32[]{:S(2)}) copy-start(f32[16]{0:T(128)} %weight_table.1) | copy-start | bytes 196
  16.1 4.6 %copy-start.12 = (f32[128]{0:T(128)S(1)}, f32[128]{0:T(128)}, u32[]{:S(2)}) copy-start(f32[128]{0:T(128)} %param.23) | copy-start | bytes 1540
  16.1 4.6 %copy-start.13 = (f32[128]{0:T(128)S(1)}, f32[128]{0:T(128)}, u32[]{:S(2)}) copy-start(f32[128]{0:T(128)} %param.24) | copy-start | bytes 1540
  16.1 4.6 %copy-start.14 = (f32[128]{0:T(128)S(1)}, f32[128]{0:T(128)}, u32[]{:S(2)}) copy-start(f32[128]{0:T(128)} %param.28) | copy-start | bytes 1540
  16.1 4.6 %copy-start.15 = (f32[128]{0:T(128)S(1)}, f32[128]{0:T(128)}, u32[]{:S(2)}) copy-start(f32[128]{0:T(128)} %param.29) | copy-start | bytes 1540
  16.2 4.6 %copy-start.17 = (f32[8,384,128]{2,1,0:T(8,128)S(1)}, f32[8,384,128]{2,1,0:T(8,128)}, u32[]{:S(2)}) copy-start(f32[8,384,128]{2,1,0:T(8,128)} %copy-done.16) | copy-start | bytes 4718596
  16.2 4.5 %collective-permute-start.3 = (bf16[14,3,128]{2,1,0:T(4,128)(2,1)S(1)}, bf16[14,3,128]{2,1,0:T(4,128)(2,1)S(1)}, u32[]{:S(2)}, u32[]{:S(2)}) collective-permute-start(bf16[14,3,128]{2,1,0:T(4,128)(2,1)S(1)} %pad_maximum_fusion.5), channel_id=1, source_target_pairs={{1,0},{2,1},{3,2},{4,3},{5,4},{6,5},{7,6},{0,7},{9,8},{10,9},{11,1... | collective-permute-start | bytes 32264 | tf_op jit(solution)/shard_map/ppermute | solution.py:431
  45.7 6.3 %collective-permute-start.4 = (bf16[8192,128]{1,0:T(8,128)(2,1)S(1)}, bf16[8192,128]{1,0:T(8,128)(2,1)S(1)}, u32[]{:S(2)}, u32[]{:S(2)}) collective-permute-start(bf16[8192,128]{1,0:T(8,128)(2,1)S(1)} %get-tuple-element.44), channel_id=1, source_target_pairs={{0,1},{1,0},{2,3},{3,2},{4,5},{5,4},{6,7},{7,6},{8,9},{9,8},{10,11... | collective-permute-start | bytes 6291464 | tf_op jit(solution)/shard_map/ppermute | solution.py:378
  52.0 1.7 %copy-start.18 = (bf16[8192,128]{1,0:T(8,128)(2,1)}, bf16[8192,128]{1,0:T(8,128)(2,1)S(1)}, u32[]{:S(2)}) copy-start(bf16[8192,128]{1,0:T(8,128)(2,1)S(1)} %collective-permute-done.4) | copy-start | bytes 6291460
  53.7 18.7 %collective-permute-start.6 = (bf16[2048,128]{1,0:T(8,128)(2,1)}, bf16[2048,128]{1,0:T(8,128)(2,1)}, u32[]{:S(2)}, u32[]{:S(2)}) collective-permute-start(bf16[2048,128]{1,0:T(8,128)(2,1)} %get-tuple-element.77), channel_id=1, source_target_pairs={{0,4},{1,5},{2,6},{3,7},{4,0},{5,1},{6,2},{7,3},{8,12},{9,13},{10,... | collective-permute-start | bytes 1572872 | tf_op jit(solution)/shard_map/ppermute | solution.py:378
  54.2 18.3 %collective-permute-start.5 = (bf16[2048,128]{1,0:T(8,128)(2,1)}, bf16[2048,128]{1,0:T(8,128)(2,1)}, u32[]{:S(2)}, u32[]{:S(2)}) collective-permute-start(bf16[2048,128]{1,0:T(8,128)(2,1)} %get-tuple-element.78), channel_id=1, source_target_pairs={{0,2},{1,3},{2,0},{3,1},{4,6},{5,7},{6,4},{7,5},{8,10},{9,11},{10,... | collective-permute-start | bytes 1572872 | tf_op jit(solution)/shard_map/ppermute | solution.py:378
  73.8 14.5 %collective-permute-start.8 = (bf16[1024,128]{1,0:T(8,128)(2,1)S(1)}, bf16[1024,128]{1,0:T(8,128)(2,1)S(1)}, u32[]{:S(2)}, u32[]{:S(2)}) collective-permute-start(bf16[1024,128]{1,0:T(8,128)(2,1)S(1)} %get-tuple-element.75), channel_id=1, source_target_pairs={{0,2},{1,3},{2,0},{3,1},{4,6},{5,7},{6,4},{7,5},{8,10},{9,11},{10,... | collective-permute-start | bytes 786440 | tf_op jit(solution)/shard_map/ppermute | solution.py:378
  75.1 13.2 %collective-permute-start.7 = (bf16[1024,128]{1,0:T(8,128)(2,1)S(1)}, bf16[1024,128]{1,0:T(8,128)(2,1)S(1)}, u32[]{:S(2)}, u32[]{:S(2)}) collective-permute-start(bf16[1024,128]{1,0:T(8,128)(2,1)S(1)} %get-tuple-element.76), channel_id=1, source_target_pairs={{0,4},{1,5},{2,6},{3,7},{4,0},{5,1},{6,2},{7,3},{8,12},{9,13},{10,... | collective-permute-start | bytes 786440 | tf_op jit(solution)/shard_map/ppermute | solution.py:378
  91.5 10.5 %all-to-all-start.2 = ((bf16[8,136,128]{2,1,0:T(8,128)(2,1)}), bf16[8,136,128]{2,1,0:T(8,128)(2,1)S(1)}, u32[]{:S(2)}, u32[]{:S(2)}) async-start(bf16[8,136,128]{2,1,0:T(8,128)(2,1)} %broadcast_in_dim.11), calls=%async_computation.2 | async-start | bytes 557056 | tf_op jit(solution)/shard_map/all_to_all | solution.py:550
  94.9 9.2 %collective-permute-start.9 = (bf16[512,128]{1,0:T(8,128)(2,1)S(1)}, bf16[512,128]{1,0:T(8,128)(2,1)S(1)}, u32[]{:S(2)}, u32[]{:S(2)}) collective-permute-start(bf16[512,128]{1,0:T(8,128)(2,1)S(1)} %pad_maximum_fusion.1), channel_id=1, source_target_pairs={{0,8},{8,0},{16,24},{24,16},{1,9},{9,1},{17,25},{25,17},{2,10},{10... | collective-permute-start | bytes 393224 | tf_op jit(solution)/shard_map/ppermute | solution.py:547
  95.6 12.9 %collective-permute-start.10 = (bf16[512,128]{1,0:T(8,128)(2,1)S(1)}, bf16[512,128]{1,0:T(8,128)(2,1)S(1)}, u32[]{:S(2)}, u32[]{:S(2)}) collective-permute-start(bf16[512,128]{1,0:T(8,128)(2,1)S(1)} %pad_maximum_fusion.2), channel_id=1, source_target_pairs={{0,16},{8,24},{16,0},{24,8},{1,17},{9,25},{17,1},{25,9},{2,18},{10... | collective-permute-start | bytes 393224 | tf_op jit(solution)/shard_map/ppermute | solution.py:547
  96.3 12.2 %collective-permute-start.11 = (bf16[512,128]{1,0:T(8,128)(2,1)S(1)}, bf16[512,128]{1,0:T(8,128)(2,1)S(1)}, u32[]{:S(2)}, u32[]{:S(2)}) collective-permute-start(bf16[512,128]{1,0:T(8,128)(2,1)S(1)} %pad_maximum_fusion.3), channel_id=1, source_target_pairs={{0,24},{8,16},{16,8},{24,0},{1,25},{9,17},{17,9},{25,1},{2,26},{10... | collective-permute-start | bytes 393224 | tf_op jit(solution)/shard_map/ppermute | solution.py:547
  (1 other events, 1.2 us)

commit v10 on v8

--- a/solution.py
+++ b/solution.py
@@ -8,12 +8,14 @@
 from jax.sharding import PartitionSpec as P
 
 A_DEV = 512
+WIDTHS = (192, 192, 128)
 PAD = 8
 TAPS = 7
 MARGIN = 3
 BATCH = 16
 BATCHES = 2
 SMALL = 8
+GROUP = 2
 gelu_scale = 0.7978845608028654
 cubic_coef = 0.044715
 f32 = jnp.float32
@@ -143,7 +145,7 @@
 def block_kernel(
     state, south, north, left, right, conv, halo, forcing, cotangent, land, weight_index, weight_table,
     target_list, clash_list, dw, dwb, gain, nbias, up, upb, down, downb, scale, up_t, down_t,
-    result, keep_0, keep_1, keep_2, keep_3, send, grad_conv, grads,
+    result, keep_0, keep_1, keep_2, keep_3, keep_4, send, grad_conv, grads,
     field, edge, acc_up, acc_down, entry_weights, spread, terms, table, targets, clash, sems,
 ):
     rows, cols, channels = state.shape
@@ -193,7 +195,7 @@
     entry_weights[...] = looked_up
     acc_up[...] = jnp.zeros_like(acc_up)
     acc_down[...] = jnp.zeros_like(acc_down)
-    group = 2
+    group = GROUP
     size = group * cols
     fan = terms.shape[0] // size
     lines = fan * size // channels
@@ -288,10 +290,12 @@
     lax.fori_loop(0, rows // group, mlp_step, 0)
     half = table.shape[0] // 2
 
-    keep_copies = [
-        pltpu.make_async_copy(table.at[pl.ds(k * (half // 4), half // 4)], keep, sems.at[2 + k])
-        for k, keep in enumerate((keep_0, keep_1, keep_2, keep_3))
-    ]
+    keep_copies = []
+    first = 0
+    for k, keep in enumerate((keep_0, keep_1, keep_2, keep_3, keep_4)):
+        from_rows = table.at[pl.ds(first, keep.shape[0])]
+        keep_copies.append(pltpu.make_async_copy(from_rows, keep, sems.at[2 + k]))
+        first += keep.shape[0]
     for copy in keep_copies:
         copy.start()
 
@@ -312,20 +316,24 @@
     lat, lon = lax.axis_index("lat"), lax.axis_index("lon")
     lon_bits = lon_count.bit_length() - 1
     half_rows = lat_count * lon_count // 2 * A_DEV
-    width = A_DEV // 2
     device = owner[...]
     at_lat = (device >> lon_bits) ^ lat
     at_lon = (device & (lon_count - 1)) ^ lon
-    numbers = []
-    for order in orders:
+    blocks = lat_count * lon_count // 2
+    row = jnp.zeros_like(device)
+    first = 0
+    for part, (order, width) in enumerate(zip(orders, WIDTHS)):
         number = jnp.zeros_like(device)
         for bit in order:
             number = number * 2 + ((at_lon >> bit) & 1)
-        numbers.append(number * lat_count + at_lat)
-    upper = (cell[...] >= width).astype(jnp.int32)
-    block = jnp.where(upper == 1, numbers[1], numbers[0])
-    row = (at_lon & 1) * half_rows + upper * (half_rows // 2) + block * width
-    row = row + cell[...] - upper * width
+        if part < 2:
+            number = number * lat_count + at_lat
+        else:
+            number = at_lat * (lon_count // 2) + number
+        place = blocks * first + number * width + (cell[...] - first)
+        row = jnp.where(cell[...] >= first, place, row)
+        first += width
+    row = row + (at_lon & 1) * half_rows
     targets[...] = row
     lane = lax.broadcasted_iota(jnp.int32, row.shape, 1)
     twice = jnp.zeros_like(row)
@@ -430,8 +438,7 @@
     right = lax.ppermute(column(slice(0, MARGIN)), "lon", backward)
 
     rest = list(range(1, lon_bits))
-    orders = [rest, rest[::-1]]
-    width = A_DEV // 2
+    orders = [rest, rest[::-1], rest]
     half_rows = devices // 2 * A_DEV
     lines = (entries // channels, channels)
     line = lambda v: v.reshape(1, -1)
@@ -458,30 +465,31 @@
         cost_estimate=cost(2),
         name="halo_conv",
     )(south, north, taps)
-    quarter = shape((half_rows // 4, channels), f32)
+    blocks = devices // 2
+    sizes = [blocks * WIDTHS[0] // 2] * 2 + [blocks * WIDTHS[1] // 2] * 2 + [blocks * WIDTHS[2]]
     result, *keep, send, grad_conv, grads = pl.pallas_call(
         block_kernel,
         out_shape=(
             shape((rows, cols, channels), bf16),
-            *(quarter,) * 4,
+            *(shape((size, channels), f32) for size in sizes),
             shape((half_rows, channels), bf16),
             shape((rows, cols, channels), f32),
             shape((2 * hid // channels, channels, channels), f32),
         ),
         in_specs=[vmem()] * 11 + [smem()] + [anywhere()] * 2 + [vmem()] * 11,
-        out_specs=[vmem()] + [anywhere()] * 4 + [vmem()] * 3,
+        out_specs=[vmem()] + [anywhere()] * 5 + [vmem()] * 3,
         scratch_shapes=[
             pltpu.VMEM((rows, cols, channels), f32),
             pltpu.VMEM((2, rows + 2 * MARGIN, 24, channels), f32),
             pltpu.VMEM((channels, hid), f32),
             pltpu.VMEM((channels, hid), f32),
             pltpu.VMEM((entries // channels, channels), f32),
-            pltpu.VMEM((2 * fan * cols, channels), f32),
-            pltpu.VMEM((2 * fan * cols, channels), f32),
+            pltpu.VMEM((GROUP * fan * cols, channels), f32),
+            pltpu.VMEM((GROUP * fan * cols, channels), f32),
             pltpu.VMEM((2 * half_rows, channels), f32),
             pltpu.SMEM((entries,), jnp.int32),
             pltpu.SMEM((entries,), jnp.int32),
-            pltpu.SemaphoreType.DMA((6,)),
+            pltpu.SemaphoreType.DMA((7,)),
         ],
         compiler_params=params(min(60, 28 + (half_rows * channels * 10 >> 20))),
         cost_estimate=cost(28),
@@ -508,50 +516,79 @@
         name="conv_grad",
     )(state, south, north, left, right, after(grad_conv, send))
 
-    size = half_rows // 4
     got = after(got, grad_dw)
-    slices = [(keep[k], got[k * size : (k + 1) * size]) for k in range(4)]
     add = lambda summands: functools.reduce(lambda x, y: x + y.astype(f32), summands)
+    slices = []
+    first = 0
+    for held, size in zip(keep, sizes):
+        slices.append((held, got[first : first + size]))
+        first += size
+
+    def to_bands(arrays):
+        return [
+            lax.ppermute(array, "lat", [(i, i ^ distance) for i in range(lat_count)])
+            for distance, array in enumerate(arrays, 1)
+        ]
+
+    def band_part(held, width, distance):
+        return add([h[distance * width : (distance + 1) * width] for h in held])
+
     sends = [add(slices[1]).astype(bf16), add(slices[3]).astype(bf16)]
-    first_sends = sends
     held = [list(slices[0]), list(slices[2])]
-    for stage in range(len(rest)):
-        arrived = [swap_bit(sends[q], orders[q][stage]) for q in range(2)]
+    z_rows = blocks // lat_count * WIDTHS[2]
+    z_held = list(slices[4])
+    z_sends = [band_part(z_held, z_rows, d).astype(bf16) for d in range(1, lat_count)]
+    arrived = [swap_bit(sends[q], orders[q][0]) for q in range(2)]
+    z_arrived = to_bands(lax.optimization_barrier((*z_sends, *sends))[: lat_count - 1])
+    z_held = [h[:z_rows] for h in z_held] + z_arrived
+
+    total = jnp.concatenate([grads.reshape(2 * hid, channels), grad_dw], axis=0).astype(bf16)
+    exchange = functools.partial(
+        lax.all_to_all, axis_name=("lat", "lon"), split_axis=0, concat_axis=0, tiled=True
+    )
+    total = exchange(after(total, *sends).reshape(devices, -1, channels))
+
+    def z_plane_step(z_held, bit, sends):
+        size = z_held[-1].shape[0] // 2
+        out = add([h[size : 2 * size] for h in z_held]).astype(bf16)
+        return [h[:size] for h in z_held] + [swap_bit(after(out, *sends), bit)]
+
+    size = sizes[0]
+    for stage in range(1, len(rest)):
         arrived = lax.optimization_barrier(tuple(arrived))
+        size //= 2
         for q in range(2):
             held[q].append(arrived[q])
-        if stage + 1 < len(rest):
-            size //= 2
-            sends = [add([h[size : 2 * size] for h in held[q]]).astype(bf16) for q in range(2)]
-            held = [[h[:size] for h in held[q]] for q in range(2)]
-    def for_band(distance):
-        at = slice(distance * width, (distance + 1) * width)
-        return jnp.concatenate([add([h[at] for h in held[q]]) for q in range(2)], axis=0)
-
-    forcing_grad = for_band(0)
-    from_bands = []
-    for distance in range(1, lat_count):
-        pairs = [(i, i ^ distance) for i in range(lat_count)]
-        from_bands.append(lax.ppermute(for_band(distance).astype(bf16), "lat", pairs))
-
-    total = jnp.concatenate([grads.reshape(2 * hid, channels), grad_dw], axis=0).astype(bf16)
-    total = after(total, *first_sends)
-    total = total.reshape(lon_count, -1, channels)
-    exchange = functools.partial(lax.all_to_all, split_axis=0, concat_axis=0, tiled=True)
-    spread = lambda x, count: jnp.broadcast_to(x, (count,) + x.shape)
-    total = jnp.sum(exchange(total, "lon").astype(f32), axis=0).astype(bf16)
-    total = jnp.sum(exchange(spread(total, lat_count), "lat").astype(f32), axis=0).astype(bf16)
-    total = exchange(spread(total, lon_count), "lon")
+        sends = [add([h[size : 2 * size] for h in held[q]]).astype(bf16) for q in range(2)]
+        held = [[h[:size] for h in held[q]] for q in range(2)]
+        arrived = [swap_bit(sends[q], orders[q][stage]) for q in range(2)]
+        if stage == 1:
+            total = jnp.sum(after(total, *sends).astype(f32), axis=0, keepdims=True).astype(bf16)
+            total = exchange(jnp.broadcast_to(total, (devices,) + total.shape[1:]))
+        z_held = z_plane_step(z_held, rest[stage - 1], sends)
+    arrived = lax.optimization_barrier(tuple(arrived))
+    for q in range(2):
+        held[q].append(arrived[q])
+    sends = [
+        jnp.concatenate([band_part(held[q], WIDTHS[q], d) for q in range(2)], axis=0).astype(bf16)
+        for d in range(1, lat_count)
+    ]
+    from_bands = to_bands(sends)
+    z_held = z_plane_step(z_held, rest[-1], sends)
+
     scale = float(cells * devices) ** (-0.5)
     total = total.reshape(-1, channels).astype(f32) * scale
     grad_up = total[:hid].reshape(hid // channels, channels, channels)
     grad_up = grad_up.transpose(1, 0, 2).reshape(channels, hid)
     grad_down = total[hid : 2 * hid]
     grad_dw = total[2 * hid : 2 * hid + tap_count].reshape(dw_weight.shape)
-    arrived, grad_dw, grad_up, grad_down = lax.optimization_barrier(
-        (from_bands, grad_dw, grad_up, grad_down)
+    from_bands, z_last, grad_dw, grad_up, grad_down = lax.optimization_barrier(
+        (from_bands, z_held[-1], grad_dw, grad_up, grad_down)
     )
-    forcing_grad = add([forcing_grad] + list(arrived))
+    from_plane = jnp.concatenate([band_part(held[q], WIDTHS[q], 0) for q in range(2)], axis=0)
+    forcing_grad = jnp.concatenate(
+        [add([from_plane] + list(from_bands)), add(z_held[:-1] + [z_last])], axis=0
+    )
     return (result, grad_dw, grad_up, grad_down, forcing_grad)
 
 

time: 118 us -> 112 us (0.949)
  blocking collectives: 27.2 us -> 0 us
  starting transfers between devices: 21.9 us -> 35.7 us
  other arithmetic: 6.79 us -> 11.3 us
  waiting for transfers between devices: 15.1 us -> 17.3 us
    all_to_all x2 -> x0, blocking collectives: 27.2 us -> none  [the longest x1 15.6 us: on_device(): total = jnp.sum(exchange(total, 'lon').astype(f32), axis=0).astype(bf16)]
    all_to_all x1 -> x2, starting transfers between devices: 3.42 us -> 12 us  [the longest x1 7.86 us: on_device(): total = exchange(jnp.broadcast_to(total, (devices,) + total.shape[1:]))]
    ppermute x3 -> x6, starting transfers between devices: 4.58 us -> 9.16 us  [to_bands(): lax.ppermute(array, 'lat', [(i, i ^ distance) for i in range(lat_count)])]
    convert_element_type x0 -> x3, other arithmetic: none -> 3.28 us  [the longest x2 2.41 us: z_plane_step(): out = add([h[size:2 * size] for h in z_held]).astype(bf16)]
    ppermute x5 -> x7, waiting for transfers between devices: 5.13 us -> 2.28 us  [swap_bit(): return lax.ppermute(array, 'lon', pairs)]
    ppermute x3 -> x6, waiting for transfers between devices: 6.47 us -> 9.02 us  [to_bands(): lax.ppermute(array, 'lat', [(i, i ^ distance) for i in range(lat_count)])]
    all_to_all x1 -> x2, waiting for transfers between devices: 2.02 us -> 3.25 us  [the longest x1 3.25 us: on_device(): total = exchange(jnp.broadcast_to(total, (devices,) + total.shape[1:]))]
    ppermute x5 -> x7, starting transfers between devices: 6.59 us -> 7.2 us  [swap_bit(): return lax.ppermute(array, 'lon', pairs)]
  transfers between devices with their start and end apart: 13 -> 19, of which waited for: 5 -> 6; matrix products, arithmetic and copies ran while one was open for 5% -> 10% of each run, Pallas kernels for 11% -> 12%
where the time goes in v10:
time: 112 us; the launch traced here: 111 us
  Pallas kernels  40.2 us (36%)
  starting transfers between devices  35.7 us (32%)
  waiting for transfers between devices  17.3 us (15%)
  other arithmetic  11.3 us (10%)
  local copies, waits for them, and re-layouts  5.45 us (5%)
  between operations  1.21 us (1%)
    pallas_call x1, Pallas kernels, on_device(): pl.pallas_call(block_kernel, out_shape=(shape((rows, cols, channels), bf1...  24.7 us
    ppermute x6, starting transfers between devices, to_bands(): lax.ppermute(array, 'lat', [(i, i ^ distance) for i in range(lat_count)])  9.16 us
    ppermute x6, waiting for transfers between devices, to_bands(): lax.ppermute(array, 'lat', [(i, i ^ distance) for i in range(lat_count)])  9.02 us
    all_to_all x1, starting transfers between devices, on_device(): total = exchange(jnp.broadcast_to(total, (devices,) + total.shape[1:]))  7.86 us
    ppermute x7, starting transfers between devices, swap_bit(): return lax.ppermute(array, 'lon', pairs)  7.2 us
    pallas_call x1, Pallas kernels, on_device(): pl.pallas_call(conv_grad_kernel, out_shape=shape((dw_rows, channels), f32...  6.17 us
    pallas_call x1, Pallas kernels, on_device(): pl.pallas_call(functools.partial(inner_conv_kernel, lat_count, lon_count,...  5.47 us
    all_to_all x1, starting transfers between devices, on_device(): total = exchange(after(total, *sends).reshape(devices, -1, channels))  4.19 us
  transfers between devices with their start and end apart: 19, of which 6 were waited for; matrix products, arithmetic and copies ran while one was open for 10% of the time, Pallas kernels for 12%

profile of v10, /device:TPU:0, one launch (start us, length us, event | category | flops | bytes accessed | tf_op | source)
XLA Modules:
  0.0 111.2 jit_solution(15661247307509509364)
XLA Ops:
  0.7 2.1 %edges.1 = (bf16[3,384,128]{2,1,0:T(8,128)(2,1)}, bf16[3,384,128]{2,1,0:T(8,128)(2,1)}) custom-call(bf16[8,384,128]{2,1,0:T(8,128)(2,1)} %state.6), custom_call_target="tpu_custom_call" | custom-call | flops 1000000000 | tf_op jit(solution)/shard_map/edges/pallas_call | solution.py:421
  2.7 3.3 %collective-permute-start.1 = (bf16[3,384,128]{2,1,0:T(8,128)(2,1)}, bf16[3,384,128]{2,1,0:T(8,128)(2,1)S(1)}, u32[]{:S(2)}, u32[]{:S(2)}) collective-permute-start(bf16[3,384,128]{2,1,0:T(8,128)(2,1)} %get-tuple-element.41), channel_id=1, source_target_pairs={{0,7},{1,6},{2,5},{3,4},{4,3},{5,2},{6,1},{7,0},{8,16},{9,17},{10,... | collective-permute-start | bytes 884744 | tf_op jit(solution)/shard_map/ppermute | solution.py:430
  6.1 1.3 %collective-permute-start = (bf16[3,384,128]{2,1,0:T(8,128)(2,1)}, bf16[3,384,128]{2,1,0:T(8,128)(2,1)}, u32[]{:S(2)}, u32[]{:S(2)}) collective-permute-start(bf16[3,384,128]{2,1,0:T(8,128)(2,1)} %get-tuple-element.40), channel_id=1, source_target_pairs={{0,8},{1,9},{2,10},{3,11},{4,12},{5,13},{6,14},{7,15},{8,0},{9,1},... | collective-permute-start | bytes 884744 | tf_op jit(solution)/shard_map/ppermute | solution.py:429
  7.4 5.5 %inner_conv.1 = (f32[8,384,128]{2,1,0:T(8,128)S(1)}, s32[48,128]{1,0:T(8,128)S(1)}, s32[48,128]{1,0:T(8,128)S(1)}) custom-call(bf16[8,384,128]{2,1,0:T(8,128)(2,1)S(1)} %copy-done.2, f32[49,128]{1,0:T(8,128)S(1)} %reshape.87.dw, f32[1,128]{1,0:T(1,128)S(1)} %bitcast.27, s32[48,128]{1,0:T(8,128)S(1)} %bitcast.23, s32[48,128]{1,0:T(8,128)S(1)} %bitcast.24), custom_call_target="tpu_custom_call" | custom-call | flops 7000000000 | tf_op jit(solution)/shard_map/inner_conv/pallas_call | solution.py:446
  13.8 2.2 %collective-permute-done = bf16[3,384,128]{2,1,0:T(8,128)(2,1)} collective-permute-done((bf16[3,384,128]{2,1,0:T(8,128)(2,1)}, bf16[3,384,128]{2,1,0:T(8,128)(2,1)}, u32[]{:S(2)}, u32[]{:S(2)}) %collective-permute-start) | collective-permute-done | bytes 294944 | tf_op jit(solution)/shard_map/ppermute | solution.py:429
  16.0 1.0 broadcast_select_fusion
  17.2 2.7 %collective-permute-start.3 = (bf16[14,3,128]{2,1,0:T(4,128)(2,1)S(1)}, bf16[14,3,128]{2,1,0:T(4,128)(2,1)S(1)}, u32[]{:S(2)}, u32[]{:S(2)}) collective-permute-start(bf16[14,3,128]{2,1,0:T(4,128)(2,1)S(1)} %pad_maximum_fusion.6), channel_id=1, source_target_pairs={{1,0},{2,1},{3,2},{4,3},{5,4},{6,5},{7,6},{0,7},{9,8},{10,9},{11,1... | collective-permute-start | bytes 32264 | tf_op jit(solution)/shard_map/ppermute | solution.py:438
  19.9 1.8 %halo_conv.1.halo = f32[6,384,128]{2,1,0:T(8,128)S(1)} custom-call(bf16[3,384,128]{2,1,0:T(8,128)(2,1)S(1)} %get-tuple-element.93.south, bf16[3,384,128]{2,1,0:T(8,128)(2,1)S(1)} %get-tuple-element.92.north, f32[49,128]{1,0:T(8,128)S(1)} %reshape.87.dw), custom_call_target="tpu_custom_call" | custom-call | flops 2000000000 | tf_op jit(solution)/shard_map/halo_conv/pallas_call | solution.py:458
  21.9 1.4 %copy-done.18 = f32[8,384,128]{2,1,0:T(8,128)S(1)} copy-done((f32[8,384,128]{2,1,0:T(8,128)S(1)}, f32[8,384,128]{2,1,0:T(8,128)}, u32[]{:S(2)}) %copy-start.18) | copy-done | bytes 1572888
  23.3 24.7 %block.1 = (bf16[8,384,128]{2,1,0:T(8,128)(2,1)}, f32[1536,128]{1,0:T(8,128)S(1)}, f32[1536,128]{1,0:T(8,128)S(1)}, f32[1536,128]{1,0:T(8,128)S(1)}, f32[1536,12...) custom-call(bf16[8,384,128]{2,1,0:T(8,128)(2,1)S(1)} %copy-done.3, ...), custom_call_target="tpu_custom_call" | custom-call | flops 28000000000 | tf_op jit(solution)/shard_map/block/pallas_call | solution.py:470
  48.0 6.2 %conv_grad.1 = f32[64,128]{1,0:T(8,128)S(1)} custom-call(bf16[8,384,128]{2,1,0:T(8,128)(2,1)S(1)} %copy-done.3, bf16[3,384,128]{2,1,0:T(8,128)(2,1)S(1)} %get-tuple-element.93.south, bf16[3,384,128]{2,1,0:T(8,128)(2,1)S(1)} %get-tuple-element.92.north, bf16[14,3,128]{2,1,0:T(4,128)(2,1)S(1)} %collective-permute-done.2.left, ...), custom_call_target="tpu_custom_call" | custom-call | flops 8999999488 | tf_op jit(solution)/shard_map/conv_grad/pallas_call | solution.py:508
  54.3 0.9 add_convert_fusion.4
  55.2 1.0 add_convert_fusion
  56.7 2.6 %collective-permute-start.5 = (bf16[1536,128]{1,0:T(8,128)(2,1)S(1)}, bf16[1536,128]{1,0:T(8,128)(2,1)}, u32[]{:S(2)}, u32[]{:S(2)}) collective-permute-start(bf16[1536,128]{1,0:T(8,128)(2,1)S(1)} %get-tuple-element.89), channel_id=1, source_target_pairs={{0,2},{1,3},{2,0},{3,1},{4,6},{5,7},{6,4},{7,5},{8,10},{9,11},{10,... | collective-permute-start | bytes 1179656 | tf_op jit(solution)/shard_map/ppermute | solution.py:385
  59.5 4.3 %collective-permute-start.13 = (bf16[512,128]{1,0:T(8,128)(2,1)}, bf16[512,128]{1,0:T(8,128)(2,1)}, u32[]{:S(2)}, u32[]{:S(2)}) collective-permute-start(bf16[512,128]{1,0:T(8,128)(2,1)} %get-tuple-element.61), channel_id=1, source_target_pairs={{0,16},{8,24},{16,0},{24,8},{1,17},{9,25},{17,1},{25,9},{2,18},{10... | collective-permute-start | bytes 393224 | tf_op jit(solution)/shard_map/ppermute | solution.py:529
  63.9 0.8 reshape.83
  64.7 4.2 %all-to-all-start = ((bf16[32,34,128]{2,1,0:T(8,128)(2,1)}), bf16[32,34,128]{2,1,0:T(8,128)(2,1)S(1)}, u32[]{:S(2)}, u32[]{:S(2)}) async-start(bf16[32,34,128]{2,1,0:T(8,128)(2,1)} %reshape.83), calls=%async_computation | async-start | bytes 655360 | tf_op jit(solution)/shard_map/all_to_all | solution.py:549
  68.9 5.4 %collective-permute-done.13 = bf16[512,128]{1,0:T(8,128)(2,1)} collective-permute-done((bf16[512,128]{1,0:T(8,128)(2,1)}, bf16[512,128]{1,0:T(8,128)(2,1)}, u32[]{:S(2)}, u32[]{:S(2)}) %collective-permute-start.13) | collective-permute-done | bytes 131104 | tf_op jit(solution)/shard_map/ppermute | solution.py:529
  74.3 1.0 add_convert_fusion.7
  75.3 2.1 %add_convert_fusion.2 = (bf16[768,128]{1,0:T(8,128)(2,1)}, bf16[768,128]{1,0:T(8,128)(2,1)}) fusion(f32[1536,128]{1,0:T(8,128)S(1)} %get-tuple-element.55, bf16[1536,128]{1,0:T(8,128)(2,1)} %collective-permute-done.6, bf16[8192,128]{1,0:T(8,128)(2,1)} %copy-done.19, bf16[1536,128]{1,0:T(8,128)(2,1)} %collective-permute-done.5, ...), kind=kLoop, calls=%fused_computation.3 | loop fusion | flops 983040 | bytes 1966080 | tf_op jit(solution)/shard_map/convert_element_type | solution.py:562
  77.4 2.0 %collective-permute-start.8 = (bf16[768,128]{1,0:T(8,128)(2,1)}, bf16[768,128]{1,0:T(8,128)(2,1)S(1)}, u32[]{:S(2)}, u32[]{:S(2)}) collective-permute-start(bf16[768,128]{1,0:T(8,128)(2,1)} %get-tuple-element.86), channel_id=1, source_target_pairs={{0,2},{1,3},{2,0},{3,1},{4,6},{5,7},{6,4},{7,5},{8,10},{9,11},{10,... | collective-permute-start | bytes 589832 | tf_op jit(solution)/shard_map/ppermute | solution.py:385
  79.6 2.3 %collective-permute-done.15 = bf16[256,128]{1,0:T(8,128)(2,1)S(1)} collective-permute-done((bf16[256,128]{1,0:T(8,128)(2,1)S(1)}, bf16[256,128]{1,0:T(8,128)(2,1)S(1)}, u32[]{:S(2)}, u32[]{:S(2)}) %collective-permute-start.15) | collective-permute-done | bytes 65568 | tf_op jit(solution)/shard_map/ppermute | solution.py:385
  81.9 1.4 %add_convert_fusion.14 = bf16[128,128]{1,0:T(8,128)(2,1)} fusion(f32[2048,128]{1,0:T(8,128)S(1)} %get-tuple-element.59, bf16[256,128]{1,0:T(8,128)(2,1)S(1)} %collective-permute-done.15, bf16[512,128]{1,0:T(8,128)(2,1)} %collective-permute-done.14, bf16[512,128]{1,0:T(8,128)(2,1)} %collective-permute-done.13, bf16[512,128]{1,0:T(8,128)(2,1)} %collective-permute-done.12, ...), kind=kLoop, calls=%fused_computation.29 | loop fusion | flops 180224 | bytes 262144 | tf_op jit(solution)/shard_map/convert_element_type | solution.py:553
  84.1 7.9 %all-to-all-start.1 = ((bf16[32,34,128]{2,1,0:T(8,128)(2,1)}), bf16[32,34,128]{2,1,0:T(8,128)(2,1)S(1)}, u32[]{:S(2)}, u32[]{:S(2)}) async-start(bf16[32,34,128]{2,1,0:T(8,128)(2,1)} %broadcast_in_dim.10), calls=%async_computation.1 | async-start | bytes 655360 | tf_op jit(solution)/shard_map/all_to_all | solution.py:567
  92.0 1.1 convert_add_fusion
  93.1 1.1 convert_add_fusion.1
  94.2 1.8 %collective-permute-start.9 = (bf16[384,128]{1,0:T(8,128)(2,1)S(1)}, bf16[384,128]{1,0:T(8,128)(2,1)S(1)}, u32[]{:S(2)}, u32[]{:S(2)}) collective-permute-start(bf16[384,128]{1,0:T(8,128)(2,1)S(1)} %pad_maximum_fusion.2), channel_id=1, source_target_pairs={{0,8},{8,0},{16,24},{24,16},{1,9},{9,1},{17,25},{25,17},{2,10},{10... | collective-permute-start | bytes 294920 | tf_op jit(solution)/shard_map/ppermute | solution.py:529
  96.0 2.5 %collective-permute-start.10 = (bf16[384,128]{1,0:T(8,128)(2,1)S(1)}, bf16[384,128]{1,0:T(8,128)(2,1)S(1)}, u32[]{:S(2)}, u32[]{:S(2)}) collective-permute-start(bf16[384,128]{1,0:T(8,128)(2,1)S(1)} %pad_maximum_fusion.3), channel_id=1, source_target_pairs={{0,16},{8,24},{16,0},{24,8},{1,17},{9,25},{17,1},{25,9},{2,18},{10... | collective-permute-start | bytes 294920 | tf_op jit(solution)/shard_map/ppermute | solution.py:529
  98.8 1.8 %collective-permute-start.16 = (bf16[128,128]{1,0:T(8,128)(2,1)}, bf16[128,128]{1,0:T(8,128)(2,1)S(1)}, u32[]{:S(2)}, u32[]{:S(2)}) collective-permute-start(bf16[128,128]{1,0:T(8,128)(2,1)} %add_convert_fusion.14), channel_id=1, source_target_pairs={{0,4},{1,5},{2,6},{3,7},{4,0},{5,1},{6,2},{7,3},{8,12},{9,13},{10,... | collective-permute-start | bytes 98312 | tf_op jit(solution)/shard_map/ppermute | solution.py:385
  100.5 3.2 %all-to-all-done.1 = bf16[32,34,128]{2,1,0:T(8,128)(2,1)S(1)} async-done(((bf16[32,34,128]{2,1,0:T(8,128)(2,1)}), bf16[32,34,128]{2,1,0:T(8,128)(2,1)S(1)}, u32[]{:S(2)}, u32[]{:S(2)}) %all-to-all-start.1) | async-done | bytes 278560 | tf_op jit(solution)/shard_map/all_to_all | solution.py:567
  106.0 3.6 %collective-permute-done.10 = bf16[384,128]{1,0:T(8,128)(2,1)S(1)} collective-permute-done((bf16[384,128]{1,0:T(8,128)(2,1)S(1)}, bf16[384,128]{1,0:T(8,128)(2,1)S(1)}, u32[]{:S(2)}, u32[]{:S(2)}) %collective-permute-start.10) | collective-permute-done | bytes 98336 | tf_op jit(solution)/shard_map/ppermute | solution.py:529
  109.6 0.8 convert_add_fusion.2
  (86 shorter events, 6.2 us)
Async XLA Ops:
  0.6 6.7 %copy-start.2 = (bf16[8,384,128]{2,1,0:T(8,128)(2,1)S(1)}, bf16[8,384,128]{2,1,0:T(8,128)(2,1)}, u32[]{:S(2)}) copy-start(bf16[8,384,128]{2,1,0:T(8,128)(2,1)} %state.6) | copy-start | bytes 2359300
  0.6 6.7 %copy-start.20 = (bf16[7,7,128]{2,1,0:T(8,128)(2,1)S(1)}, bf16[7,7,128]{2,1,0:T(8,128)(2,1)}, u32[]{:S(2)}) copy-start(bf16[7,7,128]{2,1,0:T(8,128)(2,1)} %param.21) | copy-start | bytes 37636
  0.7 6.7 %copy-start.7 = (s32[6144]{0:T(1024)S(1)}, s32[6144]{0:T(1024)}, u32[]{:S(2)}) copy-start(s32[6144]{0:T(1024)} %param.31) | copy-start | bytes 73732
  0.7 6.7 %copy-start.6 = (s32[6144,1]{0,1:T(1,128)S(1)}, s32[6144,1]{0,1:T(1,128)}, u32[]{:S(2)}) copy-start(s32[6144,1]{0,1:T(1,128)} %param.30) | copy-start | bytes 73732
  0.7 6.7 %copy-start.11 = (f32[128]{0:T(128)S(1)}, f32[128]{0:T(128)}, u32[]{:S(2)}) copy-start(f32[128]{0:T(128)} %param.22) | copy-start | bytes 1540
  2.7 11.0 %collective-permute-start.1 = (bf16[3,384,128]{2,1,0:T(8,128)(2,1)}, bf16[3,384,128]{2,1,0:T(8,128)(2,1)S(1)}, u32[]{:S(2)}, u32[]{:S(2)}) collective-permute-start(bf16[3,384,128]{2,1,0:T(8,128)(2,1)} %get-tuple-element.41), channel_id=1, source_target_pairs={{0,7},{1,6},{2,5},{3,4},{4,3},{5,2},{6,1},{7,0},{8,16},{9,17},{10,... | collective-permute-start | bytes 884744 | tf_op jit(solution)/shard_map/ppermute | solution.py:430
  6.1 9.9 %collective-permute-start = (bf16[3,384,128]{2,1,0:T(8,128)(2,1)}, bf16[3,384,128]{2,1,0:T(8,128)(2,1)}, u32[]{:S(2)}, u32[]{:S(2)}) collective-permute-start(bf16[3,384,128]{2,1,0:T(8,128)(2,1)} %get-tuple-element.40), channel_id=1, source_target_pairs={{0,8},{1,9},{2,10},{3,11},{4,12},{5,13},{6,14},{7,15},{8,0},{9,1},... | collective-permute-start | bytes 884744 | tf_op jit(solution)/shard_map/ppermute | solution.py:429
  7.4 5.5 %copy-start = (bf16[128,512]{1,0:T(8,128)(2,1)S(1)}, bf16[128,512]{1,0:T(8,128)(2,1)}, u32[]{:S(2)}) copy-start(bf16[128,512]{1,0:T(8,128)(2,1)} %up.1) | copy-start | bytes 393220
  7.4 5.7 %copy-start.1 = (bf16[512,128]{1,0:T(8,128)(2,1)S(1)}, bf16[512,128]{1,0:T(8,128)(2,1)}, u32[]{:S(2)}) copy-start(bf16[512,128]{1,0:T(8,128)(2,1)} %down.1) | copy-start | bytes 393220
  12.9 8.8 %copy-start.17 = (f32[8,384,128]{2,1,0:T(8,128)}, f32[8,384,128]{2,1,0:T(8,128)S(1)}, u32[]{:S(2)}) copy-start(f32[8,384,128]{2,1,0:T(8,128)S(1)} %get-tuple-element.43.conv) | copy-start | bytes 4718596
  17.0 4.7 %collective-permute-start.2 = (bf16[14,3,128]{2,1,0:T(4,128)(2,1)S(1)}, bf16[14,3,128]{2,1,0:T(4,128)(2,1)S(1)}, u32[]{:S(2)}, u32[]{:S(2)}) collective-permute-start(bf16[14,3,128]{2,1,0:T(4,128)(2,1)S(1)} %pad_maximum_fusion.5), channel_id=1, source_target_pairs={{0,1},{1,2},{2,3},{3,4},{4,5},{5,6},{6,7},{7,0},{8,9},{9,10},{10,1... | collective-permute-start | bytes 32264 | tf_op jit(solution)/shard_map/ppermute | solution.py:437
  17.1 4.6 %copy-start.3 = (bf16[8,384,128]{2,1,0:T(8,128)(2,1)S(1)}, bf16[8,384,128]{2,1,0:T(8,128)(2,1)}, u32[]{:S(2)}) copy-start(bf16[8,384,128]{2,1,0:T(8,128)(2,1)} %state.6) | copy-start | bytes 2359300
  17.1 4.6 %copy-start.4 = (bf16[8,384,128]{2,1,0:T(8,128)(2,1)S(1)}, bf16[8,384,128]{2,1,0:T(8,128)(2,1)}, u32[]{:S(2)}) copy-start(bf16[8,384,128]{2,1,0:T(8,128)(2,1)} %forcing.1) | copy-start | bytes 2359300
  17.1 4.6 %copy-start.5 = (bf16[8,384,128]{2,1,0:T(8,128)(2,1)S(1)}, bf16[8,384,128]{2,1,0:T(8,128)(2,1)}, u32[]{:S(2)}) copy-start(bf16[8,384,128]{2,1,0:T(8,128)(2,1)} %cotangent.1) | copy-start | bytes 2359300
  17.2 4.6 %copy-start.8 = (s32[6144]{0:T(1024)S(1)}, s32[6144]{0:T(1024)}, u32[]{:S(2)}) copy-start(s32[6144]{0:T(1024)} %param.32) | copy-start | bytes 73732
  17.2 4.6 %copy-start.9 = (s32[8,384]{1,0:T(8,128)S(1)}, s32[8,384]{1,0:T(8,128)}, u32[]{:S(2)}) copy-start(s32[8,384]{1,0:T(8,128)} %land.1) | copy-start | bytes 36868
  17.2 4.5 %collective-permute-start.3 = (bf16[14,3,128]{2,1,0:T(4,128)(2,1)S(1)}, bf16[14,3,128]{2,1,0:T(4,128)(2,1)S(1)}, u32[]{:S(2)}, u32[]{:S(2)}) collective-permute-start(bf16[14,3,128]{2,1,0:T(4,128)(2,1)S(1)} %pad_maximum_fusion.6), channel_id=1, source_target_pairs={{1,0},{2,1},{3,2},{4,3},{5,4},{6,5},{7,6},{0,7},{9,8},{10,9},{11,1... | collective-permute-start | bytes 32264 | tf_op jit(solution)/shard_map/ppermute | solution.py:438
  48.0 6.3 %collective-permute-start.4 = (bf16[8192,128]{1,0:T(8,128)(2,1)S(1)}, bf16[8192,128]{1,0:T(8,128)(2,1)S(1)}, u32[]{:S(2)}, u32[]{:S(2)}) collective-permute-start(bf16[8192,128]{1,0:T(8,128)(2,1)S(1)} %get-tuple-element.48), channel_id=1, source_target_pairs={{0,1},{1,0},{2,3},{3,2},{4,5},{5,4},{6,7},{7,6},{8,9},{9,8},{10,11... | collective-permute-start | bytes 6291464 | tf_op jit(solution)/shard_map/ppermute | solution.py:385
  56.1 19.1 %collective-permute-start.6 = (bf16[1536,128]{1,0:T(8,128)(2,1)}, bf16[1536,128]{1,0:T(8,128)(2,1)}, u32[]{:S(2)}, u32[]{:S(2)}) collective-permute-start(bf16[1536,128]{1,0:T(8,128)(2,1)} %get-tuple-element.88), channel_id=1, source_target_pairs={{0,4},{1,5},{2,6},{3,7},{4,0},{5,1},{6,2},{7,3},{8,12},{9,13},{10,... | collective-permute-start | bytes 1179656 | tf_op jit(solution)/shard_map/ppermute | solution.py:385
  56.7 18.6 %collective-permute-start.5 = (bf16[1536,128]{1,0:T(8,128)(2,1)S(1)}, bf16[1536,128]{1,0:T(8,128)(2,1)}, u32[]{:S(2)}, u32[]{:S(2)}) collective-permute-start(bf16[1536,128]{1,0:T(8,128)(2,1)S(1)} %get-tuple-element.89), channel_id=1, source_target_pairs={{0,2},{1,3},{2,0},{3,1},{4,6},{5,7},{6,4},{7,5},{8,10},{9,11},{10,... | collective-permute-start | bytes 1179656 | tf_op jit(solution)/shard_map/ppermute | solution.py:385
  59.3 9.6 %collective-permute-start.12 = (bf16[512,128]{1,0:T(8,128)(2,1)}, bf16[512,128]{1,0:T(8,128)(2,1)}, u32[]{:S(2)}, u32[]{:S(2)}) collective-permute-start(bf16[512,128]{1,0:T(8,128)(2,1)} %get-tuple-element.60), channel_id=1, source_target_pairs={{0,8},{8,0},{16,24},{24,16},{1,9},{9,1},{17,25},{25,17},{2,10},{10... | collective-permute-start | bytes 393224 | tf_op jit(solution)/shard_map/ppermute | solution.py:529
  59.5 14.7 %collective-permute-start.13 = (bf16[512,128]{1,0:T(8,128)(2,1)}, bf16[512,128]{1,0:T(8,128)(2,1)}, u32[]{:S(2)}, u32[]{:S(2)}) collective-permute-start(bf16[512,128]{1,0:T(8,128)(2,1)} %get-tuple-element.61), channel_id=1, source_target_pairs={{0,16},{8,24},{16,0},{24,8},{1,17},{9,25},{17,1},{25,9},{2,18},{10... | collective-permute-start | bytes 393224 | tf_op jit(solution)/shard_map/ppermute | solution.py:529
  63.9 10.4 %collective-permute-start.14 = (bf16[512,128]{1,0:T(8,128)(2,1)S(1)}, bf16[512,128]{1,0:T(8,128)(2,1)}, u32[]{:S(2)}, u32[]{:S(2)}) collective-permute-start(bf16[512,128]{1,0:T(8,128)(2,1)S(1)} %get-tuple-element.62), channel_id=1, source_target_pairs={{0,24},{8,16},{16,8},{24,0},{1,25},{9,17},{17,9},{25,1},{2,26},{10... | collective-permute-start | bytes 393224 | tf_op jit(solution)/shard_map/ppermute | solution.py:529
  64.7 18.6 %all-to-all-start = ((bf16[32,34,128]{2,1,0:T(8,128)(2,1)}), bf16[32,34,128]{2,1,0:T(8,128)(2,1)S(1)}, u32[]{:S(2)}, u32[]{:S(2)}) async-start(bf16[32,34,128]{2,1,0:T(8,128)(2,1)} %reshape.83), calls=%async_computation | async-start | bytes 655360 | tf_op jit(solution)/shard_map/all_to_all | solution.py:549
  77.4 4.5 %collective-permute-start.15 = (bf16[256,128]{1,0:T(8,128)(2,1)S(1)}, bf16[256,128]{1,0:T(8,128)(2,1)S(1)}, u32[]{:S(2)}, u32[]{:S(2)}) collective-permute-start(bf16[256,128]{1,0:T(8,128)(2,1)S(1)} %add_convert_fusion.7), channel_id=1, source_target_pairs={{0,2},{1,3},{2,0},{3,1},{4,6},{5,7},{6,4},{7,5},{8,10},{9,11},{10,... | collective-permute-start | bytes 196616 | tf_op jit(solution)/shard_map/ppermute | solution.py:385
  77.4 14.6 %collective-permute-start.8 = (bf16[768,128]{1,0:T(8,128)(2,1)}, bf16[768,128]{1,0:T(8,128)(2,1)S(1)}, u32[]{:S(2)}, u32[]{:S(2)}) collective-permute-start(bf16[768,128]{1,0:T(8,128)(2,1)} %get-tuple-element.86), channel_id=1, source_target_pairs={{0,2},{1,3},{2,0},{3,1},{4,6},{5,7},{6,4},{7,5},{8,10},{9,11},{10,... | collective-permute-start | bytes 589832 | tf_op jit(solution)/shard_map/ppermute | solution.py:385
  79.4 12.6 %collective-permute-start.7 = (bf16[768,128]{1,0:T(8,128)(2,1)}, bf16[768,128]{1,0:T(8,128)(2,1)S(1)}, u32[]{:S(2)}, u32[]{:S(2)}) collective-permute-start(bf16[768,128]{1,0:T(8,128)(2,1)} %get-tuple-element.87), channel_id=1, source_target_pairs={{0,4},{1,5},{2,6},{3,7},{4,0},{5,1},{6,2},{7,3},{8,12},{9,13},{10,... | collective-permute-start | bytes 589832 | tf_op jit(solution)/shard_map/ppermute | solution.py:385
  84.1 19.6 %all-to-all-start.1 = ((bf16[32,34,128]{2,1,0:T(8,128)(2,1)}), bf16[32,34,128]{2,1,0:T(8,128)(2,1)S(1)}, u32[]{:S(2)}, u32[]{:S(2)}) async-start(bf16[32,34,128]{2,1,0:T(8,128)(2,1)} %broadcast_in_dim.10), calls=%async_computation.1 | async-start | bytes 655360 | tf_op jit(solution)/shard_map/all_to_all | solution.py:567
  94.2 11.8 %collective-permute-start.9 = (bf16[384,128]{1,0:T(8,128)(2,1)S(1)}, bf16[384,128]{1,0:T(8,128)(2,1)S(1)}, u32[]{:S(2)}, u32[]{:S(2)}) collective-permute-start(bf16[384,128]{1,0:T(8,128)(2,1)S(1)} %pad_maximum_fusion.2), channel_id=1, source_target_pairs={{0,8},{8,0},{16,24},{24,16},{1,9},{9,1},{17,25},{25,17},{2,10},{10... | collective-permute-start | bytes 294920 | tf_op jit(solution)/shard_map/ppermute | solution.py:529
  96.0 13.6 %collective-permute-start.10 = (bf16[384,128]{1,0:T(8,128)(2,1)S(1)}, bf16[384,128]{1,0:T(8,128)(2,1)S(1)}, u32[]{:S(2)}, u32[]{:S(2)}) collective-permute-start(bf16[384,128]{1,0:T(8,128)(2,1)S(1)} %pad_maximum_fusion.3), channel_id=1, source_target_pairs={{0,16},{8,24},{16,0},{24,8},{1,17},{9,25},{17,1},{25,9},{2,18},{10... | collective-permute-start | bytes 294920 | tf_op jit(solution)/shard_map/ppermute | solution.py:529
  98.5 11.1 %collective-permute-start.11 = (bf16[384,128]{1,0:T(8,128)(2,1)S(1)}, bf16[384,128]{1,0:T(8,128)(2,1)S(1)}, u32[]{:S(2)}, u32[]{:S(2)}) collective-permute-start(bf16[384,128]{1,0:T(8,128)(2,1)S(1)} %pad_maximum_fusion.4), channel_id=1, source_target_pairs={{0,24},{8,16},{16,8},{24,0},{1,25},{9,17},{17,9},{25,1},{2,26},{10... | collective-permute-start | bytes 294920 | tf_op jit(solution)/shard_map/ppermute | solution.py:529
  98.8 7.2 %collective-permute-start.16 = (bf16[128,128]{1,0:T(8,128)(2,1)}, bf16[128,128]{1,0:T(8,128)(2,1)S(1)}, u32[]{:S(2)}, u32[]{:S(2)}) collective-permute-start(bf16[128,128]{1,0:T(8,128)(2,1)} %add_convert_fusion.14), channel_id=1, source_target_pairs={{0,4},{1,5},{2,6},{3,7},{4,0},{5,1},{6,2},{7,3},{8,12},{9,13},{10,... | collective-permute-start | bytes 98312 | tf_op jit(solution)/shard_map/ppermute | solution.py:385
  (8 other events, 31.0 us)

commit v11 on v8

--- a/solution.py
+++ b/solution.py
@@ -536,12 +536,11 @@
 
     total = jnp.concatenate([grads.reshape(2 * hid, channels), grad_dw], axis=0).astype(bf16)
     total = after(total, *first_sends)
-    total = total.reshape(lon_count, -1, channels)
-    exchange = functools.partial(lax.all_to_all, split_axis=0, concat_axis=0, tiled=True)
-    spread = lambda x, count: jnp.broadcast_to(x, (count,) + x.shape)
-    total = jnp.sum(exchange(total, "lon").astype(f32), axis=0).astype(bf16)
-    total = jnp.sum(exchange(spread(total, lat_count), "lat").astype(f32), axis=0).astype(bf16)
-    total = exchange(spread(total, lon_count), "lon")
+    total = total.reshape(devices, -1, channels)
+    total = lax.all_to_all(total, ("lat", "lon"), split_axis=0, concat_axis=0, tiled=True)
+    total = jnp.sum(total.astype(f32), axis=0, keepdims=True).astype(bf16)
+    total = jnp.broadcast_to(total, (devices,) + total.shape[1:])
+    total = lax.all_to_all(total, ("lat", "lon"), split_axis=0, concat_axis=0, tiled=True)
     scale = float(cells * devices) ** (-0.5)
     total = total.reshape(-1, channels).astype(f32) * scale
     grad_up = total[:hid].reshape(hid // channels, channels, channels)

time: 118 us -> 103 us (0.87)
  blocking collectives: 27.2 us -> 0 us
  waiting for transfers between devices: 15.1 us -> 21.5 us
  starting transfers between devices: 21.9 us -> 27.5 us
    all_to_all x2 -> x0, blocking collectives: 27.2 us -> none  [the longest x1 15.6 us: on_device(): total = jnp.sum(exchange(total, 'lon').astype(f32), axis=0).astype(bf16)]
    all_to_all x1 -> x2, starting transfers between devices: 3.42 us -> 9.85 us  [on_device(): lax.all_to_all(total, ('lat', 'lon'), split_axis=0, concat_axis=0, tiled=...]
    ppermute x5, waiting for transfers between devices: 5.13 us -> 9.53 us  [swap_bit(): return lax.ppermute(array, 'lon', pairs)]
    all_to_all x1 -> x2, waiting for transfers between devices: 2.02 us -> 4.75 us  [on_device(): lax.all_to_all(total, ('lat', 'lon'), split_axis=0, concat_axis=0, tiled=...]
  transfers between devices with their start and end apart: 13 -> 14, of which waited for: 5 -> 5; matrix products, arithmetic and copies ran while one was open for 5% -> 8% of each run, Pallas kernels for 11% -> 13%
where the time goes in v11:
time: 103 us; the launch traced here: 102 us
  Pallas kernels  40.2 us (39%)
  starting transfers between devices  27.5 us (27%)
  waiting for transfers between devices  21.5 us (21%)
  other arithmetic  6.31 us (6%)
  local copies, waits for them, and re-layouts  5.49 us (5%)
  between operations  1.15 us (1%)
    pallas_call x1, Pallas kernels, on_device(): pl.pallas_call(block_kernel, out_shape=(shape((rows, cols, channels), bf1...  24.7 us
    all_to_all x2, starting transfers between devices, on_device(): lax.all_to_all(total, ('lat', 'lon'), split_axis=0, concat_axis=0, tiled=...  9.85 us
    ppermute x5, waiting for transfers between devices, swap_bit(): return lax.ppermute(array, 'lon', pairs)  9.53 us
    pallas_call x1, Pallas kernels, on_device(): pl.pallas_call(conv_grad_kernel, out_shape=shape((dw_rows, channels), f32...  6.17 us
    ppermute x5, starting transfers between devices, swap_bit(): return lax.ppermute(array, 'lon', pairs)  5.72 us
    ppermute x3, waiting for transfers between devices, on_device(): lax.ppermute(for_band(distance).astype(bf16), 'lat', pairs)  5.71 us
    pallas_call x1, Pallas kernels, on_device(): pl.pallas_call(functools.partial(inner_conv_kernel, lat_count, lon_count,...  5.47 us
    all_to_all x2, waiting for transfers between devices, on_device(): lax.all_to_all(total, ('lat', 'lon'), split_axis=0, concat_axis=0, tiled=...  4.75 us
  transfers between devices with their start and end apart: 14, of which 5 were waited for; matrix products, arithmetic and copies ran while one was open for 8% of the time, Pallas kernels for 13%

profile of v11, /device:TPU:0, one launch (start us, length us, event | category | flops | bytes accessed | tf_op | source)
XLA Modules:
  0.0 102.2 jit_solution(13185397569238199598)
XLA Ops:
  0.7 2.1 %edges.1 = (bf16[3,384,128]{2,1,0:T(8,128)(2,1)}, bf16[3,384,128]{2,1,0:T(8,128)(2,1)}) custom-call(bf16[8,384,128]{2,1,0:T(8,128)(2,1)} %state.6), custom_call_target="tpu_custom_call" | custom-call | flops 1000000000 | tf_op jit(solution)/shard_map/edges/pallas_call | solution.py:413
  2.7 3.3 %collective-permute-start.1 = (bf16[3,384,128]{2,1,0:T(8,128)(2,1)}, bf16[3,384,128]{2,1,0:T(8,128)(2,1)S(1)}, u32[]{:S(2)}, u32[]{:S(2)}) collective-permute-start(bf16[3,384,128]{2,1,0:T(8,128)(2,1)} %get-tuple-element.33), channel_id=1, source_target_pairs={{0,7},{1,6},{2,5},{3,4},{4,3},{5,2},{6,1},{7,0},{8,16},{9,17},{10,... | collective-permute-start | bytes 884744 | tf_op jit(solution)/shard_map/ppermute | solution.py:422
  6.1 1.3 %collective-permute-start = (bf16[3,384,128]{2,1,0:T(8,128)(2,1)}, bf16[3,384,128]{2,1,0:T(8,128)(2,1)S(1)}, u32[]{:S(2)}, u32[]{:S(2)}) collective-permute-start(bf16[3,384,128]{2,1,0:T(8,128)(2,1)} %get-tuple-element.32), channel_id=1, source_target_pairs={{0,8},{1,9},{2,10},{3,11},{4,12},{5,13},{6,14},{7,15},{8,0},{9,1},... | collective-permute-start | bytes 884744 | tf_op jit(solution)/shard_map/ppermute | solution.py:421
  7.4 5.5 %inner_conv.1 = (f32[8,384,128]{2,1,0:T(8,128)S(1)}, s32[48,128]{1,0:T(8,128)S(1)}, s32[48,128]{1,0:T(8,128)S(1)}) custom-call(bf16[8,384,128]{2,1,0:T(8,128)(2,1)S(1)} %copy-done.2, f32[49,128]{1,0:T(8,128)S(1)} %reshape.87.dw, f32[1,128]{1,0:T(1,128)S(1)} %bitcast.27, s32[48,128]{1,0:T(8,128)S(1)} %bitcast.23, s32[48,128]{1,0:T(8,128)S(1)} %bitcast.24), custom_call_target="tpu_custom_call" | custom-call | flops 7000000000 | tf_op jit(solution)/shard_map/inner_conv/pallas_call | solution.py:439
  12.9 1.2 %copy-done.16 = f32[8,384,128]{2,1,0:T(8,128)} copy-done((f32[8,384,128]{2,1,0:T(8,128)}, f32[8,384,128]{2,1,0:T(8,128)S(1)}, u32[]{:S(2)}) %copy-start.16) | copy-done | bytes 1572888
  14.4 1.5 %collective-permute-done = bf16[3,384,128]{2,1,0:T(8,128)(2,1)S(1)} collective-permute-done((bf16[3,384,128]{2,1,0:T(8,128)(2,1)}, bf16[3,384,128]{2,1,0:T(8,128)(2,1)S(1)}, u32[]{:S(2)}, u32[]{:S(2)}) %collective-permute-start) | collective-permute-done | bytes 294944 | tf_op jit(solution)/shard_map/ppermute | solution.py:421
  16.2 2.7 %collective-permute-start.3 = (bf16[14,3,128]{2,1,0:T(4,128)(2,1)S(1)}, bf16[14,3,128]{2,1,0:T(4,128)(2,1)S(1)}, u32[]{:S(2)}, u32[]{:S(2)}) collective-permute-start(bf16[14,3,128]{2,1,0:T(4,128)(2,1)S(1)} %pad_maximum_fusion.5), channel_id=1, source_target_pairs={{1,0},{2,1},{3,2},{4,3},{5,4},{6,5},{7,6},{0,7},{9,8},{10,9},{11,1... | collective-permute-start | bytes 32264 | tf_op jit(solution)/shard_map/ppermute | solution.py:430
  18.9 1.8 %halo_conv.1.halo = f32[6,384,128]{2,1,0:T(8,128)S(1)} custom-call(bf16[3,384,128]{2,1,0:T(8,128)(2,1)S(1)} %get-tuple-element.74.south, bf16[3,384,128]{2,1,0:T(8,128)(2,1)S(1)} %get-tuple-element.73.north, f32[49,128]{1,0:T(8,128)S(1)} %reshape.87.dw), custom_call_target="tpu_custom_call" | custom-call | flops 2000000000 | tf_op jit(solution)/shard_map/halo_conv/pallas_call | solution.py:451
  20.8 24.7 %block.1 = (bf16[8,384,128]{2,1,0:T(8,128)(2,1)}, f32[2048,128]{1,0:T(8,128)S(1)}, f32[2048,128]{1,0:T(8,128)S(1)}, f32[2048,128]{1,0:T(8,128)S(1)}, f32[2048,12...) custom-call(bf16[8,384,128]{2,1,0:T(8,128)(2,1)S(1)} %copy-done.2, ...), custom_call_target="tpu_custom_call" | custom-call | flops 28000000000 | tf_op jit(solution)/shard_map/block/pallas_call | solution.py:462
  45.6 6.2 %conv_grad.1 = f32[64,128]{1,0:T(8,128)S(1)} custom-call(bf16[8,384,128]{2,1,0:T(8,128)(2,1)S(1)} %copy-done.2, bf16[3,384,128]{2,1,0:T(8,128)(2,1)S(1)} %get-tuple-element.74.south, bf16[3,384,128]{2,1,0:T(8,128)(2,1)S(1)} %get-tuple-element.73.north, bf16[14,3,128]{2,1,0:T(4,128)(2,1)S(1)} %collective-permute-done.2.left, ...), custom_call_target="tpu_custom_call" | custom-call | flops 8999999488 | tf_op jit(solution)/shard_map/conv_grad/pallas_call | solution.py:500
  51.8 1.5 %add_convert_fusion = (bf16[2048,128]{1,0:T(8,128)(2,1)}, bf16[2048,128]{1,0:T(8,128)(2,1)}) fusion(f32[2048,128]{1,0:T(8,128)S(1)} %get-tuple-element.45, bf16[8192,128]{1,0:T(8,128)(2,1)S(1)} %collective-permute-done.4, f32[2048,128]{1,0:T(8,128)S(1)} %get-tuple-element.44), kind=kLoop, calls=%fused_computation | loop fusion | flops 1572864 | bytes 4194304 | tf_op jit(solution)/shard_map/convert_element_type | solution.py:515
  53.6 0.5 collective-permute-start.6
  54.1 2.6 %collective-permute-start.5 = (bf16[2048,128]{1,0:T(8,128)(2,1)}, bf16[2048,128]{1,0:T(8,128)(2,1)}, u32[]{:S(2)}, u32[]{:S(2)}) collective-permute-start(bf16[2048,128]{1,0:T(8,128)(2,1)} %get-tuple-element.70), channel_id=1, source_target_pairs={{0,2},{1,3},{2,0},{3,1},{4,6},{5,7},{6,4},{7,5},{8,10},{9,11},{10,... | collective-permute-start | bytes 1572872 | tf_op jit(solution)/shard_map/ppermute | solution.py:377
  56.7 0.8 reshape.83
  57.6 4.4 %all-to-all-start = ((bf16[32,34,128]{2,1,0:T(8,128)(2,1)}), bf16[32,34,128]{2,1,0:T(8,128)(2,1)S(1)}, u32[]{:S(2)}, u32[]{:S(2)}) async-start(bf16[32,34,128]{2,1,0:T(8,128)(2,1)} %reshape.83), calls=%async_computation | async-start | bytes 655360 | tf_op jit(solution)/shard_map/all_to_all | solution.py:540
  61.9 8.1 %collective-permute-done.6 = bf16[2048,128]{1,0:T(8,128)(2,1)} collective-permute-done((bf16[2048,128]{1,0:T(8,128)(2,1)}, bf16[2048,128]{1,0:T(8,128)(2,1)}, u32[]{:S(2)}, u32[]{:S(2)}) %collective-permute-start.6) | collective-permute-done | bytes 524320 | tf_op jit(solution)/shard_map/ppermute | solution.py:377
  70.0 1.4 %collective-permute-done.5 = bf16[2048,128]{1,0:T(8,128)(2,1)} collective-permute-done((bf16[2048,128]{1,0:T(8,128)(2,1)}, bf16[2048,128]{1,0:T(8,128)(2,1)}, u32[]{:S(2)}, u32[]{:S(2)}) %collective-permute-start.5) | collective-permute-done | bytes 524320 | tf_op jit(solution)/shard_map/ppermute | solution.py:377
  71.4 1.4 %add_convert_fusion.2 = (bf16[1024,128]{1,0:T(8,128)(2,1)S(1)}, bf16[1024,128]{1,0:T(8,128)(2,1)S(1)}) fusion(f32[2048,128]{1,0:T(8,128)S(1)} %get-tuple-element.47, bf16[2048,128]{1,0:T(8,128)(2,1)} %collective-permute-done.6, bf16[8192,128]{1,0:T(8,128)(2,1)} %copy-done.18, bf16[2048,128]{1,0:T(8,128)(2,1)} %collective-permute-done.5, ...), kind=kLoop, calls=%fused_computation.3 | loop fusion | flops 1310720 | bytes 2621440 | tf_op jit(solution)/shard_map/convert_element_type | solution.py:525
  72.8 2.0 %collective-permute-start.8 = (bf16[1024,128]{1,0:T(8,128)(2,1)S(1)}, bf16[1024,128]{1,0:T(8,128)(2,1)S(1)}, u32[]{:S(2)}, u32[]{:S(2)}) collective-permute-start(bf16[1024,128]{1,0:T(8,128)(2,1)S(1)} %get-tuple-element.67), channel_id=1, source_target_pairs={{0,2},{1,3},{2,0},{3,1},{4,6},{5,7},{6,4},{7,5},{8,10},{9,11},{10,... | collective-permute-start | bytes 786440 | tf_op jit(solution)/shard_map/ppermute | solution.py:377
  74.8 0.6 collective-permute-start.7
  75.4 0.8 broadcast_in_dim.10
  76.2 5.5 %all-to-all-start.1 = ((bf16[32,34,128]{2,1,0:T(8,128)(2,1)}), bf16[32,34,128]{2,1,0:T(8,128)(2,1)S(1)}, u32[]{:S(2)}, u32[]{:S(2)}) async-start(bf16[32,34,128]{2,1,0:T(8,128)(2,1)} %broadcast_in_dim.10), calls=%async_computation.1 | async-start | bytes 655360 | tf_op jit(solution)/shard_map/all_to_all | solution.py:543
  81.8 1.2 %convert_add_fusion = (f32[256,128]{1,0:T(8,128)S(1)}, bf16[256,128]{1,0:T(8,128)(2,1)S(1)}, bf16[256,128]{1,0:T(8,128)(2,1)S(1)}, bf16[256,128]{1,0:T(8,128)(2,1)S(1)}) fusion(f32[2048,128]{1,0:T(8,128)S(1)} %get-tuple-element.47, bf16[1024,128]{1,0:T(8,128)(2,1)S(1)} %collective-permute-done.8, bf16[2048,128]{1,0:T(8,128)(2,1)} %collective-permute-done.6, ...), kind=kLoop, calls=%fused_computation.15 | loop fusion | flops 884736 | bytes 1638400 | tf_op jit(solution)/shard_map/add | solution.py:514
  82.9 1.2 %convert_add_fusion.1 = (f32[256,128]{1,0:T(8,128)S(1)}, bf16[256,128]{1,0:T(8,128)(2,1)S(1)}, bf16[256,128]{1,0:T(8,128)(2,1)S(1)}, bf16[256,128]{1,0:T(8,128)(2,1)S(1)}) fusion(f32[2048,128]{1,0:T(8,128)S(1)} %get-tuple-element.39, bf16[1024,128]{1,0:T(8,128)(2,1)S(1)} %collective-permute-done.7, bf16[2048,128]{1,0:T(8,128)(2,1)} %collective-permute-done.5, ...), kind=kLoop, calls=%fused_computation.16 | loop fusion | flops 884736 | bytes 1638400 | tf_op jit(solution)/shard_map/add | solution.py:514
  84.1 1.8 %collective-permute-start.9 = (bf16[512,128]{1,0:T(8,128)(2,1)S(1)}, bf16[512,128]{1,0:T(8,128)(2,1)S(1)}, u32[]{:S(2)}, u32[]{:S(2)}) collective-permute-start(bf16[512,128]{1,0:T(8,128)(2,1)S(1)} %pad_maximum_fusion.1), channel_id=1, source_target_pairs={{0,8},{8,0},{16,24},{24,16},{1,9},{9,1},{17,25},{25,17},{2,10},{10... | collective-permute-start | bytes 393224 | tf_op jit(solution)/shard_map/ppermute | solution.py:535
  86.0 2.5 %collective-permute-start.10 = (bf16[512,128]{1,0:T(8,128)(2,1)S(1)}, bf16[512,128]{1,0:T(8,128)(2,1)S(1)}, u32[]{:S(2)}, u32[]{:S(2)}) collective-permute-start(bf16[512,128]{1,0:T(8,128)(2,1)S(1)} %pad_maximum_fusion.2), channel_id=1, source_target_pairs={{0,16},{8,24},{16,0},{24,8},{1,17},{9,25},{17,1},{25,9},{2,18},{10... | collective-permute-start | bytes 393224 | tf_op jit(solution)/shard_map/ppermute | solution.py:535
  88.8 4.8 %all-to-all-done.1 = bf16[32,34,128]{2,1,0:T(8,128)(2,1)S(1)} async-done(((bf16[32,34,128]{2,1,0:T(8,128)(2,1)}), bf16[32,34,128]{2,1,0:T(8,128)(2,1)S(1)}, u32[]{:S(2)}, u32[]{:S(2)}) %all-to-all-start.1) | async-done | bytes 278560 | tf_op jit(solution)/shard_map/all_to_all | solution.py:543
  93.6 0.7 fusion.3
  94.4 0.7 copy.30
  95.1 0.6 reshape.84
  95.7 5.7 %collective-permute-done.10 = bf16[512,128]{1,0:T(8,128)(2,1)S(1)} collective-permute-done((bf16[512,128]{1,0:T(8,128)(2,1)S(1)}, bf16[512,128]{1,0:T(8,128)(2,1)S(1)}, u32[]{:S(2)}, u32[]{:S(2)}) %collective-permute-start.10) | collective-permute-done | bytes 131104 | tf_op jit(solution)/shard_map/ppermute | solution.py:535
  101.4 0.8 fusion.1
  (69 shorter events, 1.3 us)
Async XLA Ops:
  0.6 6.7 %copy-start.2 = (bf16[8,384,128]{2,1,0:T(8,128)(2,1)S(1)}, bf16[8,384,128]{2,1,0:T(8,128)(2,1)}, u32[]{:S(2)}) copy-start(bf16[8,384,128]{2,1,0:T(8,128)(2,1)} %state.6) | copy-start | bytes 2359300
  0.6 6.7 %copy-start.19 = (bf16[7,7,128]{2,1,0:T(8,128)(2,1)S(1)}, bf16[7,7,128]{2,1,0:T(8,128)(2,1)}, u32[]{:S(2)}) copy-start(bf16[7,7,128]{2,1,0:T(8,128)(2,1)} %param.21) | copy-start | bytes 37636
  0.7 6.7 %copy-start.6 = (s32[6144]{0:T(1024)S(1)}, s32[6144]{0:T(1024)}, u32[]{:S(2)}) copy-start(s32[6144]{0:T(1024)} %param.31) | copy-start | bytes 73732
  0.7 6.7 %copy-start.5 = (s32[6144,1]{0,1:T(1,128)S(1)}, s32[6144,1]{0,1:T(1,128)}, u32[]{:S(2)}) copy-start(s32[6144,1]{0,1:T(1,128)} %param.30) | copy-start | bytes 73732
  0.7 6.7 %copy-start.10 = (f32[128]{0:T(128)S(1)}, f32[128]{0:T(128)}, u32[]{:S(2)}) copy-start(f32[128]{0:T(128)} %param.22) | copy-start | bytes 1540
  2.7 11.6 %collective-permute-start.1 = (bf16[3,384,128]{2,1,0:T(8,128)(2,1)}, bf16[3,384,128]{2,1,0:T(8,128)(2,1)S(1)}, u32[]{:S(2)}, u32[]{:S(2)}) collective-permute-start(bf16[3,384,128]{2,1,0:T(8,128)(2,1)} %get-tuple-element.33), channel_id=1, source_target_pairs={{0,7},{1,6},{2,5},{3,4},{4,3},{5,2},{6,1},{7,0},{8,16},{9,17},{10,... | collective-permute-start | bytes 884744 | tf_op jit(solution)/shard_map/ppermute | solution.py:422
  6.1 9.8 %collective-permute-start = (bf16[3,384,128]{2,1,0:T(8,128)(2,1)}, bf16[3,384,128]{2,1,0:T(8,128)(2,1)S(1)}, u32[]{:S(2)}, u32[]{:S(2)}) collective-permute-start(bf16[3,384,128]{2,1,0:T(8,128)(2,1)} %get-tuple-element.32), channel_id=1, source_target_pairs={{0,8},{1,9},{2,10},{3,11},{4,12},{5,13},{6,14},{7,15},{8,0},{9,1},... | collective-permute-start | bytes 884744 | tf_op jit(solution)/shard_map/ppermute | solution.py:421
  7.4 6.7 %copy-start = (bf16[128,512]{1,0:T(8,128)(2,1)S(1)}, bf16[128,512]{1,0:T(8,128)(2,1)}, u32[]{:S(2)}) copy-start(bf16[128,512]{1,0:T(8,128)(2,1)} %up.1) | copy-start | bytes 393220
  7.4 6.8 %copy-start.1 = (bf16[512,128]{1,0:T(8,128)(2,1)S(1)}, bf16[512,128]{1,0:T(8,128)(2,1)}, u32[]{:S(2)}) copy-start(bf16[512,128]{1,0:T(8,128)(2,1)} %down.1) | copy-start | bytes 393220
  16.0 4.7 %collective-permute-start.2 = (bf16[14,3,128]{2,1,0:T(4,128)(2,1)S(1)}, bf16[14,3,128]{2,1,0:T(4,128)(2,1)S(1)}, u32[]{:S(2)}, u32[]{:S(2)}) collective-permute-start(bf16[14,3,128]{2,1,0:T(4,128)(2,1)S(1)} %pad_maximum_fusion.4), channel_id=1, source_target_pairs={{0,1},{1,2},{2,3},{3,4},{4,5},{5,6},{6,7},{7,0},{8,9},{9,10},{10,1... | collective-permute-start | bytes 32264 | tf_op jit(solution)/shard_map/ppermute | solution.py:429
  16.0 4.6 %copy-start.3 = (bf16[8,384,128]{2,1,0:T(8,128)(2,1)S(1)}, bf16[8,384,128]{2,1,0:T(8,128)(2,1)}, u32[]{:S(2)}) copy-start(bf16[8,384,128]{2,1,0:T(8,128)(2,1)} %forcing.1) | copy-start | bytes 2359300
  16.1 4.6 %copy-start.4 = (bf16[8,384,128]{2,1,0:T(8,128)(2,1)S(1)}, bf16[8,384,128]{2,1,0:T(8,128)(2,1)}, u32[]{:S(2)}) copy-start(bf16[8,384,128]{2,1,0:T(8,128)(2,1)} %cotangent.1) | copy-start | bytes 2359300
  16.1 4.6 %copy-start.7 = (s32[6144]{0:T(1024)S(1)}, s32[6144]{0:T(1024)}, u32[]{:S(2)}) copy-start(s32[6144]{0:T(1024)} %param.32) | copy-start | bytes 73732
  16.1 4.6 %copy-start.8 = (s32[8,384]{1,0:T(8,128)S(1)}, s32[8,384]{1,0:T(8,128)}, u32[]{:S(2)}) copy-start(s32[8,384]{1,0:T(8,128)} %land.1) | copy-start | bytes 36868
  16.1 4.6 %copy-start.9 = (f32[512]{0:T(512)S(1)}, f32[512]{0:T(512)}, u32[]{:S(2)}) copy-start(f32[512]{0:T(512)} %param.26) | copy-start | bytes 6148
  16.1 4.6 %copy-start.11 = (f32[16]{0:T(128)S(1)}, f32[16]{0:T(128)}, u32[]{:S(2)}) copy-start(f32[16]{0:T(128)} %weight_table.1) | copy-start | bytes 196
  16.1 4.6 %copy-start.12 = (f32[128]{0:T(128)S(1)}, f32[128]{0:T(128)}, u32[]{:S(2)}) copy-start(f32[128]{0:T(128)} %param.23) | copy-start | bytes 1540
  16.1 4.6 %copy-start.13 = (f32[128]{0:T(128)S(1)}, f32[128]{0:T(128)}, u32[]{:S(2)}) copy-start(f32[128]{0:T(128)} %param.24) | copy-start | bytes 1540
  16.1 4.6 %copy-start.14 = (f32[128]{0:T(128)S(1)}, f32[128]{0:T(128)}, u32[]{:S(2)}) copy-start(f32[128]{0:T(128)} %param.28) | copy-start | bytes 1540
  16.2 4.6 %copy-start.15 = (f32[128]{0:T(128)S(1)}, f32[128]{0:T(128)}, u32[]{:S(2)}) copy-start(f32[128]{0:T(128)} %param.29) | copy-start | bytes 1540
  16.2 4.6 %copy-start.17 = (f32[8,384,128]{2,1,0:T(8,128)S(1)}, f32[8,384,128]{2,1,0:T(8,128)}, u32[]{:S(2)}) copy-start(f32[8,384,128]{2,1,0:T(8,128)} %copy-done.16) | copy-start | bytes 4718596
  16.2 4.5 %collective-permute-start.3 = (bf16[14,3,128]{2,1,0:T(4,128)(2,1)S(1)}, bf16[14,3,128]{2,1,0:T(4,128)(2,1)S(1)}, u32[]{:S(2)}, u32[]{:S(2)}) collective-permute-start(bf16[14,3,128]{2,1,0:T(4,128)(2,1)S(1)} %pad_maximum_fusion.5), channel_id=1, source_target_pairs={{1,0},{2,1},{3,2},{4,3},{5,4},{6,5},{7,6},{0,7},{9,8},{10,9},{11,1... | collective-permute-start | bytes 32264 | tf_op jit(solution)/shard_map/ppermute | solution.py:430
  45.5 6.3 %collective-permute-start.4 = (bf16[8192,128]{1,0:T(8,128)(2,1)S(1)}, bf16[8192,128]{1,0:T(8,128)(2,1)S(1)}, u32[]{:S(2)}, u32[]{:S(2)}) collective-permute-start(bf16[8192,128]{1,0:T(8,128)(2,1)S(1)} %get-tuple-element.40), channel_id=1, source_target_pairs={{0,1},{1,0},{2,3},{3,2},{4,5},{5,4},{6,7},{7,6},{8,9},{9,8},{10,11... | collective-permute-start | bytes 6291464 | tf_op jit(solution)/shard_map/ppermute | solution.py:377
  53.6 16.4 %collective-permute-start.6 = (bf16[2048,128]{1,0:T(8,128)(2,1)}, bf16[2048,128]{1,0:T(8,128)(2,1)}, u32[]{:S(2)}, u32[]{:S(2)}) collective-permute-start(bf16[2048,128]{1,0:T(8,128)(2,1)} %get-tuple-element.69), channel_id=1, source_target_pairs={{0,4},{1,5},{2,6},{3,7},{4,0},{5,1},{6,2},{7,3},{8,12},{9,13},{10,... | collective-permute-start | bytes 1572872 | tf_op jit(solution)/shard_map/ppermute | solution.py:377
  54.1 17.3 %collective-permute-start.5 = (bf16[2048,128]{1,0:T(8,128)(2,1)}, bf16[2048,128]{1,0:T(8,128)(2,1)}, u32[]{:S(2)}, u32[]{:S(2)}) collective-permute-start(bf16[2048,128]{1,0:T(8,128)(2,1)} %get-tuple-element.70), channel_id=1, source_target_pairs={{0,2},{1,3},{2,0},{3,1},{4,6},{5,7},{6,4},{7,5},{8,10},{9,11},{10,... | collective-permute-start | bytes 1572872 | tf_op jit(solution)/shard_map/ppermute | solution.py:377
  57.6 17.8 %all-to-all-start = ((bf16[32,34,128]{2,1,0:T(8,128)(2,1)}), bf16[32,34,128]{2,1,0:T(8,128)(2,1)S(1)}, u32[]{:S(2)}, u32[]{:S(2)}) async-start(bf16[32,34,128]{2,1,0:T(8,128)(2,1)} %reshape.83), calls=%async_computation | async-start | bytes 655360 | tf_op jit(solution)/shard_map/all_to_all | solution.py:540
  72.8 8.9 %collective-permute-start.8 = (bf16[1024,128]{1,0:T(8,128)(2,1)S(1)}, bf16[1024,128]{1,0:T(8,128)(2,1)S(1)}, u32[]{:S(2)}, u32[]{:S(2)}) collective-permute-start(bf16[1024,128]{1,0:T(8,128)(2,1)S(1)} %get-tuple-element.67), channel_id=1, source_target_pairs={{0,2},{1,3},{2,0},{3,1},{4,6},{5,7},{6,4},{7,5},{8,10},{9,11},{10,... | collective-permute-start | bytes 786440 | tf_op jit(solution)/shard_map/ppermute | solution.py:377
  74.8 7.0 %collective-permute-start.7 = (bf16[1024,128]{1,0:T(8,128)(2,1)S(1)}, bf16[1024,128]{1,0:T(8,128)(2,1)S(1)}, u32[]{:S(2)}, u32[]{:S(2)}) collective-permute-start(bf16[1024,128]{1,0:T(8,128)(2,1)S(1)} %get-tuple-element.68), channel_id=1, source_target_pairs={{0,4},{1,5},{2,6},{3,7},{4,0},{5,1},{6,2},{7,3},{8,12},{9,13},{10,... | collective-permute-start | bytes 786440 | tf_op jit(solution)/shard_map/ppermute | solution.py:377
  76.2 17.3 %all-to-all-start.1 = ((bf16[32,34,128]{2,1,0:T(8,128)(2,1)}), bf16[32,34,128]{2,1,0:T(8,128)(2,1)S(1)}, u32[]{:S(2)}, u32[]{:S(2)}) async-start(bf16[32,34,128]{2,1,0:T(8,128)(2,1)} %broadcast_in_dim.10), calls=%async_computation.1 | async-start | bytes 655360 | tf_op jit(solution)/shard_map/all_to_all | solution.py:543
  84.1 11.6 %collective-permute-start.9 = (bf16[512,128]{1,0:T(8,128)(2,1)S(1)}, bf16[512,128]{1,0:T(8,128)(2,1)S(1)}, u32[]{:S(2)}, u32[]{:S(2)}) collective-permute-start(bf16[512,128]{1,0:T(8,128)(2,1)S(1)} %pad_maximum_fusion.1), channel_id=1, source_target_pairs={{0,8},{8,0},{16,24},{24,16},{1,9},{9,1},{17,25},{25,17},{2,10},{10... | collective-permute-start | bytes 393224 | tf_op jit(solution)/shard_map/ppermute | solution.py:535
  86.0 15.4 %collective-permute-start.10 = (bf16[512,128]{1,0:T(8,128)(2,1)S(1)}, bf16[512,128]{1,0:T(8,128)(2,1)S(1)}, u32[]{:S(2)}, u32[]{:S(2)}) collective-permute-start(bf16[512,128]{1,0:T(8,128)(2,1)S(1)} %pad_maximum_fusion.2), channel_id=1, source_target_pairs={{0,16},{8,24},{16,0},{24,8},{1,17},{9,25},{17,1},{25,9},{2,18},{10... | collective-permute-start | bytes 393224 | tf_op jit(solution)/shard_map/ppermute | solution.py:535
  88.5 12.9 %collective-permute-start.11 = (bf16[512,128]{1,0:T(8,128)(2,1)S(1)}, bf16[512,128]{1,0:T(8,128)(2,1)S(1)}, u32[]{:S(2)}, u32[]{:S(2)}) collective-permute-start(bf16[512,128]{1,0:T(8,128)(2,1)S(1)} %pad_maximum_fusion.3), channel_id=1, source_target_pairs={{0,24},{8,16},{16,8},{24,0},{1,25},{9,17},{17,9},{25,1},{2,26},{10... | collective-permute-start | bytes 393224 | tf_op jit(solution)/shard_map/ppermute | solution.py:535
  (2 other events, 2.9 us)

commit v12 on v11

--- a/solution.py
+++ b/solution.py
@@ -14,6 +14,7 @@
 BATCH = 16
 BATCHES = 2
 SMALL = 8
+ROUND = 2
 gelu_scale = 0.7978845608028654
 cubic_coef = 0.044715
 f32 = jnp.float32
@@ -21,7 +22,7 @@
 shape = jax.ShapeDtypeStruct
 
 
-def params(mebibytes=40):
+def params(mebibytes):
     return pltpu.CompilerParams(vmem_limit_bytes=mebibytes << 20)
 
 
@@ -144,7 +145,7 @@
     state, south, north, left, right, conv, halo, forcing, cotangent, land, weight_index, weight_table,
     target_list, clash_list, dw, dwb, gain, nbias, up, upb, down, downb, scale, up_t, down_t,
     result, keep_0, keep_1, keep_2, keep_3, send, grad_conv, grads,
-    field, edge, acc_up, acc_down, entry_weights, spread, terms, table, targets, clash, sems,
+    field, edge, acc_up, acc_down, entry_weights, spread, terms, table, outgoing, targets, clash, sems,
 ):
     rows, cols, channels = state.shape
     scalar_copies = [
@@ -195,7 +196,7 @@
     acc_down[...] = jnp.zeros_like(acc_down)
     group = 2
     size = group * cols
-    fan = terms.shape[0] // size
+    fan = terms.shape[0] // (ROUND * size)
     lines = fan * size // channels
 
     def column(ref, first, count):
@@ -208,7 +209,7 @@
             axis=0,
         )
 
-    def mlp_step(step, _):
+    def mlp_step(step, place):
         first = step * group
         here = field[pl.ds(first, group)].reshape(size, channels)
         average = jnp.mean(here, axis=-1, keepdims=True)
@@ -239,7 +240,7 @@
         spread[...] = column(entry_weights, step * lines, lines)
         for k in range(fan):
             weights = spread[pl.ds(k, size, stride=fan), :]
-            terms[pl.ds(k * size, size), :] = weights * gmix
+            terms[pl.ds(k * ROUND * size + place * size, size), :] = weights * gmix
         gained = gmix * gain[...]
         gconv = inv_std * (
             gained
@@ -251,23 +252,27 @@
         acc_up[...] += lax.dot_general(mixed, grad_pre, contract, preferred_element_type=f32)
         acc_down[...] += lax.dot_general(grad_out, hidden, contract, preferred_element_type=f32)
 
-        @pl.when(step == 0)
+    unit = BATCH * BATCHES
+    units = terms.shape[0] // unit
+
+    def round_of(index, _):
+        for place in range(ROUND):
+            mlp_step(index * ROUND + place, place)
+
+        @pl.when(index == 0)
         def _():
             for copy in scalar_copies:
                 copy.wait()
 
-        unit = BATCH * BATCHES
-        units = fan * size // unit
-
-        def add_unit(index, _):
-            first_cell = index * (unit // fan)
-            first_entry = step * (fan * size) + index * unit
+        def add_unit(at, _):
+            first_cell = at * (unit // fan)
+            first_entry = index * terms.shape[0] + at * unit
 
             def add_batch(first, count):
                 found = []
                 for k in range(first, first + count):
-                    value = terms[pl.ds((k % fan) * size + first_cell + k // fan, 1), :]
-                    found.append((targets[first_entry + k], value))
+                    place = (k % fan) * (ROUND * size) + first_cell + k // fan
+                    found.append((targets[first_entry + k], terms[pl.ds(place, 1), :]))
                 sums = [table[pl.ds(t, 1), :] + v for t, v in found]
                 for (t, _), value in zip(found, sums):
                     table[pl.ds(t, 1), :] = value
@@ -285,7 +290,7 @@
         lax.fori_loop(0, units, add_unit, 0)
         return 0
 
-    lax.fori_loop(0, rows // group, mlp_step, 0)
+    lax.fori_loop(0, rows // (group * ROUND), round_of, 0)
     half = table.shape[0] // 2
 
     keep_copies = [
@@ -295,10 +300,18 @@
     for copy in keep_copies:
         copy.start()
 
-    def give(at):
-        send[at, :] = table[pl.ds(half + at.start, at.size), :].astype(bf16)
-
-    in_chunks(half, give)
+    buffer_rows = outgoing.shape[0]
+    for first in range(0, half, buffer_rows):
+
+        def give(at):
+            outgoing[at, :] = table[pl.ds(half + first + at.start, at.size), :].astype(bf16)
+
+        in_chunks(buffer_rows, give)
+        copy = pltpu.make_async_copy(outgoing, send.at[pl.ds(first, buffer_rows)], sems.at[6])
+        copy.start()
+        if first + buffer_rows < half:
+            copy.wait()
+    keep_copies.append(copy)
     blocks = up.shape[1] // channels
     for k in range(blocks):
         part = slice(k * channels, (k + 1) * channels)
@@ -415,6 +428,7 @@
         out_shape=(edge_rows, edge_rows),
         in_specs=[vmem()],
         out_specs=[vmem()] * 2,
+        compiler_params=params(8),
         cost_estimate=cost(1),
         name="edges",
     )(state)
@@ -442,7 +456,7 @@
         in_specs=[vmem()] * 5,
         out_specs=[vmem()] * 3,
         scratch_shapes=[pltpu.VMEM((rows, cols + 2 * PAD, channels), f32)],
-        compiler_params=params(),
+        compiler_params=params(12),
         cost_estimate=cost(7),
         name="inner_conv",
     )(
@@ -454,7 +468,7 @@
         in_specs=[vmem()] * 3,
         out_specs=vmem(),
         scratch_shapes=[pltpu.VMEM((2 * MARGIN, cols + 2 * PAD, channels), f32)],
-        compiler_params=params(),
+        compiler_params=params(8),
         cost_estimate=cost(2),
         name="halo_conv",
     )(south, north, taps)
@@ -469,7 +483,7 @@
             shape((2 * hid // channels, channels, channels), f32),
         ),
         in_specs=[vmem()] * 11 + [smem()] + [anywhere()] * 2 + [vmem()] * 11,
-        out_specs=[vmem()] + [anywhere()] * 4 + [vmem()] * 3,
+        out_specs=[vmem()] + [anywhere()] * 5 + [vmem()] * 2,
         scratch_shapes=[
             pltpu.VMEM((rows, cols, channels), f32),
             pltpu.VMEM((2, rows + 2 * MARGIN, 24, channels), f32),
@@ -477,11 +491,12 @@
             pltpu.VMEM((channels, hid), f32),
             pltpu.VMEM((entries // channels, channels), f32),
             pltpu.VMEM((2 * fan * cols, channels), f32),
-            pltpu.VMEM((2 * fan * cols, channels), f32),
+            pltpu.VMEM((ROUND * 2 * fan * cols, channels), f32),
             pltpu.VMEM((2 * half_rows, channels), f32),
+            pltpu.VMEM((min(half_rows, 8192), channels), bf16),
             pltpu.SMEM((entries,), jnp.int32),
             pltpu.SMEM((entries,), jnp.int32),
-            pltpu.SemaphoreType.DMA((6,)),
+            pltpu.SemaphoreType.DMA((7,)),
         ],
         compiler_params=params(min(60, 28 + (half_rows * channels * 10 >> 20))),
         cost_estimate=cost(28),
@@ -503,7 +518,7 @@
         in_specs=[vmem()] * 6,
         out_specs=vmem(),
         scratch_shapes=[pltpu.VMEM((rows + 2 * MARGIN, cols + 2 * PAD, channels), f32)],
-        compiler_params=params(),
+        compiler_params=params(16),
         cost_estimate=cost(9),
         name="conv_grad",
     )(state, south, north, left, right, after(grad_conv, send))

time: 103 us -> 101 us (0.981)
  Pallas kernels: 40.2 us -> 38 us
  local copies, waits for them, and re-layouts: 5.49 us -> 6.59 us
    pallas_call x1, Pallas kernels: 2.05 us -> 0.06 us  [on_device(): pl.pallas_call(functools.partial(edge_kernel, bands=lat_count), out_shape...]
    unnamed x42 -> x44, local copies, waits for them, and re-layouts: 1.72 us -> 2.84 us
where the time goes in v12:
time: 101 us
  Pallas kernels  38 us (38%)
  starting transfers between devices  27.6 us (27%)
  waiting for transfers between devices  21.3 us (21%)
  local copies, waits for them, and re-layouts  6.59 us (7%)
  other arithmetic  6.3 us (6%)
  between operations  1.14 us (1%)
    pallas_call x1, Pallas kernels, on_device(): pl.pallas_call(block_kernel, out_shape=(shape((rows, cols, channels), bf1...  24.5 us
    all_to_all x2, starting transfers between devices, on_device(): lax.all_to_all(total, ('lat', 'lon'), split_axis=0, concat_axis=0, tiled=...  9.8 us
    ppermute x5, waiting for transfers between devices, swap_bit(): return lax.ppermute(array, 'lon', pairs)  9.52 us
    pallas_call x1, Pallas kernels, on_device(): pl.pallas_call(conv_grad_kernel, out_shape=shape((dw_rows, channels), f32...  6.17 us
    ppermute x5, starting transfers between devices, swap_bit(): return lax.ppermute(array, 'lon', pairs)  5.81 us
    ppermute x3, waiting for transfers between devices, on_device(): lax.ppermute(for_band(distance).astype(bf16), 'lat', pairs)  5.71 us
    pallas_call x1, Pallas kernels, on_device(): pl.pallas_call(functools.partial(inner_conv_kernel, lat_count, lon_count,...  5.47 us
    all_to_all x2, waiting for transfers between devices, on_device(): lax.all_to_all(total, ('lat', 'lon'), split_axis=0, concat_axis=0, tiled=...  4.75 us
  transfers between devices with their start and end apart: 14, of which 5 were waited for; matrix products, arithmetic and copies ran while one was open for 8% of the time, Pallas kernels for 13%

profile of v12, /device:TPU:0, one launch (start us, length us, event | category | flops | bytes accessed | tf_op | source)
XLA Modules:
  0.0 100.9 jit_solution(14001923301645763117)
XLA Ops:
  0.6 1.1 %copy-done.2 = bf16[8,384,128]{2,1,0:T(8,128)(2,1)S(1)} copy-done((bf16[8,384,128]{2,1,0:T(8,128)(2,1)S(1)}, bf16[8,384,128]{2,1,0:T(8,128)(2,1)}, u32[]{:S(2)}) %copy-start.2) | copy-done | bytes 786456
  1.9 3.4 %collective-permute-start.1 = (bf16[3,384,128]{2,1,0:T(8,128)(2,1)S(1)}, bf16[3,384,128]{2,1,0:T(8,128)(2,1)S(1)}, u32[]{:S(2)}, u32[]{:S(2)}) collective-permute-start(bf16[3,384,128]{2,1,0:T(8,128)(2,1)S(1)} %get-tuple-element.33), channel_id=1, source_target_pairs={{0,7},{1,6},{2,5},{3,4},{4,3},{5,2},{6,1},{7,0},{8,16},{9,17},{10,... | collective-permute-start | bytes 884744 | tf_op jit(solution)/shard_map/ppermute | solution.py:436
  5.3 1.3 %collective-permute-start = (bf16[3,384,128]{2,1,0:T(8,128)(2,1)S(1)}, bf16[3,384,128]{2,1,0:T(8,128)(2,1)S(1)}, u32[]{:S(2)}, u32[]{:S(2)}) collective-permute-start(bf16[3,384,128]{2,1,0:T(8,128)(2,1)S(1)} %get-tuple-element.32), channel_id=1, source_target_pairs={{0,8},{1,9},{2,10},{3,11},{4,12},{5,13},{6,14},{7,15},{8,0},{9,1},... | collective-permute-start | bytes 884744 | tf_op jit(solution)/shard_map/ppermute | solution.py:435
  6.6 5.5 %inner_conv.1 = (f32[8,384,128]{2,1,0:T(8,128)S(1)}, s32[48,128]{1,0:T(8,128)S(1)}, s32[48,128]{1,0:T(8,128)S(1)}) custom-call(bf16[8,384,128]{2,1,0:T(8,128)(2,1)S(1)} %copy-done.3, f32[49,128]{1,0:T(8,128)S(1)} %reshape.87.dw, f32[1,128]{1,0:T(1,128)S(1)} %bitcast.27, s32[48,128]{1,0:T(8,128)S(1)} %bitcast.23, s32[48,128]{1,0:T(8,128)S(1)} %bitcast.24), custom_call_target="tpu_custom_call" | custom-call | flops 7000000000 | tf_op jit(solution)/shard_map/inner_conv/pallas_call | solution.py:453
  12.1 1.2 %copy-done.17 = f32[8,384,128]{2,1,0:T(8,128)} copy-done((f32[8,384,128]{2,1,0:T(8,128)}, f32[8,384,128]{2,1,0:T(8,128)S(1)}, u32[]{:S(2)}) %copy-start.17) | copy-done | bytes 1572888
  13.5 1.3 %collective-permute-done = bf16[3,384,128]{2,1,0:T(8,128)(2,1)S(1)} collective-permute-done((bf16[3,384,128]{2,1,0:T(8,128)(2,1)S(1)}, bf16[3,384,128]{2,1,0:T(8,128)(2,1)S(1)}, u32[]{:S(2)}, u32[]{:S(2)}) %collective-permute-start) | collective-permute-done | bytes 294944 | tf_op jit(solution)/shard_map/ppermute | solution.py:435
  15.2 2.7 %collective-permute-start.3 = (bf16[14,3,128]{2,1,0:T(4,128)(2,1)S(1)}, bf16[14,3,128]{2,1,0:T(4,128)(2,1)S(1)}, u32[]{:S(2)}, u32[]{:S(2)}) collective-permute-start(bf16[14,3,128]{2,1,0:T(4,128)(2,1)S(1)} %pad_maximum_fusion.5), channel_id=1, source_target_pairs={{1,0},{2,1},{3,2},{4,3},{5,4},{6,5},{7,6},{0,7},{9,8},{10,9},{11,1... | collective-permute-start | bytes 32264 | tf_op jit(solution)/shard_map/ppermute | solution.py:444
  17.8 1.8 %halo_conv.1.halo = f32[6,384,128]{2,1,0:T(8,128)S(1)} custom-call(bf16[3,384,128]{2,1,0:T(8,128)(2,1)S(1)} %get-tuple-element.74.south, bf16[3,384,128]{2,1,0:T(8,128)(2,1)S(1)} %get-tuple-element.73.north, f32[49,128]{1,0:T(8,128)S(1)} %reshape.87.dw), custom_call_target="tpu_custom_call" | custom-call | flops 2000000000 | tf_op jit(solution)/shard_map/halo_conv/pallas_call | solution.py:465
  19.8 24.5 %block.1 = (bf16[8,384,128]{2,1,0:T(8,128)(2,1)}, f32[2048,128]{1,0:T(8,128)S(1)}, f32[2048,128]{1,0:T(8,128)S(1)}, f32[2048,128]{1,0:T(8,128)S(1)}, f32[2048,12...) custom-call(bf16[8,384,128]{2,1,0:T(8,128)(2,1)S(1)} %copy-done.3, ...), custom_call_target="tpu_custom_call" | custom-call | flops 28000000000 | tf_op jit(solution)/shard_map/block/pallas_call | solution.py:476
  44.4 6.2 %conv_grad.1 = f32[64,128]{1,0:T(8,128)S(1)} custom-call(bf16[8,384,128]{2,1,0:T(8,128)(2,1)S(1)} %copy-done.3, bf16[3,384,128]{2,1,0:T(8,128)(2,1)S(1)} %get-tuple-element.74.south, bf16[3,384,128]{2,1,0:T(8,128)(2,1)S(1)} %get-tuple-element.73.north, bf16[14,3,128]{2,1,0:T(4,128)(2,1)S(1)} %collective-permute-done.2.left, ...), custom_call_target="tpu_custom_call" | custom-call | flops 8999999488 | tf_op jit(solution)/shard_map/conv_grad/pallas_call | solution.py:515
  50.6 1.5 %add_convert_fusion = (bf16[2048,128]{1,0:T(8,128)(2,1)}, bf16[2048,128]{1,0:T(8,128)(2,1)}) fusion(f32[2048,128]{1,0:T(8,128)S(1)} %get-tuple-element.45, bf16[8192,128]{1,0:T(8,128)(2,1)S(1)} %collective-permute-done.4, f32[2048,128]{1,0:T(8,128)S(1)} %get-tuple-element.44), kind=kLoop, calls=%fused_computation | loop fusion | flops 1572864 | bytes 4194304 | tf_op jit(solution)/shard_map/convert_element_type | solution.py:530
  52.3 0.6 collective-permute-start.6
  52.9 2.5 %collective-permute-start.5 = (bf16[2048,128]{1,0:T(8,128)(2,1)}, bf16[2048,128]{1,0:T(8,128)(2,1)}, u32[]{:S(2)}, u32[]{:S(2)}) collective-permute-start(bf16[2048,128]{1,0:T(8,128)(2,1)} %get-tuple-element.70), channel_id=1, source_target_pairs={{0,2},{1,3},{2,0},{3,1},{4,6},{5,7},{6,4},{7,5},{8,10},{9,11},{10,... | collective-permute-start | bytes 1572872 | tf_op jit(solution)/shard_map/ppermute | solution.py:390
  55.5 0.8 reshape.83
  56.3 4.4 %all-to-all-start = ((bf16[32,34,128]{2,1,0:T(8,128)(2,1)}), bf16[32,34,128]{2,1,0:T(8,128)(2,1)S(1)}, u32[]{:S(2)}, u32[]{:S(2)}) async-start(bf16[32,34,128]{2,1,0:T(8,128)(2,1)} %reshape.83), calls=%async_computation | async-start | bytes 655360 | tf_op jit(solution)/shard_map/all_to_all | solution.py:555
  60.7 8.1 %collective-permute-done.6 = bf16[2048,128]{1,0:T(8,128)(2,1)} collective-permute-done((bf16[2048,128]{1,0:T(8,128)(2,1)}, bf16[2048,128]{1,0:T(8,128)(2,1)}, u32[]{:S(2)}, u32[]{:S(2)}) %collective-permute-start.6) | collective-permute-done | bytes 524320 | tf_op jit(solution)/shard_map/ppermute | solution.py:390
  68.7 1.5 %collective-permute-done.5 = bf16[2048,128]{1,0:T(8,128)(2,1)} collective-permute-done((bf16[2048,128]{1,0:T(8,128)(2,1)}, bf16[2048,128]{1,0:T(8,128)(2,1)}, u32[]{:S(2)}, u32[]{:S(2)}) %collective-permute-start.5) | collective-permute-done | bytes 524320 | tf_op jit(solution)/shard_map/ppermute | solution.py:390
  70.2 1.4 %add_convert_fusion.2 = (bf16[1024,128]{1,0:T(8,128)(2,1)S(1)}, bf16[1024,128]{1,0:T(8,128)(2,1)S(1)}) fusion(f32[2048,128]{1,0:T(8,128)S(1)} %get-tuple-element.47, bf16[2048,128]{1,0:T(8,128)(2,1)} %collective-permute-done.6, bf16[8192,128]{1,0:T(8,128)(2,1)} %copy-done.19, bf16[2048,128]{1,0:T(8,128)(2,1)} %collective-permute-done.5, ...), kind=kLoop, calls=%fused_computation.3 | loop fusion | flops 1310720 | bytes 2621440 | tf_op jit(solution)/shard_map/convert_element_type | solution.py:540
  71.5 2.0 %collective-permute-start.8 = (bf16[1024,128]{1,0:T(8,128)(2,1)S(1)}, bf16[1024,128]{1,0:T(8,128)(2,1)S(1)}, u32[]{:S(2)}, u32[]{:S(2)}) collective-permute-start(bf16[1024,128]{1,0:T(8,128)(2,1)S(1)} %get-tuple-element.67), channel_id=1, source_target_pairs={{0,2},{1,3},{2,0},{3,1},{4,6},{5,7},{6,4},{7,5},{8,10},{9,11},{10,... | collective-permute-start | bytes 786440 | tf_op jit(solution)/shard_map/ppermute | solution.py:390
  73.5 0.7 collective-permute-start.7
  74.2 0.8 broadcast_in_dim.10
  75.0 5.4 %all-to-all-start.1 = ((bf16[32,34,128]{2,1,0:T(8,128)(2,1)}), bf16[32,34,128]{2,1,0:T(8,128)(2,1)S(1)}, u32[]{:S(2)}, u32[]{:S(2)}) async-start(bf16[32,34,128]{2,1,0:T(8,128)(2,1)} %broadcast_in_dim.10), calls=%async_computation.1 | async-start | bytes 655360 | tf_op jit(solution)/shard_map/all_to_all | solution.py:558
  80.5 1.2 %convert_add_fusion = (f32[256,128]{1,0:T(8,128)S(1)}, bf16[256,128]{1,0:T(8,128)(2,1)S(1)}, bf16[256,128]{1,0:T(8,128)(2,1)S(1)}, bf16[256,128]{1,0:T(8,128)(2,1)S(1)}) fusion(f32[2048,128]{1,0:T(8,128)S(1)} %get-tuple-element.47, bf16[1024,128]{1,0:T(8,128)(2,1)S(1)} %collective-permute-done.8, bf16[2048,128]{1,0:T(8,128)(2,1)} %collective-permute-done.6, ...), kind=kLoop, calls=%fused_computation.15 | loop fusion | flops 884736 | bytes 1638400 | tf_op jit(solution)/shard_map/add | solution.py:529
  81.7 1.2 %convert_add_fusion.1 = (f32[256,128]{1,0:T(8,128)S(1)}, bf16[256,128]{1,0:T(8,128)(2,1)S(1)}, bf16[256,128]{1,0:T(8,128)(2,1)S(1)}, bf16[256,128]{1,0:T(8,128)(2,1)S(1)}) fusion(f32[2048,128]{1,0:T(8,128)S(1)} %get-tuple-element.39, bf16[1024,128]{1,0:T(8,128)(2,1)S(1)} %collective-permute-done.7, bf16[2048,128]{1,0:T(8,128)(2,1)} %collective-permute-done.5, ...), kind=kLoop, calls=%fused_computation.16 | loop fusion | flops 884736 | bytes 1638400 | tf_op jit(solution)/shard_map/add | solution.py:529
  82.9 1.8 %collective-permute-start.9 = (bf16[512,128]{1,0:T(8,128)(2,1)S(1)}, bf16[512,128]{1,0:T(8,128)(2,1)S(1)}, u32[]{:S(2)}, u32[]{:S(2)}) collective-permute-start(bf16[512,128]{1,0:T(8,128)(2,1)S(1)} %pad_maximum_fusion.1), channel_id=1, source_target_pairs={{0,8},{8,0},{16,24},{24,16},{1,9},{9,1},{17,25},{25,17},{2,10},{10... | collective-permute-start | bytes 393224 | tf_op jit(solution)/shard_map/ppermute | solution.py:550
  84.7 2.5 %collective-permute-start.10 = (bf16[512,128]{1,0:T(8,128)(2,1)S(1)}, bf16[512,128]{1,0:T(8,128)(2,1)S(1)}, u32[]{:S(2)}, u32[]{:S(2)}) collective-permute-start(bf16[512,128]{1,0:T(8,128)(2,1)S(1)} %pad_maximum_fusion.2), channel_id=1, source_target_pairs={{0,16},{8,24},{16,0},{24,8},{1,17},{9,25},{17,1},{25,9},{2,18},{10... | collective-permute-start | bytes 393224 | tf_op jit(solution)/shard_map/ppermute | solution.py:550
  87.5 4.8 %all-to-all-done.1 = bf16[32,34,128]{2,1,0:T(8,128)(2,1)S(1)} async-done(((bf16[32,34,128]{2,1,0:T(8,128)(2,1)}), bf16[32,34,128]{2,1,0:T(8,128)(2,1)S(1)}, u32[]{:S(2)}, u32[]{:S(2)}) %all-to-all-start.1) | async-done | bytes 278560 | tf_op jit(solution)/shard_map/all_to_all | solution.py:558
  92.4 0.7 fusion.3
  93.1 0.7 copy.30
  93.8 0.6 reshape.84
  94.5 5.7 %collective-permute-done.10 = bf16[512,128]{1,0:T(8,128)(2,1)S(1)} collective-permute-done((bf16[512,128]{1,0:T(8,128)(2,1)S(1)}, bf16[512,128]{1,0:T(8,128)(2,1)S(1)}, u32[]{:S(2)}, u32[]{:S(2)}) %collective-permute-start.10) | collective-permute-done | bytes 131104 | tf_op jit(solution)/shard_map/ppermute | solution.py:550
  100.2 0.8 fusion.1
  (71 shorter events, 1.4 us)
Async XLA Ops:
  1.8 4.8 %copy-start.20 = (bf16[7,7,128]{2,1,0:T(8,128)(2,1)S(1)}, bf16[7,7,128]{2,1,0:T(8,128)(2,1)}, u32[]{:S(2)}) copy-start(bf16[7,7,128]{2,1,0:T(8,128)(2,1)} %param.21) | copy-start | bytes 37636
  1.8 4.8 %copy-start.3 = (bf16[8,384,128]{2,1,0:T(8,128)(2,1)S(1)}, bf16[8,384,128]{2,1,0:T(8,128)(2,1)}, u32[]{:S(2)}) copy-start(bf16[8,384,128]{2,1,0:T(8,128)(2,1)} %state.6) | copy-start | bytes 2359300
  1.8 4.8 %copy-start.6 = (s32[6144,1]{0,1:T(1,128)S(1)}, s32[6144,1]{0,1:T(1,128)}, u32[]{:S(2)}) copy-start(s32[6144,1]{0,1:T(1,128)} %param.30) | copy-start | bytes 73732
  1.8 4.8 %copy-start.7 = (s32[6144]{0:T(1024)S(1)}, s32[6144]{0:T(1024)}, u32[]{:S(2)}) copy-start(s32[6144]{0:T(1024)} %param.31) | copy-start | bytes 73732
  1.8 4.8 %copy-start.11 = (f32[128]{0:T(128)S(1)}, f32[128]{0:T(128)}, u32[]{:S(2)}) copy-start(f32[128]{0:T(128)} %param.22) | copy-start | bytes 1540
  1.9 11.7 %collective-permute-start.1 = (bf16[3,384,128]{2,1,0:T(8,128)(2,1)S(1)}, bf16[3,384,128]{2,1,0:T(8,128)(2,1)S(1)}, u32[]{:S(2)}, u32[]{:S(2)}) collective-permute-start(bf16[3,384,128]{2,1,0:T(8,128)(2,1)S(1)} %get-tuple-element.33), channel_id=1, source_target_pairs={{0,7},{1,6},{2,5},{3,4},{4,3},{5,2},{6,1},{7,0},{8,16},{9,17},{10,... | collective-permute-start | bytes 884744 | tf_op jit(solution)/shard_map/ppermute | solution.py:436
  5.3 9.6 %collective-permute-start = (bf16[3,384,128]{2,1,0:T(8,128)(2,1)S(1)}, bf16[3,384,128]{2,1,0:T(8,128)(2,1)S(1)}, u32[]{:S(2)}, u32[]{:S(2)}) collective-permute-start(bf16[3,384,128]{2,1,0:T(8,128)(2,1)S(1)} %get-tuple-element.32), channel_id=1, source_target_pairs={{0,8},{1,9},{2,10},{3,11},{4,12},{5,13},{6,14},{7,15},{8,0},{9,1},... | collective-permute-start | bytes 884744 | tf_op jit(solution)/shard_map/ppermute | solution.py:435
  6.6 6.7 %copy-start = (bf16[128,512]{1,0:T(8,128)(2,1)S(1)}, bf16[128,512]{1,0:T(8,128)(2,1)}, u32[]{:S(2)}) copy-start(bf16[128,512]{1,0:T(8,128)(2,1)} %up.1) | copy-start | bytes 393220
  6.6 6.8 %copy-start.1 = (bf16[512,128]{1,0:T(8,128)(2,1)S(1)}, bf16[512,128]{1,0:T(8,128)(2,1)}, u32[]{:S(2)}) copy-start(bf16[512,128]{1,0:T(8,128)(2,1)} %down.1) | copy-start | bytes 393220
  14.9 4.7 %collective-permute-start.2 = (bf16[14,3,128]{2,1,0:T(4,128)(2,1)S(1)}, bf16[14,3,128]{2,1,0:T(4,128)(2,1)S(1)}, u32[]{:S(2)}, u32[]{:S(2)}) collective-permute-start(bf16[14,3,128]{2,1,0:T(4,128)(2,1)S(1)} %pad_maximum_fusion.4), channel_id=1, source_target_pairs={{0,1},{1,2},{2,3},{3,4},{4,5},{5,6},{6,7},{7,0},{8,9},{9,10},{10,1... | collective-permute-start | bytes 32264 | tf_op jit(solution)/shard_map/ppermute | solution.py:443
  15.0 4.6 %copy-start.4 = (bf16[8,384,128]{2,1,0:T(8,128)(2,1)S(1)}, bf16[8,384,128]{2,1,0:T(8,128)(2,1)}, u32[]{:S(2)}) copy-start(bf16[8,384,128]{2,1,0:T(8,128)(2,1)} %forcing.1) | copy-start | bytes 2359300
  15.0 4.6 %copy-start.5 = (bf16[8,384,128]{2,1,0:T(8,128)(2,1)S(1)}, bf16[8,384,128]{2,1,0:T(8,128)(2,1)}, u32[]{:S(2)}) copy-start(bf16[8,384,128]{2,1,0:T(8,128)(2,1)} %cotangent.1) | copy-start | bytes 2359300
  15.1 4.6 %copy-start.8 = (s32[6144]{0:T(1024)S(1)}, s32[6144]{0:T(1024)}, u32[]{:S(2)}) copy-start(s32[6144]{0:T(1024)} %param.32) | copy-start | bytes 73732
  15.1 4.6 %copy-start.9 = (s32[8,384]{1,0:T(8,128)S(1)}, s32[8,384]{1,0:T(8,128)}, u32[]{:S(2)}) copy-start(s32[8,384]{1,0:T(8,128)} %land.1) | copy-start | bytes 36868
  15.1 4.6 %copy-start.10 = (f32[512]{0:T(512)S(1)}, f32[512]{0:T(512)}, u32[]{:S(2)}) copy-start(f32[512]{0:T(512)} %param.26) | copy-start | bytes 6148
  15.1 4.6 %copy-start.12 = (f32[16]{0:T(128)S(1)}, f32[16]{0:T(128)}, u32[]{:S(2)}) copy-start(f32[16]{0:T(128)} %weight_table.1) | copy-start | bytes 196
  15.1 4.6 %copy-start.13 = (f32[128]{0:T(128)S(1)}, f32[128]{0:T(128)}, u32[]{:S(2)}) copy-start(f32[128]{0:T(128)} %param.23) | copy-start | bytes 1540
  15.1 4.6 %copy-start.14 = (f32[128]{0:T(128)S(1)}, f32[128]{0:T(128)}, u32[]{:S(2)}) copy-start(f32[128]{0:T(128)} %param.24) | copy-start | bytes 1540
  15.1 4.6 %copy-start.15 = (f32[128]{0:T(128)S(1)}, f32[128]{0:T(128)}, u32[]{:S(2)}) copy-start(f32[128]{0:T(128)} %param.28) | copy-start | bytes 1540
  15.1 4.6 %copy-start.16 = (f32[128]{0:T(128)S(1)}, f32[128]{0:T(128)}, u32[]{:S(2)}) copy-start(f32[128]{0:T(128)} %param.29) | copy-start | bytes 1540
  15.1 4.6 %copy-start.18 = (f32[8,384,128]{2,1,0:T(8,128)S(1)}, f32[8,384,128]{2,1,0:T(8,128)}, u32[]{:S(2)}) copy-start(f32[8,384,128]{2,1,0:T(8,128)} %copy-done.17) | copy-start | bytes 4718596
  15.2 4.5 %collective-permute-start.3 = (bf16[14,3,128]{2,1,0:T(4,128)(2,1)S(1)}, bf16[14,3,128]{2,1,0:T(4,128)(2,1)S(1)}, u32[]{:S(2)}, u32[]{:S(2)}) collective-permute-start(bf16[14,3,128]{2,1,0:T(4,128)(2,1)S(1)} %pad_maximum_fusion.5), channel_id=1, source_target_pairs={{1,0},{2,1},{3,2},{4,3},{5,4},{6,5},{7,6},{0,7},{9,8},{10,9},{11,1... | collective-permute-start | bytes 32264 | tf_op jit(solution)/shard_map/ppermute | solution.py:444
  44.3 6.3 %collective-permute-start.4 = (bf16[8192,128]{1,0:T(8,128)(2,1)S(1)}, bf16[8192,128]{1,0:T(8,128)(2,1)S(1)}, u32[]{:S(2)}, u32[]{:S(2)}) collective-permute-start(bf16[8192,128]{1,0:T(8,128)(2,1)S(1)} %get-tuple-element.40), channel_id=1, source_target_pairs={{0,1},{1,0},{2,3},{3,2},{4,5},{5,4},{6,7},{7,6},{8,9},{9,8},{10,11... | collective-permute-start | bytes 6291464 | tf_op jit(solution)/shard_map/ppermute | solution.py:390
  52.3 16.4 %collective-permute-start.6 = (bf16[2048,128]{1,0:T(8,128)(2,1)}, bf16[2048,128]{1,0:T(8,128)(2,1)}, u32[]{:S(2)}, u32[]{:S(2)}) collective-permute-start(bf16[2048,128]{1,0:T(8,128)(2,1)} %get-tuple-element.69), channel_id=1, source_target_pairs={{0,4},{1,5},{2,6},{3,7},{4,0},{5,1},{6,2},{7,3},{8,12},{9,13},{10,... | collective-permute-start | bytes 1572872 | tf_op jit(solution)/shard_map/ppermute | solution.py:390
  52.9 17.3 %collective-permute-start.5 = (bf16[2048,128]{1,0:T(8,128)(2,1)}, bf16[2048,128]{1,0:T(8,128)(2,1)}, u32[]{:S(2)}, u32[]{:S(2)}) collective-permute-start(bf16[2048,128]{1,0:T(8,128)(2,1)} %get-tuple-element.70), channel_id=1, source_target_pairs={{0,2},{1,3},{2,0},{3,1},{4,6},{5,7},{6,4},{7,5},{8,10},{9,11},{10,... | collective-permute-start | bytes 1572872 | tf_op jit(solution)/shard_map/ppermute | solution.py:390
  56.3 17.9 %all-to-all-start = ((bf16[32,34,128]{2,1,0:T(8,128)(2,1)}), bf16[32,34,128]{2,1,0:T(8,128)(2,1)S(1)}, u32[]{:S(2)}, u32[]{:S(2)}) async-start(bf16[32,34,128]{2,1,0:T(8,128)(2,1)} %reshape.83), calls=%async_computation | async-start | bytes 655360 | tf_op jit(solution)/shard_map/all_to_all | solution.py:555
  71.5 8.9 %collective-permute-start.8 = (bf16[1024,128]{1,0:T(8,128)(2,1)S(1)}, bf16[1024,128]{1,0:T(8,128)(2,1)S(1)}, u32[]{:S(2)}, u32[]{:S(2)}) collective-permute-start(bf16[1024,128]{1,0:T(8,128)(2,1)S(1)} %get-tuple-element.67), channel_id=1, source_target_pairs={{0,2},{1,3},{2,0},{3,1},{4,6},{5,7},{6,4},{7,5},{8,10},{9,11},{10,... | collective-permute-start | bytes 786440 | tf_op jit(solution)/shard_map/ppermute | solution.py:390
  73.5 7.0 %collective-permute-start.7 = (bf16[1024,128]{1,0:T(8,128)(2,1)S(1)}, bf16[1024,128]{1,0:T(8,128)(2,1)S(1)}, u32[]{:S(2)}, u32[]{:S(2)}) collective-permute-start(bf16[1024,128]{1,0:T(8,128)(2,1)S(1)} %get-tuple-element.68), channel_id=1, source_target_pairs={{0,4},{1,5},{2,6},{3,7},{4,0},{5,1},{6,2},{7,3},{8,12},{9,13},{10,... | collective-permute-start | bytes 786440 | tf_op jit(solution)/shard_map/ppermute | solution.py:390
  75.0 17.2 %all-to-all-start.1 = ((bf16[32,34,128]{2,1,0:T(8,128)(2,1)}), bf16[32,34,128]{2,1,0:T(8,128)(2,1)S(1)}, u32[]{:S(2)}, u32[]{:S(2)}) async-start(bf16[32,34,128]{2,1,0:T(8,128)(2,1)} %broadcast_in_dim.10), calls=%async_computation.1 | async-start | bytes 655360 | tf_op jit(solution)/shard_map/all_to_all | solution.py:558
  82.9 11.6 %collective-permute-start.9 = (bf16[512,128]{1,0:T(8,128)(2,1)S(1)}, bf16[512,128]{1,0:T(8,128)(2,1)S(1)}, u32[]{:S(2)}, u32[]{:S(2)}) collective-permute-start(bf16[512,128]{1,0:T(8,128)(2,1)S(1)} %pad_maximum_fusion.1), channel_id=1, source_target_pairs={{0,8},{8,0},{16,24},{24,16},{1,9},{9,1},{17,25},{25,17},{2,10},{10... | collective-permute-start | bytes 393224 | tf_op jit(solution)/shard_map/ppermute | solution.py:550
  84.7 15.4 %collective-permute-start.10 = (bf16[512,128]{1,0:T(8,128)(2,1)S(1)}, bf16[512,128]{1,0:T(8,128)(2,1)S(1)}, u32[]{:S(2)}, u32[]{:S(2)}) collective-permute-start(bf16[512,128]{1,0:T(8,128)(2,1)S(1)} %pad_maximum_fusion.2), channel_id=1, source_target_pairs={{0,16},{8,24},{16,0},{24,8},{1,17},{9,25},{17,1},{25,9},{2,18},{10... | collective-permute-start | bytes 393224 | tf_op jit(solution)/shard_map/ppermute | solution.py:550
  87.3 12.9 %collective-permute-start.11 = (bf16[512,128]{1,0:T(8,128)(2,1)S(1)}, bf16[512,128]{1,0:T(8,128)(2,1)S(1)}, u32[]{:S(2)}, u32[]{:S(2)}) collective-permute-start(bf16[512,128]{1,0:T(8,128)(2,1)S(1)} %pad_maximum_fusion.3), channel_id=1, source_target_pairs={{0,24},{8,16},{16,8},{24,0},{1,25},{9,17},{17,9},{25,1},{2,26},{10... | collective-permute-start | bytes 393224 | tf_op jit(solution)/shard_map/ppermute | solution.py:550
  (3 other events, 4.1 us)

commit v13 on v12

--- a/solution.py
+++ b/solution.py
@@ -12,7 +12,7 @@
 TAPS = 7
 MARGIN = 3
 BATCH = 16
-BATCHES = 2
+BATCHES = 4
 SMALL = 8
 ROUND = 2
 gelu_scale = 0.7978845608028654
@@ -191,23 +191,26 @@
     looked_up = jnp.zeros(index.shape, f32)
     for k in range(weight_table.shape[0]):
         looked_up = jnp.where(index == k, weight_table[k], looked_up)
-    entry_weights[...] = looked_up
     acc_up[...] = jnp.zeros_like(acc_up)
     acc_down[...] = jnp.zeros_like(acc_down)
     group = 2
     size = group * cols
     fan = terms.shape[0] // (ROUND * size)
     lines = fan * size // channels
-
-    def column(ref, first, count):
-        width = ref.shape[1]
-        return jnp.concatenate(
-            [
-                jnp.broadcast_to(ref[pl.ds(first + k, 1), :].astype(f32), (channels, width)).T
-                for k in range(count)
-            ],
-            axis=0,
-        )
+    for k in range(rows // group):
+        entry_weights[k] = looked_up[k * lines : (k + 1) * lines]
+
+    def columns(step):
+        first = step * group
+        stacked = [entry_weights[step]]
+        for k in range(group):
+            mask = land[pl.ds(first + k, 1), :].astype(f32)
+            stacked += [mask[:, at : at + channels] for at in range(0, cols, channels)]
+        used = lines + group * cols // channels
+        stacked.append(jnp.zeros((channels - used, channels), f32))
+        turned = jnp.concatenate(stacked, axis=0).T
+        wide = [jnp.broadcast_to(turned[:, j : j + 1], (channels, channels)) for j in range(used)]
+        return jnp.concatenate(wide[:lines], axis=0), jnp.concatenate(wide[lines:], axis=0)
 
     def mlp_step(step, place):
         first = step * group
@@ -228,7 +231,7 @@
             0.5 * gelu_scale + 1.5 * gelu_scale * cubic_coef * square
         )
         projected = jnp.dot(hidden, down[...], preferred_element_type=f32) + downb[...]
-        ocean = column(land, first, group)
+        spread[...], ocean = columns(step)
         own = state[pl.ds(first, group)].reshape(size, channels).astype(f32)
         out = ocean * (own + scale[...] * projected)
         result[pl.ds(first, group)] = out.astype(bf16).reshape(group, cols, channels)
@@ -237,7 +240,6 @@
         grad_hidden = jnp.dot(grad_out, down_t[...], preferred_element_type=f32)
         grad_pre = (grad_hidden * slope).astype(bf16)
         gmix = jnp.dot(grad_pre, up_t[...], preferred_element_type=f32)
-        spread[...] = column(entry_weights, step * lines, lines)
         for k in range(fan):
             weights = spread[pl.ds(k, size, stride=fan), :]
             terms[pl.ds(k * ROUND * size + place * size, size), :] = weights * gmix
@@ -489,7 +491,7 @@
             pltpu.VMEM((2, rows + 2 * MARGIN, 24, channels), f32),
             pltpu.VMEM((channels, hid), f32),
             pltpu.VMEM((channels, hid), f32),
-            pltpu.VMEM((entries // channels, channels), f32),
+            pltpu.VMEM((rows // 2, 2 * entries // rows // channels, channels), f32),
             pltpu.VMEM((2 * fan * cols, channels), f32),
             pltpu.VMEM((ROUND * 2 * fan * cols, channels), f32),
             pltpu.VMEM((2 * half_rows, channels), f32),

time: 101 us -> 98.4 us (0.974)
  Pallas kernels: 38 us -> 35.1 us
    pallas_call x1, Pallas kernels: 24.5 us -> 21.5 us  [on_device(): pl.pallas_call(block_kernel, out_shape=(shape((rows, cols, channels), bf1...]
  transfers between devices with their start and end apart: 14 -> 14, of which waited for: 5 -> 5; matrix products, arithmetic and copies ran while one was open for 8% -> 8% of each run, Pallas kernels for 13% -> 14%
where the time goes in v13:
time: 98.4 us; the launch traced here: 97.9 us
  Pallas kernels  35.1 us (36%)
  starting transfers between devices  27.5 us (28%)
  waiting for transfers between devices  21.3 us (22%)
  local copies, waits for them, and re-layouts  6.59 us (7%)
  other arithmetic  6.3 us (6%)
  between operations  1.14 us (1%)
    pallas_call x1, Pallas kernels, on_device(): pl.pallas_call(block_kernel, out_shape=(shape((rows, cols, channels), bf1...  21.5 us
    all_to_all x2, starting transfers between devices, on_device(): lax.all_to_all(total, ('lat', 'lon'), split_axis=0, concat_axis=0, tiled=...  9.86 us
    ppermute x5, waiting for transfers between devices, swap_bit(): return lax.ppermute(array, 'lon', pairs)  9.55 us
    pallas_call x1, Pallas kernels, on_device(): pl.pallas_call(conv_grad_kernel, out_shape=shape((dw_rows, channels), f32...  6.17 us
    ppermute x3, waiting for transfers between devices, on_device(): lax.ppermute(for_band(distance).astype(bf16), 'lat', pairs)  5.71 us
    ppermute x5, starting transfers between devices, swap_bit(): return lax.ppermute(array, 'lon', pairs)  5.64 us
    pallas_call x1, Pallas kernels, on_device(): pl.pallas_call(functools.partial(inner_conv_kernel, lat_count, lon_count,...  5.54 us
    all_to_all x2, waiting for transfers between devices, on_device(): lax.all_to_all(total, ('lat', 'lon'), split_axis=0, concat_axis=0, tiled=...  4.75 us
  transfers between devices with their start and end apart: 14, of which 5 were waited for; matrix products, arithmetic and copies ran while one was open for 8% of the time, Pallas kernels for 14%

profile of v13, /device:TPU:0, one launch (start us, length us, event | category | flops | bytes accessed | tf_op | source)
XLA Modules:
  0.0 97.9 jit_solution(15412423206801245610)
XLA Ops:
  0.6 1.1 %copy-done.2 = bf16[8,384,128]{2,1,0:T(8,128)(2,1)S(1)} copy-done((bf16[8,384,128]{2,1,0:T(8,128)(2,1)S(1)}, bf16[8,384,128]{2,1,0:T(8,128)(2,1)}, u32[]{:S(2)}) %copy-start.2) | copy-done | bytes 786456
  1.9 3.4 %collective-permute-start.1 = (bf16[3,384,128]{2,1,0:T(8,128)(2,1)S(1)}, bf16[3,384,128]{2,1,0:T(8,128)(2,1)S(1)}, u32[]{:S(2)}, u32[]{:S(2)}) collective-permute-start(bf16[3,384,128]{2,1,0:T(8,128)(2,1)S(1)} %get-tuple-element.33), channel_id=1, source_target_pairs={{0,7},{1,6},{2,5},{3,4},{4,3},{5,2},{6,1},{7,0},{8,16},{9,17},{10,... | collective-permute-start | bytes 884744 | tf_op jit(solution)/shard_map/ppermute | solution.py:438
  5.3 1.3 %collective-permute-start = (bf16[3,384,128]{2,1,0:T(8,128)(2,1)S(1)}, bf16[3,384,128]{2,1,0:T(8,128)(2,1)S(1)}, u32[]{:S(2)}, u32[]{:S(2)}) collective-permute-start(bf16[3,384,128]{2,1,0:T(8,128)(2,1)S(1)} %get-tuple-element.32), channel_id=1, source_target_pairs={{0,8},{1,9},{2,10},{3,11},{4,12},{5,13},{6,14},{7,15},{8,0},{9,1},... | collective-permute-start | bytes 884744 | tf_op jit(solution)/shard_map/ppermute | solution.py:437
  6.6 5.5 %inner_conv.1 = (f32[8,384,128]{2,1,0:T(8,128)S(1)}, s32[48,128]{1,0:T(8,128)S(1)}, s32[48,128]{1,0:T(8,128)S(1)}) custom-call(bf16[8,384,128]{2,1,0:T(8,128)(2,1)S(1)} %copy-done.3, f32[49,128]{1,0:T(8,128)S(1)} %reshape.87.dw, f32[1,128]{1,0:T(1,128)S(1)} %bitcast.27, s32[48,128]{1,0:T(8,128)S(1)} %bitcast.23, s32[48,128]{1,0:T(8,128)S(1)} %bitcast.24), custom_call_target="tpu_custom_call" | custom-call | flops 7000000000 | tf_op jit(solution)/shard_map/inner_conv/pallas_call | solution.py:455
  12.2 1.2 %copy-done.17 = f32[8,384,128]{2,1,0:T(8,128)} copy-done((f32[8,384,128]{2,1,0:T(8,128)}, f32[8,384,128]{2,1,0:T(8,128)S(1)}, u32[]{:S(2)}) %copy-start.17) | copy-done | bytes 1572888
  13.6 1.2 %collective-permute-done = bf16[3,384,128]{2,1,0:T(8,128)(2,1)S(1)} collective-permute-done((bf16[3,384,128]{2,1,0:T(8,128)(2,1)S(1)}, bf16[3,384,128]{2,1,0:T(8,128)(2,1)S(1)}, u32[]{:S(2)}, u32[]{:S(2)}) %collective-permute-start) | collective-permute-done | bytes 294944 | tf_op jit(solution)/shard_map/ppermute | solution.py:437
  15.2 2.7 %collective-permute-start.3 = (bf16[14,3,128]{2,1,0:T(4,128)(2,1)S(1)}, bf16[14,3,128]{2,1,0:T(4,128)(2,1)S(1)}, u32[]{:S(2)}, u32[]{:S(2)}) collective-permute-start(bf16[14,3,128]{2,1,0:T(4,128)(2,1)S(1)} %pad_maximum_fusion.5), channel_id=1, source_target_pairs={{1,0},{2,1},{3,2},{4,3},{5,4},{6,5},{7,6},{0,7},{9,8},{10,9},{11,1... | collective-permute-start | bytes 32264 | tf_op jit(solution)/shard_map/ppermute | solution.py:446
  17.8 1.8 %halo_conv.1.halo = f32[6,384,128]{2,1,0:T(8,128)S(1)} custom-call(bf16[3,384,128]{2,1,0:T(8,128)(2,1)S(1)} %get-tuple-element.74.south, bf16[3,384,128]{2,1,0:T(8,128)(2,1)S(1)} %get-tuple-element.73.north, f32[49,128]{1,0:T(8,128)S(1)} %reshape.87.dw), custom_call_target="tpu_custom_call" | custom-call | flops 2000000000 | tf_op jit(solution)/shard_map/halo_conv/pallas_call | solution.py:467
  19.8 21.5 %block.1 = (bf16[8,384,128]{2,1,0:T(8,128)(2,1)}, f32[2048,128]{1,0:T(8,128)S(1)}, f32[2048,128]{1,0:T(8,128)S(1)}, f32[2048,128]{1,0:T(8,128)S(1)}, f32[2048,12...) custom-call(bf16[8,384,128]{2,1,0:T(8,128)(2,1)S(1)} %copy-done.3, ...), custom_call_target="tpu_custom_call" | custom-call | flops 28000000000 | tf_op jit(solution)/shard_map/block/pallas_call | solution.py:478
  41.4 6.2 %conv_grad.1 = f32[64,128]{1,0:T(8,128)S(1)} custom-call(bf16[8,384,128]{2,1,0:T(8,128)(2,1)S(1)} %copy-done.3, bf16[3,384,128]{2,1,0:T(8,128)(2,1)S(1)} %get-tuple-element.74.south, bf16[3,384,128]{2,1,0:T(8,128)(2,1)S(1)} %get-tuple-element.73.north, bf16[14,3,128]{2,1,0:T(4,128)(2,1)S(1)} %collective-permute-done.2.left, ...), custom_call_target="tpu_custom_call" | custom-call | flops 8999999488 | tf_op jit(solution)/shard_map/conv_grad/pallas_call | solution.py:517
  47.6 1.5 %add_convert_fusion = (bf16[2048,128]{1,0:T(8,128)(2,1)}, bf16[2048,128]{1,0:T(8,128)(2,1)}) fusion(f32[2048,128]{1,0:T(8,128)S(1)} %get-tuple-element.45, bf16[8192,128]{1,0:T(8,128)(2,1)S(1)} %collective-permute-done.4, f32[2048,128]{1,0:T(8,128)S(1)} %get-tuple-element.44), kind=kLoop, calls=%fused_computation | loop fusion | flops 1572864 | bytes 4194304 | tf_op jit(solution)/shard_map/convert_element_type | solution.py:532
  49.3 0.5 collective-permute-start.6
  49.9 2.7 %collective-permute-start.5 = (bf16[2048,128]{1,0:T(8,128)(2,1)}, bf16[2048,128]{1,0:T(8,128)(2,1)}, u32[]{:S(2)}, u32[]{:S(2)}) collective-permute-start(bf16[2048,128]{1,0:T(8,128)(2,1)} %get-tuple-element.70), channel_id=1, source_target_pairs={{0,2},{1,3},{2,0},{3,1},{4,6},{5,7},{6,4},{7,5},{8,10},{9,11},{10,... | collective-permute-start | bytes 1572872 | tf_op jit(solution)/shard_map/ppermute | solution.py:392
  52.7 0.8 reshape.83
  53.5 4.3 %all-to-all-start = ((bf16[32,34,128]{2,1,0:T(8,128)(2,1)}), bf16[32,34,128]{2,1,0:T(8,128)(2,1)S(1)}, u32[]{:S(2)}, u32[]{:S(2)}) async-start(bf16[32,34,128]{2,1,0:T(8,128)(2,1)} %reshape.83), calls=%async_computation | async-start | bytes 655360 | tf_op jit(solution)/shard_map/all_to_all | solution.py:557
  57.8 7.9 %collective-permute-done.6 = bf16[2048,128]{1,0:T(8,128)(2,1)} collective-permute-done((bf16[2048,128]{1,0:T(8,128)(2,1)}, bf16[2048,128]{1,0:T(8,128)(2,1)}, u32[]{:S(2)}, u32[]{:S(2)}) %collective-permute-start.6) | collective-permute-done | bytes 524320 | tf_op jit(solution)/shard_map/ppermute | solution.py:392
  65.7 1.6 %collective-permute-done.5 = bf16[2048,128]{1,0:T(8,128)(2,1)} collective-permute-done((bf16[2048,128]{1,0:T(8,128)(2,1)}, bf16[2048,128]{1,0:T(8,128)(2,1)}, u32[]{:S(2)}, u32[]{:S(2)}) %collective-permute-start.5) | collective-permute-done | bytes 524320 | tf_op jit(solution)/shard_map/ppermute | solution.py:392
  67.4 1.4 %add_convert_fusion.2 = (bf16[1024,128]{1,0:T(8,128)(2,1)S(1)}, bf16[1024,128]{1,0:T(8,128)(2,1)S(1)}) fusion(f32[2048,128]{1,0:T(8,128)S(1)} %get-tuple-element.47, bf16[2048,128]{1,0:T(8,128)(2,1)} %collective-permute-done.6, bf16[8192,128]{1,0:T(8,128)(2,1)} %copy-done.19, bf16[2048,128]{1,0:T(8,128)(2,1)} %collective-permute-done.5, ...), kind=kLoop, calls=%fused_computation.3 | loop fusion | flops 1310720 | bytes 2621440 | tf_op jit(solution)/shard_map/convert_element_type | solution.py:542
  68.7 2.0 %collective-permute-start.8 = (bf16[1024,128]{1,0:T(8,128)(2,1)S(1)}, bf16[1024,128]{1,0:T(8,128)(2,1)S(1)}, u32[]{:S(2)}, u32[]{:S(2)}) collective-permute-start(bf16[1024,128]{1,0:T(8,128)(2,1)S(1)} %get-tuple-element.67), channel_id=1, source_target_pairs={{0,2},{1,3},{2,0},{3,1},{4,6},{5,7},{6,4},{7,5},{8,10},{9,11},{10,... | collective-permute-start | bytes 786440 | tf_op jit(solution)/shard_map/ppermute | solution.py:392
  70.7 0.3 collective-permute-start.7
  71.1 0.8 broadcast_in_dim.10
  71.9 5.5 %all-to-all-start.1 = ((bf16[32,34,128]{2,1,0:T(8,128)(2,1)}), bf16[32,34,128]{2,1,0:T(8,128)(2,1)S(1)}, u32[]{:S(2)}, u32[]{:S(2)}) async-start(bf16[32,34,128]{2,1,0:T(8,128)(2,1)} %broadcast_in_dim.10), calls=%async_computation.1 | async-start | bytes 655360 | tf_op jit(solution)/shard_map/all_to_all | solution.py:560
  77.5 1.2 %convert_add_fusion = (f32[256,128]{1,0:T(8,128)S(1)}, bf16[256,128]{1,0:T(8,128)(2,1)S(1)}, bf16[256,128]{1,0:T(8,128)(2,1)S(1)}, bf16[256,128]{1,0:T(8,128)(2,1)S(1)}) fusion(f32[2048,128]{1,0:T(8,128)S(1)} %get-tuple-element.47, bf16[1024,128]{1,0:T(8,128)(2,1)S(1)} %collective-permute-done.8, bf16[2048,128]{1,0:T(8,128)(2,1)} %collective-permute-done.6, ...), kind=kLoop, calls=%fused_computation.15 | loop fusion | flops 884736 | bytes 1638400 | tf_op jit(solution)/shard_map/add | solution.py:531
  78.6 1.2 %convert_add_fusion.1 = (f32[256,128]{1,0:T(8,128)S(1)}, bf16[256,128]{1,0:T(8,128)(2,1)S(1)}, bf16[256,128]{1,0:T(8,128)(2,1)S(1)}, bf16[256,128]{1,0:T(8,128)(2,1)S(1)}) fusion(f32[2048,128]{1,0:T(8,128)S(1)} %get-tuple-element.39, bf16[1024,128]{1,0:T(8,128)(2,1)S(1)} %collective-permute-done.7, bf16[2048,128]{1,0:T(8,128)(2,1)} %collective-permute-done.5, ...), kind=kLoop, calls=%fused_computation.16 | loop fusion | flops 884736 | bytes 1638400 | tf_op jit(solution)/shard_map/add | solution.py:531
  79.9 1.8 %collective-permute-start.9 = (bf16[512,128]{1,0:T(8,128)(2,1)S(1)}, bf16[512,128]{1,0:T(8,128)(2,1)S(1)}, u32[]{:S(2)}, u32[]{:S(2)}) collective-permute-start(bf16[512,128]{1,0:T(8,128)(2,1)S(1)} %pad_maximum_fusion.1), channel_id=1, source_target_pairs={{0,8},{8,0},{16,24},{24,16},{1,9},{9,1},{17,25},{25,17},{2,10},{10... | collective-permute-start | bytes 393224 | tf_op jit(solution)/shard_map/ppermute | solution.py:552
  81.7 2.5 %collective-permute-start.10 = (bf16[512,128]{1,0:T(8,128)(2,1)S(1)}, bf16[512,128]{1,0:T(8,128)(2,1)S(1)}, u32[]{:S(2)}, u32[]{:S(2)}) collective-permute-start(bf16[512,128]{1,0:T(8,128)(2,1)S(1)} %pad_maximum_fusion.2), channel_id=1, source_target_pairs={{0,16},{8,24},{16,0},{24,8},{1,17},{9,25},{17,1},{25,9},{2,18},{10... | collective-permute-start | bytes 393224 | tf_op jit(solution)/shard_map/ppermute | solution.py:552
  84.5 4.8 %all-to-all-done.1 = bf16[32,34,128]{2,1,0:T(8,128)(2,1)S(1)} async-done(((bf16[32,34,128]{2,1,0:T(8,128)(2,1)}), bf16[32,34,128]{2,1,0:T(8,128)(2,1)S(1)}, u32[]{:S(2)}, u32[]{:S(2)}) %all-to-all-start.1) | async-done | bytes 278560 | tf_op jit(solution)/shard_map/all_to_all | solution.py:560
  89.3 0.7 fusion.3
  90.1 0.7 copy.30
  90.8 0.6 reshape.84
  91.4 5.7 %collective-permute-done.10 = bf16[512,128]{1,0:T(8,128)(2,1)S(1)} collective-permute-done((bf16[512,128]{1,0:T(8,128)(2,1)S(1)}, bf16[512,128]{1,0:T(8,128)(2,1)S(1)}, u32[]{:S(2)}, u32[]{:S(2)}) %collective-permute-start.10) | collective-permute-done | bytes 131104 | tf_op jit(solution)/shard_map/ppermute | solution.py:552
  97.1 0.8 fusion.1
  (71 shorter events, 1.4 us)
Async XLA Ops:
  1.8 4.8 %copy-start.20 = (bf16[7,7,128]{2,1,0:T(8,128)(2,1)S(1)}, bf16[7,7,128]{2,1,0:T(8,128)(2,1)}, u32[]{:S(2)}) copy-start(bf16[7,7,128]{2,1,0:T(8,128)(2,1)} %param.21) | copy-start | bytes 37636
  1.8 4.8 %copy-start.3 = (bf16[8,384,128]{2,1,0:T(8,128)(2,1)S(1)}, bf16[8,384,128]{2,1,0:T(8,128)(2,1)}, u32[]{:S(2)}) copy-start(bf16[8,384,128]{2,1,0:T(8,128)(2,1)} %state.6) | copy-start | bytes 2359300
  1.8 4.8 %copy-start.6 = (s32[6144,1]{0,1:T(1,128)S(1)}, s32[6144,1]{0,1:T(1,128)}, u32[]{:S(2)}) copy-start(s32[6144,1]{0,1:T(1,128)} %param.30) | copy-start | bytes 73732
  1.8 4.8 %copy-start.7 = (s32[6144]{0:T(1024)S(1)}, s32[6144]{0:T(1024)}, u32[]{:S(2)}) copy-start(s32[6144]{0:T(1024)} %param.31) | copy-start | bytes 73732
  1.8 4.8 %copy-start.11 = (f32[128]{0:T(128)S(1)}, f32[128]{0:T(128)}, u32[]{:S(2)}) copy-start(f32[128]{0:T(128)} %param.22) | copy-start | bytes 1540
  1.9 11.7 %collective-permute-start.1 = (bf16[3,384,128]{2,1,0:T(8,128)(2,1)S(1)}, bf16[3,384,128]{2,1,0:T(8,128)(2,1)S(1)}, u32[]{:S(2)}, u32[]{:S(2)}) collective-permute-start(bf16[3,384,128]{2,1,0:T(8,128)(2,1)S(1)} %get-tuple-element.33), channel_id=1, source_target_pairs={{0,7},{1,6},{2,5},{3,4},{4,3},{5,2},{6,1},{7,0},{8,16},{9,17},{10,... | collective-permute-start | bytes 884744 | tf_op jit(solution)/shard_map/ppermute | solution.py:438
  5.3 9.6 %collective-permute-start = (bf16[3,384,128]{2,1,0:T(8,128)(2,1)S(1)}, bf16[3,384,128]{2,1,0:T(8,128)(2,1)S(1)}, u32[]{:S(2)}, u32[]{:S(2)}) collective-permute-start(bf16[3,384,128]{2,1,0:T(8,128)(2,1)S(1)} %get-tuple-element.32), channel_id=1, source_target_pairs={{0,8},{1,9},{2,10},{3,11},{4,12},{5,13},{6,14},{7,15},{8,0},{9,1},... | collective-permute-start | bytes 884744 | tf_op jit(solution)/shard_map/ppermute | solution.py:437
  6.6 6.7 %copy-start = (bf16[128,512]{1,0:T(8,128)(2,1)S(1)}, bf16[128,512]{1,0:T(8,128)(2,1)}, u32[]{:S(2)}) copy-start(bf16[128,512]{1,0:T(8,128)(2,1)} %up.1) | copy-start | bytes 393220
  6.6 6.9 %copy-start.1 = (bf16[512,128]{1,0:T(8,128)(2,1)S(1)}, bf16[512,128]{1,0:T(8,128)(2,1)}, u32[]{:S(2)}) copy-start(bf16[512,128]{1,0:T(8,128)(2,1)} %down.1) | copy-start | bytes 393220
  14.9 4.7 %collective-permute-start.2 = (bf16[14,3,128]{2,1,0:T(4,128)(2,1)S(1)}, bf16[14,3,128]{2,1,0:T(4,128)(2,1)S(1)}, u32[]{:S(2)}, u32[]{:S(2)}) collective-permute-start(bf16[14,3,128]{2,1,0:T(4,128)(2,1)S(1)} %pad_maximum_fusion.4), channel_id=1, source_target_pairs={{0,1},{1,2},{2,3},{3,4},{4,5},{5,6},{6,7},{7,0},{8,9},{9,10},{10,1... | collective-permute-start | bytes 32264 | tf_op jit(solution)/shard_map/ppermute | solution.py:445
  15.0 4.6 %copy-start.4 = (bf16[8,384,128]{2,1,0:T(8,128)(2,1)S(1)}, bf16[8,384,128]{2,1,0:T(8,128)(2,1)}, u32[]{:S(2)}) copy-start(bf16[8,384,128]{2,1,0:T(8,128)(2,1)} %forcing.1) | copy-start | bytes 2359300
  15.0 4.6 %copy-start.5 = (bf16[8,384,128]{2,1,0:T(8,128)(2,1)S(1)}, bf16[8,384,128]{2,1,0:T(8,128)(2,1)}, u32[]{:S(2)}) copy-start(bf16[8,384,128]{2,1,0:T(8,128)(2,1)} %cotangent.1) | copy-start | bytes 2359300
  15.1 4.6 %copy-start.8 = (s32[6144]{0:T(1024)S(1)}, s32[6144]{0:T(1024)}, u32[]{:S(2)}) copy-start(s32[6144]{0:T(1024)} %param.32) | copy-start | bytes 73732
  15.1 4.6 %copy-start.9 = (s32[8,384]{1,0:T(8,128)S(1)}, s32[8,384]{1,0:T(8,128)}, u32[]{:S(2)}) copy-start(s32[8,384]{1,0:T(8,128)} %land.1) | copy-start | bytes 36868
  15.1 4.6 %copy-start.10 = (f32[512]{0:T(512)S(1)}, f32[512]{0:T(512)}, u32[]{:S(2)}) copy-start(f32[512]{0:T(512)} %param.26) | copy-start | bytes 6148
  15.1 4.6 %copy-start.12 = (f32[16]{0:T(128)S(1)}, f32[16]{0:T(128)}, u32[]{:S(2)}) copy-start(f32[16]{0:T(128)} %weight_table.1) | copy-start | bytes 196
  15.1 4.6 %copy-start.13 = (f32[128]{0:T(128)S(1)}, f32[128]{0:T(128)}, u32[]{:S(2)}) copy-start(f32[128]{0:T(128)} %param.23) | copy-start | bytes 1540
  15.1 4.6 %copy-start.14 = (f32[128]{0:T(128)S(1)}, f32[128]{0:T(128)}, u32[]{:S(2)}) copy-start(f32[128]{0:T(128)} %param.24) | copy-start | bytes 1540
  15.1 4.6 %copy-start.15 = (f32[128]{0:T(128)S(1)}, f32[128]{0:T(128)}, u32[]{:S(2)}) copy-start(f32[128]{0:T(128)} %param.28) | copy-start | bytes 1540
  15.1 4.6 %copy-start.16 = (f32[128]{0:T(128)S(1)}, f32[128]{0:T(128)}, u32[]{:S(2)}) copy-start(f32[128]{0:T(128)} %param.29) | copy-start | bytes 1540
  15.1 4.6 %copy-start.18 = (f32[8,384,128]{2,1,0:T(8,128)S(1)}, f32[8,384,128]{2,1,0:T(8,128)}, u32[]{:S(2)}) copy-start(f32[8,384,128]{2,1,0:T(8,128)} %copy-done.17) | copy-start | bytes 4718596
  15.2 4.5 %collective-permute-start.3 = (bf16[14,3,128]{2,1,0:T(4,128)(2,1)S(1)}, bf16[14,3,128]{2,1,0:T(4,128)(2,1)S(1)}, u32[]{:S(2)}, u32[]{:S(2)}) collective-permute-start(bf16[14,3,128]{2,1,0:T(4,128)(2,1)S(1)} %pad_maximum_fusion.5), channel_id=1, source_target_pairs={{1,0},{2,1},{3,2},{4,3},{5,4},{6,5},{7,6},{0,7},{9,8},{10,9},{11,1... | collective-permute-start | bytes 32264 | tf_op jit(solution)/shard_map/ppermute | solution.py:446
  41.3 6.3 %collective-permute-start.4 = (bf16[8192,128]{1,0:T(8,128)(2,1)S(1)}, bf16[8192,128]{1,0:T(8,128)(2,1)S(1)}, u32[]{:S(2)}, u32[]{:S(2)}) collective-permute-start(bf16[8192,128]{1,0:T(8,128)(2,1)S(1)} %get-tuple-element.40), channel_id=1, source_target_pairs={{0,1},{1,0},{2,3},{3,2},{4,5},{5,4},{6,7},{7,6},{8,9},{9,8},{10,11... | collective-permute-start | bytes 6291464 | tf_op jit(solution)/shard_map/ppermute | solution.py:392
  49.3 16.4 %collective-permute-start.6 = (bf16[2048,128]{1,0:T(8,128)(2,1)}, bf16[2048,128]{1,0:T(8,128)(2,1)}, u32[]{:S(2)}, u32[]{:S(2)}) collective-permute-start(bf16[2048,128]{1,0:T(8,128)(2,1)} %get-tuple-element.69), channel_id=1, source_target_pairs={{0,4},{1,5},{2,6},{3,7},{4,0},{5,1},{6,2},{7,3},{8,12},{9,13},{10,... | collective-permute-start | bytes 1572872 | tf_op jit(solution)/shard_map/ppermute | solution.py:392
  49.9 17.5 %collective-permute-start.5 = (bf16[2048,128]{1,0:T(8,128)(2,1)}, bf16[2048,128]{1,0:T(8,128)(2,1)}, u32[]{:S(2)}, u32[]{:S(2)}) collective-permute-start(bf16[2048,128]{1,0:T(8,128)(2,1)} %get-tuple-element.70), channel_id=1, source_target_pairs={{0,2},{1,3},{2,0},{3,1},{4,6},{5,7},{6,4},{7,5},{8,10},{9,11},{10,... | collective-permute-start | bytes 1572872 | tf_op jit(solution)/shard_map/ppermute | solution.py:392
  53.5 17.6 %all-to-all-start = ((bf16[32,34,128]{2,1,0:T(8,128)(2,1)}), bf16[32,34,128]{2,1,0:T(8,128)(2,1)S(1)}, u32[]{:S(2)}, u32[]{:S(2)}) async-start(bf16[32,34,128]{2,1,0:T(8,128)(2,1)} %reshape.83), calls=%async_computation | async-start | bytes 655360 | tf_op jit(solution)/shard_map/all_to_all | solution.py:557
  68.7 8.7 %collective-permute-start.8 = (bf16[1024,128]{1,0:T(8,128)(2,1)S(1)}, bf16[1024,128]{1,0:T(8,128)(2,1)S(1)}, u32[]{:S(2)}, u32[]{:S(2)}) collective-permute-start(bf16[1024,128]{1,0:T(8,128)(2,1)S(1)} %get-tuple-element.67), channel_id=1, source_target_pairs={{0,2},{1,3},{2,0},{3,1},{4,6},{5,7},{6,4},{7,5},{8,10},{9,11},{10,... | collective-permute-start | bytes 786440 | tf_op jit(solution)/shard_map/ppermute | solution.py:392
  70.7 6.7 %collective-permute-start.7 = (bf16[1024,128]{1,0:T(8,128)(2,1)S(1)}, bf16[1024,128]{1,0:T(8,128)(2,1)S(1)}, u32[]{:S(2)}, u32[]{:S(2)}) collective-permute-start(bf16[1024,128]{1,0:T(8,128)(2,1)S(1)} %get-tuple-element.68), channel_id=1, source_target_pairs={{0,4},{1,5},{2,6},{3,7},{4,0},{5,1},{6,2},{7,3},{8,12},{9,13},{10,... | collective-permute-start | bytes 786440 | tf_op jit(solution)/shard_map/ppermute | solution.py:392
  71.9 17.3 %all-to-all-start.1 = ((bf16[32,34,128]{2,1,0:T(8,128)(2,1)}), bf16[32,34,128]{2,1,0:T(8,128)(2,1)S(1)}, u32[]{:S(2)}, u32[]{:S(2)}) async-start(bf16[32,34,128]{2,1,0:T(8,128)(2,1)} %broadcast_in_dim.10), calls=%async_computation.1 | async-start | bytes 655360 | tf_op jit(solution)/shard_map/all_to_all | solution.py:560
  79.9 11.6 %collective-permute-start.9 = (bf16[512,128]{1,0:T(8,128)(2,1)S(1)}, bf16[512,128]{1,0:T(8,128)(2,1)S(1)}, u32[]{:S(2)}, u32[]{:S(2)}) collective-permute-start(bf16[512,128]{1,0:T(8,128)(2,1)S(1)} %pad_maximum_fusion.1), channel_id=1, source_target_pairs={{0,8},{8,0},{16,24},{24,16},{1,9},{9,1},{17,25},{25,17},{2,10},{10... | collective-permute-start | bytes 393224 | tf_op jit(solution)/shard_map/ppermute | solution.py:552
  81.7 15.4 %collective-permute-start.10 = (bf16[512,128]{1,0:T(8,128)(2,1)S(1)}, bf16[512,128]{1,0:T(8,128)(2,1)S(1)}, u32[]{:S(2)}, u32[]{:S(2)}) collective-permute-start(bf16[512,128]{1,0:T(8,128)(2,1)S(1)} %pad_maximum_fusion.2), channel_id=1, source_target_pairs={{0,16},{8,24},{16,0},{24,8},{1,17},{9,25},{17,1},{25,9},{2,18},{10... | collective-permute-start | bytes 393224 | tf_op jit(solution)/shard_map/ppermute | solution.py:552
  84.2 12.9 %collective-permute-start.11 = (bf16[512,128]{1,0:T(8,128)(2,1)S(1)}, bf16[512,128]{1,0:T(8,128)(2,1)S(1)}, u32[]{:S(2)}, u32[]{:S(2)}) collective-permute-start(bf16[512,128]{1,0:T(8,128)(2,1)S(1)} %pad_maximum_fusion.3), channel_id=1, source_target_pairs={{0,24},{8,16},{16,8},{24,0},{1,25},{9,17},{17,9},{25,1},{2,26},{10... | collective-permute-start | bytes 393224 | tf_op jit(solution)/shard_map/ppermute | solution.py:552
  (3 other events, 4.1 us)

commit v14 on v13

--- a/solution.py
+++ b/solution.py
@@ -212,12 +212,22 @@
         wide = [jnp.broadcast_to(turned[:, j : j + 1], (channels, channels)) for j in range(used)]
         return jnp.concatenate(wide[:lines], axis=0), jnp.concatenate(wide[lines:], axis=0)
 
+    share = 1.0 / channels
+    mean_one = jnp.full((channels, channels), share, bf16)
+    mean_both = jnp.full((2 * channels, channels), share, bf16)
+    corner = [
+        lax.broadcasted_iota(jnp.int32, (2 * channels, 2 * channels), d) < channels for d in range(2)
+    ]
+    mean_each = jnp.where(corner[0] == corner[1], share, 0.0).astype(bf16)
+
     def mlp_step(step, place):
         first = step * group
         here = field[pl.ds(first, group)].reshape(size, channels)
-        average = jnp.mean(here, axis=-1, keepdims=True)
+        high = here.astype(bf16)
+        low = (here - high.astype(f32)).astype(bf16)
+        average = jnp.dot(jnp.concatenate([high, low], axis=1), mean_both, preferred_element_type=f32)
         centred = here - average
-        variance = jnp.mean(centred * centred, axis=-1, keepdims=True)
+        variance = jnp.dot((centred * centred).astype(bf16), mean_one, preferred_element_type=f32)
         inv_std = lax.rsqrt(variance + 1e-06)
         normed = centred * inv_std
         force = forcing[pl.ds(first, group)].reshape(size, channels).astype(f32)
@@ -244,11 +254,9 @@
             weights = spread[pl.ds(k, size, stride=fan), :]
             terms[pl.ds(k * ROUND * size + place * size, size), :] = weights * gmix
         gained = gmix * gain[...]
-        gconv = inv_std * (
-            gained
-            - jnp.mean(gained, axis=-1, keepdims=True)
-            - normed * jnp.mean(gained * normed, axis=-1, keepdims=True)
-        )
+        pair = jnp.concatenate([gained.astype(bf16), (gained * normed).astype(bf16)], axis=1)
+        means = jnp.dot(pair, mean_each, preferred_element_type=f32)
+        gconv = inv_std * (gained - means[:, :channels] - normed * means[:, channels:])
         grad_conv[pl.ds(first, group)] = gconv.reshape(group, cols, channels)
         contract = (((0,), (0,)), ((), ()))
         acc_up[...] += lax.dot_general(mixed, grad_pre, contract, preferred_element_type=f32)

time: 98.4 us -> 99.9 us (1.015)
  Pallas kernels: 35.1 us -> 36.7 us
    pallas_call x1, Pallas kernels: 21.5 us -> 23.1 us  [on_device(): pl.pallas_call(block_kernel, out_shape=(shape((rows, cols, channels), bf1...]
where the time goes in v14:
time: 99.9 us; the launch traced here: 99.4 us
  Pallas kernels  36.7 us (37%)
  starting transfers between devices  27.4 us (27%)
  waiting for transfers between devices  21.3 us (21%)
  local copies, waits for them, and re-layouts  6.59 us (7%)
  other arithmetic  6.3 us (6%)
  between operations  1.14 us (1%)
    pallas_call x1, Pallas kernels, on_device(): pl.pallas_call(block_kernel, out_shape=(shape((rows, cols, channels), bf1...  23.1 us
    all_to_all x2, starting transfers between devices, on_device(): lax.all_to_all(total, ('lat', 'lon'), split_axis=0, concat_axis=0, tiled=...  9.65 us
    ppermute x5, waiting for transfers between devices, swap_bit(): return lax.ppermute(array, 'lon', pairs)  9.62 us
    pallas_call x1, Pallas kernels, on_device(): pl.pallas_call(conv_grad_kernel, out_shape=shape((dw_rows, channels), f32...  6.17 us
    ppermute x5, starting transfers between devices, swap_bit(): return lax.ppermute(array, 'lon', pairs)  5.72 us
    ppermute x3, waiting for transfers between devices, on_device(): lax.ppermute(for_band(distance).astype(bf16), 'lat', pairs)  5.71 us
    pallas_call x1, Pallas kernels, on_device(): pl.pallas_call(functools.partial(inner_conv_kernel, lat_count, lon_count,...  5.54 us
    all_to_all x2, waiting for transfers between devices, on_device(): lax.all_to_all(total, ('lat', 'lon'), split_axis=0, concat_axis=0, tiled=...  4.75 us
  transfers between devices with their start and end apart: 14, of which 5 were waited for; matrix products, arithmetic and copies ran while one was open for 8% of the time, Pallas kernels for 14%

profile of v14, /device:TPU:0, one launch (start us, length us, event | category | flops | bytes accessed | tf_op | source)
XLA Modules:
  0.0 99.4 jit_solution(10122309600242721843)
XLA Ops:
  0.6 1.1 %copy-done.2 = bf16[8,384,128]{2,1,0:T(8,128)(2,1)S(1)} copy-done((bf16[8,384,128]{2,1,0:T(8,128)(2,1)S(1)}, bf16[8,384,128]{2,1,0:T(8,128)(2,1)}, u32[]{:S(2)}) %copy-start.2) | copy-done | bytes 786456
  1.9 3.4 %collective-permute-start.1 = (bf16[3,384,128]{2,1,0:T(8,128)(2,1)S(1)}, bf16[3,384,128]{2,1,0:T(8,128)(2,1)S(1)}, u32[]{:S(2)}, u32[]{:S(2)}) collective-permute-start(bf16[3,384,128]{2,1,0:T(8,128)(2,1)S(1)} %get-tuple-element.33), channel_id=1, source_target_pairs={{0,7},{1,6},{2,5},{3,4},{4,3},{5,2},{6,1},{7,0},{8,16},{9,17},{10,... | collective-permute-start | bytes 884744 | tf_op jit(solution)/shard_map/ppermute | solution.py:446
  5.3 1.3 %collective-permute-start = (bf16[3,384,128]{2,1,0:T(8,128)(2,1)S(1)}, bf16[3,384,128]{2,1,0:T(8,128)(2,1)S(1)}, u32[]{:S(2)}, u32[]{:S(2)}) collective-permute-start(bf16[3,384,128]{2,1,0:T(8,128)(2,1)S(1)} %get-tuple-element.32), channel_id=1, source_target_pairs={{0,8},{1,9},{2,10},{3,11},{4,12},{5,13},{6,14},{7,15},{8,0},{9,1},... | collective-permute-start | bytes 884744 | tf_op jit(solution)/shard_map/ppermute | solution.py:445
  6.6 5.5 %inner_conv.1 = (f32[8,384,128]{2,1,0:T(8,128)S(1)}, s32[48,128]{1,0:T(8,128)S(1)}, s32[48,128]{1,0:T(8,128)S(1)}) custom-call(bf16[8,384,128]{2,1,0:T(8,128)(2,1)S(1)} %copy-done.3, f32[49,128]{1,0:T(8,128)S(1)} %reshape.87.dw, f32[1,128]{1,0:T(1,128)S(1)} %bitcast.27, s32[48,128]{1,0:T(8,128)S(1)} %bitcast.23, s32[48,128]{1,0:T(8,128)S(1)} %bitcast.24), custom_call_target="tpu_custom_call" | custom-call | flops 7000000000 | tf_op jit(solution)/shard_map/inner_conv/pallas_call | solution.py:463
  12.2 1.2 %copy-done.17 = f32[8,384,128]{2,1,0:T(8,128)} copy-done((f32[8,384,128]{2,1,0:T(8,128)}, f32[8,384,128]{2,1,0:T(8,128)S(1)}, u32[]{:S(2)}) %copy-start.17) | copy-done | bytes 1572888
  13.6 1.2 %collective-permute-done = bf16[3,384,128]{2,1,0:T(8,128)(2,1)S(1)} collective-permute-done((bf16[3,384,128]{2,1,0:T(8,128)(2,1)S(1)}, bf16[3,384,128]{2,1,0:T(8,128)(2,1)S(1)}, u32[]{:S(2)}, u32[]{:S(2)}) %collective-permute-start) | collective-permute-done | bytes 294944 | tf_op jit(solution)/shard_map/ppermute | solution.py:445
  15.2 2.7 %collective-permute-start.3 = (bf16[14,3,128]{2,1,0:T(4,128)(2,1)S(1)}, bf16[14,3,128]{2,1,0:T(4,128)(2,1)S(1)}, u32[]{:S(2)}, u32[]{:S(2)}) collective-permute-start(bf16[14,3,128]{2,1,0:T(4,128)(2,1)S(1)} %pad_maximum_fusion.5), channel_id=1, source_target_pairs={{1,0},{2,1},{3,2},{4,3},{5,4},{6,5},{7,6},{0,7},{9,8},{10,9},{11,1... | collective-permute-start | bytes 32264 | tf_op jit(solution)/shard_map/ppermute | solution.py:454
  17.8 1.8 %halo_conv.1.halo = f32[6,384,128]{2,1,0:T(8,128)S(1)} custom-call(bf16[3,384,128]{2,1,0:T(8,128)(2,1)S(1)} %get-tuple-element.74.south, bf16[3,384,128]{2,1,0:T(8,128)(2,1)S(1)} %get-tuple-element.73.north, f32[49,128]{1,0:T(8,128)S(1)} %reshape.87.dw), custom_call_target="tpu_custom_call" | custom-call | flops 2000000000 | tf_op jit(solution)/shard_map/halo_conv/pallas_call | solution.py:475
  19.8 23.1 %block.1 = (bf16[8,384,128]{2,1,0:T(8,128)(2,1)}, f32[2048,128]{1,0:T(8,128)S(1)}, f32[2048,128]{1,0:T(8,128)S(1)}, f32[2048,128]{1,0:T(8,128)S(1)}, f32[2048,12...) custom-call(bf16[8,384,128]{2,1,0:T(8,128)(2,1)S(1)} %copy-done.3, ...), custom_call_target="tpu_custom_call" | custom-call | flops 28000000000 | tf_op jit(solution)/shard_map/block/pallas_call | solution.py:486
  43.0 6.2 %conv_grad.1 = f32[64,128]{1,0:T(8,128)S(1)} custom-call(bf16[8,384,128]{2,1,0:T(8,128)(2,1)S(1)} %copy-done.3, bf16[3,384,128]{2,1,0:T(8,128)(2,1)S(1)} %get-tuple-element.74.south, bf16[3,384,128]{2,1,0:T(8,128)(2,1)S(1)} %get-tuple-element.73.north, bf16[14,3,128]{2,1,0:T(4,128)(2,1)S(1)} %collective-permute-done.2.left, ...), custom_call_target="tpu_custom_call" | custom-call | flops 8999999488 | tf_op jit(solution)/shard_map/conv_grad/pallas_call | solution.py:525
  49.2 1.5 %add_convert_fusion = (bf16[2048,128]{1,0:T(8,128)(2,1)}, bf16[2048,128]{1,0:T(8,128)(2,1)}) fusion(f32[2048,128]{1,0:T(8,128)S(1)} %get-tuple-element.45, bf16[8192,128]{1,0:T(8,128)(2,1)S(1)} %collective-permute-done.4, f32[2048,128]{1,0:T(8,128)S(1)} %get-tuple-element.44), kind=kLoop, calls=%fused_computation | loop fusion | flops 1572864 | bytes 4194304 | tf_op jit(solution)/shard_map/convert_element_type | solution.py:540
  50.9 0.5 collective-permute-start.6
  51.4 2.5 %collective-permute-start.5 = (bf16[2048,128]{1,0:T(8,128)(2,1)}, bf16[2048,128]{1,0:T(8,128)(2,1)}, u32[]{:S(2)}, u32[]{:S(2)}) collective-permute-start(bf16[2048,128]{1,0:T(8,128)(2,1)} %get-tuple-element.70), channel_id=1, source_target_pairs={{0,2},{1,3},{2,0},{3,1},{4,6},{5,7},{6,4},{7,5},{8,10},{9,11},{10,... | collective-permute-start | bytes 1572872 | tf_op jit(solution)/shard_map/ppermute | solution.py:400
  54.0 0.8 reshape.83
  54.8 4.3 %all-to-all-start = ((bf16[32,34,128]{2,1,0:T(8,128)(2,1)}), bf16[32,34,128]{2,1,0:T(8,128)(2,1)S(1)}, u32[]{:S(2)}, u32[]{:S(2)}) async-start(bf16[32,34,128]{2,1,0:T(8,128)(2,1)} %reshape.83), calls=%async_computation | async-start | bytes 655360 | tf_op jit(solution)/shard_map/all_to_all | solution.py:565
  59.1 8.3 %collective-permute-done.6 = bf16[2048,128]{1,0:T(8,128)(2,1)} collective-permute-done((bf16[2048,128]{1,0:T(8,128)(2,1)}, bf16[2048,128]{1,0:T(8,128)(2,1)}, u32[]{:S(2)}, u32[]{:S(2)}) %collective-permute-start.6) | collective-permute-done | bytes 524320 | tf_op jit(solution)/shard_map/ppermute | solution.py:400
  67.4 1.3 %collective-permute-done.5 = bf16[2048,128]{1,0:T(8,128)(2,1)} collective-permute-done((bf16[2048,128]{1,0:T(8,128)(2,1)}, bf16[2048,128]{1,0:T(8,128)(2,1)}, u32[]{:S(2)}, u32[]{:S(2)}) %collective-permute-start.5) | collective-permute-done | bytes 524320 | tf_op jit(solution)/shard_map/ppermute | solution.py:400
  68.7 1.4 %add_convert_fusion.2 = (bf16[1024,128]{1,0:T(8,128)(2,1)S(1)}, bf16[1024,128]{1,0:T(8,128)(2,1)S(1)}) fusion(f32[2048,128]{1,0:T(8,128)S(1)} %get-tuple-element.47, bf16[2048,128]{1,0:T(8,128)(2,1)} %collective-permute-done.6, bf16[8192,128]{1,0:T(8,128)(2,1)} %copy-done.19, bf16[2048,128]{1,0:T(8,128)(2,1)} %collective-permute-done.5, ...), kind=kLoop, calls=%fused_computation.3 | loop fusion | flops 1310720 | bytes 2621440 | tf_op jit(solution)/shard_map/convert_element_type | solution.py:550
  70.1 2.0 %collective-permute-start.8 = (bf16[1024,128]{1,0:T(8,128)(2,1)S(1)}, bf16[1024,128]{1,0:T(8,128)(2,1)S(1)}, u32[]{:S(2)}, u32[]{:S(2)}) collective-permute-start(bf16[1024,128]{1,0:T(8,128)(2,1)S(1)} %get-tuple-element.67), channel_id=1, source_target_pairs={{0,2},{1,3},{2,0},{3,1},{4,6},{5,7},{6,4},{7,5},{8,10},{9,11},{10,... | collective-permute-start | bytes 786440 | tf_op jit(solution)/shard_map/ppermute | solution.py:400
  72.1 0.7 collective-permute-start.7
  72.8 0.8 broadcast_in_dim.10
  73.6 5.4 %all-to-all-start.1 = ((bf16[32,34,128]{2,1,0:T(8,128)(2,1)}), bf16[32,34,128]{2,1,0:T(8,128)(2,1)S(1)}, u32[]{:S(2)}, u32[]{:S(2)}) async-start(bf16[32,34,128]{2,1,0:T(8,128)(2,1)} %broadcast_in_dim.10), calls=%async_computation.1 | async-start | bytes 655360 | tf_op jit(solution)/shard_map/all_to_all | solution.py:568
  79.0 1.2 %convert_add_fusion = (f32[256,128]{1,0:T(8,128)S(1)}, bf16[256,128]{1,0:T(8,128)(2,1)S(1)}, bf16[256,128]{1,0:T(8,128)(2,1)S(1)}, bf16[256,128]{1,0:T(8,128)(2,1)S(1)}) fusion(f32[2048,128]{1,0:T(8,128)S(1)} %get-tuple-element.47, bf16[1024,128]{1,0:T(8,128)(2,1)S(1)} %collective-permute-done.8, bf16[2048,128]{1,0:T(8,128)(2,1)} %collective-permute-done.6, ...), kind=kLoop, calls=%fused_computation.15 | loop fusion | flops 884736 | bytes 1638400 | tf_op jit(solution)/shard_map/add | solution.py:539
  80.2 1.2 %convert_add_fusion.1 = (f32[256,128]{1,0:T(8,128)S(1)}, bf16[256,128]{1,0:T(8,128)(2,1)S(1)}, bf16[256,128]{1,0:T(8,128)(2,1)S(1)}, bf16[256,128]{1,0:T(8,128)(2,1)S(1)}) fusion(f32[2048,128]{1,0:T(8,128)S(1)} %get-tuple-element.39, bf16[1024,128]{1,0:T(8,128)(2,1)S(1)} %collective-permute-done.7, bf16[2048,128]{1,0:T(8,128)(2,1)} %collective-permute-done.5, ...), kind=kLoop, calls=%fused_computation.16 | loop fusion | flops 884736 | bytes 1638400 | tf_op jit(solution)/shard_map/add | solution.py:539
  81.4 1.8 %collective-permute-start.9 = (bf16[512,128]{1,0:T(8,128)(2,1)S(1)}, bf16[512,128]{1,0:T(8,128)(2,1)S(1)}, u32[]{:S(2)}, u32[]{:S(2)}) collective-permute-start(bf16[512,128]{1,0:T(8,128)(2,1)S(1)} %pad_maximum_fusion.1), channel_id=1, source_target_pairs={{0,8},{8,0},{16,24},{24,16},{1,9},{9,1},{17,25},{25,17},{2,10},{10... | collective-permute-start | bytes 393224 | tf_op jit(solution)/shard_map/ppermute | solution.py:560
  83.2 2.5 %collective-permute-start.10 = (bf16[512,128]{1,0:T(8,128)(2,1)S(1)}, bf16[512,128]{1,0:T(8,128)(2,1)S(1)}, u32[]{:S(2)}, u32[]{:S(2)}) collective-permute-start(bf16[512,128]{1,0:T(8,128)(2,1)S(1)} %pad_maximum_fusion.2), channel_id=1, source_target_pairs={{0,16},{8,24},{16,0},{24,8},{1,17},{9,25},{17,1},{25,9},{2,18},{10... | collective-permute-start | bytes 393224 | tf_op jit(solution)/shard_map/ppermute | solution.py:560
  86.0 4.8 %all-to-all-done.1 = bf16[32,34,128]{2,1,0:T(8,128)(2,1)S(1)} async-done(((bf16[32,34,128]{2,1,0:T(8,128)(2,1)}), bf16[32,34,128]{2,1,0:T(8,128)(2,1)S(1)}, u32[]{:S(2)}, u32[]{:S(2)}) %all-to-all-start.1) | async-done | bytes 278560 | tf_op jit(solution)/shard_map/all_to_all | solution.py:568
  90.8 0.7 fusion.3
  91.6 0.7 copy.30
  92.3 0.6 reshape.84
  92.9 5.7 %collective-permute-done.10 = bf16[512,128]{1,0:T(8,128)(2,1)S(1)} collective-permute-done((bf16[512,128]{1,0:T(8,128)(2,1)S(1)}, bf16[512,128]{1,0:T(8,128)(2,1)S(1)}, u32[]{:S(2)}, u32[]{:S(2)}) %collective-permute-start.10) | collective-permute-done | bytes 131104 | tf_op jit(solution)/shard_map/ppermute | solution.py:560
  98.6 0.8 fusion.1
  (71 shorter events, 1.4 us)
Async XLA Ops:
  1.8 4.8 %copy-start.20 = (bf16[7,7,128]{2,1,0:T(8,128)(2,1)S(1)}, bf16[7,7,128]{2,1,0:T(8,128)(2,1)}, u32[]{:S(2)}) copy-start(bf16[7,7,128]{2,1,0:T(8,128)(2,1)} %param.21) | copy-start | bytes 37636
  1.8 4.8 %copy-start.3 = (bf16[8,384,128]{2,1,0:T(8,128)(2,1)S(1)}, bf16[8,384,128]{2,1,0:T(8,128)(2,1)}, u32[]{:S(2)}) copy-start(bf16[8,384,128]{2,1,0:T(8,128)(2,1)} %state.6) | copy-start | bytes 2359300
  1.8 4.8 %copy-start.6 = (s32[6144,1]{0,1:T(1,128)S(1)}, s32[6144,1]{0,1:T(1,128)}, u32[]{:S(2)}) copy-start(s32[6144,1]{0,1:T(1,128)} %param.30) | copy-start | bytes 73732
  1.8 4.8 %copy-start.7 = (s32[6144]{0:T(1024)S(1)}, s32[6144]{0:T(1024)}, u32[]{:S(2)}) copy-start(s32[6144]{0:T(1024)} %param.31) | copy-start | bytes 73732
  1.8 4.8 %copy-start.11 = (f32[128]{0:T(128)S(1)}, f32[128]{0:T(128)}, u32[]{:S(2)}) copy-start(f32[128]{0:T(128)} %param.22) | copy-start | bytes 1540
  1.9 11.7 %collective-permute-start.1 = (bf16[3,384,128]{2,1,0:T(8,128)(2,1)S(1)}, bf16[3,384,128]{2,1,0:T(8,128)(2,1)S(1)}, u32[]{:S(2)}, u32[]{:S(2)}) collective-permute-start(bf16[3,384,128]{2,1,0:T(8,128)(2,1)S(1)} %get-tuple-element.33), channel_id=1, source_target_pairs={{0,7},{1,6},{2,5},{3,4},{4,3},{5,2},{6,1},{7,0},{8,16},{9,17},{10,... | collective-permute-start | bytes 884744 | tf_op jit(solution)/shard_map/ppermute | solution.py:446
  5.3 9.6 %collective-permute-start = (bf16[3,384,128]{2,1,0:T(8,128)(2,1)S(1)}, bf16[3,384,128]{2,1,0:T(8,128)(2,1)S(1)}, u32[]{:S(2)}, u32[]{:S(2)}) collective-permute-start(bf16[3,384,128]{2,1,0:T(8,128)(2,1)S(1)} %get-tuple-element.32), channel_id=1, source_target_pairs={{0,8},{1,9},{2,10},{3,11},{4,12},{5,13},{6,14},{7,15},{8,0},{9,1},... | collective-permute-start | bytes 884744 | tf_op jit(solution)/shard_map/ppermute | solution.py:445
  6.6 6.7 %copy-start = (bf16[128,512]{1,0:T(8,128)(2,1)S(1)}, bf16[128,512]{1,0:T(8,128)(2,1)}, u32[]{:S(2)}) copy-start(bf16[128,512]{1,0:T(8,128)(2,1)} %up.1) | copy-start | bytes 393220
  6.6 6.9 %copy-start.1 = (bf16[512,128]{1,0:T(8,128)(2,1)S(1)}, bf16[512,128]{1,0:T(8,128)(2,1)}, u32[]{:S(2)}) copy-start(bf16[512,128]{1,0:T(8,128)(2,1)} %down.1) | copy-start | bytes 393220
  14.9 4.7 %collective-permute-start.2 = (bf16[14,3,128]{2,1,0:T(4,128)(2,1)S(1)}, bf16[14,3,128]{2,1,0:T(4,128)(2,1)S(1)}, u32[]{:S(2)}, u32[]{:S(2)}) collective-permute-start(bf16[14,3,128]{2,1,0:T(4,128)(2,1)S(1)} %pad_maximum_fusion.4), channel_id=1, source_target_pairs={{0,1},{1,2},{2,3},{3,4},{4,5},{5,6},{6,7},{7,0},{8,9},{9,10},{10,1... | collective-permute-start | bytes 32264 | tf_op jit(solution)/shard_map/ppermute | solution.py:453
  15.0 4.6 %copy-start.4 = (bf16[8,384,128]{2,1,0:T(8,128)(2,1)S(1)}, bf16[8,384,128]{2,1,0:T(8,128)(2,1)}, u32[]{:S(2)}) copy-start(bf16[8,384,128]{2,1,0:T(8,128)(2,1)} %forcing.1) | copy-start | bytes 2359300
  15.0 4.6 %copy-start.5 = (bf16[8,384,128]{2,1,0:T(8,128)(2,1)S(1)}, bf16[8,384,128]{2,1,0:T(8,128)(2,1)}, u32[]{:S(2)}) copy-start(bf16[8,384,128]{2,1,0:T(8,128)(2,1)} %cotangent.1) | copy-start | bytes 2359300
  15.1 4.6 %copy-start.8 = (s32[6144]{0:T(1024)S(1)}, s32[6144]{0:T(1024)}, u32[]{:S(2)}) copy-start(s32[6144]{0:T(1024)} %param.32) | copy-start | bytes 73732
  15.1 4.6 %copy-start.9 = (s32[8,384]{1,0:T(8,128)S(1)}, s32[8,384]{1,0:T(8,128)}, u32[]{:S(2)}) copy-start(s32[8,384]{1,0:T(8,128)} %land.1) | copy-start | bytes 36868
  15.1 4.6 %copy-start.10 = (f32[512]{0:T(512)S(1)}, f32[512]{0:T(512)}, u32[]{:S(2)}) copy-start(f32[512]{0:T(512)} %param.26) | copy-start | bytes 6148
  15.1 4.6 %copy-start.12 = (f32[16]{0:T(128)S(1)}, f32[16]{0:T(128)}, u32[]{:S(2)}) copy-start(f32[16]{0:T(128)} %weight_table.1) | copy-start | bytes 196
  15.1 4.6 %copy-start.13 = (f32[128]{0:T(128)S(1)}, f32[128]{0:T(128)}, u32[]{:S(2)}) copy-start(f32[128]{0:T(128)} %param.23) | copy-start | bytes 1540
  15.1 4.6 %copy-start.14 = (f32[128]{0:T(128)S(1)}, f32[128]{0:T(128)}, u32[]{:S(2)}) copy-start(f32[128]{0:T(128)} %param.24) | copy-start | bytes 1540
  15.1 4.6 %copy-start.15 = (f32[128]{0:T(128)S(1)}, f32[128]{0:T(128)}, u32[]{:S(2)}) copy-start(f32[128]{0:T(128)} %param.28) | copy-start | bytes 1540
  15.1 4.6 %copy-start.16 = (f32[128]{0:T(128)S(1)}, f32[128]{0:T(128)}, u32[]{:S(2)}) copy-start(f32[128]{0:T(128)} %param.29) | copy-start | bytes 1540
  15.1 4.6 %copy-start.18 = (f32[8,384,128]{2,1,0:T(8,128)S(1)}, f32[8,384,128]{2,1,0:T(8,128)}, u32[]{:S(2)}) copy-start(f32[8,384,128]{2,1,0:T(8,128)} %copy-done.17) | copy-start | bytes 4718596
  15.2 4.5 %collective-permute-start.3 = (bf16[14,3,128]{2,1,0:T(4,128)(2,1)S(1)}, bf16[14,3,128]{2,1,0:T(4,128)(2,1)S(1)}, u32[]{:S(2)}, u32[]{:S(2)}) collective-permute-start(bf16[14,3,128]{2,1,0:T(4,128)(2,1)S(1)} %pad_maximum_fusion.5), channel_id=1, source_target_pairs={{1,0},{2,1},{3,2},{4,3},{5,4},{6,5},{7,6},{0,7},{9,8},{10,9},{11,1... | collective-permute-start | bytes 32264 | tf_op jit(solution)/shard_map/ppermute | solution.py:454
  42.9 6.3 %collective-permute-start.4 = (bf16[8192,128]{1,0:T(8,128)(2,1)S(1)}, bf16[8192,128]{1,0:T(8,128)(2,1)S(1)}, u32[]{:S(2)}, u32[]{:S(2)}) collective-permute-start(bf16[8192,128]{1,0:T(8,128)(2,1)S(1)} %get-tuple-element.40), channel_id=1, source_target_pairs={{0,1},{1,0},{2,3},{3,2},{4,5},{5,4},{6,7},{7,6},{8,9},{9,8},{10,11... | collective-permute-start | bytes 6291464 | tf_op jit(solution)/shard_map/ppermute | solution.py:400
  50.9 16.5 %collective-permute-start.6 = (bf16[2048,128]{1,0:T(8,128)(2,1)}, bf16[2048,128]{1,0:T(8,128)(2,1)}, u32[]{:S(2)}, u32[]{:S(2)}) collective-permute-start(bf16[2048,128]{1,0:T(8,128)(2,1)} %get-tuple-element.69), channel_id=1, source_target_pairs={{0,4},{1,5},{2,6},{3,7},{4,0},{5,1},{6,2},{7,3},{8,12},{9,13},{10,... | collective-permute-start | bytes 1572872 | tf_op jit(solution)/shard_map/ppermute | solution.py:400
  51.4 17.3 %collective-permute-start.5 = (bf16[2048,128]{1,0:T(8,128)(2,1)}, bf16[2048,128]{1,0:T(8,128)(2,1)}, u32[]{:S(2)}, u32[]{:S(2)}) collective-permute-start(bf16[2048,128]{1,0:T(8,128)(2,1)} %get-tuple-element.70), channel_id=1, source_target_pairs={{0,2},{1,3},{2,0},{3,1},{4,6},{5,7},{6,4},{7,5},{8,10},{9,11},{10,... | collective-permute-start | bytes 1572872 | tf_op jit(solution)/shard_map/ppermute | solution.py:400
  54.8 17.9 %all-to-all-start = ((bf16[32,34,128]{2,1,0:T(8,128)(2,1)}), bf16[32,34,128]{2,1,0:T(8,128)(2,1)S(1)}, u32[]{:S(2)}, u32[]{:S(2)}) async-start(bf16[32,34,128]{2,1,0:T(8,128)(2,1)} %reshape.83), calls=%async_computation | async-start | bytes 655360 | tf_op jit(solution)/shard_map/all_to_all | solution.py:565
  70.1 8.8 %collective-permute-start.8 = (bf16[1024,128]{1,0:T(8,128)(2,1)S(1)}, bf16[1024,128]{1,0:T(8,128)(2,1)S(1)}, u32[]{:S(2)}, u32[]{:S(2)}) collective-permute-start(bf16[1024,128]{1,0:T(8,128)(2,1)S(1)} %get-tuple-element.67), channel_id=1, source_target_pairs={{0,2},{1,3},{2,0},{3,1},{4,6},{5,7},{6,4},{7,5},{8,10},{9,11},{10,... | collective-permute-start | bytes 786440 | tf_op jit(solution)/shard_map/ppermute | solution.py:400
  72.1 6.9 %collective-permute-start.7 = (bf16[1024,128]{1,0:T(8,128)(2,1)S(1)}, bf16[1024,128]{1,0:T(8,128)(2,1)S(1)}, u32[]{:S(2)}, u32[]{:S(2)}) collective-permute-start(bf16[1024,128]{1,0:T(8,128)(2,1)S(1)} %get-tuple-element.68), channel_id=1, source_target_pairs={{0,4},{1,5},{2,6},{3,7},{4,0},{5,1},{6,2},{7,3},{8,12},{9,13},{10,... | collective-permute-start | bytes 786440 | tf_op jit(solution)/shard_map/ppermute | solution.py:400
  73.6 17.1 %all-to-all-start.1 = ((bf16[32,34,128]{2,1,0:T(8,128)(2,1)}), bf16[32,34,128]{2,1,0:T(8,128)(2,1)S(1)}, u32[]{:S(2)}, u32[]{:S(2)}) async-start(bf16[32,34,128]{2,1,0:T(8,128)(2,1)} %broadcast_in_dim.10), calls=%async_computation.1 | async-start | bytes 655360 | tf_op jit(solution)/shard_map/all_to_all | solution.py:568
  81.4 11.6 %collective-permute-start.9 = (bf16[512,128]{1,0:T(8,128)(2,1)S(1)}, bf16[512,128]{1,0:T(8,128)(2,1)S(1)}, u32[]{:S(2)}, u32[]{:S(2)}) collective-permute-start(bf16[512,128]{1,0:T(8,128)(2,1)S(1)} %pad_maximum_fusion.1), channel_id=1, source_target_pairs={{0,8},{8,0},{16,24},{24,16},{1,9},{9,1},{17,25},{25,17},{2,10},{10... | collective-permute-start | bytes 393224 | tf_op jit(solution)/shard_map/ppermute | solution.py:560
  83.2 15.4 %collective-permute-start.10 = (bf16[512,128]{1,0:T(8,128)(2,1)S(1)}, bf16[512,128]{1,0:T(8,128)(2,1)S(1)}, u32[]{:S(2)}, u32[]{:S(2)}) collective-permute-start(bf16[512,128]{1,0:T(8,128)(2,1)S(1)} %pad_maximum_fusion.2), channel_id=1, source_target_pairs={{0,16},{8,24},{16,0},{24,8},{1,17},{9,25},{17,1},{25,9},{2,18},{10... | collective-permute-start | bytes 393224 | tf_op jit(solution)/shard_map/ppermute | solution.py:560
  85.7 12.9 %collective-permute-start.11 = (bf16[512,128]{1,0:T(8,128)(2,1)S(1)}, bf16[512,128]{1,0:T(8,128)(2,1)S(1)}, u32[]{:S(2)}, u32[]{:S(2)}) collective-permute-start(bf16[512,128]{1,0:T(8,128)(2,1)S(1)} %pad_maximum_fusion.3), channel_id=1, source_target_pairs={{0,24},{8,16},{16,8},{24,0},{1,25},{9,17},{17,9},{25,1},{2,26},{10... | collective-permute-start | bytes 393224 | tf_op jit(solution)/shard_map/ppermute | solution.py:560
  (3 other events, 4.1 us)

commit v15 on v13

--- a/solution.py
+++ b/solution.py
@@ -214,6 +214,10 @@
 
     def mlp_step(step, place):
         first = step * group
+        spread[...], ocean = columns(step)
+        cot = cotangent[pl.ds(first, group)].reshape(size, channels).astype(f32)
+        grad_out = (ocean * scale[...] * cot).astype(bf16)
+        grad_hidden = jnp.dot(grad_out, down_t[...], preferred_element_type=f32)
         here = field[pl.ds(first, group)].reshape(size, channels)
         average = jnp.mean(here, axis=-1, keepdims=True)
         centred = here - average
@@ -230,19 +234,15 @@
         slope = half + pre * (1.0 - tanh_value * tanh_value) * (
             0.5 * gelu_scale + 1.5 * gelu_scale * cubic_coef * square
         )
-        projected = jnp.dot(hidden, down[...], preferred_element_type=f32) + downb[...]
-        spread[...], ocean = columns(step)
-        own = state[pl.ds(first, group)].reshape(size, channels).astype(f32)
-        out = ocean * (own + scale[...] * projected)
-        result[pl.ds(first, group)] = out.astype(bf16).reshape(group, cols, channels)
-        cot = cotangent[pl.ds(first, group)].reshape(size, channels).astype(f32)
-        grad_out = (ocean * scale[...] * cot).astype(bf16)
-        grad_hidden = jnp.dot(grad_out, down_t[...], preferred_element_type=f32)
         grad_pre = (grad_hidden * slope).astype(bf16)
         gmix = jnp.dot(grad_pre, up_t[...], preferred_element_type=f32)
         for k in range(fan):
             weights = spread[pl.ds(k, size, stride=fan), :]
             terms[pl.ds(k * ROUND * size + place * size, size), :] = weights * gmix
+        projected = jnp.dot(hidden, down[...], preferred_element_type=f32) + downb[...]
+        own = state[pl.ds(first, group)].reshape(size, channels).astype(f32)
+        out = ocean * (own + scale[...] * projected)
+        result[pl.ds(first, group)] = out.astype(bf16).reshape(group, cols, channels)
         gained = gmix * gain[...]
         gconv = inv_std * (
             gained

time: 98.4 us -> 99.4 us (1.010)
  Pallas kernels: 35.1 us -> 36.2 us
    pallas_call x1, Pallas kernels: 21.5 us -> 22.6 us  [on_device(): pl.pallas_call(block_kernel, out_shape=(shape((rows, cols, channels), bf1...]
where the time goes in v15:
time: 99.4 us; the launch traced here: 98.9 us
  Pallas kernels  36.2 us (36%)
  starting transfers between devices  27.6 us (28%)
  waiting for transfers between devices  21.1 us (21%)
  local copies, waits for them, and re-layouts  6.59 us (7%)
  other arithmetic  6.3 us (6%)
  between operations  1.14 us (1%)
    pallas_call x1, Pallas kernels, on_device(): pl.pallas_call(block_kernel, out_shape=(shape((rows, cols, channels), bf1...  22.6 us
    all_to_all x2, starting transfers between devices, on_device(): lax.all_to_all(total, ('lat', 'lon'), split_axis=0, concat_axis=0, tiled=...  10.2 us
    ppermute x5, waiting for transfers between devices, swap_bit(): return lax.ppermute(array, 'lon', pairs)  9.39 us
    pallas_call x1, Pallas kernels, on_device(): pl.pallas_call(conv_grad_kernel, out_shape=shape((dw_rows, channels), f32...  6.17 us
    ppermute x3, waiting for transfers between devices, on_device(): lax.ppermute(for_band(distance).astype(bf16), 'lat', pairs)  5.71 us
    pallas_call x1, Pallas kernels, on_device(): pl.pallas_call(functools.partial(inner_conv_kernel, lat_count, lon_count,...  5.54 us
    ppermute x5, starting transfers between devices, swap_bit(): return lax.ppermute(array, 'lon', pairs)  5.43 us
    all_to_all x2, waiting for transfers between devices, on_device(): lax.all_to_all(total, ('lat', 'lon'), split_axis=0, concat_axis=0, tiled=...  4.75 us
  transfers between devices with their start and end apart: 14, of which 5 were waited for; matrix products, arithmetic and copies ran while one was open for 8% of the time, Pallas kernels for 14%

profile of v15, /device:TPU:0, one launch (start us, length us, event | category | flops | bytes accessed | tf_op | source)
XLA Modules:
  0.0 98.9 jit_solution(2639747885297876269)
XLA Ops:
  0.6 1.1 %copy-done.2 = bf16[8,384,128]{2,1,0:T(8,128)(2,1)S(1)} copy-done((bf16[8,384,128]{2,1,0:T(8,128)(2,1)S(1)}, bf16[8,384,128]{2,1,0:T(8,128)(2,1)}, u32[]{:S(2)}) %copy-start.2) | copy-done | bytes 786456
  1.9 3.4 %collective-permute-start.1 = (bf16[3,384,128]{2,1,0:T(8,128)(2,1)S(1)}, bf16[3,384,128]{2,1,0:T(8,128)(2,1)S(1)}, u32[]{:S(2)}, u32[]{:S(2)}) collective-permute-start(bf16[3,384,128]{2,1,0:T(8,128)(2,1)S(1)} %get-tuple-element.33), channel_id=1, source_target_pairs={{0,7},{1,6},{2,5},{3,4},{4,3},{5,2},{6,1},{7,0},{8,16},{9,17},{10,... | collective-permute-start | bytes 884744 | tf_op jit(solution)/shard_map/ppermute | solution.py:438
  5.3 1.3 %collective-permute-start = (bf16[3,384,128]{2,1,0:T(8,128)(2,1)S(1)}, bf16[3,384,128]{2,1,0:T(8,128)(2,1)S(1)}, u32[]{:S(2)}, u32[]{:S(2)}) collective-permute-start(bf16[3,384,128]{2,1,0:T(8,128)(2,1)S(1)} %get-tuple-element.32), channel_id=1, source_target_pairs={{0,8},{1,9},{2,10},{3,11},{4,12},{5,13},{6,14},{7,15},{8,0},{9,1},... | collective-permute-start | bytes 884744 | tf_op jit(solution)/shard_map/ppermute | solution.py:437
  6.6 5.5 %inner_conv.1 = (f32[8,384,128]{2,1,0:T(8,128)S(1)}, s32[48,128]{1,0:T(8,128)S(1)}, s32[48,128]{1,0:T(8,128)S(1)}) custom-call(bf16[8,384,128]{2,1,0:T(8,128)(2,1)S(1)} %copy-done.3, f32[49,128]{1,0:T(8,128)S(1)} %reshape.87.dw, f32[1,128]{1,0:T(1,128)S(1)} %bitcast.27, s32[48,128]{1,0:T(8,128)S(1)} %bitcast.23, s32[48,128]{1,0:T(8,128)S(1)} %bitcast.24), custom_call_target="tpu_custom_call" | custom-call | flops 7000000000 | tf_op jit(solution)/shard_map/inner_conv/pallas_call | solution.py:455
  12.2 1.2 %copy-done.17 = f32[8,384,128]{2,1,0:T(8,128)} copy-done((f32[8,384,128]{2,1,0:T(8,128)}, f32[8,384,128]{2,1,0:T(8,128)S(1)}, u32[]{:S(2)}) %copy-start.17) | copy-done | bytes 1572888
  13.6 1.2 %collective-permute-done = bf16[3,384,128]{2,1,0:T(8,128)(2,1)S(1)} collective-permute-done((bf16[3,384,128]{2,1,0:T(8,128)(2,1)S(1)}, bf16[3,384,128]{2,1,0:T(8,128)(2,1)S(1)}, u32[]{:S(2)}, u32[]{:S(2)}) %collective-permute-start) | collective-permute-done | bytes 294944 | tf_op jit(solution)/shard_map/ppermute | solution.py:437
  15.2 2.7 %collective-permute-start.3 = (bf16[14,3,128]{2,1,0:T(4,128)(2,1)S(1)}, bf16[14,3,128]{2,1,0:T(4,128)(2,1)S(1)}, u32[]{:S(2)}, u32[]{:S(2)}) collective-permute-start(bf16[14,3,128]{2,1,0:T(4,128)(2,1)S(1)} %pad_maximum_fusion.5), channel_id=1, source_target_pairs={{1,0},{2,1},{3,2},{4,3},{5,4},{6,5},{7,6},{0,7},{9,8},{10,9},{11,1... | collective-permute-start | bytes 32264 | tf_op jit(solution)/shard_map/ppermute | solution.py:446
  17.8 1.8 %halo_conv.1.halo = f32[6,384,128]{2,1,0:T(8,128)S(1)} custom-call(bf16[3,384,128]{2,1,0:T(8,128)(2,1)S(1)} %get-tuple-element.74.south, bf16[3,384,128]{2,1,0:T(8,128)(2,1)S(1)} %get-tuple-element.73.north, f32[49,128]{1,0:T(8,128)S(1)} %reshape.87.dw), custom_call_target="tpu_custom_call" | custom-call | flops 2000000000 | tf_op jit(solution)/shard_map/halo_conv/pallas_call | solution.py:467
  19.8 22.6 %block.1 = (bf16[8,384,128]{2,1,0:T(8,128)(2,1)}, f32[2048,128]{1,0:T(8,128)S(1)}, f32[2048,128]{1,0:T(8,128)S(1)}, f32[2048,128]{1,0:T(8,128)S(1)}, f32[2048,12...) custom-call(bf16[8,384,128]{2,1,0:T(8,128)(2,1)S(1)} %copy-done.3, ...), custom_call_target="tpu_custom_call" | custom-call | flops 28000000000 | tf_op jit(solution)/shard_map/block/pallas_call | solution.py:478
  42.5 6.2 %conv_grad.1 = f32[64,128]{1,0:T(8,128)S(1)} custom-call(bf16[8,384,128]{2,1,0:T(8,128)(2,1)S(1)} %copy-done.3, bf16[3,384,128]{2,1,0:T(8,128)(2,1)S(1)} %get-tuple-element.74.south, bf16[3,384,128]{2,1,0:T(8,128)(2,1)S(1)} %get-tuple-element.73.north, bf16[14,3,128]{2,1,0:T(4,128)(2,1)S(1)} %collective-permute-done.2.left, ...), custom_call_target="tpu_custom_call" | custom-call | flops 8999999488 | tf_op jit(solution)/shard_map/conv_grad/pallas_call | solution.py:517
  48.7 1.5 %add_convert_fusion = (bf16[2048,128]{1,0:T(8,128)(2,1)}, bf16[2048,128]{1,0:T(8,128)(2,1)}) fusion(f32[2048,128]{1,0:T(8,128)S(1)} %get-tuple-element.45, bf16[8192,128]{1,0:T(8,128)(2,1)S(1)} %collective-permute-done.4, f32[2048,128]{1,0:T(8,128)S(1)} %get-tuple-element.44), kind=kLoop, calls=%fused_computation | loop fusion | flops 1572864 | bytes 4194304 | tf_op jit(solution)/shard_map/convert_element_type | solution.py:532
  50.4 0.4 collective-permute-start.6
  50.8 2.5 %collective-permute-start.5 = (bf16[2048,128]{1,0:T(8,128)(2,1)}, bf16[2048,128]{1,0:T(8,128)(2,1)}, u32[]{:S(2)}, u32[]{:S(2)}) collective-permute-start(bf16[2048,128]{1,0:T(8,128)(2,1)} %get-tuple-element.70), channel_id=1, source_target_pairs={{0,2},{1,3},{2,0},{3,1},{4,6},{5,7},{6,4},{7,5},{8,10},{9,11},{10,... | collective-permute-start | bytes 1572872 | tf_op jit(solution)/shard_map/ppermute | solution.py:392
  53.4 0.8 reshape.83
  54.2 4.5 %all-to-all-start = ((bf16[32,34,128]{2,1,0:T(8,128)(2,1)}), bf16[32,34,128]{2,1,0:T(8,128)(2,1)S(1)}, u32[]{:S(2)}, u32[]{:S(2)}) async-start(bf16[32,34,128]{2,1,0:T(8,128)(2,1)} %reshape.83), calls=%async_computation | async-start | bytes 655360 | tf_op jit(solution)/shard_map/all_to_all | solution.py:557
  58.7 8.3 %collective-permute-done.6 = bf16[2048,128]{1,0:T(8,128)(2,1)} collective-permute-done((bf16[2048,128]{1,0:T(8,128)(2,1)}, bf16[2048,128]{1,0:T(8,128)(2,1)}, u32[]{:S(2)}, u32[]{:S(2)}) %collective-permute-start.6) | collective-permute-done | bytes 524320 | tf_op jit(solution)/shard_map/ppermute | solution.py:392
  66.9 1.1 %collective-permute-done.5 = bf16[2048,128]{1,0:T(8,128)(2,1)} collective-permute-done((bf16[2048,128]{1,0:T(8,128)(2,1)}, bf16[2048,128]{1,0:T(8,128)(2,1)}, u32[]{:S(2)}, u32[]{:S(2)}) %collective-permute-start.5) | collective-permute-done | bytes 524320 | tf_op jit(solution)/shard_map/ppermute | solution.py:392
  68.1 1.4 %add_convert_fusion.2 = (bf16[1024,128]{1,0:T(8,128)(2,1)S(1)}, bf16[1024,128]{1,0:T(8,128)(2,1)S(1)}) fusion(f32[2048,128]{1,0:T(8,128)S(1)} %get-tuple-element.47, bf16[2048,128]{1,0:T(8,128)(2,1)} %collective-permute-done.6, bf16[8192,128]{1,0:T(8,128)(2,1)} %copy-done.19, bf16[2048,128]{1,0:T(8,128)(2,1)} %collective-permute-done.5, ...), kind=kLoop, calls=%fused_computation.3 | loop fusion | flops 1310720 | bytes 2621440 | tf_op jit(solution)/shard_map/convert_element_type | solution.py:542
  69.4 2.0 %collective-permute-start.8 = (bf16[1024,128]{1,0:T(8,128)(2,1)S(1)}, bf16[1024,128]{1,0:T(8,128)(2,1)S(1)}, u32[]{:S(2)}, u32[]{:S(2)}) collective-permute-start(bf16[1024,128]{1,0:T(8,128)(2,1)S(1)} %get-tuple-element.67), channel_id=1, source_target_pairs={{0,2},{1,3},{2,0},{3,1},{4,6},{5,7},{6,4},{7,5},{8,10},{9,11},{10,... | collective-permute-start | bytes 786440 | tf_op jit(solution)/shard_map/ppermute | solution.py:392
  71.4 0.5 collective-permute-start.7
  72.0 0.8 broadcast_in_dim.10
  72.8 5.7 %all-to-all-start.1 = ((bf16[32,34,128]{2,1,0:T(8,128)(2,1)}), bf16[32,34,128]{2,1,0:T(8,128)(2,1)S(1)}, u32[]{:S(2)}, u32[]{:S(2)}) async-start(bf16[32,34,128]{2,1,0:T(8,128)(2,1)} %broadcast_in_dim.10), calls=%async_computation.1 | async-start | bytes 655360 | tf_op jit(solution)/shard_map/all_to_all | solution.py:560
  78.5 1.2 %convert_add_fusion = (f32[256,128]{1,0:T(8,128)S(1)}, bf16[256,128]{1,0:T(8,128)(2,1)S(1)}, bf16[256,128]{1,0:T(8,128)(2,1)S(1)}, bf16[256,128]{1,0:T(8,128)(2,1)S(1)}) fusion(f32[2048,128]{1,0:T(8,128)S(1)} %get-tuple-element.47, bf16[1024,128]{1,0:T(8,128)(2,1)S(1)} %collective-permute-done.8, bf16[2048,128]{1,0:T(8,128)(2,1)} %collective-permute-done.6, ...), kind=kLoop, calls=%fused_computation.15 | loop fusion | flops 884736 | bytes 1638400 | tf_op jit(solution)/shard_map/add | solution.py:531
  79.7 1.2 %convert_add_fusion.1 = (f32[256,128]{1,0:T(8,128)S(1)}, bf16[256,128]{1,0:T(8,128)(2,1)S(1)}, bf16[256,128]{1,0:T(8,128)(2,1)S(1)}, bf16[256,128]{1,0:T(8,128)(2,1)S(1)}) fusion(f32[2048,128]{1,0:T(8,128)S(1)} %get-tuple-element.39, bf16[1024,128]{1,0:T(8,128)(2,1)S(1)} %collective-permute-done.7, bf16[2048,128]{1,0:T(8,128)(2,1)} %collective-permute-done.5, ...), kind=kLoop, calls=%fused_computation.16 | loop fusion | flops 884736 | bytes 1638400 | tf_op jit(solution)/shard_map/add | solution.py:531
  80.9 1.8 %collective-permute-start.9 = (bf16[512,128]{1,0:T(8,128)(2,1)S(1)}, bf16[512,128]{1,0:T(8,128)(2,1)S(1)}, u32[]{:S(2)}, u32[]{:S(2)}) collective-permute-start(bf16[512,128]{1,0:T(8,128)(2,1)S(1)} %pad_maximum_fusion.1), channel_id=1, source_target_pairs={{0,8},{8,0},{16,24},{24,16},{1,9},{9,1},{17,25},{25,17},{2,10},{10... | collective-permute-start | bytes 393224 | tf_op jit(solution)/shard_map/ppermute | solution.py:552
  82.8 2.5 %collective-permute-start.10 = (bf16[512,128]{1,0:T(8,128)(2,1)S(1)}, bf16[512,128]{1,0:T(8,128)(2,1)S(1)}, u32[]{:S(2)}, u32[]{:S(2)}) collective-permute-start(bf16[512,128]{1,0:T(8,128)(2,1)S(1)} %pad_maximum_fusion.2), channel_id=1, source_target_pairs={{0,16},{8,24},{16,0},{24,8},{1,17},{9,25},{17,1},{25,9},{2,18},{10... | collective-permute-start | bytes 393224 | tf_op jit(solution)/shard_map/ppermute | solution.py:552
  85.5 4.8 %all-to-all-done.1 = bf16[32,34,128]{2,1,0:T(8,128)(2,1)S(1)} async-done(((bf16[32,34,128]{2,1,0:T(8,128)(2,1)}), bf16[32,34,128]{2,1,0:T(8,128)(2,1)S(1)}, u32[]{:S(2)}, u32[]{:S(2)}) %all-to-all-start.1) | async-done | bytes 278560 | tf_op jit(solution)/shard_map/all_to_all | solution.py:560
  90.4 0.7 fusion.3
  91.1 0.7 copy.30
  91.9 0.6 reshape.84
  92.5 5.7 %collective-permute-done.10 = bf16[512,128]{1,0:T(8,128)(2,1)S(1)} collective-permute-done((bf16[512,128]{1,0:T(8,128)(2,1)S(1)}, bf16[512,128]{1,0:T(8,128)(2,1)S(1)}, u32[]{:S(2)}, u32[]{:S(2)}) %collective-permute-start.10) | collective-permute-done | bytes 131104 | tf_op jit(solution)/shard_map/ppermute | solution.py:552
  98.2 0.8 fusion.1
  (71 shorter events, 1.4 us)
Async XLA Ops:
  1.8 4.8 %copy-start.20 = (bf16[7,7,128]{2,1,0:T(8,128)(2,1)S(1)}, bf16[7,7,128]{2,1,0:T(8,128)(2,1)}, u32[]{:S(2)}) copy-start(bf16[7,7,128]{2,1,0:T(8,128)(2,1)} %param.21) | copy-start | bytes 37636
  1.8 4.8 %copy-start.3 = (bf16[8,384,128]{2,1,0:T(8,128)(2,1)S(1)}, bf16[8,384,128]{2,1,0:T(8,128)(2,1)}, u32[]{:S(2)}) copy-start(bf16[8,384,128]{2,1,0:T(8,128)(2,1)} %state.6) | copy-start | bytes 2359300
  1.8 4.8 %copy-start.6 = (s32[6144,1]{0,1:T(1,128)S(1)}, s32[6144,1]{0,1:T(1,128)}, u32[]{:S(2)}) copy-start(s32[6144,1]{0,1:T(1,128)} %param.30) | copy-start | bytes 73732
  1.8 4.8 %copy-start.7 = (s32[6144]{0:T(1024)S(1)}, s32[6144]{0:T(1024)}, u32[]{:S(2)}) copy-start(s32[6144]{0:T(1024)} %param.31) | copy-start | bytes 73732
  1.8 4.8 %copy-start.11 = (f32[128]{0:T(128)S(1)}, f32[128]{0:T(128)}, u32[]{:S(2)}) copy-start(f32[128]{0:T(128)} %param.22) | copy-start | bytes 1540
  1.9 11.7 %collective-permute-start.1 = (bf16[3,384,128]{2,1,0:T(8,128)(2,1)S(1)}, bf16[3,384,128]{2,1,0:T(8,128)(2,1)S(1)}, u32[]{:S(2)}, u32[]{:S(2)}) collective-permute-start(bf16[3,384,128]{2,1,0:T(8,128)(2,1)S(1)} %get-tuple-element.33), channel_id=1, source_target_pairs={{0,7},{1,6},{2,5},{3,4},{4,3},{5,2},{6,1},{7,0},{8,16},{9,17},{10,... | collective-permute-start | bytes 884744 | tf_op jit(solution)/shard_map/ppermute | solution.py:438
  5.3 9.6 %collective-permute-start = (bf16[3,384,128]{2,1,0:T(8,128)(2,1)S(1)}, bf16[3,384,128]{2,1,0:T(8,128)(2,1)S(1)}, u32[]{:S(2)}, u32[]{:S(2)}) collective-permute-start(bf16[3,384,128]{2,1,0:T(8,128)(2,1)S(1)} %get-tuple-element.32), channel_id=1, source_target_pairs={{0,8},{1,9},{2,10},{3,11},{4,12},{5,13},{6,14},{7,15},{8,0},{9,1},... | collective-permute-start | bytes 884744 | tf_op jit(solution)/shard_map/ppermute | solution.py:437
  6.6 6.7 %copy-start = (bf16[128,512]{1,0:T(8,128)(2,1)S(1)}, bf16[128,512]{1,0:T(8,128)(2,1)}, u32[]{:S(2)}) copy-start(bf16[128,512]{1,0:T(8,128)(2,1)} %up.1) | copy-start | bytes 393220
  6.6 6.9 %copy-start.1 = (bf16[512,128]{1,0:T(8,128)(2,1)S(1)}, bf16[512,128]{1,0:T(8,128)(2,1)}, u32[]{:S(2)}) copy-start(bf16[512,128]{1,0:T(8,128)(2,1)} %down.1) | copy-start | bytes 393220
  14.9 4.7 %collective-permute-start.2 = (bf16[14,3,128]{2,1,0:T(4,128)(2,1)S(1)}, bf16[14,3,128]{2,1,0:T(4,128)(2,1)S(1)}, u32[]{:S(2)}, u32[]{:S(2)}) collective-permute-start(bf16[14,3,128]{2,1,0:T(4,128)(2,1)S(1)} %pad_maximum_fusion.4), channel_id=1, source_target_pairs={{0,1},{1,2},{2,3},{3,4},{4,5},{5,6},{6,7},{7,0},{8,9},{9,10},{10,1... | collective-permute-start | bytes 32264 | tf_op jit(solution)/shard_map/ppermute | solution.py:445
  15.0 4.6 %copy-start.4 = (bf16[8,384,128]{2,1,0:T(8,128)(2,1)S(1)}, bf16[8,384,128]{2,1,0:T(8,128)(2,1)}, u32[]{:S(2)}) copy-start(bf16[8,384,128]{2,1,0:T(8,128)(2,1)} %forcing.1) | copy-start | bytes 2359300
  15.0 4.6 %copy-start.5 = (bf16[8,384,128]{2,1,0:T(8,128)(2,1)S(1)}, bf16[8,384,128]{2,1,0:T(8,128)(2,1)}, u32[]{:S(2)}) copy-start(bf16[8,384,128]{2,1,0:T(8,128)(2,1)} %cotangent.1) | copy-start | bytes 2359300
  15.1 4.6 %copy-start.8 = (s32[6144]{0:T(1024)S(1)}, s32[6144]{0:T(1024)}, u32[]{:S(2)}) copy-start(s32[6144]{0:T(1024)} %param.32) | copy-start | bytes 73732
  15.1 4.6 %copy-start.9 = (s32[8,384]{1,0:T(8,128)S(1)}, s32[8,384]{1,0:T(8,128)}, u32[]{:S(2)}) copy-start(s32[8,384]{1,0:T(8,128)} %land.1) | copy-start | bytes 36868
  15.1 4.6 %copy-start.10 = (f32[512]{0:T(512)S(1)}, f32[512]{0:T(512)}, u32[]{:S(2)}) copy-start(f32[512]{0:T(512)} %param.26) | copy-start | bytes 6148
  15.1 4.6 %copy-start.12 = (f32[16]{0:T(128)S(1)}, f32[16]{0:T(128)}, u32[]{:S(2)}) copy-start(f32[16]{0:T(128)} %weight_table.1) | copy-start | bytes 196
  15.1 4.6 %copy-start.13 = (f32[128]{0:T(128)S(1)}, f32[128]{0:T(128)}, u32[]{:S(2)}) copy-start(f32[128]{0:T(128)} %param.23) | copy-start | bytes 1540
  15.1 4.6 %copy-start.14 = (f32[128]{0:T(128)S(1)}, f32[128]{0:T(128)}, u32[]{:S(2)}) copy-start(f32[128]{0:T(128)} %param.24) | copy-start | bytes 1540
  15.1 4.6 %copy-start.15 = (f32[128]{0:T(128)S(1)}, f32[128]{0:T(128)}, u32[]{:S(2)}) copy-start(f32[128]{0:T(128)} %param.28) | copy-start | bytes 1540
  15.1 4.6 %copy-start.16 = (f32[128]{0:T(128)S(1)}, f32[128]{0:T(128)}, u32[]{:S(2)}) copy-start(f32[128]{0:T(128)} %param.29) | copy-start | bytes 1540
  15.1 4.6 %copy-start.18 = (f32[8,384,128]{2,1,0:T(8,128)S(1)}, f32[8,384,128]{2,1,0:T(8,128)}, u32[]{:S(2)}) copy-start(f32[8,384,128]{2,1,0:T(8,128)} %copy-done.17) | copy-start | bytes 4718596
  15.2 4.5 %collective-permute-start.3 = (bf16[14,3,128]{2,1,0:T(4,128)(2,1)S(1)}, bf16[14,3,128]{2,1,0:T(4,128)(2,1)S(1)}, u32[]{:S(2)}, u32[]{:S(2)}) collective-permute-start(bf16[14,3,128]{2,1,0:T(4,128)(2,1)S(1)} %pad_maximum_fusion.5), channel_id=1, source_target_pairs={{1,0},{2,1},{3,2},{4,3},{5,4},{6,5},{7,6},{0,7},{9,8},{10,9},{11,1... | collective-permute-start | bytes 32264 | tf_op jit(solution)/shard_map/ppermute | solution.py:446
  42.4 6.3 %collective-permute-start.4 = (bf16[8192,128]{1,0:T(8,128)(2,1)S(1)}, bf16[8192,128]{1,0:T(8,128)(2,1)S(1)}, u32[]{:S(2)}, u32[]{:S(2)}) collective-permute-start(bf16[8192,128]{1,0:T(8,128)(2,1)S(1)} %get-tuple-element.40), channel_id=1, source_target_pairs={{0,1},{1,0},{2,3},{3,2},{4,5},{5,4},{6,7},{7,6},{8,9},{9,8},{10,11... | collective-permute-start | bytes 6291464 | tf_op jit(solution)/shard_map/ppermute | solution.py:392
  50.4 16.5 %collective-permute-start.6 = (bf16[2048,128]{1,0:T(8,128)(2,1)}, bf16[2048,128]{1,0:T(8,128)(2,1)}, u32[]{:S(2)}, u32[]{:S(2)}) collective-permute-start(bf16[2048,128]{1,0:T(8,128)(2,1)} %get-tuple-element.69), channel_id=1, source_target_pairs={{0,4},{1,5},{2,6},{3,7},{4,0},{5,1},{6,2},{7,3},{8,12},{9,13},{10,... | collective-permute-start | bytes 1572872 | tf_op jit(solution)/shard_map/ppermute | solution.py:392
  50.8 17.3 %collective-permute-start.5 = (bf16[2048,128]{1,0:T(8,128)(2,1)}, bf16[2048,128]{1,0:T(8,128)(2,1)}, u32[]{:S(2)}, u32[]{:S(2)}) collective-permute-start(bf16[2048,128]{1,0:T(8,128)(2,1)} %get-tuple-element.70), channel_id=1, source_target_pairs={{0,2},{1,3},{2,0},{3,1},{4,6},{5,7},{6,4},{7,5},{8,10},{9,11},{10,... | collective-permute-start | bytes 1572872 | tf_op jit(solution)/shard_map/ppermute | solution.py:392
  54.2 17.7 %all-to-all-start = ((bf16[32,34,128]{2,1,0:T(8,128)(2,1)}), bf16[32,34,128]{2,1,0:T(8,128)(2,1)S(1)}, u32[]{:S(2)}, u32[]{:S(2)}) async-start(bf16[32,34,128]{2,1,0:T(8,128)(2,1)} %reshape.83), calls=%async_computation | async-start | bytes 655360 | tf_op jit(solution)/shard_map/all_to_all | solution.py:557
  69.4 9.1 %collective-permute-start.8 = (bf16[1024,128]{1,0:T(8,128)(2,1)S(1)}, bf16[1024,128]{1,0:T(8,128)(2,1)S(1)}, u32[]{:S(2)}, u32[]{:S(2)}) collective-permute-start(bf16[1024,128]{1,0:T(8,128)(2,1)S(1)} %get-tuple-element.67), channel_id=1, source_target_pairs={{0,2},{1,3},{2,0},{3,1},{4,6},{5,7},{6,4},{7,5},{8,10},{9,11},{10,... | collective-permute-start | bytes 786440 | tf_op jit(solution)/shard_map/ppermute | solution.py:392
  71.4 7.1 %collective-permute-start.7 = (bf16[1024,128]{1,0:T(8,128)(2,1)S(1)}, bf16[1024,128]{1,0:T(8,128)(2,1)S(1)}, u32[]{:S(2)}, u32[]{:S(2)}) collective-permute-start(bf16[1024,128]{1,0:T(8,128)(2,1)S(1)} %get-tuple-element.68), channel_id=1, source_target_pairs={{0,4},{1,5},{2,6},{3,7},{4,0},{5,1},{6,2},{7,3},{8,12},{9,13},{10,... | collective-permute-start | bytes 786440 | tf_op jit(solution)/shard_map/ppermute | solution.py:392
  72.8 17.5 %all-to-all-start.1 = ((bf16[32,34,128]{2,1,0:T(8,128)(2,1)}), bf16[32,34,128]{2,1,0:T(8,128)(2,1)S(1)}, u32[]{:S(2)}, u32[]{:S(2)}) async-start(bf16[32,34,128]{2,1,0:T(8,128)(2,1)} %broadcast_in_dim.10), calls=%async_computation.1 | async-start | bytes 655360 | tf_op jit(solution)/shard_map/all_to_all | solution.py:560
  80.9 11.6 %collective-permute-start.9 = (bf16[512,128]{1,0:T(8,128)(2,1)S(1)}, bf16[512,128]{1,0:T(8,128)(2,1)S(1)}, u32[]{:S(2)}, u32[]{:S(2)}) collective-permute-start(bf16[512,128]{1,0:T(8,128)(2,1)S(1)} %pad_maximum_fusion.1), channel_id=1, source_target_pairs={{0,8},{8,0},{16,24},{24,16},{1,9},{9,1},{17,25},{25,17},{2,10},{10... | collective-permute-start | bytes 393224 | tf_op jit(solution)/shard_map/ppermute | solution.py:552
  82.8 15.4 %collective-permute-start.10 = (bf16[512,128]{1,0:T(8,128)(2,1)S(1)}, bf16[512,128]{1,0:T(8,128)(2,1)S(1)}, u32[]{:S(2)}, u32[]{:S(2)}) collective-permute-start(bf16[512,128]{1,0:T(8,128)(2,1)S(1)} %pad_maximum_fusion.2), channel_id=1, source_target_pairs={{0,16},{8,24},{16,0},{24,8},{1,17},{9,25},{17,1},{25,9},{2,18},{10... | collective-permute-start | bytes 393224 | tf_op jit(solution)/shard_map/ppermute | solution.py:552
  85.3 12.9 %collective-permute-start.11 = (bf16[512,128]{1,0:T(8,128)(2,1)S(1)}, bf16[512,128]{1,0:T(8,128)(2,1)S(1)}, u32[]{:S(2)}, u32[]{:S(2)}) collective-permute-start(bf16[512,128]{1,0:T(8,128)(2,1)S(1)} %pad_maximum_fusion.3), channel_id=1, source_target_pairs={{0,24},{8,16},{16,8},{24,0},{1,25},{9,17},{17,9},{25,1},{2,26},{10... | collective-permute-start | bytes 393224 | tf_op jit(solution)/shard_map/ppermute | solution.py:552
  (3 other events, 4.1 us)

commit v16 on v13

--- a/solution.py
+++ b/solution.py
@@ -183,10 +183,6 @@
             here = here + halo[r - rows + 2 * MARGIN, inner, :]
         field[r, inner, :] = here
 
-    def clear(at):
-        table[at, :] = jnp.zeros((at.size, channels), f32)
-
-    in_chunks(table.shape[0], clear)
     index = weight_index[...]
     looked_up = jnp.zeros(index.shape, f32)
     for k in range(weight_table.shape[0]):
@@ -257,12 +253,13 @@
     unit = BATCH * BATCHES
     units = terms.shape[0] // unit
 
-    def round_of(index, _):
+    def round_of(index):
         for place in range(ROUND):
             mlp_step(index * ROUND + place, place)
-
-        @pl.when(index == 0)
-        def _():
+            if index == 0:
+                share = table.shape[0] // ROUND
+                table[place * share : (place + 1) * share] = jnp.zeros((share, channels), f32)
+        if index == 0:
             for copy in scalar_copies:
                 copy.wait()
 
@@ -290,9 +287,9 @@
             return 0
 
         lax.fori_loop(0, units, add_unit, 0)
-        return 0
-
-    lax.fori_loop(0, rows // (group * ROUND), round_of, 0)
+
+    for index in range(rows // (group * ROUND)):
+        round_of(index)
     half = table.shape[0] // 2
 
     keep_copies = [
@@ -545,11 +542,13 @@
         at = slice(distance * width, (distance + 1) * width)
         return jnp.concatenate([add([h[at] for h in held[q]]) for q in range(2)], axis=0)
 
-    forcing_grad = for_band(0)
+    sends = [for_band(distance).astype(bf16) for distance in range(1, lat_count)]
     from_bands = []
     for distance in range(1, lat_count):
         pairs = [(i, i ^ distance) for i in range(lat_count)]
-        from_bands.append(lax.ppermute(for_band(distance).astype(bf16), "lat", pairs))
+        from_bands.append(lax.ppermute(sends[distance - 1], "lat", pairs))
+    held, _ = lax.optimization_barrier((held, sends))
+    forcing_grad = for_band(0)
 
     total = jnp.concatenate([grads.reshape(2 * hid, channels), grad_dw], axis=0).astype(bf16)
     total = after(total, *first_sends)

time: 98.4 us -> 103 us (1.047)
  local copies, waits for them, and re-layouts: 6.59 us -> 10.4 us
  other arithmetic: 6.3 us -> 9.33 us
  waiting for transfers between devices: 21.3 us -> 19.3 us
    slice x0 -> x3, local copies, waits for them, and re-layouts: none -> 3.82 us  [on_device(): held = [[h[:size] for h in held[q]] for q in range(2)]]
    another operation x2 -> x4, other arithmetic: 0.04 us -> 2.43 us
    all_to_all x2, waiting for transfers between devices: 4.75 us -> 2.78 us  [on_device(): lax.all_to_all(total, ('lat', 'lon'), split_axis=0, concat_axis=0, tiled=...]
    convert_element_type x1, other arithmetic: 1.36 us -> 2.42 us  [on_device(): add([h[size:2 * size] for h in held[q]]).astype(bf16)]
  transfers between devices with their start and end apart: 14 -> 14, of which waited for: 5 -> 5; matrix products, arithmetic and copies ran while one was open for 8% -> 14% of each run, Pallas kernels for 14% -> 13%
where the time goes in v16:
time: 103 us
  Pallas kernels  35.3 us (34%)
  starting transfers between devices  27.3 us (27%)
  waiting for transfers between devices  19.3 us (19%)
  local copies, waits for them, and re-layouts  10.4 us (10%)
  other arithmetic  9.33 us (9%)
  between operations  1.16 us (1%)
    pallas_call x1, Pallas kernels, on_device(): pl.pallas_call(block_kernel, out_shape=(shape((rows, cols, channels), bf1...  21.7 us
    all_to_all x2, starting transfers between devices, on_device(): lax.all_to_all(total, ('lat', 'lon'), split_axis=0, concat_axis=0, tiled=...  10.2 us
    ppermute x5, waiting for transfers between devices, swap_bit(): return lax.ppermute(array, 'lon', pairs)  9.53 us
    pallas_call x1, Pallas kernels, on_device(): pl.pallas_call(conv_grad_kernel, out_shape=shape((dw_rows, channels), f32...  6.17 us
    ppermute x3, waiting for transfers between devices, on_device(): from_bands.append(lax.ppermute(sends[distance - 1], 'lat', pairs))  5.71 us
    pallas_call x1, Pallas kernels, on_device(): pl.pallas_call(functools.partial(inner_conv_kernel, lat_count, lon_count,...  5.54 us
    ppermute x5, starting transfers between devices, swap_bit(): return lax.ppermute(array, 'lon', pairs)  5.1 us
    ppermute x3, starting transfers between devices, on_device(): from_bands.append(lax.ppermute(sends[distance - 1], 'lat', pairs))  4.58 us
  transfers between devices with their start and end apart: 14, of which 5 were waited for; matrix products, arithmetic and copies ran while one was open for 14% of the time, Pallas kernels for 13%

profile of v16, /device:TPU:0, one launch (start us, length us, event | category | flops | bytes accessed | tf_op | source)
XLA Modules:
  0.0 102.8 jit_solution(16809682284713132018)
XLA Ops:
  0.6 1.1 %copy-done.2 = bf16[8,384,128]{2,1,0:T(8,128)(2,1)S(1)} copy-done((bf16[8,384,128]{2,1,0:T(8,128)(2,1)S(1)}, bf16[8,384,128]{2,1,0:T(8,128)(2,1)}, u32[]{:S(2)}) %copy-start.2) | copy-done | bytes 786456
  1.9 3.4 %collective-permute-start.1 = (bf16[3,384,128]{2,1,0:T(8,128)(2,1)S(1)}, bf16[3,384,128]{2,1,0:T(8,128)(2,1)S(1)}, u32[]{:S(2)}, u32[]{:S(2)}) collective-permute-start(bf16[3,384,128]{2,1,0:T(8,128)(2,1)S(1)} %get-tuple-element.41), channel_id=1, source_target_pairs={{0,7},{1,6},{2,5},{3,4},{4,3},{5,2},{6,1},{7,0},{8,16},{9,17},{10,... | collective-permute-start | bytes 884744 | tf_op jit(solution)/shard_map/ppermute | solution.py:435
  5.3 1.3 %collective-permute-start = (bf16[3,384,128]{2,1,0:T(8,128)(2,1)S(1)}, bf16[3,384,128]{2,1,0:T(8,128)(2,1)S(1)}, u32[]{:S(2)}, u32[]{:S(2)}) collective-permute-start(bf16[3,384,128]{2,1,0:T(8,128)(2,1)S(1)} %get-tuple-element.40), channel_id=1, source_target_pairs={{0,8},{1,9},{2,10},{3,11},{4,12},{5,13},{6,14},{7,15},{8,0},{9,1},... | collective-permute-start | bytes 884744 | tf_op jit(solution)/shard_map/ppermute | solution.py:434
  6.6 5.5 %inner_conv.1 = (f32[8,384,128]{2,1,0:T(8,128)S(1)}, s32[48,128]{1,0:T(8,128)S(1)}, s32[48,128]{1,0:T(8,128)S(1)}) custom-call(bf16[8,384,128]{2,1,0:T(8,128)(2,1)S(1)} %copy-done.3, f32[49,128]{1,0:T(8,128)S(1)} %reshape.87.dw, f32[1,128]{1,0:T(1,128)S(1)} %bitcast.27, s32[48,128]{1,0:T(8,128)S(1)} %bitcast.23, s32[48,128]{1,0:T(8,128)S(1)} %bitcast.24), custom_call_target="tpu_custom_call" | custom-call | flops 7000000000 | tf_op jit(solution)/shard_map/inner_conv/pallas_call | solution.py:452
  12.2 1.2 %copy-done.17 = f32[8,384,128]{2,1,0:T(8,128)} copy-done((f32[8,384,128]{2,1,0:T(8,128)}, f32[8,384,128]{2,1,0:T(8,128)S(1)}, u32[]{:S(2)}) %copy-start.17) | copy-done | bytes 1572888
  13.6 1.2 %collective-permute-done = bf16[3,384,128]{2,1,0:T(8,128)(2,1)S(1)} collective-permute-done((bf16[3,384,128]{2,1,0:T(8,128)(2,1)S(1)}, bf16[3,384,128]{2,1,0:T(8,128)(2,1)S(1)}, u32[]{:S(2)}, u32[]{:S(2)}) %collective-permute-start) | collective-permute-done | bytes 294944 | tf_op jit(solution)/shard_map/ppermute | solution.py:434
  15.2 2.7 %collective-permute-start.3 = (bf16[14,3,128]{2,1,0:T(4,128)(2,1)S(1)}, bf16[14,3,128]{2,1,0:T(4,128)(2,1)S(1)}, u32[]{:S(2)}, u32[]{:S(2)}) collective-permute-start(bf16[14,3,128]{2,1,0:T(4,128)(2,1)S(1)} %pad_maximum_fusion.5), channel_id=1, source_target_pairs={{1,0},{2,1},{3,2},{4,3},{5,4},{6,5},{7,6},{0,7},{9,8},{10,9},{11,1... | collective-permute-start | bytes 32264 | tf_op jit(solution)/shard_map/ppermute | solution.py:443
  17.8 1.8 %halo_conv.1.halo = f32[6,384,128]{2,1,0:T(8,128)S(1)} custom-call(bf16[3,384,128]{2,1,0:T(8,128)(2,1)S(1)} %get-tuple-element.92.south, bf16[3,384,128]{2,1,0:T(8,128)(2,1)S(1)} %get-tuple-element.91.north, f32[49,128]{1,0:T(8,128)S(1)} %reshape.87.dw), custom_call_target="tpu_custom_call" | custom-call | flops 2000000000 | tf_op jit(solution)/shard_map/halo_conv/pallas_call | solution.py:464
  19.8 21.7 %block.1 = (bf16[8,384,128]{2,1,0:T(8,128)(2,1)}, f32[2048,128]{1,0:T(8,128)S(1)}, f32[2048,128]{1,0:T(8,128)S(1)}, f32[2048,128]{1,0:T(8,128)S(1)}, f32[2048,12...) custom-call(bf16[8,384,128]{2,1,0:T(8,128)(2,1)S(1)} %copy-done.3, ...), custom_call_target="tpu_custom_call" | custom-call | flops 28000000000 | tf_op jit(solution)/shard_map/block/pallas_call | solution.py:475
  41.6 6.2 %conv_grad.1 = f32[64,128]{1,0:T(8,128)S(1)} custom-call(bf16[8,384,128]{2,1,0:T(8,128)(2,1)S(1)} %copy-done.3, bf16[3,384,128]{2,1,0:T(8,128)(2,1)S(1)} %get-tuple-element.92.south, bf16[3,384,128]{2,1,0:T(8,128)(2,1)S(1)} %get-tuple-element.91.north, bf16[14,3,128]{2,1,0:T(4,128)(2,1)S(1)} %collective-permute-done.2.left, ...), custom_call_target="tpu_custom_call" | custom-call | flops 8999999488 | tf_op jit(solution)/shard_map/conv_grad/pallas_call | solution.py:514
  47.8 1.5 %add_convert_fusion = (bf16[2048,128]{1,0:T(8,128)(2,1)}, bf16[2048,128]{1,0:T(8,128)(2,1)}) fusion(f32[2048,128]{1,0:T(8,128)S(1)} %get-tuple-element.53, bf16[8192,128]{1,0:T(8,128)(2,1)S(1)} %collective-permute-done.4, f32[2048,128]{1,0:T(8,128)S(1)} %get-tuple-element.52), kind=kLoop, calls=%fused_computation | loop fusion | flops 1572864 | bytes 4194304 | tf_op jit(solution)/shard_map/convert_element_type | solution.py:529
  49.9 2.6 %collective-permute-start.5 = (bf16[2048,128]{1,0:T(8,128)(2,1)}, bf16[2048,128]{1,0:T(8,128)(2,1)}, u32[]{:S(2)}, u32[]{:S(2)}) collective-permute-start(bf16[2048,128]{1,0:T(8,128)(2,1)} %get-tuple-element.86), channel_id=1, source_target_pairs={{0,2},{1,3},{2,0},{3,1},{4,6},{5,7},{6,4},{7,5},{8,10},{9,11},{10,... | collective-permute-start | bytes 1572872 | tf_op jit(solution)/shard_map/ppermute | solution.py:389
  52.5 0.8 reshape.83
  53.3 4.4 %all-to-all-start = ((bf16[32,34,128]{2,1,0:T(8,128)(2,1)}), bf16[32,34,128]{2,1,0:T(8,128)(2,1)S(1)}, u32[]{:S(2)}, u32[]{:S(2)}) async-start(bf16[32,34,128]{2,1,0:T(8,128)(2,1)} %reshape.83), calls=%async_computation | async-start | bytes 655360 | tf_op jit(solution)/shard_map/all_to_all | solution.py:556
  57.7 8.3 %collective-permute-done.6 = bf16[2048,128]{1,0:T(8,128)(2,1)} collective-permute-done((bf16[2048,128]{1,0:T(8,128)(2,1)}, bf16[2048,128]{1,0:T(8,128)(2,1)}, u32[]{:S(2)}, u32[]{:S(2)}) %collective-permute-start.6) | collective-permute-done | bytes 524320 | tf_op jit(solution)/shard_map/ppermute | solution.py:389
  66.0 1.2 %collective-permute-done.5 = bf16[2048,128]{1,0:T(8,128)(2,1)} collective-permute-done((bf16[2048,128]{1,0:T(8,128)(2,1)}, bf16[2048,128]{1,0:T(8,128)(2,1)}, u32[]{:S(2)}, u32[]{:S(2)}) %collective-permute-start.5) | collective-permute-done | bytes 524320 | tf_op jit(solution)/shard_map/ppermute | solution.py:389
  67.2 2.4 %add_convert_fusion.2 = (bf16[1024,128]{1,0:T(8,128)(2,1)}, bf16[1024,128]{1,0:T(8,128)(2,1)}, f32[1024,128]{1,0:T(8,128)}, f32[1024,128]{1,0:T(8,128)}) fusion(f32[2048,128]{1,0:T(8,128)S(1)} %get-tuple-element.55, bf16[2048,128]{1,0:T(8,128)(2,1)} %collective-permute-done.6, bf16[8192,128]{1,0:T(8,128)(2,1)} %copy-done.19, ...), kind=kLoop, calls=%fused_computation.3 | loop fusion | flops 1310720 | bytes 4718592 | tf_op jit(solution)/shard_map/convert_element_type | solution.py:539
  69.6 1.9 %collective-permute-start.8 = (bf16[1024,128]{1,0:T(8,128)(2,1)}, bf16[1024,128]{1,0:T(8,128)(2,1)}, u32[]{:S(2)}, u32[]{:S(2)}) collective-permute-start(bf16[1024,128]{1,0:T(8,128)(2,1)} %get-tuple-element.83), channel_id=1, source_target_pairs={{0,2},{1,3},{2,0},{3,1},{4,6},{5,7},{6,4},{7,5},{8,10},{9,11},{10,... | collective-permute-start | bytes 786440 | tf_op jit(solution)/shard_map/ppermute | solution.py:389
  71.7 1.9 %fusion.2 = (bf16[1024,128]{1,0:T(8,128)(2,1)}, bf16[1024,128]{1,0:T(8,128)(2,1)}) fusion(bf16[8192,128]{1,0:T(8,128)(2,1)} %copy-done.19), kind=kLoop, calls=%fused_computation.25 | loop fusion | bytes 1048576 | tf_op jit(solution)/shard_map/slice | solution.py:540
  73.6 1.0 slice.232
  74.6 1.0 slice.235
  75.6 0.8 broadcast_in_dim.10
  76.4 5.9 %all-to-all-start.1 = ((bf16[32,34,128]{2,1,0:T(8,128)(2,1)}), bf16[32,34,128]{2,1,0:T(8,128)(2,1)S(1)}, u32[]{:S(2)}, u32[]{:S(2)}) async-start(bf16[32,34,128]{2,1,0:T(8,128)(2,1)} %broadcast_in_dim.10), calls=%async_computation.1 | async-start | bytes 655360 | tf_op jit(solution)/shard_map/all_to_all | solution.py:559
  82.4 1.2 %add_convert_fusion.4 = (bf16[256,128]{1,0:T(8,128)(2,1)S(1)}, bf16[256,128]{1,0:T(8,128)(2,1)S(1)}, bf16[256,128]{1,0:T(8,128)(2,1)S(1)}) fusion(f32[2048,128]{1,0:T(8,128)S(1)} %get-tuple-element.55, bf16[1024,128]{1,0:T(8,128)(2,1)} %collective-permute-done.8, bf16[2048,128]{1,0:T(8,128)(2,1)} %collective-permute-done.6, bf16[8192,128]{1,0:T(8,128)(2,1)} %copy-done.19), kind=kLoop, calls=%fused_computation.17 | loop fusion | flops 688128 | bytes 1179648 | tf_op jit(solution)/shard_map/convert.6
  83.6 1.2 %add_convert_fusion.5 = (bf16[256,128]{1,0:T(8,128)(2,1)S(1)}, bf16[256,128]{1,0:T(8,128)(2,1)S(1)}, bf16[256,128]{1,0:T(8,128)(2,1)S(1)}) fusion(f32[2048,128]{1,0:T(8,128)S(1)} %get-tuple-element.47, bf16[1024,128]{1,0:T(8,128)(2,1)} %collective-permute-done.7, bf16[2048,128]{1,0:T(8,128)(2,1)} %collective-permute-done.5, bf16[8192,128]{1,0:T(8,128)(2,1)} %copy-done.19), kind=kLoop, calls=%fused_computation.18 | loop fusion | flops 688128 | bytes 1179648 | tf_op jit(solution)/shard_map/convert.5
  84.8 1.8 %collective-permute-start.9 = (bf16[512,128]{1,0:T(8,128)(2,1)S(1)}, bf16[512,128]{1,0:T(8,128)(2,1)S(1)}, u32[]{:S(2)}, u32[]{:S(2)}) collective-permute-start(bf16[512,128]{1,0:T(8,128)(2,1)S(1)} %pad_maximum_fusion.1), channel_id=1, source_target_pairs={{0,8},{8,0},{16,24},{24,16},{1,9},{9,1},{17,25},{25,17},{2,10},{10... | collective-permute-start | bytes 393224 | tf_op jit(solution)/shard_map/ppermute | solution.py:549
  86.6 2.5 %collective-permute-start.10 = (bf16[512,128]{1,0:T(8,128)(2,1)S(1)}, bf16[512,128]{1,0:T(8,128)(2,1)S(1)}, u32[]{:S(2)}, u32[]{:S(2)}) collective-permute-start(bf16[512,128]{1,0:T(8,128)(2,1)S(1)} %pad_maximum_fusion.2), channel_id=1, source_target_pairs={{0,16},{8,24},{16,0},{24,8},{1,17},{9,25},{17,1},{25,9},{2,18},{10... | collective-permute-start | bytes 393224 | tf_op jit(solution)/shard_map/ppermute | solution.py:549
  89.4 1.0 convert_add_fusion.1
  90.4 1.0 convert_add_fusion
  91.3 2.8 %all-to-all-done.1 = bf16[32,34,128]{2,1,0:T(8,128)(2,1)S(1)} async-done(((bf16[32,34,128]{2,1,0:T(8,128)(2,1)}), bf16[32,34,128]{2,1,0:T(8,128)(2,1)S(1)}, u32[]{:S(2)}, u32[]{:S(2)}) %all-to-all-start.1) | async-done | bytes 278560 | tf_op jit(solution)/shard_map/all_to_all | solution.py:559
  96.3 5.7 %collective-permute-done.10 = bf16[512,128]{1,0:T(8,128)(2,1)S(1)} collective-permute-done((bf16[512,128]{1,0:T(8,128)(2,1)S(1)}, bf16[512,128]{1,0:T(8,128)(2,1)S(1)}, u32[]{:S(2)}, u32[]{:S(2)}) %collective-permute-start.10) | collective-permute-done | bytes 131104 | tf_op jit(solution)/shard_map/ppermute | solution.py:549
  102.0 0.8 fusion.1
  (76 shorter events, 4.0 us)
Async XLA Ops:
  1.8 4.8 %copy-start.20 = (bf16[7,7,128]{2,1,0:T(8,128)(2,1)S(1)}, bf16[7,7,128]{2,1,0:T(8,128)(2,1)}, u32[]{:S(2)}) copy-start(bf16[7,7,128]{2,1,0:T(8,128)(2,1)} %param.21) | copy-start | bytes 37636
  1.8 4.8 %copy-start.3 = (bf16[8,384,128]{2,1,0:T(8,128)(2,1)S(1)}, bf16[8,384,128]{2,1,0:T(8,128)(2,1)}, u32[]{:S(2)}) copy-start(bf16[8,384,128]{2,1,0:T(8,128)(2,1)} %state.6) | copy-start | bytes 2359300
  1.8 4.8 %copy-start.6 = (s32[6144,1]{0,1:T(1,128)S(1)}, s32[6144,1]{0,1:T(1,128)}, u32[]{:S(2)}) copy-start(s32[6144,1]{0,1:T(1,128)} %param.30) | copy-start | bytes 73732
  1.8 4.8 %copy-start.7 = (s32[6144]{0:T(1024)S(1)}, s32[6144]{0:T(1024)}, u32[]{:S(2)}) copy-start(s32[6144]{0:T(1024)} %param.31) | copy-start | bytes 73732
  1.8 4.8 %copy-start.11 = (f32[128]{0:T(128)S(1)}, f32[128]{0:T(128)}, u32[]{:S(2)}) copy-start(f32[128]{0:T(128)} %param.22) | copy-start | bytes 1540
  1.9 11.8 %collective-permute-start.1 = (bf16[3,384,128]{2,1,0:T(8,128)(2,1)S(1)}, bf16[3,384,128]{2,1,0:T(8,128)(2,1)S(1)}, u32[]{:S(2)}, u32[]{:S(2)}) collective-permute-start(bf16[3,384,128]{2,1,0:T(8,128)(2,1)S(1)} %get-tuple-element.41), channel_id=1, source_target_pairs={{0,7},{1,6},{2,5},{3,4},{4,3},{5,2},{6,1},{7,0},{8,16},{9,17},{10,... | collective-permute-start | bytes 884744 | tf_op jit(solution)/shard_map/ppermute | solution.py:435
  5.3 9.6 %collective-permute-start = (bf16[3,384,128]{2,1,0:T(8,128)(2,1)S(1)}, bf16[3,384,128]{2,1,0:T(8,128)(2,1)S(1)}, u32[]{:S(2)}, u32[]{:S(2)}) collective-permute-start(bf16[3,384,128]{2,1,0:T(8,128)(2,1)S(1)} %get-tuple-element.40), channel_id=1, source_target_pairs={{0,8},{1,9},{2,10},{3,11},{4,12},{5,13},{6,14},{7,15},{8,0},{9,1},... | collective-permute-start | bytes 884744 | tf_op jit(solution)/shard_map/ppermute | solution.py:434
  6.6 6.8 %copy-start = (bf16[128,512]{1,0:T(8,128)(2,1)S(1)}, bf16[128,512]{1,0:T(8,128)(2,1)}, u32[]{:S(2)}) copy-start(bf16[128,512]{1,0:T(8,128)(2,1)} %up.1) | copy-start | bytes 393220
  6.6 6.9 %copy-start.1 = (bf16[512,128]{1,0:T(8,128)(2,1)S(1)}, bf16[512,128]{1,0:T(8,128)(2,1)}, u32[]{:S(2)}) copy-start(bf16[512,128]{1,0:T(8,128)(2,1)} %down.1) | copy-start | bytes 393220
  14.9 4.7 %collective-permute-start.2 = (bf16[14,3,128]{2,1,0:T(4,128)(2,1)S(1)}, bf16[14,3,128]{2,1,0:T(4,128)(2,1)S(1)}, u32[]{:S(2)}, u32[]{:S(2)}) collective-permute-start(bf16[14,3,128]{2,1,0:T(4,128)(2,1)S(1)} %pad_maximum_fusion.4), channel_id=1, source_target_pairs={{0,1},{1,2},{2,3},{3,4},{4,5},{5,6},{6,7},{7,0},{8,9},{9,10},{10,1... | collective-permute-start | bytes 32264 | tf_op jit(solution)/shard_map/ppermute | solution.py:442
  15.0 4.6 %copy-start.4 = (bf16[8,384,128]{2,1,0:T(8,128)(2,1)S(1)}, bf16[8,384,128]{2,1,0:T(8,128)(2,1)}, u32[]{:S(2)}) copy-start(bf16[8,384,128]{2,1,0:T(8,128)(2,1)} %forcing.1) | copy-start | bytes 2359300
  15.0 4.6 %copy-start.5 = (bf16[8,384,128]{2,1,0:T(8,128)(2,1)S(1)}, bf16[8,384,128]{2,1,0:T(8,128)(2,1)}, u32[]{:S(2)}) copy-start(bf16[8,384,128]{2,1,0:T(8,128)(2,1)} %cotangent.1) | copy-start | bytes 2359300
  15.1 4.6 %copy-start.8 = (s32[6144]{0:T(1024)S(1)}, s32[6144]{0:T(1024)}, u32[]{:S(2)}) copy-start(s32[6144]{0:T(1024)} %param.32) | copy-start | bytes 73732
  15.1 4.6 %copy-start.9 = (s32[8,384]{1,0:T(8,128)S(1)}, s32[8,384]{1,0:T(8,128)}, u32[]{:S(2)}) copy-start(s32[8,384]{1,0:T(8,128)} %land.1) | copy-start | bytes 36868
  15.1 4.6 %copy-start.10 = (f32[512]{0:T(512)S(1)}, f32[512]{0:T(512)}, u32[]{:S(2)}) copy-start(f32[512]{0:T(512)} %param.26) | copy-start | bytes 6148
  15.1 4.6 %copy-start.12 = (f32[16]{0:T(128)S(1)}, f32[16]{0:T(128)}, u32[]{:S(2)}) copy-start(f32[16]{0:T(128)} %weight_table.1) | copy-start | bytes 196
  15.1 4.6 %copy-start.13 = (f32[128]{0:T(128)S(1)}, f32[128]{0:T(128)}, u32[]{:S(2)}) copy-start(f32[128]{0:T(128)} %param.23) | copy-start | bytes 1540
  15.1 4.6 %copy-start.14 = (f32[128]{0:T(128)S(1)}, f32[128]{0:T(128)}, u32[]{:S(2)}) copy-start(f32[128]{0:T(128)} %param.24) | copy-start | bytes 1540
  15.1 4.6 %copy-start.15 = (f32[128]{0:T(128)S(1)}, f32[128]{0:T(128)}, u32[]{:S(2)}) copy-start(f32[128]{0:T(128)} %param.28) | copy-start | bytes 1540
  15.1 4.6 %copy-start.16 = (f32[128]{0:T(128)S(1)}, f32[128]{0:T(128)}, u32[]{:S(2)}) copy-start(f32[128]{0:T(128)} %param.29) | copy-start | bytes 1540
  15.1 4.6 %copy-start.18 = (f32[8,384,128]{2,1,0:T(8,128)S(1)}, f32[8,384,128]{2,1,0:T(8,128)}, u32[]{:S(2)}) copy-start(f32[8,384,128]{2,1,0:T(8,128)} %copy-done.17) | copy-start | bytes 4718596
  15.2 4.5 %collective-permute-start.3 = (bf16[14,3,128]{2,1,0:T(4,128)(2,1)S(1)}, bf16[14,3,128]{2,1,0:T(4,128)(2,1)S(1)}, u32[]{:S(2)}, u32[]{:S(2)}) collective-permute-start(bf16[14,3,128]{2,1,0:T(4,128)(2,1)S(1)} %pad_maximum_fusion.5), channel_id=1, source_target_pairs={{1,0},{2,1},{3,2},{4,3},{5,4},{6,5},{7,6},{0,7},{9,8},{10,9},{11,1... | collective-permute-start | bytes 32264 | tf_op jit(solution)/shard_map/ppermute | solution.py:443
  41.5 6.3 %collective-permute-start.4 = (bf16[8192,128]{1,0:T(8,128)(2,1)S(1)}, bf16[8192,128]{1,0:T(8,128)(2,1)S(1)}, u32[]{:S(2)}, u32[]{:S(2)}) collective-permute-start(bf16[8192,128]{1,0:T(8,128)(2,1)S(1)} %get-tuple-element.48), channel_id=1, source_target_pairs={{0,1},{1,0},{2,3},{3,2},{4,5},{5,4},{6,7},{7,6},{8,9},{9,8},{10,11... | collective-permute-start | bytes 6291464 | tf_op jit(solution)/shard_map/ppermute | solution.py:389
  49.5 16.5 %collective-permute-start.6 = (bf16[2048,128]{1,0:T(8,128)(2,1)}, bf16[2048,128]{1,0:T(8,128)(2,1)}, u32[]{:S(2)}, u32[]{:S(2)}) collective-permute-start(bf16[2048,128]{1,0:T(8,128)(2,1)} %get-tuple-element.85), channel_id=1, source_target_pairs={{0,4},{1,5},{2,6},{3,7},{4,0},{5,1},{6,2},{7,3},{8,12},{9,13},{10,... | collective-permute-start | bytes 1572872 | tf_op jit(solution)/shard_map/ppermute | solution.py:389
  49.9 17.4 %collective-permute-start.5 = (bf16[2048,128]{1,0:T(8,128)(2,1)}, bf16[2048,128]{1,0:T(8,128)(2,1)}, u32[]{:S(2)}, u32[]{:S(2)}) collective-permute-start(bf16[2048,128]{1,0:T(8,128)(2,1)} %get-tuple-element.86), channel_id=1, source_target_pairs={{0,2},{1,3},{2,0},{3,1},{4,6},{5,7},{6,4},{7,5},{8,10},{9,11},{10,... | collective-permute-start | bytes 1572872 | tf_op jit(solution)/shard_map/ppermute | solution.py:389
  53.3 22.2 %all-to-all-start = ((bf16[32,34,128]{2,1,0:T(8,128)(2,1)}), bf16[32,34,128]{2,1,0:T(8,128)(2,1)S(1)}, u32[]{:S(2)}, u32[]{:S(2)}) async-start(bf16[32,34,128]{2,1,0:T(8,128)(2,1)} %reshape.83), calls=%async_computation | async-start | bytes 655360 | tf_op jit(solution)/shard_map/all_to_all | solution.py:556
  69.6 12.7 %collective-permute-start.8 = (bf16[1024,128]{1,0:T(8,128)(2,1)}, bf16[1024,128]{1,0:T(8,128)(2,1)}, u32[]{:S(2)}, u32[]{:S(2)}) collective-permute-start(bf16[1024,128]{1,0:T(8,128)(2,1)} %get-tuple-element.83), channel_id=1, source_target_pairs={{0,2},{1,3},{2,0},{3,1},{4,6},{5,7},{6,4},{7,5},{8,10},{9,11},{10,... | collective-permute-start | bytes 786440 | tf_op jit(solution)/shard_map/ppermute | solution.py:389
  71.6 10.8 %collective-permute-start.7 = (bf16[1024,128]{1,0:T(8,128)(2,1)}, bf16[1024,128]{1,0:T(8,128)(2,1)}, u32[]{:S(2)}, u32[]{:S(2)}) collective-permute-start(bf16[1024,128]{1,0:T(8,128)(2,1)} %get-tuple-element.84), channel_id=1, source_target_pairs={{0,4},{1,5},{2,6},{3,7},{4,0},{5,1},{6,2},{7,3},{8,12},{9,13},{10,... | collective-permute-start | bytes 786440 | tf_op jit(solution)/shard_map/ppermute | solution.py:389
  76.4 17.7 %all-to-all-start.1 = ((bf16[32,34,128]{2,1,0:T(8,128)(2,1)}), bf16[32,34,128]{2,1,0:T(8,128)(2,1)S(1)}, u32[]{:S(2)}, u32[]{:S(2)}) async-start(bf16[32,34,128]{2,1,0:T(8,128)(2,1)} %broadcast_in_dim.10), calls=%async_computation.1 | async-start | bytes 655360 | tf_op jit(solution)/shard_map/all_to_all | solution.py:559
  84.8 11.6 %collective-permute-start.9 = (bf16[512,128]{1,0:T(8,128)(2,1)S(1)}, bf16[512,128]{1,0:T(8,128)(2,1)S(1)}, u32[]{:S(2)}, u32[]{:S(2)}) collective-permute-start(bf16[512,128]{1,0:T(8,128)(2,1)S(1)} %pad_maximum_fusion.1), channel_id=1, source_target_pairs={{0,8},{8,0},{16,24},{24,16},{1,9},{9,1},{17,25},{25,17},{2,10},{10... | collective-permute-start | bytes 393224 | tf_op jit(solution)/shard_map/ppermute | solution.py:549
  86.6 15.4 %collective-permute-start.10 = (bf16[512,128]{1,0:T(8,128)(2,1)S(1)}, bf16[512,128]{1,0:T(8,128)(2,1)S(1)}, u32[]{:S(2)}, u32[]{:S(2)}) collective-permute-start(bf16[512,128]{1,0:T(8,128)(2,1)S(1)} %pad_maximum_fusion.2), channel_id=1, source_target_pairs={{0,16},{8,24},{16,0},{24,8},{1,17},{9,25},{17,1},{25,9},{2,18},{10... | collective-permute-start | bytes 393224 | tf_op jit(solution)/shard_map/ppermute | solution.py:549
  89.1 12.9 %collective-permute-start.11 = (bf16[512,128]{1,0:T(8,128)(2,1)S(1)}, bf16[512,128]{1,0:T(8,128)(2,1)S(1)}, u32[]{:S(2)}, u32[]{:S(2)}) collective-permute-start(bf16[512,128]{1,0:T(8,128)(2,1)S(1)} %pad_maximum_fusion.3), channel_id=1, source_target_pairs={{0,24},{8,16},{16,8},{24,0},{1,25},{9,17},{17,9},{25,1},{2,26},{10... | collective-permute-start | bytes 393224 | tf_op jit(solution)/shard_map/ppermute | solution.py:549
  (3 other events, 4.1 us)
